TPU v7x, 32 devices: a whole 2x2x4 slice. The times are simulated.
32 devices in a mesh: row: 8 (over y, x, core), col: 4 (over z).
Axes of the slice: x: 2, y: 2, z: 4, core: 2. Of those that a mesh axis runs over, the one named last changes fastest.
Arguments:
- weight: bfloat16 [8192, 24576], P('row', 'col'), may hold values from -6 to 6
- gradient: bfloat16 [8192, 24576], P('row', 'col'), may hold values from -80 to 80
- momentum: float32 [8192, 24576], P('row', 'col'), may hold values from -6 to 6
- old_basis: bfloat16 [256, 24576], P(None, 'col'), may hold values from -6 to 6
Outputs:
- new_weight: bfloat16 [8192, 24576], P('row', 'col')
- new_momentum: float32 [8192, 24576], P('row', 'col')
- new_basis: bfloat16 [256, 24576], P(None, 'col')
All inputs are finite; a program needn't handle non-finite values.
Results may differ from a plain program's by a relative error of at most 0.0056.
Values may be sent and summed in bfloat16 or wider, within the bound.
No kernel may reach another device: no remote copies, remote signals or barrier semaphores. Data moves between devices by JAX's collectives and lax.ppermute only.
A program may use at most 192 MiB of HBM per device.

v0:
```python
import math

import jax
import jax.numpy as jnp
from jax import lax
from jax.sharding import PartitionSpec as P

D = 8192
FF = 24576
RANK = 256


epsilon = 1e-06
momentum_decay = 0.6
step_rate = 0.5


def orthonormalize(left_rows, gram_matrix):
    chol_factor = jnp.linalg.cholesky(gram_matrix)
    return lax.linalg.triangular_solve(
        chol_factor, left_rows, left_side=False, lower=True, transpose_a=True
    ).astype(jnp.bfloat16)


def gram_of(left_rows):
    return lax.dot_general(
        left_rows,
        left_rows,
        (((0,), (0,)), ((), ())),
        precision=lax.Precision.HIGHEST,
        preferred_element_type=jnp.float32,
    )


def per_device(weight, gradient, momentum, old_basis):
    buffer = momentum + gradient.astype(jnp.float32)
    buffer_low = buffer.astype(jnp.bfloat16)
    local_left = lax.dot_general(
        buffer_low, old_basis, (((1,), (1,)), ((), ())), preferred_element_type=jnp.float32
    )
    left_factor = lax.psum(local_left, "col")
    gram_matrix = lax.psum(gram_of(left_factor), "row")
    orthonormal = orthonormalize(left_factor, gram_matrix)
    right_share = lax.psum_scatter(
        lax.dot_general(
            orthonormal, buffer_low, (((0,), (0,)), ((), ())), preferred_element_type=jnp.float32
        ),
        "row",
        scatter_dimension=0,
        tiled=True,
    )
    sum_squares = lax.psum(jnp.sum(right_share * right_share, axis=1), "col")
    scale_share = jnp.sqrt(sum_squares / FF + epsilon)
    basis_share = (right_share / scale_share[:, None]).astype(jnp.bfloat16)
    new_basis = lax.all_gather(basis_share, "row", axis=0, tiled=True)
    col_scale = lax.all_gather(scale_share, "row", axis=0, tiled=True)
    scaled = (orthonormal.astype(jnp.float32) * col_scale[None, :]).astype(jnp.bfloat16)
    correction = jnp.dot(scaled, new_basis, preferred_element_type=jnp.float32)
    change = jnp.dot(orthonormal, new_basis, preferred_element_type=jnp.float32)
    new_momentum = buffer - (1.0 - momentum_decay) * correction
    factor = step_rate * math.sqrt(D / RANK)
    new_weight = (weight.astype(jnp.float32) - factor * change).astype(jnp.bfloat16)
    return (new_weight, new_momentum, new_basis)


def solution(mesh):
    return jax.shard_map(
        per_device,
        mesh=mesh,
        in_specs=(P("row", "col"), P("row", "col"), P("row", "col"), P(None, "col")),
        out_specs=(P("row", "col"), P("row", "col"), P(None, "col")),
        check_vma=False,
    )
```

profile of v0, /device:TPU:0, one launch (start us, length us, event | category | flops | bytes accessed | tf_op | source)
XLA Modules:
  0.0 376.3 jit_solution(7399516804229239195)
XLA Ops:
  7.2 0.0 copy-start
  7.2 0.0 all-reduce.5.cloned.1.call-start
  7.2 1.8 copy-done
  9.1 16.2 %fusion.15 = f32[1024,256]{1,0:T(8,128)} fusion(bf16[256,6144]{1,0:T(8,128)(2,1)S(1)} %copy-done, f32[1024,6144]{1,0:T(8,128)} %param.6, bf16[1024,6144]{1,0:T(8,128)(2,1)} %param.5), kind=kOutput, calls=%fused_computation.42 | convolution fusion | flops 3240099840 | bytes 41943040 | tf_op jit(solution)/shard_map/dot_general | solution.py:38
  25.2 0.0 all-reduce.5.cloned.1.call-update
  25.2 0.0 all-reduce.7.cloned.1.call-start
  25.3 54.6 %all-reduce.5.cloned.1.call-done = f32[1024,256]{1,0:T(8,128)} async-done(((f32[1024,256]{1,0:T(8,128)}), f32[1024,256]{1,0:T(8,128)}) %all-reduce.5.cloned.1.call-update) | async-done | bytes 1048592 | tf_op jit(solution)/shard_map/psum | solution.py:41
  79.9 4.1 %fusion.19 = f32[256,256]{0,1:T(8,128)} fusion(f32[1024,256]{1,0:T(8,128)} %all-reduce.5.cloned.1.call-done), kind=kOutput, calls=%fused_computation.45 | convolution fusion | flops 805306368 | bytes 1310720 | tf_op jit(solution)/shard_map/dot_general | solution.py:26
  84.0 0.0 all-reduce.7.cloned.1.call-update
  84.0 0.2 reduce-scatter.2.cloned.1.call-start
  84.3 52.8 %all-reduce.7.cloned.1.call-done = f32[256,256]{0,1:T(8,128)} async-done(((f32[256,256]{0,1:T(8,128)}), f32[256,256]{0,1:T(8,128)}) %all-reduce.7.cloned.1.call-update) | async-done | bytes 262160 | tf_op jit(solution)/shard_map/psum | solution.py:42
  137.1 1.1 copy.8
  138.2 1.0 fusion.4
  139.2 11.7 %cholesky.50 = f32[128,128]{1,0:T(8,128)S(1)} custom-call(f32[128,128]{1,0:T(8,128)S(1)} %cholesky.118), custom_call_target="Cholesky" | custom-call | tf_op jit(solution)/shard_map/jit(cholesky)/cholesky | solution.py:19
  150.9 9.8 %custom-call.14 = f32[1,128,128]{1,2,0:T(8,128)S(1)} custom-call(f32[1,128,128]{2,1,0:T(8,128)S(1)} %get-tuple-element.24), custom_call_target="InvertDiagBlocksLowerTriangular" | custom-call | tf_op jit(solution)/shard_map/jit(cholesky)/cholesky | solution.py:19
  160.8 0.2 constant_dynamic-update-slice_fusion.1
  161.0 0.3 convolution_subtract_fusion.1
  161.2 11.7 %cholesky.105 = f32[128,128]{1,0:T(8,128)S(1)} custom-call(f32[128,128]{1,0:T(8,128)S(1)} %convolution_subtract_fusion.1), custom_call_target="Cholesky" | custom-call | tf_op jit(solution)/shard_map/jit(cholesky)/cholesky | solution.py:19
  173.0 0.6 compare_reduce_fusion
  175.0 0.1 triangular_solve.58
  175.1 4.2 %while.1 = (s32[]{:T(128)}, f32[256,256]{1,0:T(8,128)S(1)}, s32[2,2]{1,0:T(2,128)S(1)}, f32[2,128,128]{2,1,0:T(8,128)S(1)}, s32[]{:T(128)}) while((s32[]{:T(128)}, f32[256,256]{1,0:T(8,128)S(1)}, s32[2,2]{1,0:T(2,128)S(1)}, f32[2,128,128]{2,1,0:T(8,128)S(1)}, s32[]{:T(128)}) %tuple.29), condition=%wide.while_cond, body=%wide.while_body.sunk | while | flops 2 | bytes 131181 | solution.py:20
  175.2 0.6 fusion.30
  175.8 1.4 bitcast_dynamic-update-slice_fusion.2
  177.2 0.6 fusion.30
  177.8 1.4 bitcast_dynamic-update-slice_fusion.2
  179.2 19.7 %custom-call.15 = f32[2,128,128]{1,2,0:T(8,128)S(1)} custom-call(f32[2,128,128]{2,1,0:T(8,128)S(1)} %get-tuple-element.10), custom_call_target="InvertDiagBlocksLowerTriangular" | custom-call | tf_op jit(solution)/shard_map/triangular_solve | solution.py:20
  198.9 1.7 fusion.18
  200.6 0.0 copy-start.2
  200.6 2.1 convolution_subtract_fusion
  202.7 0.6 convolution_convert_fusion
  203.3 0.0 copy-start.3
  203.4 18.0 %fusion.5 = f32[256,6144]{1,0:T(8,128)} fusion(bf16[1024,128]{0,1:T(8,128)(2,1)S(1)} %convolution_convert_fusion, bf16[1024,128]{0,1:T(8,128)(2,1)S(1)} %get-tuple-element.29, f32[1024,6144]{1,0:T(8,128)} %param.6, bf16[1024,6144]{1,0:T(8,128)(2,1)} %param.5), kind=kOutput, calls=%fused_computation.20 | convolution fusion | flops 3241148416 | bytes 44564480 | tf_op jit(solution)/shard_map/dot_general | solution.py:45
  221.3 0.0 reduce-scatter.2.cloned.1.call-update
  221.3 0.0 all-gather.2.cloned.1.call-start
  221.4 0.0 copy-done.3
  221.4 0.6 dynamic-slice.3
  222.6 60.0 %reduce-scatter.2.cloned.1.call-done = f32[32,6144]{1,0:T(8,128)} async-done(((f32[256,6144]{1,0:T(8,128)}), f32[32,6144]{1,0:T(8,128)}) %reduce-scatter.2.cloned.1.call-update) | async-done | bytes 786448 | tf_op jit(solution)/shard_map/reduce_scatter | solution.py:44
  282.6 1.3 multiply_reduce_fusion
  283.9 11.7 %psum.23 = f32[32]{0:T(128)S(1)} all-reduce(f32[32]{0:T(128)S(1)} %multiply_reduce_fusion), channel_id=1, replica_groups=mesh['row'=8,'col'=4] {'col'}, use_global_device_ids=true, to_apply=%region_8.9 | all-reduce | flops 32 | bytes 256 | tf_op jit(solution)/shard_map/psum | solution.py:52
  295.6 0.1 fusion.13
  295.7 2.0 divide_convert_fusion
  297.7 0.0 all-gather.2.cloned.1.call-update
  297.7 12.2 %all-reduce.1 = f32[256]{0:T(256)S(1)} all-reduce(f32[256]{0:T(256)S(1)} %get-tuple-element.25), channel_id=1, replica_groups=mesh['row'=8,'col'=4] {'row'}, use_global_device_ids=true, to_apply=%add.1 | all-reduce | flops 256 | bytes 2048
  309.9 17.5 %all-gather.2.cloned.1.call-done = bf16[256,6144]{1,0:T(8,128)(2,1)} async-done(((bf16[32,6144]{1,0:T(8,128)(2,1)}), bf16[256,6144]{1,0:T(8,128)(2,1)}) %all-gather.2.cloned.1.call-update) | async-done | bytes 3145744 | tf_op jit(solution)/shard_map/all_gather | solution.py:55
  327.4 24.6 %multiply_subtract_fusion = f32[1024,6144]{1,0:T(8,128)} fusion(f32[1024,6144]{1,0:T(8,128)} %param.6, bf16[1024,6144]{1,0:T(8,128)(2,1)} %param.5, bf16[256,6144]{1,0:T(8,128)(2,1)} %all-gather.2.cloned.1.call-done, f32[256]{0:T(256)S(1)} %all-reduce.1, bf16[1024,128]{0,1:T(8,128)(2,1)S(1)} %convolution_convert_fusion, bf16[1024,128]{0,1:T(8,128)(2,1)} %copy-done.2), kind=kOutput, calls=%fused_computation.2 | convolution fusion | flops 3247964160 | bytes 66585600 | tf_op jit(solution)/shard_map/dot_general | solution.py:58
  352.1 13.9 %subtract_convert_fusion = bf16[1024,6144]{1,0:T(8,128)(2,1)} fusion(bf16[1024,6144]{1,0:T(8,128)(2,1)} %param.4, bf16[256,6144]{1,0:T(8,128)(2,1)} %all-gather.2.cloned.1.call-done, bf16[1024,128]{0,1:T(8,128)(2,1)S(1)} %convolution_convert_fusion, bf16[1024,128]{0,1:T(8,128)(2,1)} %copy-done.2), kind=kOutput, calls=%fused_computation.3 | convolution fusion | flops 3247439872 | bytes 28835840 | tf_op jit(solution)/shard_map/dot_general | solution.py:59
  365.9 3.9 %copy.25 = bf16[256,6144]{1,0:T(8,128)(2,1)} copy(bf16[256,6144]{1,0:T(8,128)(2,1)} %all-gather.2.cloned.1.call-done) | data formatting | bytes 6291456
  369.8 0.0 copy-done.1
  (12 shorter events, 0.2 us)
Async XLA Ops:
  7.2 1.9 copy-start
  7.2 72.7 %all-reduce.5.cloned.1.call-start = ((), (), s32[]{:S(2)}) async-start(), calls=%async_computation.1 | async-start | bytes 2097152 | tf_op jit(solution)/shard_map/psum | solution.py:41
  25.2 111.8 %all-reduce.7.cloned.1.call-start = ((), (), s32[]{:S(2)}) async-start(), calls=%async_computation.2 | async-start | bytes 524288 | tf_op jit(solution)/shard_map/psum | solution.py:42
  84.0 198.6 %reduce-scatter.2.cloned.1.call-start = ((), (), s32[]{:S(2)}) async-start(), calls=%async_computation.3 | async-start | bytes 7077888 | tf_op jit(solution)/shard_map/reduce_scatter | solution.py:44
  200.6 20.7 %copy-start.2 = (bf16[1024,128]{0,1:T(8,128)(2,1)}, bf16[1024,128]{0,1:T(8,128)(2,1)S(1)}, u32[]{:S(2)}) copy-start(bf16[1024,128]{0,1:T(8,128)(2,1)S(1)} %get-tuple-element.29) | copy-start | bytes 786436
  203.3 18.1 %copy-start.3 = (u32[32]{0:T(128)S(1)}, u32[32]{0:T(128)}, u32[]{:S(2)}) copy-start(u32[32]{0:T(128)} %constant.105) | copy-start | bytes 388
  221.3 106.1 %all-gather.2.cloned.1.call-start = ((), (), s32[]{:S(2)}) async-start(), calls=%async_computation.4 | async-start | bytes 3538944 | tf_op jit(solution)/shard_map/all_gather | solution.py:55
  327.4 42.4 %copy-start.1 = (bf16[256,6144]{1,0:T(8,128)(2,1)S(1)}, bf16[256,6144]{1,0:T(8,128)(2,1)}, u32[]{:S(2)}) copy-start(bf16[256,6144]{1,0:T(8,128)(2,1)} %param.7) | copy-start | bytes 9437188
Sparse Core Ops, SparseCore 0:
  25.4 54.5 all-reduce.4
  84.1 52.9 all-reduce.6
  221.5 61.0 reduce-scatter.1
  297.8 29.5 all-gather.1
where the time goes:
time: 377 us; the launch traced here: 376 us
  waiting for transfers between devices  185 us (49%)
  matrix products  81.6 us (22%)
  other arithmetic  58 us (15%)
  blocking collectives  23.9 us (6%)
  between operations  15.9 us (4%)
  local copies, waits for them, and re-layouts  11.4 us (3%)
    reduce_scatter x1, waiting for transfers between devices, per_device(): lax.psum_scatter(lax.dot_general(orthonormal, buffer_low, (((0,), (0,)),...  60 us
    psum x1, waiting for transfers between devices, per_device(): left_factor = lax.psum(local_left, 'col')  54.6 us
    psum x1, waiting for transfers between devices, per_device(): gram_matrix = lax.psum(gram_of(left_factor), 'row')  52.8 us
    another operation x6, other arithmetic, orthonormalize(): chol_factor = jnp.linalg.cholesky(gram_matrix)  34 us
    dot_general x1, matrix products, per_device(): correction = jnp.dot(scaled, new_basis, preferred_element_type=jnp.float32)  24.6 us
    another operation x3, other arithmetic, orthonormalize(): lax.linalg.triangular_solve(chol_factor, left_rows, left_side=False, lowe...  19.7 us
    dot_general x1, matrix products, per_device(): lax.dot_general(orthonormal, buffer_low, (((0,), (0,)), ((), ())), prefer...  18 us
    all_gather x1, waiting for transfers between devices, per_device(): new_basis = lax.all_gather(basis_share, 'row', axis=0, tiled=True)  17.5 us
  transfers between devices with their start and end apart: 4, of which 4 were waited for; matrix products, arithmetic and copies ran while one was open for 0% of the time, Pallas kernels for 0%

commit v1 on v0

v1 whole, which is shorter than its diff:
```python
import functools
import math

import jax
import jax.numpy as jnp
from jax import lax
from jax.experimental import pallas as pl
from jax.experimental.pallas import tpu as pltpu
from jax.sharding import PartitionSpec as P

D = 8192
FF = 24576
RANK = 256

epsilon = 1e-06
momentum_decay = 0.6
step_rate = 0.5

bf16, f32 = jnp.bfloat16, jnp.float32
VMEM = pl.BlockSpec(memory_space=pltpu.VMEM)
ANY = pl.BlockSpec(memory_space=pl.ANY)
MIB = 1 << 20


def shape(dims, kind):
    return jax.ShapeDtypeStruct(dims, kind)


def params(mib):
    return pltpu.CompilerParams(vmem_limit_bytes=mib * MIB)


def dot(a, b, dims=((1,), (0,))):
    return lax.dot_general(a, b, (dims, ((), ())), preferred_element_type=f32)


def split(x, terms):
    parts = []
    for _ in range(terms):
        part = x.astype(bf16)
        parts.append(part)
        x = x - part.astype(f32)
    return parts


def flip(i, d):
    return lax.bitwise_xor(i, jnp.int32(d))


def swap(x, axis, d):
    return lax.ppermute(x, axis, [(i, i ^ d) for i in range(lax.axis_size(axis))])


def project_kernel(mom, grad, basis, buf, *rest):
    parts = len(rest) - 2
    lefts, gbuf, sems = rest[:parts], rest[parts], rest[parts + 1]
    m, n = buf.shape
    block = m // parts
    tile = min(128, block)
    me = lax.axis_index("col")
    chunk = 1536 if n % 1536 == 0 else n

    def copies(d, i):
        rows = pl.ds(pl.multiple_of(flip(me, d) * block + i * tile, tile), tile)
        k = d * (block // tile) + i
        return (
            pltpu.make_async_copy(mom.at[rows, :], buf.at[rows, :], sems.at[0, k]),
            pltpu.make_async_copy(grad.at[rows, :], gbuf.at[rows, :], sems.at[1, k]),
        )

    order = [(d, i) for d in reversed(range(parts)) for i in range(block // tile)]
    for d, i in order:
        for copy in copies(d, i):
            copy.start()
    for d, i in order:
        for copy in copies(d, i):
            copy.wait()
        rows = pl.ds(pl.multiple_of(flip(me, d) * block + i * tile, tile), tile)

        def step(k, acc):
            cols = pl.ds(pl.multiple_of(k * chunk, 128), chunk)
            total = buf[rows, cols] + gbuf[rows, cols].astype(f32)
            buf[rows, cols] = total
            return acc + dot(basis[:, cols], total.astype(bf16), ((1,), (1,)))

        acc = lax.fori_loop(0, n // chunk, step, jnp.zeros((basis.shape[0], tile), f32))
        lefts[d][:, i * tile : (i + 1) * tile] = acc.astype(lefts[d].dtype)


def project(momentum, gradient, basis, parts):
    m, n = momentum.shape
    r = basis.shape[0]
    block = m // parts
    kinds = [f32] + [bf16] * (parts - 1)
    return pl.pallas_call(
        project_kernel,
        out_shape=(pltpu.VMEM((m, n), f32), *[shape((r, block), k) for k in kinds]),
        in_specs=[ANY, ANY, VMEM],
        out_specs=(VMEM,) * (parts + 1),
        scratch_shapes=[
            pltpu.VMEM((m, n), bf16),
            pltpu.SemaphoreType.DMA((2, m // min(128, block))),
        ],
        compiler_params=params(20),
        name="project",
    )(momentum, gradient, basis)


def half_product_kernel(half_of, blocks, buf, *rest):
    lefts, out, whole = rest[:blocks], rest[blocks], rest[blocks + 1]
    m, n = buf.shape
    block = m // blocks
    me = lax.axis_index("col")
    half = half_of(lax.bitwise_and(lax.axis_index("row"), jnp.int32(1)))
    for d in range(blocks):
        cols = pl.ds(pl.multiple_of(flip(me, d) * block, block), block)
        whole[:, cols] = lefts[d][...]
    width = 256

    def step(k, carry):
        cols = pl.ds(pl.multiple_of(half * (n // 2) + k * width, 128), width)
        b = buf[:, cols].astype(bf16)
        out[:, pl.ds(pl.multiple_of(k * width, 128), width)] = dot(whole[...], b).astype(out.dtype)
        return carry

    lax.fori_loop(0, n // 2 // width, step, 0)


def half_product(buf, lefts, mine, kind):
    m, n = buf.shape
    r = lefts[0].shape[0]
    half_of = (lambda core: core) if mine else (lambda core: 1 - core)
    return pl.pallas_call(
        functools.partial(half_product_kernel, half_of, len(lefts)),
        out_shape=shape((r, n // 2), kind),
        in_specs=[VMEM] * (1 + len(lefts)),
        out_specs=VMEM,
        scratch_shapes=[pltpu.VMEM((r, m), bf16)],
        compiler_params=params(8),
        name="mine_product" if mine else "other_product",
    )(buf, *lefts)


def pair_sum_kernel(chips, mine, received, *outs):
    me = lax.div(lax.axis_index("row"), jnp.int32(2))
    width = outs[0].shape[1]
    for d in range(chips):
        cols = pl.ds(pl.multiple_of(flip(me, d) * width, 128), width)
        outs[d][...] = (mine[:, cols] + received[:, cols].astype(f32)).astype(outs[d].dtype)


def pair_sum(mine, received, chips):
    r, n = mine.shape
    kinds = [f32] + [bf16] * (chips - 1)
    return pl.pallas_call(
        functools.partial(pair_sum_kernel, chips),
        out_shape=[shape((r, n // chips), k) for k in kinds],
        in_specs=[VMEM, VMEM],
        out_specs=[VMEM] * chips,
        compiler_params=params(8),
        name="pair_sum",
    )(mine, received)


def gram_kernel(blocks, *refs):
    lefts, mine, other, total = refs[:blocks], refs[blocks], refs[blocks + 1], refs[blocks + 2]
    core = lax.bitwise_and(lax.axis_index("row"), jnp.int32(1))
    total[...] = sum(dot(ref[...], ref[...], ((1,), (1,))) for ref in lefts)
    h = mine.shape[0]
    mine[...] = total[pl.ds(pl.multiple_of(core * h, h), h), :]
    other[...] = total[pl.ds(pl.multiple_of((1 - core) * h, h), h), :]


def gram(lefts):
    r = lefts[0].shape[0]
    return pl.pallas_call(
        functools.partial(gram_kernel, len(lefts)),
        out_shape=[shape((r // 2, r), f32)] * 2,
        in_specs=[VMEM] * len(lefts),
        out_specs=[VMEM] * 2,
        scratch_shapes=[pltpu.VMEM((r, r), f32)],
        compiler_params=params(8),
        name="gram",
    )(*lefts)


def chol_inverse_kernel(mine, other, out, work):
    n = out.shape[0]
    h = n // 2
    core = lax.bitwise_and(lax.axis_index("row"), jnp.int32(1))
    work[pl.ds(pl.multiple_of(core * h, h), h), :n] = mine[...]
    work[pl.ds(pl.multiple_of((1 - core) * h, h), h), :n] = other[...]
    r_id = lax.broadcasted_iota(jnp.int32, (n, n), 0)
    c_id = lax.broadcasted_iota(jnp.int32, (n, n), 1)
    work[:, n:] = jnp.where(r_id == c_id, 1.0, 0.0).astype(f32)
    nb = 32
    sub = lax.broadcasted_iota(jnp.int32, (nb, 1), 0)
    for p in range(n // nb):
        lo = p * nb
        left = (lo // 128) * 128
        right = n + ((lo + nb + 127) // 128) * 128
        s = work[lo : lo + nb, left:right]
        scale = jnp.zeros((nb, 1), f32)
        for t in range(nb):
            at = lo - left + t
            col = s[:, at : at + 1]
            row = s[t : t + 1, :]
            pivot = s[t : t + 1, at : at + 1]
            factor = jnp.where(sub > t, col, 0.0) * (1.0 / pivot)
            scale = jnp.where(sub == t, lax.rsqrt(pivot), scale)
            s = s - factor * row
        s = s * scale
        work[lo : lo + nb, left:right] = s
        if lo + nb < n:
            lead = s[:, lo + nb - left : n - left]
            work[lo + nb :, left:right] -= lax.dot_general(
                lead, s, (((0,), (0,)), ((), ())), precision=lax.Precision.HIGHEST, preferred_element_type=f32
            )
    out[...] = jnp.where(r_id >= c_id, work[:, n:], 0.0)


def chol_inverse(mine, other):
    n = mine.shape[1]
    return pl.pallas_call(
        chol_inverse_kernel,
        out_shape=shape((n, n), f32),
        in_specs=[VMEM, VMEM],
        out_specs=VMEM,
        scratch_shapes=[pltpu.VMEM((n, 2 * n), f32)],
        compiler_params=params(8),
        name="chol_inverse",
    )(mine, other)


def ortho_kernel(blocks, inverse, *refs):
    lefts, out = refs[:blocks], refs[blocks]
    block = lefts[0].shape[1]
    me = lax.axis_index("col")
    parts = split(inverse[...], 3)
    for d in range(blocks):
        rows = pl.ds(pl.multiple_of(flip(me, d) * block, block), block)
        o = sum(dot(lefts[d][...], part, ((0,), (1,))) for part in reversed(parts))
        out[rows, :] = o.astype(bf16)


def ortho(inverse, lefts):
    r, block = lefts[0].shape
    return pl.pallas_call(
        functools.partial(ortho_kernel, len(lefts)),
        out_shape=shape((block * len(lefts), r), bf16),
        in_specs=[VMEM] * (1 + len(lefts)),
        out_specs=VMEM,
        compiler_params=params(8),
        name="ortho",
    )(inverse, *lefts)


def share_sum_kernel(own, *refs):
    received, out = refs[:-1], refs[-1]
    out[...] = (own[...] + sum(ref[...].astype(f32) for ref in received)).astype(bf16)


def share_sum(own, received):
    return pl.pallas_call(
        share_sum_kernel,
        out_shape=shape(own.shape, bf16),
        in_specs=[VMEM] * (1 + len(received)),
        out_specs=VMEM,
        compiler_params=params(8),
        name="share_sum",
    )(own, *received)


def right_kernel(chips, inverse, *refs):
    blocks, right, squares = refs[: 2 * chips], refs[2 * chips], refs[2 * chips + 1]
    n = right.shape[1]
    r = right.shape[0]
    row = lax.axis_index("row")
    core = lax.bitwise_and(row, jnp.int32(1))
    chip = lax.div(row, jnp.int32(2))
    width = n // (2 * chips)
    parts = split(inverse[...], 2)
    total = jnp.zeros((r, 1), f32)
    for b in range(2 * chips):
        half = core if b < chips else 1 - core
        start = half * (n // 2) + flip(chip, b % chips) * width
        block = blocks[b][...]
        value = dot(parts[1], block) + dot(parts[0], block)
        right[:, pl.ds(pl.multiple_of(start, 128), width)] = value
    for b in range(2 * chips):
        value = right[:, b * width : (b + 1) * width]
        total = total + jnp.sum(value * value, axis=1, keepdims=True)
    wide = jnp.broadcast_to(total, (r, 128))
    squares[...] = jnp.transpose(wide)[:8, :]


def right_of(inverse, blocks):
    r, width = blocks[0].shape
    n = width * len(blocks)
    return pl.pallas_call(
        functools.partial(right_kernel, len(blocks) // 2),
        out_shape=(shape((r, n), f32), shape((8, r), f32)),
        in_specs=[VMEM] * (1 + len(blocks)),
        out_specs=(VMEM, VMEM),
        compiler_params=params(16),
        name="right_factor",
    )(inverse, *blocks)


def momentum_kernel(buf, ortho_ref, right, out, obuf, sems):
    m, n = buf.shape
    width = obuf.shape[2]
    tiles = n // width
    chunk = min(256, m)

    def copy(i):
        return pltpu.make_async_copy(obuf.at[i % 2], out.at[:, pl.ds(i * width, width)], sems.at[i % 2])

    for i in range(tiles):
        cols = slice(i * width, (i + 1) * width)
        if i >= 2:
            copy(i - 2).wait()
        low = right[:, cols].astype(bf16)

        def step(k, carry):
            rows = pl.ds(pl.multiple_of(k * chunk, chunk), chunk)
            correction = dot(ortho_ref[rows, :], low)
            obuf[i % 2, rows, :] = buf[rows, cols] - (1.0 - momentum_decay) * correction
            return carry

        lax.fori_loop(0, m // chunk, step, 0)
        copy(i).start()
    for i in range(max(tiles - 2, 0), tiles):
        copy(i).wait()


def momentum_out(buf, ortho_bf, right, width):
    m, n = buf.shape
    return pl.pallas_call(
        momentum_kernel,
        out_shape=shape((m, n), f32),
        in_specs=[VMEM] * 3,
        out_specs=ANY,
        scratch_shapes=[pltpu.VMEM((2, m, width), f32), pltpu.SemaphoreType.DMA((2,))],
        compiler_params=params(12),
        name="momentum_out",
    )(buf, ortho_bf, right)


def weight_kernel(factor, weight, ortho_ref, right, *refs):
    squares, (new_weight, basis, obuf, nbuf, sems) = refs[:-5], refs[-5:]
    m, n = weight.shape
    r = right.shape[0]
    width = obuf.shape[2]
    tiles = n // width
    chunk = min(256, m)
    terms = [ref[...] for ref in squares]
    while len(terms) > 1:
        terms = [terms[2 * i] + terms[2 * i + 1] for i in range(len(terms) // 2)]
    inverse = lax.rsqrt(terms[0] / FF + epsilon)
    inverse = jnp.transpose(jnp.concatenate([inverse] * 16, axis=0))[:, :1]

    def copies(i):
        cols = pl.ds(i * width, width)
        return (
            pltpu.make_async_copy(obuf.at[i % 2], new_weight.at[:, cols], sems.at[0, i % 2]),
            pltpu.make_async_copy(nbuf.at[i % 2], basis.at[:, cols], sems.at[1, i % 2]),
        )

    for i in range(tiles):
        cols = slice(i * width, (i + 1) * width)
        if i >= 2:
            for copy in copies(i - 2):
                copy.wait()
        nbuf[i % 2] = (right[:, cols] * inverse).astype(bf16)
        low = nbuf[i % 2]

        def step(k, carry):
            rows = pl.ds(pl.multiple_of(k * chunk, chunk), chunk)
            change = dot(ortho_ref[rows, :], low)
            obuf[i % 2, rows, :] = (weight[rows, cols].astype(f32) - factor * change).astype(bf16)
            return carry

        lax.fori_loop(0, m // chunk, step, 0)
        for copy in copies(i):
            copy.start()
    for i in range(max(tiles - 2, 0), tiles):
        for copy in copies(i):
            copy.wait()


def weight_out(weight, ortho_bf, right, squares, width, factor):
    m, n = weight.shape
    r = right.shape[0]
    return pl.pallas_call(
        functools.partial(weight_kernel, factor),
        out_shape=(shape((m, n), bf16), shape((r, n), bf16)),
        in_specs=[VMEM] * (3 + len(squares)),
        out_specs=(ANY, ANY),
        scratch_shapes=[
            pltpu.VMEM((2, m, width), bf16),
            pltpu.VMEM((2, r, width), bf16),
            pltpu.SemaphoreType.DMA((2, 2)),
        ],
        compiler_params=params(12),
        name="weight_out",
    )(weight, ortho_bf, right, *squares)


def per_device(weight, gradient, momentum, old_basis):
    depth, rows = lax.axis_size("col"), lax.axis_size("row")
    chips = rows // 2
    m, n = momentum.shape
    buf, own, *sent = project(momentum, gradient, old_basis, depth)
    got = [swap(x, "col", d + 1) for d, x in enumerate(sent)]
    low = share_sum(own, got)
    lefts = [low] + [swap(low, "col", d) for d in range(1, depth)]

    other = half_product(buf, lefts, False, bf16)
    other = swap(other, "row", 1)
    g_mine, g_other = gram(lefts)
    mine = half_product(buf, lefts, True, f32)
    own, *sent = pair_sum(mine, other, chips)
    got = [swap(x, "row", 2 * (d + 1)) for d, x in enumerate(sent)]

    g_mine = g_mine + swap(g_other, "row", 1)
    terms = [g_mine] + [swap(g_mine, "row", 2 * d) for d in range(1, chips)]
    while len(terms) > 1:
        terms = [terms[2 * i] + terms[2 * i + 1] for i in range(len(terms) // 2)]
    g_mine = terms[0]
    g_other = swap(g_mine, "row", 1)
    inverse = chol_inverse(g_mine, g_other)
    ortho_bf = ortho(inverse, lefts)

    share = share_sum(own, got)
    blocks = [share] + [swap(share, "row", 2 * d) for d in range(1, chips)]
    blocks = blocks + [swap(x, "row", 1) for x in blocks]
    right, squares = right_of(inverse, blocks)
    squares = [squares] + [swap(squares, "col", d) for d in range(1, depth)]
    new_momentum = momentum_out(buf, ortho_bf, right, n // rows)
    factor = step_rate * math.sqrt(D / RANK)
    new_weight, new_basis = weight_out(weight, ortho_bf, right, squares, n // rows, factor)
    return (new_weight, new_momentum, new_basis)


def plain_per_device(weight, gradient, momentum, old_basis):
    buffer = momentum + gradient.astype(f32)
    buffer_low = buffer.astype(bf16)
    left_factor = lax.psum(dot(buffer_low, old_basis, ((1,), (1,))), "col")
    gram_share = lax.dot_general(
        left_factor,
        left_factor,
        (((0,), (0,)), ((), ())),
        precision=lax.Precision.HIGHEST,
        preferred_element_type=f32,
    )
    chol_factor = jnp.linalg.cholesky(lax.psum(gram_share, "row"))
    orthonormal = lax.linalg.triangular_solve(
        chol_factor, left_factor, left_side=False, lower=True, transpose_a=True
    ).astype(bf16)
    right_share = lax.psum_scatter(
        dot(orthonormal, buffer_low, ((0,), (0,))), "row", scatter_dimension=0, tiled=True
    )
    sum_squares = lax.psum(jnp.sum(right_share * right_share, axis=1), "col")
    scale_share = jnp.sqrt(sum_squares / FF + epsilon)
    basis_share = (right_share / scale_share[:, None]).astype(bf16)
    new_basis = lax.all_gather(basis_share, "row", axis=0, tiled=True)
    col_scale = lax.all_gather(scale_share, "row", axis=0, tiled=True)
    scaled = (orthonormal.astype(f32) * col_scale[None, :]).astype(bf16)
    new_momentum = buffer - (1.0 - momentum_decay) * dot(scaled, new_basis)
    factor = step_rate * math.sqrt(D / RANK)
    new_weight = (weight.astype(f32) - factor * dot(orthonormal, new_basis)).astype(bf16)
    return (new_weight, new_momentum, new_basis)


def power_of_two(k):
    return k > 1 and k & (k - 1) == 0


def solution(mesh):
    rows, depth = mesh.shape["row"], mesh.shape["col"]
    tiled = (
        power_of_two(rows)
        and power_of_two(depth)
        and D % (rows * depth * 128) == 0
        and FF % (rows * depth * 256) == 0
    )
    return jax.shard_map(
        per_device if tiled else plain_per_device,
        mesh=mesh,
        in_specs=(P("row", "col"), P("row", "col"), P("row", "col"), P(None, "col")),
        out_specs=(P("row", "col"), P("row", "col"), P(None, "col")),
        check_vma=False,
    )
```

time: 377 us -> 188 us (0.50)
  waiting for transfers between devices: 185 us -> 56.6 us
  matrix products: 81.6 us -> 0 us
  Pallas kernels: 0 us -> 76.3 us
  other arithmetic: 58 us -> 0.05 us
  starting transfers between devices: 0.34 us -> 27 us
  blocking collectives: 23.9 us -> 0 us
  local copies, waits for them, and re-layouts: 11.4 us -> 27.1 us
  between operations: 15.9 us -> 1.05 us
    psum x2 -> x0, waiting for transfers between devices: 107 us -> none  [the longest x1 54.6 us: per_device(): left_factor = lax.psum(local_left, 'col')]
    dot_general x5 -> x0, matrix products: 76.7 us -> none  [the longest x1 24.6 us: per_device(): correction = jnp.dot(scaled, new_basis, preferred_element_type=jnp.float32)]
    pallas_call x0 -> x12, Pallas kernels: none -> 76.3 us  [the longest x1 25.1 us: chol_inverse(): pl.pallas_call(chol_inverse_kernel, out_shape=shape((n, n), f32), in_spec...]
    reduce_scatter x1 -> x0, waiting for transfers between devices: 60 us -> none  [per_device(): lax.psum_scatter(lax.dot_general(orthonormal, buffer_low, (((0,), (0,)),...]
    ppermute x0 -> x25, waiting for transfers between devices: none -> 56.6 us  [swap(): lax.ppermute(x, axis, [(i, i ^ d) for i in range(lax.axis_size(axis))])]
    another operation x9 -> x0, other arithmetic: 53.7 us -> none  [the longest x6 34 us: orthonormalize(): chol_factor = jnp.linalg.cholesky(gram_matrix)]
    ppermute x0 -> x25, starting transfers between devices: none -> 27 us  [swap(): lax.ppermute(x, axis, [(i, i ^ d) for i in range(lax.axis_size(axis))])]
    unnamed x11 -> x14, local copies, waits for them, and re-layouts: 6.33 us -> 27.1 us
  transfers between devices with their start and end apart: 4 -> 25, of which waited for: 4 -> 11; matrix products, arithmetic and copies ran while one was open for 0% -> 0% of each run, Pallas kernels for 0% -> 23%
where the time goes in v1:
time: 188 us
  Pallas kernels  76.3 us (41%)
  waiting for transfers between devices  56.6 us (30%)
  local copies, waits for them, and re-layouts  27.1 us (14%)
  starting transfers between devices  27 us (14%)
    ppermute x25, waiting for transfers between devices, swap(): lax.ppermute(x, axis, [(i, i ^ d) for i in range(lax.axis_size(axis))])  56.6 us
    unnamed x14, local copies, waits for them, and re-layouts  27.1 us
    ppermute x25, starting transfers between devices, swap(): lax.ppermute(x, axis, [(i, i ^ d) for i in range(lax.axis_size(axis))])  27 us
    pallas_call x1, Pallas kernels, chol_inverse(): pl.pallas_call(chol_inverse_kernel, out_shape=shape((n, n), f32), in_spec...  25.1 us
    pallas_call x1, Pallas kernels, project(): pl.pallas_call(project_kernel, out_shape=(pltpu.VMEM((m, n), f32), *[shap...  15.4 us
    pallas_call x1, Pallas kernels, momentum_out(): pl.pallas_call(momentum_kernel, out_shape=shape((m, n), f32), in_specs=[V...  13 us
    pallas_call x1, Pallas kernels, weight_out(): pl.pallas_call(functools.partial(weight_kernel, factor), out_shape=(shape...  11.1 us
    pallas_call x2, Pallas kernels, half_product(): pl.pallas_call(functools.partial(half_product_kernel, half_of, len(lefts)...  7.9 us
  transfers between devices with their start and end apart: 25, of which 11 were waited for; matrix products, arithmetic and copies ran while one was open for 0% of the time, Pallas kernels for 23%

profile of v1, /device:TPU:0, one launch (start us, length us, event | category | flops | bytes accessed | tf_op | source)
XLA Modules:
  0.0 188.1 jit_solution(15246780637912025599)
XLA Ops:
  0.6 1.9 copy-done.3
  2.5 15.4 %project.1 = (f32[1024,6144]{1,0:T(8,128)S(1)}, f32[256,256]{1,0:T(8,128)S(1)}, bf16[256,256]{1,0:T(8,128)(2,1)S(1)}, bf16[256,256]{1,0:T(8,128)(2,1)S(1)}, bf16[256,256]{1,0:T(8,128)(2,1)S(1)}) custom-call(f32[1024,6144]{1,0:T(8,128)} %mom.1, bf16[1024,6144]{1,0:T(8,128)(2,1)} %grad.1, bf16[256,6144]{1,0:T(8,128)(2,1)S(1)} %copy-done.3), custom_call_target="tpu_custom_call" | custom-call | tf_op jit(solution)/shard_map/project/pallas_call | solution.py:95
  17.9 8.9 %copy-done = f32[1024,6144]{1,0:T(8,128)} copy-done((f32[1024,6144]{1,0:T(8,128)}, f32[1024,6144]{1,0:T(8,128)S(1)}, u32[]{:S(2)}) %copy-start) | copy-done | bytes 25165848
  26.8 3.0 %collective-permute-start = (bf16[256,256]{1,0:T(8,128)(2,1)S(1)}, bf16[256,256]{1,0:T(8,128)(2,1)S(1)}, u32[]{:S(2)}, u32[]{:S(2)}) collective-permute-start(bf16[256,256]{1,0:T(8,128)(2,1)S(1)} %get-tuple-element.19), channel_id=1, source_target_pairs={{0,1},{1,0},{2,3},{3,2},{4,5},{5,4},{6,7},{7,6},{8,9},{9,8},{10,11... | collective-permute-start | bytes 393224 | tf_op jit(solution)/shard_map/ppermute | solution.py:51
  29.8 2.6 %collective-permute-start.1 = (bf16[256,256]{1,0:T(8,128)(2,1)S(1)}, bf16[256,256]{1,0:T(8,128)(2,1)S(1)}, u32[]{:S(2)}, u32[]{:S(2)}) collective-permute-start(bf16[256,256]{1,0:T(8,128)(2,1)S(1)} %get-tuple-element.20), channel_id=1, source_target_pairs={{0,2},{1,3},{2,0},{3,1},{4,6},{5,7},{6,4},{7,5},{8,10},{9,11},{10,... | collective-permute-start | bytes 393224 | tf_op jit(solution)/shard_map/ppermute | solution.py:51
  32.4 2.4 %collective-permute-done.refs_0_ = bf16[256,256]{1,0:T(8,128)(2,1)S(1)} collective-permute-done((bf16[256,256]{1,0:T(8,128)(2,1)S(1)}, bf16[256,256]{1,0:T(8,128)(2,1)S(1)}, u32[]{:S(2)}, u32[]{:S(2)}) %collective-permute-start) | collective-permute-done | bytes 131104 | tf_op jit(solution)/shard_map/ppermute | solution.py:51
  34.9 7.9 %collective-permute-done.1.refs_1_ = bf16[256,256]{1,0:T(8,128)(2,1)S(1)} collective-permute-done((bf16[256,256]{1,0:T(8,128)(2,1)S(1)}, bf16[256,256]{1,0:T(8,128)(2,1)S(1)}, u32[]{:S(2)}, u32[]{:S(2)}) %collective-permute-start.1) | collective-permute-done | bytes 131104 | tf_op jit(solution)/shard_map/ppermute | solution.py:51
  42.8 2.4 %collective-permute-start.5 = (bf16[256,256]{1,0:T(8,128)(2,1)S(1)}, bf16[256,256]{1,0:T(8,128)(2,1)S(1)}, u32[]{:S(2)}, u32[]{:S(2)}) collective-permute-start(bf16[256,256]{1,0:T(8,128)(2,1)S(1)} %share_sum.2.refs_0_.rest_0_), channel_id=1, source_target_pairs={{0,3},{1,2},{2,1},{3,0},{4,7},{5,6},{6,5},{7,4},{8,11},{9,10},{10,... | collective-permute-start | bytes 393224 | tf_op jit(solution)/shard_map/ppermute | solution.py:51
  45.2 1.1 collective-permute-start.4
  46.3 1.0 collective-permute-start.3
  47.3 3.8 %collective-permute-done.5.refs_3_.rest_3_ = bf16[256,256]{1,0:T(8,128)(2,1)S(1)} collective-permute-done((bf16[256,256]{1,0:T(8,128)(2,1)S(1)}, bf16[256,256]{1,0:T(8,128)(2,1)S(1)}, u32[]{:S(2)}, u32[]{:S(2)}) %collective-permute-start.5) | collective-permute-done | bytes 131104 | tf_op jit(solution)/shard_map/ppermute | solution.py:51
  51.1 4.8 %collective-permute-done.4.refs_2_.rest_2_ = bf16[256,256]{1,0:T(8,128)(2,1)S(1)} collective-permute-done((bf16[256,256]{1,0:T(8,128)(2,1)S(1)}, bf16[256,256]{1,0:T(8,128)(2,1)S(1)}, u32[]{:S(2)}, u32[]{:S(2)}) %collective-permute-start.4) | collective-permute-done | bytes 131104 | tf_op jit(solution)/shard_map/ppermute | solution.py:51
  55.9 8.2 %copy-done.1 = f32[1024,6144]{1,0:T(8,128)S(1)} copy-done((f32[1024,6144]{1,0:T(8,128)S(1)}, f32[1024,6144]{1,0:T(8,128)}, u32[]{:S(2)}) %copy-start.1) | copy-done | bytes 25165848
  64.1 3.9 %other_product.1 = bf16[256,3072]{1,0:T(8,128)(2,1)S(1)} custom-call(f32[1024,6144]{1,0:T(8,128)S(1)} %copy-done.1, bf16[256,256]{1,0:T(8,128)(2,1)S(1)} %share_sum.2.refs_0_.rest_0_, bf16[256,256]{1,0:T(8,128)(2,1)S(1)} %collective-permute-done.3.refs_1_.rest_1_, bf16[256,256]{1,0:T(8,128)(2,1)S(1)} %collective-permute-done.4.refs_2_.rest_2_, ...), custom_call_target="tpu_custom_call" | custom-call | tf_op jit(solution)/shard_map/other_product/pallas_call | solution.py:133
  67.9 0.1 collective-permute-start.11
  68.0 4.0 %mine_product.1.mine = f32[256,3072]{1,0:T(8,128)S(1)} custom-call(f32[1024,6144]{1,0:T(8,128)S(1)} %copy-done.1, bf16[256,256]{1,0:T(8,128)(2,1)S(1)} %share_sum.2.refs_0_.rest_0_, bf16[256,256]{1,0:T(8,128)(2,1)S(1)} %collective-permute-done.3.refs_1_.rest_1_, bf16[256,256]{1,0:T(8,128)(2,1)S(1)} %collective-permute-done.4.refs_2_.rest_2_, ...), custom_call_target="tpu_custom_call" | custom-call | tf_op jit(solution)/shard_map/mine_product/pallas_call | solution.py:133
  72.1 0.3 pair_sum.1
  72.4 1.6 collective-permute-start.12
  74.0 1.5 collective-permute-start.13
  75.5 0.5 collective-permute-start.14
  76.0 8.4 %collective-permute-done.12.refs_0_ = bf16[256,768]{1,0:T(8,128)(2,1)S(1)} collective-permute-done((bf16[256,768]{1,0:T(8,128)(2,1)S(1)}, bf16[256,768]{1,0:T(8,128)(2,1)S(1)}, u32[]{:S(2)}, u32[]{:S(2)}) %collective-permute-start.12) | collective-permute-done | bytes 393248 | tf_op jit(solution)/shard_map/ppermute | solution.py:51
  84.4 9.2 %collective-permute-done.13.refs_1_ = bf16[256,768]{1,0:T(8,128)(2,1)S(1)} collective-permute-done((bf16[256,768]{1,0:T(8,128)(2,1)S(1)}, bf16[256,768]{1,0:T(8,128)(2,1)S(1)}, u32[]{:S(2)}, u32[]{:S(2)}) %collective-permute-start.13) | collective-permute-done | bytes 393248 | tf_op jit(solution)/shard_map/ppermute | solution.py:51
  93.7 0.2 share_sum.3.refs_0_
  93.8 1.6 collective-permute-start.17
  95.4 1.2 collective-permute-start.16
  96.6 0.8 collective-permute-start.15
  97.4 0.4 gram.1
  97.8 0.1 collective-permute-start.6
  97.8 1.3 collective-permute-done.6
  99.2 1.5 collective-permute-start.9
  100.7 1.2 collective-permute-start.8
  101.9 14.8 %collective-permute-done.9 = f32[128,256]{1,0:T(8,128)S(1)} collective-permute-done((f32[128,256]{1,0:T(8,128)S(1)}, f32[128,256]{1,0:T(8,128)S(1)}, u32[]{:S(2)}, u32[]{:S(2)}) %collective-permute-start.9) | collective-permute-done | bytes 131104 | tf_op jit(solution)/shard_map/ppermute | solution.py:51
  116.7 1.4 collective-permute-start.7
  118.1 1.2 collective-permute-done.8
  119.4 0.5 collective-permute-start.21
  119.9 0.1 collective-permute-start.20
  119.9 0.4 collective-permute-start.19
  120.4 1.3 collective-permute-done.7
  121.7 0.1 collective-permute-start.10
  121.8 1.3 collective-permute-done.10.other
  123.1 25.1 %chol_inverse.1.inverse = f32[256,256]{1,0:T(8,128)S(1)} custom-call(f32[128,256]{1,0:T(8,128)S(1)} %add_add_fusion.mine, f32[128,256]{1,0:T(8,128)S(1)} %collective-permute-done.10.other), custom_call_target="tpu_custom_call" | custom-call | tf_op jit(solution)/shard_map/chol_inverse/pallas_call | solution.py:224
  148.3 2.3 %right_factor.1 = (f32[256,6144]{1,0:T(8,128)S(1)}, f32[8,256]{1,0:T(8,128)S(1)}) custom-call(f32[256,256]{1,0:T(8,128)S(1)} %chol_inverse.1.inverse, bf16[256,768]{1,0:T(8,128)(2,1)S(1)} %share_sum.3.refs_0_, bf16[256,768]{1,0:T(8,128)(2,1)S(1)} %collective-permute-done.15.refs_1_, bf16[256,768]{1,0:T(8,128)(2,1)S(1)} %collective-permute-done.16.refs_2_, ...), custom_call_target="tpu_custom_call" | custom-call | tf_op jit(solution)/shard_map/right_factor/pallas_call | solution.py:300
  150.6 2.4 %collective-permute-start.24 = (f32[8,256]{1,0:T(8,128)S(1)}, f32[8,256]{1,0:T(8,128)S(1)}, u32[]{:S(2)}, u32[]{:S(2)}) collective-permute-start(f32[8,256]{1,0:T(8,128)S(1)} %get-tuple-element.30.refs_0_), channel_id=1, source_target_pairs={{0,3},{1,2},{2,1},{3,0},{4,7},{5,6},{6,5},{7,4},{8,11},{9,10},{10,... | collective-permute-start | bytes 24584 | tf_op jit(solution)/shard_map/ppermute | solution.py:51
  153.0 2.0 %collective-permute-start.22 = (f32[8,256]{1,0:T(8,128)S(1)}, f32[8,256]{1,0:T(8,128)S(1)}, u32[]{:S(2)}, u32[]{:S(2)}) collective-permute-start(f32[8,256]{1,0:T(8,128)S(1)} %get-tuple-element.30.refs_0_), channel_id=1, source_target_pairs={{0,1},{1,0},{2,3},{3,2},{4,5},{5,4},{6,7},{7,6},{8,9},{9,8},{10,11... | collective-permute-start | bytes 24584 | tf_op jit(solution)/shard_map/ppermute | solution.py:51
  155.0 0.6 ortho.1.ortho_ref
  155.7 8.1 %copy-done.2 = f32[1024,6144]{1,0:T(8,128)S(1)} copy-done((f32[1024,6144]{1,0:T(8,128)S(1)}, f32[1024,6144]{1,0:T(8,128)}, u32[]{:S(2)}) %copy-start.2) | copy-done | bytes 25165848
  163.8 13.0 %momentum_out.1 = f32[1024,6144]{1,0:T(8,128)} custom-call(f32[1024,6144]{1,0:T(8,128)S(1)} %copy-done.2, bf16[1024,256]{1,0:T(8,128)(2,1)S(1)} %ortho.1.ortho_ref, f32[256,6144]{1,0:T(8,128)S(1)} %get-tuple-element.29.right), custom_call_target="tpu_custom_call" | custom-call | tf_op jit(solution)/shard_map/momentum_out/pallas_call | solution.py:339
  176.9 11.1 %weight_out.1 = (bf16[1024,6144]{1,0:T(8,128)(2,1)}, bf16[256,6144]{1,0:T(8,128)(2,1)}) custom-call(bf16[1024,6144]{1,0:T(8,128)(2,1)S(1)} %bitcast.1, bf16[1024,256]{1,0:T(8,128)(2,1)S(1)} %ortho.1.ortho_ref, f32[256,6144]{1,0:T(8,128)S(1)} %get-tuple-element.29.right, f32[8,256]{1,0:T(8,128)S(1)} %get-tuple-element.30.refs_0_, ...), custom_call_target="tpu_custom_call" | custom-call | tf_op jit(solution)/shard_map/weight_out/pallas_call | solution.py:395
  (31 shorter events, 0.2 us)
Async XLA Ops:
  0.6 1.9 %copy-start.3 = (bf16[256,6144]{1,0:T(8,128)(2,1)S(1)}, bf16[256,6144]{1,0:T(8,128)(2,1)}, u32[]{:S(2)}) copy-start(bf16[256,6144]{1,0:T(8,128)(2,1)} %basis.1) | copy-start | bytes 9437188
  17.9 8.9 %copy-start = (f32[1024,6144]{1,0:T(8,128)}, f32[1024,6144]{1,0:T(8,128)S(1)}, u32[]{:S(2)}) copy-start(f32[1024,6144]{1,0:T(8,128)S(1)} %get-tuple-element.24.buf) | copy-start | bytes 75497472
  26.8 8.1 %collective-permute-start = (bf16[256,256]{1,0:T(8,128)(2,1)S(1)}, bf16[256,256]{1,0:T(8,128)(2,1)S(1)}, u32[]{:S(2)}, u32[]{:S(2)}) collective-permute-start(bf16[256,256]{1,0:T(8,128)(2,1)S(1)} %get-tuple-element.19), channel_id=1, source_target_pairs={{0,1},{1,0},{2,3},{3,2},{4,5},{5,4},{6,7},{7,6},{8,9},{9,8},{10,11... | collective-permute-start | bytes 393224 | tf_op jit(solution)/shard_map/ppermute | solution.py:51
  29.8 12.9 %collective-permute-start.1 = (bf16[256,256]{1,0:T(8,128)(2,1)S(1)}, bf16[256,256]{1,0:T(8,128)(2,1)S(1)}, u32[]{:S(2)}, u32[]{:S(2)}) collective-permute-start(bf16[256,256]{1,0:T(8,128)(2,1)S(1)} %get-tuple-element.20), channel_id=1, source_target_pairs={{0,2},{1,3},{2,0},{3,1},{4,6},{5,7},{6,4},{7,5},{8,10},{9,11},{10,... | collective-permute-start | bytes 393224 | tf_op jit(solution)/shard_map/ppermute | solution.py:51
  32.4 10.3 %collective-permute-start.2 = (bf16[256,256]{1,0:T(8,128)(2,1)S(1)}, bf16[256,256]{1,0:T(8,128)(2,1)S(1)}, u32[]{:S(2)}, u32[]{:S(2)}) collective-permute-start(bf16[256,256]{1,0:T(8,128)(2,1)S(1)} %get-tuple-element.21), channel_id=1, source_target_pairs={{0,3},{1,2},{2,1},{3,0},{4,7},{5,6},{6,5},{7,4},{8,11},{9,10},{10,... | collective-permute-start | bytes 393224 | tf_op jit(solution)/shard_map/ppermute | solution.py:51
  42.8 8.3 %collective-permute-start.5 = (bf16[256,256]{1,0:T(8,128)(2,1)S(1)}, bf16[256,256]{1,0:T(8,128)(2,1)S(1)}, u32[]{:S(2)}, u32[]{:S(2)}) collective-permute-start(bf16[256,256]{1,0:T(8,128)(2,1)S(1)} %share_sum.2.refs_0_.rest_0_), channel_id=1, source_target_pairs={{0,3},{1,2},{2,1},{3,0},{4,7},{5,6},{6,5},{7,4},{8,11},{9,10},{10,... | collective-permute-start | bytes 393224 | tf_op jit(solution)/shard_map/ppermute | solution.py:51
  45.2 10.7 %collective-permute-start.4 = (bf16[256,256]{1,0:T(8,128)(2,1)S(1)}, bf16[256,256]{1,0:T(8,128)(2,1)S(1)}, u32[]{:S(2)}, u32[]{:S(2)}) collective-permute-start(bf16[256,256]{1,0:T(8,128)(2,1)S(1)} %share_sum.2.refs_0_.rest_0_), channel_id=1, source_target_pairs={{0,2},{1,3},{2,0},{3,1},{4,6},{5,7},{6,4},{7,5},{8,10},{9,11},{10,... | collective-permute-start | bytes 393224 | tf_op jit(solution)/shard_map/ppermute | solution.py:51
  46.3 9.6 %collective-permute-start.3 = (bf16[256,256]{1,0:T(8,128)(2,1)S(1)}, bf16[256,256]{1,0:T(8,128)(2,1)S(1)}, u32[]{:S(2)}, u32[]{:S(2)}) collective-permute-start(bf16[256,256]{1,0:T(8,128)(2,1)S(1)} %share_sum.2.refs_0_.rest_0_), channel_id=1, source_target_pairs={{0,1},{1,0},{2,3},{3,2},{4,5},{5,4},{6,7},{7,6},{8,9},{9,8},{10,11... | collective-permute-start | bytes 393224 | tf_op jit(solution)/shard_map/ppermute | solution.py:51
  55.9 8.2 %copy-start.1 = (f32[1024,6144]{1,0:T(8,128)S(1)}, f32[1024,6144]{1,0:T(8,128)}, u32[]{:S(2)}) copy-start(f32[1024,6144]{1,0:T(8,128)} %copy-done) | copy-start | bytes 75497472
  67.9 4.1 %collective-permute-start.11 = (bf16[256,3072]{1,0:T(8,128)(2,1)S(1)}, bf16[256,3072]{1,0:T(8,128)(2,1)S(1)}, u32[]{:S(2)}, u32[]{:S(2)}) collective-permute-start(bf16[256,3072]{1,0:T(8,128)(2,1)S(1)} %other_product.1), channel_id=1, source_target_pairs={{0,4},{4,0},{8,12},{12,8},{16,20},{20,16},{24,28},{28,24},{1,5},{5... | collective-permute-start | bytes 4718600 | tf_op jit(solution)/shard_map/ppermute | solution.py:51
  72.4 12.0 %collective-permute-start.12 = (bf16[256,768]{1,0:T(8,128)(2,1)S(1)}, bf16[256,768]{1,0:T(8,128)(2,1)S(1)}, u32[]{:S(2)}, u32[]{:S(2)}) collective-permute-start(bf16[256,768]{1,0:T(8,128)(2,1)S(1)} %get-tuple-element.26), channel_id=1, source_target_pairs={{0,8},{4,12},{8,0},{12,4},{16,24},{20,28},{24,16},{28,20},{1,9},{5... | collective-permute-start | bytes 1179656 | tf_op jit(solution)/shard_map/ppermute | solution.py:51
  74.0 19.7 %collective-permute-start.13 = (bf16[256,768]{1,0:T(8,128)(2,1)S(1)}, bf16[256,768]{1,0:T(8,128)(2,1)S(1)}, u32[]{:S(2)}, u32[]{:S(2)}) collective-permute-start(bf16[256,768]{1,0:T(8,128)(2,1)S(1)} %get-tuple-element.27), channel_id=1, source_target_pairs={{0,16},{4,20},{8,24},{12,28},{16,0},{20,4},{24,8},{28,12},{1,17},{... | collective-permute-start | bytes 1179656 | tf_op jit(solution)/shard_map/ppermute | solution.py:51
  75.5 18.2 %collective-permute-start.14 = (bf16[256,768]{1,0:T(8,128)(2,1)S(1)}, bf16[256,768]{1,0:T(8,128)(2,1)S(1)}, u32[]{:S(2)}, u32[]{:S(2)}) collective-permute-start(bf16[256,768]{1,0:T(8,128)(2,1)S(1)} %get-tuple-element.28), channel_id=1, source_target_pairs={{0,24},{4,28},{8,16},{12,20},{16,8},{20,12},{24,0},{28,4},{1,25},{... | collective-permute-start | bytes 1179656 | tf_op jit(solution)/shard_map/ppermute | solution.py:51
  93.7 83.2 %slice-start = ((s8[12582912]{0:T(1024)(128)(4,1)}), s8[4194304]{0:T(1024)(128)(4,1)S(1)}, s32[]{:S(2)}) async-start(s8[12582912]{0:T(1024)(128)(4,1)} %bitcast), calls=%async_computation | async-start | bytes 8388608
  93.8 25.6 %collective-permute-start.17 = (bf16[256,768]{1,0:T(8,128)(2,1)S(1)}, bf16[256,768]{1,0:T(8,128)(2,1)S(1)}, u32[]{:S(2)}, u32[]{:S(2)}) collective-permute-start(bf16[256,768]{1,0:T(8,128)(2,1)S(1)} %share_sum.3.refs_0_), channel_id=1, source_target_pairs={{0,24},{4,28},{8,16},{12,20},{16,8},{20,12},{24,0},{28,4},{1,25},{... | collective-permute-start | bytes 1179656 | tf_op jit(solution)/shard_map/ppermute | solution.py:51
  95.4 24.5 %collective-permute-start.16 = (bf16[256,768]{1,0:T(8,128)(2,1)S(1)}, bf16[256,768]{1,0:T(8,128)(2,1)S(1)}, u32[]{:S(2)}, u32[]{:S(2)}) collective-permute-start(bf16[256,768]{1,0:T(8,128)(2,1)S(1)} %share_sum.3.refs_0_), channel_id=1, source_target_pairs={{0,16},{4,20},{8,24},{12,28},{16,0},{20,4},{24,8},{28,12},{1,17},{... | collective-permute-start | bytes 1179656 | tf_op jit(solution)/shard_map/ppermute | solution.py:51
  96.6 23.4 %collective-permute-start.15 = (bf16[256,768]{1,0:T(8,128)(2,1)S(1)}, bf16[256,768]{1,0:T(8,128)(2,1)S(1)}, u32[]{:S(2)}, u32[]{:S(2)}) collective-permute-start(bf16[256,768]{1,0:T(8,128)(2,1)S(1)} %share_sum.3.refs_0_), channel_id=1, source_target_pairs={{0,8},{4,12},{8,0},{12,4},{16,24},{20,28},{24,16},{28,20},{1,9},{5... | collective-permute-start | bytes 1179656 | tf_op jit(solution)/shard_map/ppermute | solution.py:51
  97.8 1.4 collective-permute-start.6
  99.2 17.5 %collective-permute-start.9 = (f32[128,256]{1,0:T(8,128)S(1)}, f32[128,256]{1,0:T(8,128)S(1)}, u32[]{:S(2)}, u32[]{:S(2)}) collective-permute-start(f32[128,256]{1,0:T(8,128)S(1)} %add.12), channel_id=1, source_target_pairs={{0,24},{4,28},{8,16},{12,20},{16,8},{20,12},{24,0},{28,4},{1,25},{... | collective-permute-start | bytes 393224 | tf_op jit(solution)/shard_map/ppermute | solution.py:51
  100.7 18.6 %collective-permute-start.8 = (f32[128,256]{1,0:T(8,128)S(1)}, f32[128,256]{1,0:T(8,128)S(1)}, u32[]{:S(2)}, u32[]{:S(2)}) collective-permute-start(f32[128,256]{1,0:T(8,128)S(1)} %add.12), channel_id=1, source_target_pairs={{0,16},{4,20},{8,24},{12,28},{16,0},{20,4},{24,8},{28,12},{1,17},{... | collective-permute-start | bytes 393224 | tf_op jit(solution)/shard_map/ppermute | solution.py:51
  116.7 5.0 %collective-permute-start.7 = (f32[128,256]{1,0:T(8,128)S(1)}, f32[128,256]{1,0:T(8,128)S(1)}, u32[]{:S(2)}, u32[]{:S(2)}) collective-permute-start(f32[128,256]{1,0:T(8,128)S(1)} %add.12), channel_id=1, source_target_pairs={{0,8},{4,12},{8,0},{12,4},{16,24},{20,28},{24,16},{28,20},{1,9},{5... | collective-permute-start | bytes 393224 | tf_op jit(solution)/shard_map/ppermute | solution.py:51
  119.4 28.9 %collective-permute-start.18 = (bf16[256,768]{1,0:T(8,128)(2,1)S(1)}, bf16[256,768]{1,0:T(8,128)(2,1)S(1)}, u32[]{:S(2)}, u32[]{:S(2)}) collective-permute-start(bf16[256,768]{1,0:T(8,128)(2,1)S(1)} %share_sum.3.refs_0_), channel_id=1, source_target_pairs={{0,4},{4,0},{8,12},{12,8},{16,20},{20,16},{24,28},{28,24},{1,5},{5... | collective-permute-start | bytes 1179656 | tf_op jit(solution)/shard_map/ppermute | solution.py:51
  119.4 28.9 %collective-permute-start.21 = (bf16[256,768]{1,0:T(8,128)(2,1)S(1)}, bf16[256,768]{1,0:T(8,128)(2,1)S(1)}, u32[]{:S(2)}, u32[]{:S(2)}) collective-permute-start(bf16[256,768]{1,0:T(8,128)(2,1)S(1)} %collective-permute-done.17.refs_3_), channel_id=1, source_target_pairs={{0,4},{4,0},{8,12},{12,8},{16,20},{20,16},{24,28},{28,24},{1,5},{5... | collective-permute-start | bytes 1179656 | tf_op jit(solution)/shard_map/ppermute | solution.py:51
  119.9 28.4 %collective-permute-start.20 = (bf16[256,768]{1,0:T(8,128)(2,1)S(1)}, bf16[256,768]{1,0:T(8,128)(2,1)S(1)}, u32[]{:S(2)}, u32[]{:S(2)}) collective-permute-start(bf16[256,768]{1,0:T(8,128)(2,1)S(1)} %collective-permute-done.16.refs_2_), channel_id=1, source_target_pairs={{0,4},{4,0},{8,12},{12,8},{16,20},{20,16},{24,28},{28,24},{1,5},{5... | collective-permute-start | bytes 1179656 | tf_op jit(solution)/shard_map/ppermute | solution.py:51
  119.9 28.3 %collective-permute-start.19 = (bf16[256,768]{1,0:T(8,128)(2,1)S(1)}, bf16[256,768]{1,0:T(8,128)(2,1)S(1)}, u32[]{:S(2)}, u32[]{:S(2)}) collective-permute-start(bf16[256,768]{1,0:T(8,128)(2,1)S(1)} %collective-permute-done.15.refs_1_), channel_id=1, source_target_pairs={{0,4},{4,0},{8,12},{12,8},{16,20},{20,16},{24,28},{28,24},{1,5},{5... | collective-permute-start | bytes 1179656 | tf_op jit(solution)/shard_map/ppermute | solution.py:51
  121.7 1.4 collective-permute-start.10
  150.6 26.2 %collective-permute-start.24 = (f32[8,256]{1,0:T(8,128)S(1)}, f32[8,256]{1,0:T(8,128)S(1)}, u32[]{:S(2)}, u32[]{:S(2)}) collective-permute-start(f32[8,256]{1,0:T(8,128)S(1)} %get-tuple-element.30.refs_0_), channel_id=1, source_target_pairs={{0,3},{1,2},{2,1},{3,0},{4,7},{5,6},{6,5},{7,4},{8,11},{9,10},{10,... | collective-permute-start | bytes 24584 | tf_op jit(solution)/shard_map/ppermute | solution.py:51
  153.0 23.8 %collective-permute-start.23 = (f32[8,256]{1,0:T(8,128)S(1)}, f32[8,256]{1,0:T(8,128)S(1)}, u32[]{:S(2)}, u32[]{:S(2)}) collective-permute-start(f32[8,256]{1,0:T(8,128)S(1)} %get-tuple-element.30.refs_0_), channel_id=1, source_target_pairs={{0,2},{1,3},{2,0},{3,1},{4,6},{5,7},{6,4},{7,5},{8,10},{9,11},{10,... | collective-permute-start | bytes 24584 | tf_op jit(solution)/shard_map/ppermute | solution.py:51
  153.0 23.8 %collective-permute-start.22 = (f32[8,256]{1,0:T(8,128)S(1)}, f32[8,256]{1,0:T(8,128)S(1)}, u32[]{:S(2)}, u32[]{:S(2)}) collective-permute-start(f32[8,256]{1,0:T(8,128)S(1)} %get-tuple-element.30.refs_0_), channel_id=1, source_target_pairs={{0,1},{1,0},{2,3},{3,2},{4,5},{5,4},{6,7},{7,6},{8,9},{9,8},{10,11... | collective-permute-start | bytes 24584 | tf_op jit(solution)/shard_map/ppermute | solution.py:51
  155.6 8.2 %copy-start.2 = (f32[1024,6144]{1,0:T(8,128)S(1)}, f32[1024,6144]{1,0:T(8,128)}, u32[]{:S(2)}) copy-start(f32[1024,6144]{1,0:T(8,128)} %copy-done) | copy-start | bytes 75497472
  163.8 13.0 %slice-start.1 = ((s8[12582912]{0:T(1024)(128)(4,1)}), s8[4194304]{0:T(1024)(128)(4,1)S(1)}, s32[]{:S(2)}) async-start(s8[12582912]{0:T(1024)(128)(4,1)} %bitcast), calls=%async_computation.1 | async-start | bytes 8388608
  163.8 13.0 %slice-start.2 = ((s8[12582912]{0:T(1024)(128)(4,1)}), s8[4194304]{0:T(1024)(128)(4,1)S(1)}, s32[]{:S(2)}) async-start(s8[12582912]{0:T(1024)(128)(4,1)} %bitcast), calls=%async_computation.2 | async-start | bytes 8388608

commit v2 on v0

v2 whole, which is shorter than its diff:
```python
import functools
import math

import jax
import jax.numpy as jnp
from jax import lax
from jax.experimental import pallas as pl
from jax.experimental.pallas import tpu as pltpu
from jax.sharding import PartitionSpec as P

D = 8192
FF = 24576
RANK = 256

epsilon = 1e-06
momentum_decay = 0.6
step_rate = 0.5

bf16, f32 = jnp.bfloat16, jnp.float32
VMEM = pl.BlockSpec(memory_space=pltpu.VMEM)
ANY = pl.BlockSpec(memory_space=pl.ANY)
MIB = 1 << 20


def shape(dims, kind):
    return jax.ShapeDtypeStruct(dims, kind)


def params(mib):
    return pltpu.CompilerParams(vmem_limit_bytes=mib * MIB)


def dot(a, b, dims=((1,), (0,))):
    return lax.dot_general(a, b, (dims, ((), ())), preferred_element_type=f32)


def split(x, terms):
    parts = []
    for _ in range(terms):
        part = x.astype(bf16)
        parts.append(part)
        x = x - part.astype(f32)
    return parts


def flip(i, d):
    return lax.bitwise_xor(i, jnp.int32(d))


def swap(x, axis, d):
    return lax.ppermute(x, axis, [(i, i ^ d) for i in range(lax.axis_size(axis))])


def project_kernel(part, depth, mom, grad, basis, *rest):
    rest = rest[-(depth + 5) :]
    buf, lefts, gbuf, bbuf, sems, bsem = rest[0], rest[1 : depth + 1], *rest[depth + 1 :]
    m, n = buf.shape
    half = m // depth
    me = lax.axis_index("col")
    chunk = 1536 if n % 1536 == 0 else n

    def copies(d):
        block = flip(me, d)
        there = pl.ds(pl.multiple_of((2 * block + part) * half, half), half)
        here = pl.ds(pl.multiple_of(block * half, half), half)
        return (
            pltpu.make_async_copy(mom.at[there, :], buf.at[here, :], sems.at[0, d]),
            pltpu.make_async_copy(grad.at[there, :], gbuf.at[here, :], sems.at[1, d]),
        )

    load_basis = pltpu.make_async_copy(basis, bbuf, bsem)
    order = list(reversed(range(depth)))
    for k, d in enumerate(order):
        for copy in copies(d):
            copy.start()
        if k == 0:
            load_basis.start()
    for k, d in enumerate(order):
        for copy in copies(d):
            copy.wait()
        if k == 0:
            load_basis.wait()
        rows = pl.ds(pl.multiple_of(flip(me, d) * half, half), half)

        def step(k, acc):
            cols = pl.ds(pl.multiple_of(k * chunk, 128), chunk)
            total = buf[rows, cols] + gbuf[rows, cols].astype(f32)
            buf[rows, cols] = total
            return acc + dot(bbuf[:, cols], total.astype(bf16), ((1,), (1,)))

        acc = lax.fori_loop(0, n // chunk, step, jnp.zeros((bbuf.shape[0], half), f32))
        lefts[d][...] = acc.astype(lefts[d].dtype)


def project(momentum, gradient, basis, depth, part, after=()):
    m, n = momentum.shape
    m = m // 2
    r = basis.shape[0]
    kinds = [f32] + [bf16] * (depth - 1)
    return pl.pallas_call(
        functools.partial(project_kernel, part, depth),
        out_shape=(pltpu.VMEM((m, n), f32), *[shape((r, m // depth), k) for k in kinds]),
        in_specs=[ANY] * (3 + len(after)),
        out_specs=(VMEM,) * (depth + 1),
        scratch_shapes=[
            pltpu.VMEM((m, n), bf16),
            pltpu.VMEM((r, n), bf16),
            pltpu.SemaphoreType.DMA((2, depth)),
            pltpu.SemaphoreType.DMA,
        ],
        compiler_params=params(12),
        name="project",
    )(stay(momentum), stay(gradient), stay(basis), *after)


def keep(x):
    return pltpu.with_memory_space_constraint(x, pltpu.VMEM)


def stay(x):
    return pltpu.with_memory_space_constraint(x, pltpu.HBM)


def gather_left(lefts, whole):
    half = lefts[0].shape[1]
    me = lax.axis_index("col")
    for d, ref in enumerate(lefts):
        whole[:, pl.ds(pl.multiple_of(flip(me, d) * half, half), half)] = ref[...]
    return whole


def self_product(whole):
    return dot(whole[...], whole[...], ((1,), (1,)))


def first_kernel(depth, width, buf, *rest):
    lefts, (other, mine, gram, whole) = rest[:depth], rest[depth:]
    core = lax.bitwise_and(lax.axis_index("row"), jnp.int32(1))
    size = other.shape[1]
    gather_left(lefts, whole)
    gram[...] = self_product(whole)
    for out, half in ((other, 1 - core), (mine, core)):

        def step(k, carry, out=out, half=half):
            cols = pl.ds(pl.multiple_of(half * size + k * width, 128), width)
            out[:, pl.ds(pl.multiple_of(k * width, 128), width)] = dot(whole[...], buf[:, cols].astype(bf16))
            return carry

        lax.fori_loop(0, size // width, step, 0)


def first_product(buf, lefts, width):
    m, n = buf.shape
    r = lefts[0].shape[0]
    return pl.pallas_call(
        functools.partial(first_kernel, len(lefts), width),
        out_shape=(shape((r, n // 2), f32), shape((r, n // 2), f32), shape((r, r), f32)),
        in_specs=[VMEM] * (1 + len(lefts)),
        out_specs=[VMEM] * 3,
        scratch_shapes=[pltpu.VMEM((r, m), bf16)],
        compiler_params=params(8),
        name="first_product",
    )(keep(buf), *lefts)


def other_kernel(depth, width, buf, sums, gram, *rest):
    lefts, (out, g_mine, g_other, whole, total) = rest[:depth], rest[depth:]
    core = lax.bitwise_and(lax.axis_index("row"), jnp.int32(1))
    size = out.shape[1]
    gather_left(lefts, whole)
    total[...] = gram[...] + self_product(whole)
    h = g_mine.shape[0]
    g_mine[...] = total[pl.ds(pl.multiple_of(core * h, h), h), :]
    g_other[...] = total[pl.ds(pl.multiple_of((1 - core) * h, h), h), :]

    def step(k, carry):
        cols = pl.ds(pl.multiple_of((1 - core) * size + k * width, 128), width)
        at = pl.ds(pl.multiple_of(k * width, 128), width)
        out[:, at] = (sums[:, at] + dot(whole[...], buf[:, cols].astype(bf16))).astype(bf16)
        return carry

    lax.fori_loop(0, size // width, step, 0)


def other_product(buf, sums, gram, lefts, width):
    m, n = buf.shape
    r = lefts[0].shape[0]
    return pl.pallas_call(
        functools.partial(other_kernel, len(lefts), width),
        out_shape=(shape((r, n // 2), bf16), shape((r // 2, r), f32), shape((r // 2, r), f32)),
        in_specs=[VMEM] * (3 + len(lefts)),
        out_specs=[VMEM] * 3,
        scratch_shapes=[pltpu.VMEM((r, m), bf16), pltpu.VMEM((r, r), f32)],
        compiler_params=params(8),
        name="other_product",
    )(keep(buf), sums, gram, *lefts)


def mine_kernel(depth, width, buf, sums, *rest):
    lefts, (out, whole) = rest[:depth], rest[-2:]
    core = lax.bitwise_and(lax.axis_index("row"), jnp.int32(1))
    size = out.shape[1]
    gather_left(lefts, whole)

    def step(k, carry):
        cols = pl.ds(pl.multiple_of(core * size + k * width, 128), width)
        at = pl.ds(pl.multiple_of(k * width, 128), width)
        out[:, at] = sums[:, at] + dot(whole[...], buf[:, cols].astype(bf16))
        return carry

    lax.fori_loop(0, size // width, step, 0)


def mine_product(buf, sums, lefts, width, after):
    m, n = buf.shape
    r = lefts[0].shape[0]
    return pl.pallas_call(
        functools.partial(mine_kernel, len(lefts), width),
        out_shape=shape((r, n // 2), f32),
        in_specs=[VMEM] * (2 + len(lefts)) + [ANY],
        out_specs=VMEM,
        scratch_shapes=[pltpu.VMEM((r, m), bf16)],
        compiler_params=params(8),
        name="mine_product",
    )(keep(buf), sums, *lefts, after)


def pair_sum_kernel(chips, mine, received, _, *outs):
    me = lax.div(lax.axis_index("row"), jnp.int32(2))
    width = outs[0].shape[1]
    for d in range(chips):
        cols = pl.ds(pl.multiple_of(flip(me, d) * width, 128), width)
        outs[d][...] = (mine[:, cols] + received[:, cols].astype(f32)).astype(outs[d].dtype)


def pair_sum(mine, received, chips, after):
    r, n = mine.shape
    kinds = [f32] + [bf16] * (chips - 1)
    return pl.pallas_call(
        functools.partial(pair_sum_kernel, chips),
        out_shape=[shape((r, n // chips), k) for k in kinds],
        in_specs=[VMEM, VMEM, ANY],
        out_specs=[VMEM] * chips,
        compiler_params=params(8),
        name="pair_sum",
    )(mine, received, after)


def share_sum_kernel(own, *refs):
    received, out = refs[:-1], refs[-1]
    out[...] = (own[...] + sum(ref[...].astype(f32) for ref in received)).astype(bf16)


def share_sum(own, received):
    return pl.pallas_call(
        share_sum_kernel,
        out_shape=shape(own.shape, bf16),
        in_specs=[VMEM] * (1 + len(received)),
        out_specs=VMEM,
        compiler_params=params(8),
        name="share_sum",
    )(own, *received)


def eliminate(tiles, at, nb, group):
    sub = lax.broadcasted_iota(jnp.int32, (nb, 128), 0)
    scale = jnp.zeros((nb, 128), f32)
    for g in range(0, nb, group):
        cols = [
            jnp.broadcast_to(tiles[0][:, at + g + j : at + g + j + 1], (nb, 128)) for j in range(group)
        ]
        for j in range(group):
            t = g + j
            pivot = cols[j][t : t + 1, :]
            factor = jnp.where(sub > t, cols[j], 0.0) * (1.0 / pivot)
            scale = jnp.where(sub == t, lax.rsqrt(pivot), scale)
            for l in range(j + 1, group):
                cols[l] = cols[l] - factor * cols[l][t : t + 1, :]
            tiles = [x - factor * x[t : t + 1, :] for x in tiles]
    return [x * scale for x in tiles]


def chol_inverse_kernel(mine, other, out, work):
    n = out.shape[0]
    h = n // 2
    core = lax.bitwise_and(lax.axis_index("row"), jnp.int32(1))
    work[pl.ds(pl.multiple_of(core * h, h), h), :n] = mine[...]
    work[pl.ds(pl.multiple_of((1 - core) * h, h), h), :n] = other[...]
    r_id = lax.broadcasted_iota(jnp.int32, (n, n), 0)
    c_id = lax.broadcasted_iota(jnp.int32, (n, n), 1)
    work[:, n:] = jnp.where(r_id == c_id, 1.0, 0.0).astype(f32)
    nb = 32
    for p in range(n // nb):
        lo = p * nb
        left = (lo // 128) * 128
        right = n + ((lo + nb + 127) // 128) * 128
        tiles = [work[lo : lo + nb, c : c + 128] for c in range(left, right, 128)]
        s = jnp.concatenate(eliminate(tiles, lo - left, nb, 8), axis=1)
        work[lo : lo + nb, left:right] = s
        if lo + nb < n:
            lead = s[:, lo + nb - left : n - left]
            work[lo + nb :, left:right] -= lax.dot_general(
                lead, s, (((0,), (0,)), ((), ())), precision=lax.Precision.HIGHEST, preferred_element_type=f32
            )
    out[...] = jnp.where(r_id >= c_id, work[:, n:], 0.0)


def chol_inverse(mine, other):
    n = mine.shape[1]
    return pl.pallas_call(
        chol_inverse_kernel,
        out_shape=shape((n, n), f32),
        in_specs=[VMEM, VMEM],
        out_specs=VMEM,
        scratch_shapes=[pltpu.VMEM((n, 2 * n), f32)],
        compiler_params=params(8),
        name="chol_inverse",
    )(mine, other)


def ortho_kernel(depth, inverse, *refs):
    lefts, out = refs[: 2 * depth], refs[2 * depth]
    half = lefts[0].shape[1]
    me = lax.axis_index("col")
    parts = split(inverse[...], 3)
    for k, ref in enumerate(lefts):
        part, d = divmod(k, depth)
        rows = pl.ds(pl.multiple_of((2 * flip(me, d) + part) * half, half), half)
        out[rows, :] = sum(dot(ref[...], x, ((0,), (1,))) for x in reversed(parts)).astype(bf16)


def ortho(inverse, lefts):
    r, half = lefts[0].shape
    return pl.pallas_call(
        functools.partial(ortho_kernel, len(lefts) // 2),
        out_shape=shape((half * len(lefts), r), bf16),
        in_specs=[VMEM] * (1 + len(lefts)),
        out_specs=VMEM,
        compiler_params=params(8),
        name="ortho",
    )(inverse, *lefts)


def apply_inverse(parts, block):
    return sum(dot(x, block) for x in reversed(parts))


def share_kernel(inverse, own, *refs):
    received, (out, squares) = refs[:-2], refs[-2:]
    out[...] = (own[...] + sum(ref[...].astype(f32) for ref in received)).astype(bf16)
    value = apply_inverse(split(inverse[...], 2), out[...])
    total = jnp.sum(value * value, axis=1, keepdims=True)
    squares[...] = jnp.transpose(jnp.broadcast_to(total, (total.shape[0], 128)))[:8, :]


def share_of(inverse, own, received):
    r = own.shape[0]
    return pl.pallas_call(
        share_kernel,
        out_shape=(shape(own.shape, bf16), shape((8, r), f32)),
        in_specs=[VMEM] * (2 + len(received)),
        out_specs=(VMEM, VMEM),
        compiler_params=params(8),
        name="share",
    )(inverse, own, *received)


def result_kernel(d, factor, buf0, buf1, ortho_ref, inverse, squares, block0, block1, weight, *rest):
    new_weight, new_momentum, basis, mbuf, wbuf, vbuf, nbuf, in_sems, out_sems = rest[-9:]
    m = ortho_ref.shape[0]
    r, width = block0.shape
    half = width * (lax.axis_size("row") // 2)
    row = lax.axis_index("row")
    core = lax.bitwise_and(row, jnp.int32(1))
    chip = flip(lax.div(row, jnp.int32(2)), d)
    starts = [core * half + chip * width, (1 - core) * half + chip * width]
    cols = [pl.ds(pl.multiple_of(start, 128), width) for start in starts]
    loads = [pltpu.make_async_copy(weight.at[:, cols[b]], wbuf.at[b], in_sems.at[b]) for b in range(2)]
    stores = [
        pltpu.make_async_copy(src.at[b], dst.at[:, cols[b]], out_sems.at[k, b])
        for b in range(2)
        for k, (src, dst) in enumerate(((mbuf, new_momentum), (vbuf, new_weight), (nbuf, basis)))
    ]
    for load in loads:
        load.start()
    scale = lax.rsqrt(squares[...] / FF + epsilon)
    scale = jnp.transpose(jnp.concatenate([scale] * 16, axis=0))[:, :1]
    parts = split(inverse[...], 2)
    lows = []
    for b, block in enumerate((block0, block1)):
        right = apply_inverse(parts, block[...])
        lows.append(right.astype(bf16))
        nbuf[b] = (right * scale).astype(bf16)
    depth = lax.axis_size("col")
    size = m // (2 * depth)
    for b in range(2):
        loads[b].wait()

        def step(k, carry, b=b):
            for part, buf in enumerate((buf0, buf1)):
                here = pl.ds(pl.multiple_of(k * size, size), size)
                rows = pl.ds(pl.multiple_of((2 * k + part) * size, size), size)
                correction = dot(ortho_ref[rows, :], lows[b])
                mbuf[b, rows, :] = buf[here, cols[b]] - (1.0 - momentum_decay) * correction
                change = dot(ortho_ref[rows, :], nbuf[b])
                vbuf[b, rows, :] = (wbuf[b, rows, :].astype(f32) - factor * change).astype(bf16)
            return carry

        lax.fori_loop(0, depth, step, 0, unroll=2)
        for store in stores[3 * b : 3 * b + 3]:
            store.start()
    for store in stores:
        store.wait()


def results(d, factor, bufs, ortho_bf, inverse, squares, blocks, weight, before):
    m, n = weight.shape
    r, width = blocks[0].shape
    ins = [*map(keep, bufs), ortho_bf, inverse, squares, *blocks, stay(weight), *map(stay, before)]
    return pl.pallas_call(
        functools.partial(result_kernel, d, factor),
        out_shape=(shape((m, n), bf16), shape((m, n), f32), shape((r, n), bf16)),
        in_specs=[VMEM] * 7 + [ANY] * (1 + len(before)),
        out_specs=[ANY] * 3,
        input_output_aliases={8 + k: k for k in range(len(before))},
        scratch_shapes=[
            pltpu.VMEM((2, m, width), f32),
            pltpu.VMEM((2, m, width), bf16),
            pltpu.VMEM((2, m, width), bf16),
            pltpu.VMEM((2, r, width), bf16),
            pltpu.SemaphoreType.DMA((2,)),
            pltpu.SemaphoreType.DMA((3, 2)),
        ],
        compiler_params=params(20),
        name="results",
    )(*ins)


def pair_up(terms):
    while len(terms) > 1:
        terms = [terms[2 * i] + terms[2 * i + 1] for i in range(len(terms) // 2)]
    return terms[0]


def exchange(x, axis, count, unit=1):
    return [x] + [swap(x, axis, unit * d) for d in range(1, count)]


def per_device(weight, gradient, momentum, old_basis):
    depth, rows = lax.axis_size("col"), lax.axis_size("row")
    chips = rows // 2
    m, n = momentum.shape
    width = n // rows

    bufs, lefts, after = [], [], ()
    for part in range(2):
        buf, own, *sent = project(momentum, gradient, old_basis, depth, part, after)
        after = (sent[0],)
        low = share_sum(own, [swap(x, "col", d + 1) for d, x in enumerate(sent)])
        bufs.append(buf)
        lefts.append(exchange(low, "col", depth))

    other, mine, gram = first_product(bufs[0], lefts[0], width)
    other, g_mine, g_other = other_product(bufs[1], other, gram, lefts[1], width)
    received = swap(other, "row", 1)
    g_mine = g_mine + swap(g_other, "row", 1)
    mine = mine_product(bufs[1], mine, lefts[1], width, other)
    own, *sent = pair_sum(mine, received, chips, g_mine)
    g_mine = pair_up(exchange(g_mine, "row", chips, 2))
    got = [swap(x, "row", 2 * (d + 1)) for d, x in enumerate(sent)]

    inverse = chol_inverse(g_mine, swap(g_mine, "row", 1))
    ortho_bf = ortho(inverse, lefts[0] + lefts[1])

    share, squares = share_of(inverse, own, got)
    blocks = exchange(share, "row", chips, 2)
    squares = squares + swap(squares, "row", 1)
    squares = pair_up(exchange(squares, "row", chips, 2))
    squares = pair_up(exchange(squares, "col", depth))
    factor = step_rate * math.sqrt(D / RANK)
    outs = ()
    for d, block in enumerate(blocks):
        pair = (block, swap(block, "row", 1))
        outs = results(d, factor, bufs, ortho_bf, inverse, squares, pair, weight, outs)
    return tuple(outs)


def plain_per_device(weight, gradient, momentum, old_basis):
    buffer = momentum + gradient.astype(f32)
    buffer_low = buffer.astype(bf16)
    left_factor = lax.psum(dot(buffer_low, old_basis, ((1,), (1,))), "col")
    gram_share = lax.dot_general(
        left_factor,
        left_factor,
        (((0,), (0,)), ((), ())),
        precision=lax.Precision.HIGHEST,
        preferred_element_type=f32,
    )
    chol_factor = jnp.linalg.cholesky(lax.psum(gram_share, "row"))
    orthonormal = lax.linalg.triangular_solve(
        chol_factor, left_factor, left_side=False, lower=True, transpose_a=True
    ).astype(bf16)
    right_share = lax.psum_scatter(
        dot(orthonormal, buffer_low, ((0,), (0,))), "row", scatter_dimension=0, tiled=True
    )
    sum_squares = lax.psum(jnp.sum(right_share * right_share, axis=1), "col")
    scale_share = jnp.sqrt(sum_squares / FF + epsilon)
    basis_share = (right_share / scale_share[:, None]).astype(bf16)
    new_basis = lax.all_gather(basis_share, "row", axis=0, tiled=True)
    col_scale = lax.all_gather(scale_share, "row", axis=0, tiled=True)
    scaled = (orthonormal.astype(f32) * col_scale[None, :]).astype(bf16)
    new_momentum = buffer - (1.0 - momentum_decay) * dot(scaled, new_basis)
    factor = step_rate * math.sqrt(D / RANK)
    new_weight = (weight.astype(f32) - factor * dot(orthonormal, new_basis)).astype(bf16)
    return (new_weight, new_momentum, new_basis)


def power_of_two(k):
    return k > 1 and k & (k - 1) == 0


def solution(mesh):
    rows, depth = mesh.shape["row"], mesh.shape["col"]
    tiled = (
        power_of_two(rows)
        and power_of_two(depth)
        and D % (rows * depth * 128) == 0
        and FF % (rows * depth * 256) == 0
    )
    return jax.shard_map(
        per_device if tiled else plain_per_device,
        mesh=mesh,
        in_specs=(P("row", "col"), P("row", "col"), P("row", "col"), P(None, "col")),
        out_specs=(P("row", "col"), P("row", "col"), P(None, "col")),
        check_vma=False,
    )
```

time: 377 us -> 146 us (0.39)
  waiting for transfers between devices: 185 us -> 38.7 us
  matrix products: 81.6 us -> 0 us
  Pallas kernels: 0 us -> 65.4 us
  other arithmetic: 58 us -> 0.06 us
  starting transfers between devices: 0.34 us -> 40.3 us
  blocking collectives: 23.9 us -> 0 us
  between operations: 15.9 us -> 1.02 us
  local copies, waits for them, and re-layouts: 11.4 us -> 0 us
    psum x2 -> x0, waiting for transfers between devices: 107 us -> none  [the longest x1 54.6 us: per_device(): left_factor = lax.psum(local_left, 'col')]
    dot_general x5 -> x0, matrix products: 76.7 us -> none  [the longest x1 24.6 us: per_device(): correction = jnp.dot(scaled, new_basis, preferred_element_type=jnp.float32)]
    pallas_call x0 -> x15, Pallas kernels: none -> 65.4 us  [the longest x4 27.7 us: results(): pl.pallas_call(functools.partial(result_kernel, d, factor), out_shape=(sh...]
    reduce_scatter x1 -> x0, waiting for transfers between devices: 60 us -> none  [per_device(): lax.psum_scatter(lax.dot_general(orthonormal, buffer_low, (((0,), (0,)),...]
    another operation x9 -> x0, other arithmetic: 53.7 us -> none  [the longest x6 34 us: orthonormalize(): chol_factor = jnp.linalg.cholesky(gram_matrix)]
    ppermute x0 -> x35, starting transfers between devices: none -> 40.3 us  [swap(): lax.ppermute(x, axis, [(i, i ^ d) for i in range(lax.axis_size(axis))])]
    ppermute x0 -> x35, waiting for transfers between devices: none -> 38.7 us  [swap(): lax.ppermute(x, axis, [(i, i ^ d) for i in range(lax.axis_size(axis))])]
    all_gather x1 -> x0, waiting for transfers between devices: 17.5 us -> none  [per_device(): new_basis = lax.all_gather(basis_share, 'row', axis=0, tiled=True)]
  transfers between devices with their start and end apart: 4 -> 35, of which waited for: 4 -> 12; matrix products, arithmetic and copies ran while one was open for 0% -> 0% of each run, Pallas kernels for 0% -> 32%
where the time goes in v2:
time: 146 us; the launch traced here: 145 us
  Pallas kernels  65.4 us (45%)
  starting transfers between devices  40.3 us (28%)
  waiting for transfers between devices  38.7 us (27%)
    ppermute x35, starting transfers between devices, swap(): lax.ppermute(x, axis, [(i, i ^ d) for i in range(lax.axis_size(axis))])  40.3 us
    ppermute x35, waiting for transfers between devices, swap(): lax.ppermute(x, axis, [(i, i ^ d) for i in range(lax.axis_size(axis))])  38.7 us
    pallas_call x4, Pallas kernels, results(): pl.pallas_call(functools.partial(result_kernel, d, factor), out_shape=(sh...  27.7 us
    pallas_call x2, Pallas kernels, project(): pl.pallas_call(functools.partial(project_kernel, part, depth), out_shape=...  19.3 us
    pallas_call x1, Pallas kernels, chol_inverse(): pl.pallas_call(chol_inverse_kernel, out_shape=shape((n, n), f32), in_spec...  9.14 us
    pallas_call x1, Pallas kernels, first_product(): pl.pallas_call(functools.partial(first_kernel, len(lefts), width), out_sh...  3.36 us
  transfers between devices with their start and end apart: 35, of which 12 were waited for; matrix products, arithmetic and copies ran while one was open for 0% of the time, Pallas kernels for 32%

profile of v2, /device:TPU:0, one launch (start us, length us, event | category | flops | bytes accessed | tf_op | source)
XLA Modules:
  0.0 145.5 jit_solution(8214813707051447188)
XLA Ops:
  0.6 9.7 %project.2 = (f32[512,6144]{1,0:T(8,128)S(1)}, f32[256,128]{1,0:T(8,128)S(1)}, bf16[256,128]{1,0:T(8,128)(2,1)S(1)}, bf16[256,128]{1,0:T(8,128)(2,1)S(1)}, bf16[256,128]{1,0:T(8,128)(2,1)S(1)}) custom-call(f32[1024,6144]{1,0:T(8,128)} %mom.3, bf16[1024,6144]{1,0:T(8,128)(2,1)} %grad.3, bf16[256,6144]{1,0:T(8,128)(2,1)} %basis.3), custom_call_target="tpu_custom_call" | custom-call | tf_op jit(solution)/shard_map/project/pallas_call | solution.py:100
  10.3 3.1 %collective-permute-start = (bf16[256,128]{1,0:T(8,128)(2,1)S(1)}, bf16[256,128]{1,0:T(8,128)(2,1)S(1)}, u32[]{:S(2)}, u32[]{:S(2)}) collective-permute-start(bf16[256,128]{1,0:T(8,128)(2,1)S(1)} %get-tuple-element.35.rest_0_), channel_id=1, source_target_pairs={{0,1},{1,0},{2,3},{3,2},{4,5},{5,4},{6,7},{7,6},{8,9},{9,8},{10,11... | collective-permute-start | bytes 196616 | tf_op jit(solution)/shard_map/ppermute | solution.py:51
  13.4 2.6 %collective-permute-start.1 = (bf16[256,128]{1,0:T(8,128)(2,1)S(1)}, bf16[256,128]{1,0:T(8,128)(2,1)S(1)}, u32[]{:S(2)}, u32[]{:S(2)}) collective-permute-start(bf16[256,128]{1,0:T(8,128)(2,1)S(1)} %get-tuple-element.38), channel_id=1, source_target_pairs={{0,2},{1,3},{2,0},{3,1},{4,6},{5,7},{6,4},{7,5},{8,10},{9,11},{10,... | collective-permute-start | bytes 196616 | tf_op jit(solution)/shard_map/ppermute | solution.py:51
  16.0 9.7 %project.3 = (f32[512,6144]{1,0:T(8,128)S(1)}, f32[256,128]{1,0:T(8,128)S(1)}, bf16[256,128]{1,0:T(8,128)(2,1)S(1)}, bf16[256,128]{1,0:T(8,128)(2,1)S(1)}, bf16[256,128]{1,0:T(8,128)(2,1)S(1)}) custom-call(f32[1024,6144]{1,0:T(8,128)} %mom.3, bf16[1024,6144]{1,0:T(8,128)(2,1)} %grad.3, bf16[256,6144]{1,0:T(8,128)(2,1)} %basis.3, ...), custom_call_target="tpu_custom_call" | custom-call | tf_op jit(solution)/shard_map/project/pallas_call | solution.py:100
  25.7 1.0 collective-permute-start.6
  26.6 3.5 %collective-permute-start.7 = (bf16[256,128]{1,0:T(8,128)(2,1)S(1)}, bf16[256,128]{1,0:T(8,128)(2,1)S(1)}, u32[]{:S(2)}, u32[]{:S(2)}) collective-permute-start(bf16[256,128]{1,0:T(8,128)(2,1)S(1)} %get-tuple-element.44), channel_id=1, source_target_pairs={{0,2},{1,3},{2,0},{3,1},{4,6},{5,7},{6,4},{7,5},{8,10},{9,11},{10,... | collective-permute-start | bytes 196616 | tf_op jit(solution)/shard_map/ppermute | solution.py:51
  30.2 0.6 collective-permute-start.3
  30.8 3.8 %collective-permute-start.4 = (bf16[256,128]{1,0:T(8,128)(2,1)S(1)}, bf16[256,128]{1,0:T(8,128)(2,1)S(1)}, u32[]{:S(2)}, u32[]{:S(2)}) collective-permute-start(bf16[256,128]{1,0:T(8,128)(2,1)S(1)} %share_sum.2.rest_0_.refs_0_), channel_id=1, source_target_pairs={{0,2},{1,3},{2,0},{3,1},{4,6},{5,7},{6,4},{7,5},{8,10},{9,11},{10,... | collective-permute-start | bytes 196616 | tf_op jit(solution)/shard_map/ppermute | solution.py:51
  34.6 1.5 %collective-permute-done.8.refs_2_ = bf16[256,128]{1,0:T(8,128)(2,1)S(1)} collective-permute-done((bf16[256,128]{1,0:T(8,128)(2,1)S(1)}, bf16[256,128]{1,0:T(8,128)(2,1)S(1)}, u32[]{:S(2)}, u32[]{:S(2)}) %collective-permute-start.8) | collective-permute-done | bytes 65568 | tf_op jit(solution)/shard_map/ppermute | solution.py:51
  36.2 5.6 %collective-permute-start.10 = (bf16[256,128]{1,0:T(8,128)(2,1)S(1)}, bf16[256,128]{1,0:T(8,128)(2,1)S(1)}, u32[]{:S(2)}, u32[]{:S(2)}) collective-permute-start(bf16[256,128]{1,0:T(8,128)(2,1)S(1)} %share_sum.3.rest_0_.refs_4_), channel_id=1, source_target_pairs={{0,2},{1,3},{2,0},{3,1},{4,6},{5,7},{6,4},{7,5},{8,10},{9,11},{10,... | collective-permute-start | bytes 196616 | tf_op jit(solution)/shard_map/ppermute | solution.py:51
  41.9 0.6 collective-permute-start.9
  42.5 3.4 %first_product.1 = (f32[256,3072]{1,0:T(8,128)S(1)}, f32[256,3072]{1,0:T(8,128)S(1)}, f32[256,256]{1,0:T(8,128)S(1)}) custom-call(f32[512,6144]{1,0:T(8,128)S(1)} %get-tuple-element.34.buf.buf0, bf16[256,128]{1,0:T(8,128)(2,1)S(1)} %share_sum.2.rest_0_.refs_0_, bf16[256,128]{1,0:T(8,128)(2,1)S(1)} %collective-permute-done.3.rest_1_.refs_1_, ...), custom_call_target="tpu_custom_call" | custom-call | tf_op jit(solution)/shard_map/first_product/pallas_call | solution.py:155
  45.9 2.0 %collective-permute-done.11.rest_3_.refs_7_ = bf16[256,128]{1,0:T(8,128)(2,1)S(1)} collective-permute-done((bf16[256,128]{1,0:T(8,128)(2,1)S(1)}, bf16[256,128]{1,0:T(8,128)(2,1)S(1)}, u32[]{:S(2)}, u32[]{:S(2)}) %collective-permute-start.11) | collective-permute-done | bytes 65568 | tf_op jit(solution)/shard_map/ppermute | solution.py:51
  47.9 1.9 %other_product.1 = (bf16[256,3072]{1,0:T(8,128)(2,1)S(1)}, f32[128,256]{1,0:T(8,128)S(1)}, f32[128,256]{1,0:T(8,128)S(1)}) custom-call(f32[512,6144]{1,0:T(8,128)S(1)} %get-tuple-element.36.buf.buf1, f32[256,3072]{1,0:T(8,128)S(1)} %get-tuple-element.40.sums, f32[256,256]{1,0:T(8,128)S(1)} %get-tuple-element.41.gram, ...), custom_call_target="tpu_custom_call" | custom-call | tf_op jit(solution)/shard_map/other_product/pallas_call | solution.py:188
  49.9 0.5 collective-permute-start.12
  50.4 3.1 %collective-permute-done.12 = f32[128,256]{1,0:T(8,128)S(1)} collective-permute-done((f32[128,256]{1,0:T(8,128)S(1)}, f32[128,256]{1,0:T(8,128)S(1)}, u32[]{:S(2)}, u32[]{:S(2)}) %collective-permute-start.12) | collective-permute-done | bytes 131104 | tf_op jit(solution)/shard_map/ppermute | solution.py:51
  53.5 1.6 %collective-permute-start.13 = (f32[128,256]{1,0:T(8,128)S(1)}, f32[128,256]{1,0:T(8,128)S(1)}, u32[]{:S(2)}, u32[]{:S(2)}) collective-permute-start(f32[128,256]{1,0:T(8,128)S(1)} %add.33._), channel_id=1, source_target_pairs={{0,8},{4,12},{8,0},{12,4},{16,24},{20,28},{24,16},{28,20},{1,9},{5... | collective-permute-start | bytes 393224 | tf_op jit(solution)/shard_map/ppermute | solution.py:51
  55.0 1.5 %collective-permute-start.14 = (f32[128,256]{1,0:T(8,128)S(1)}, f32[128,256]{1,0:T(8,128)S(1)}, u32[]{:S(2)}, u32[]{:S(2)}) collective-permute-start(f32[128,256]{1,0:T(8,128)S(1)} %add.33._), channel_id=1, source_target_pairs={{0,16},{4,20},{8,24},{12,28},{16,0},{20,4},{24,8},{28,12},{1,17},{... | collective-permute-start | bytes 393224 | tf_op jit(solution)/shard_map/ppermute | solution.py:51
  56.5 0.5 collective-permute-start.15
  57.0 1.8 %mine_product.1.mine = f32[256,3072]{1,0:T(8,128)S(1)} custom-call(f32[512,6144]{1,0:T(8,128)S(1)} %get-tuple-element.36.buf.buf1, f32[256,3072]{1,0:T(8,128)S(1)} %get-tuple-element.48.sums, bf16[256,128]{1,0:T(8,128)(2,1)S(1)} %share_sum.3.rest_0_.refs_4_, bf16[256,128]{1,0:T(8,128)(2,1)S(1)} %collective-permute-done.9.rest_1_.refs_5_, ...), custom_call_target="tpu_custom_call" | custom-call | tf_op jit(solution)/shard_map/mine_product/pallas_call | solution.py:217
  59.2 1.6 %collective-permute-start.18 = (bf16[256,768]{1,0:T(8,128)(2,1)S(1)}, bf16[256,768]{1,0:T(8,128)(2,1)S(1)}, u32[]{:S(2)}, u32[]{:S(2)}) collective-permute-start(bf16[256,768]{1,0:T(8,128)(2,1)S(1)} %get-tuple-element.51), channel_id=1, source_target_pairs={{0,8},{4,12},{8,0},{12,4},{16,24},{20,28},{24,16},{28,20},{1,9},{5... | collective-permute-start | bytes 1179656 | tf_op jit(solution)/shard_map/ppermute | solution.py:51
  60.7 1.5 %collective-permute-start.19 = (bf16[256,768]{1,0:T(8,128)(2,1)S(1)}, bf16[256,768]{1,0:T(8,128)(2,1)S(1)}, u32[]{:S(2)}, u32[]{:S(2)}) collective-permute-start(bf16[256,768]{1,0:T(8,128)(2,1)S(1)} %get-tuple-element.52), channel_id=1, source_target_pairs={{0,16},{4,20},{8,24},{12,28},{16,0},{20,4},{24,8},{28,12},{1,17},{... | collective-permute-start | bytes 1179656 | tf_op jit(solution)/shard_map/ppermute | solution.py:51
  62.2 0.5 collective-permute-start.20
  62.7 1.0 collective-permute-done.15
  63.8 1.3 collective-permute-done.16.other
  65.2 9.1 %chol_inverse.1.inverse = f32[256,256]{1,0:T(8,128)S(1)} custom-call(f32[128,256]{1,0:T(8,128)S(1)} %add_add_fusion.mine, f32[128,256]{1,0:T(8,128)S(1)} %collective-permute-done.16.other), custom_call_target="tpu_custom_call" | custom-call | tf_op jit(solution)/shard_map/chol_inverse/pallas_call | solution.py:310
  74.3 5.6 %collective-permute-done.19.refs_1_ = bf16[256,768]{1,0:T(8,128)(2,1)S(1)} collective-permute-done((bf16[256,768]{1,0:T(8,128)(2,1)S(1)}, bf16[256,768]{1,0:T(8,128)(2,1)S(1)}, u32[]{:S(2)}, u32[]{:S(2)}) %collective-permute-start.19) | collective-permute-done | bytes 393248 | tf_op jit(solution)/shard_map/ppermute | solution.py:51
  80.0 0.6 share.1
  80.5 1.3 collective-permute-start.32
  81.8 0.8 collective-permute-start.30
  82.6 1.4 collective-permute-start.28
  84.1 1.2 collective-permute-done.21
  85.2 1.2 collective-permute-start.22
  86.5 0.8 collective-permute-start.23
  87.3 12.0 %collective-permute-done.22 = f32[8,256]{1,0:T(8,128)S(1)} collective-permute-done((f32[8,256]{1,0:T(8,128)S(1)}, f32[8,256]{1,0:T(8,128)S(1)}, u32[]{:S(2)}, u32[]{:S(2)}) %collective-permute-start.22) | collective-permute-done | bytes 8224 | tf_op jit(solution)/shard_map/ppermute | solution.py:51
  99.3 1.4 collective-permute-start.24
  100.7 0.5 collective-permute-start.33
  101.7 2.1 %collective-permute-done.24 = f32[8,256]{1,0:T(8,128)S(1)} collective-permute-done((f32[8,256]{1,0:T(8,128)S(1)}, f32[8,256]{1,0:T(8,128)S(1)}, u32[]{:S(2)}, u32[]{:S(2)}) %collective-permute-start.24) | collective-permute-done | bytes 8224 | tf_op jit(solution)/shard_map/ppermute | solution.py:51
  103.8 3.6 %collective-permute-done.25 = f32[8,256]{1,0:T(8,128)S(1)} collective-permute-done((f32[8,256]{1,0:T(8,128)S(1)}, f32[8,256]{1,0:T(8,128)S(1)}, u32[]{:S(2)}, u32[]{:S(2)}) %collective-permute-start.25) | collective-permute-done | bytes 8224 | tf_op jit(solution)/shard_map/ppermute | solution.py:51
  107.5 1.7 %collective-permute-start.26 = (f32[8,256]{1,0:T(8,128)S(1)}, f32[8,256]{1,0:T(8,128)S(1)}, u32[]{:S(2)}, u32[]{:S(2)}) collective-permute-start(f32[8,256]{1,0:T(8,128)S(1)} %add_add_fusion.2), channel_id=1, source_target_pairs={{0,2},{1,3},{2,0},{3,1},{4,6},{5,7},{6,4},{7,5},{8,10},{9,11},{10,... | collective-permute-start | bytes 24584 | tf_op jit(solution)/shard_map/ppermute | solution.py:51
  109.2 2.9 %collective-permute-done.26 = f32[8,256]{1,0:T(8,128)S(1)} collective-permute-done((f32[8,256]{1,0:T(8,128)S(1)}, f32[8,256]{1,0:T(8,128)S(1)}, u32[]{:S(2)}, u32[]{:S(2)}) %collective-permute-start.26) | collective-permute-done | bytes 8224 | tf_op jit(solution)/shard_map/ppermute | solution.py:51
  112.0 2.0 %collective-permute-start.27 = (f32[8,256]{1,0:T(8,128)S(1)}, f32[8,256]{1,0:T(8,128)S(1)}, u32[]{:S(2)}, u32[]{:S(2)}) collective-permute-start(f32[8,256]{1,0:T(8,128)S(1)} %add_add_fusion.2), channel_id=1, source_target_pairs={{0,3},{1,2},{2,1},{3,0},{4,7},{5,6},{6,5},{7,4},{8,11},{9,10},{10,... | collective-permute-start | bytes 24584 | tf_op jit(solution)/shard_map/ppermute | solution.py:51
  114.0 1.2 ortho.1.ortho_ref
  115.2 2.3 %collective-permute-done.27 = f32[8,256]{1,0:T(8,128)S(1)} collective-permute-done((f32[8,256]{1,0:T(8,128)S(1)}, f32[8,256]{1,0:T(8,128)S(1)}, u32[]{:S(2)}, u32[]{:S(2)}) %collective-permute-start.27) | collective-permute-done | bytes 8224 | tf_op jit(solution)/shard_map/ppermute | solution.py:51
  117.5 6.9 %results.4 = (bf16[1024,6144]{1,0:T(8,128)(2,1)}, f32[1024,6144]{1,0:T(8,128)}, bf16[256,6144]{1,0:T(8,128)(2,1)}) custom-call(f32[512,6144]{1,0:T(8,128)S(1)} %get-tuple-element.34.buf.buf0, f32[512,6144]{1,0:T(8,128)S(1)} %get-tuple-element.36.buf.buf1, bf16[1024,256]{1,0:T(8,128)(2,1)S(1)} %ortho.1.ortho_ref, f32[256,256]{1,0:T(8,128)S(1)} %chol_inverse.1.inverse, ...), custom_call_target="tpu_custom_call" | custom-call | tf_op jit(solution)/shard_map/results/pallas_call | solution.py:420
  124.4 7.0 %results.5 = (bf16[1024,6144]{1,0:T(8,128)(2,1)}, f32[1024,6144]{1,0:T(8,128)}, bf16[256,6144]{1,0:T(8,128)(2,1)}) custom-call(f32[512,6144]{1,0:T(8,128)S(1)} %get-tuple-element.34.buf.buf0, f32[512,6144]{1,0:T(8,128)S(1)} %get-tuple-element.36.buf.buf1, ...), custom_call_target="tpu_custom_call", output_to_operand_aliasing={{0}: (8, {}), {1}: (9, {}), {2}: (10, {})} | custom-call | tf_op jit(solution)/shard_map/results/pallas_call | solution.py:420
  131.4 6.9 %results.6 = (bf16[1024,6144]{1,0:T(8,128)(2,1)}, f32[1024,6144]{1,0:T(8,128)}, bf16[256,6144]{1,0:T(8,128)(2,1)}) custom-call(f32[512,6144]{1,0:T(8,128)S(1)} %get-tuple-element.34.buf.buf0, f32[512,6144]{1,0:T(8,128)S(1)} %get-tuple-element.36.buf.buf1, ...), custom_call_target="tpu_custom_call", output_to_operand_aliasing={{0}: (8, {}), {1}: (9, {}), {2}: (10, {})} | custom-call | tf_op jit(solution)/shard_map/results/pallas_call | solution.py:420
  138.3 7.0 %results.7 = (bf16[1024,6144]{1,0:T(8,128)(2,1)}, f32[1024,6144]{1,0:T(8,128)}, bf16[256,6144]{1,0:T(8,128)(2,1)}) custom-call(f32[512,6144]{1,0:T(8,128)S(1)} %get-tuple-element.34.buf.buf0, f32[512,6144]{1,0:T(8,128)S(1)} %get-tuple-element.36.buf.buf1, ...), custom_call_target="tpu_custom_call", output_to_operand_aliasing={{0}: (8, {}), {1}: (9, {}), {2}: (10, {})} | custom-call | tf_op jit(solution)/shard_map/results/pallas_call | solution.py:420
  (42 shorter events, 1.3 us)
Async XLA Ops:
  10.3 19.8 %collective-permute-start = (bf16[256,128]{1,0:T(8,128)(2,1)S(1)}, bf16[256,128]{1,0:T(8,128)(2,1)S(1)}, u32[]{:S(2)}, u32[]{:S(2)}) collective-permute-start(bf16[256,128]{1,0:T(8,128)(2,1)S(1)} %get-tuple-element.35.rest_0_), channel_id=1, source_target_pairs={{0,1},{1,0},{2,3},{3,2},{4,5},{5,4},{6,7},{7,6},{8,9},{9,8},{10,11... | collective-permute-start | bytes 196616 | tf_op jit(solution)/shard_map/ppermute | solution.py:51
  13.4 16.7 %collective-permute-start.1 = (bf16[256,128]{1,0:T(8,128)(2,1)S(1)}, bf16[256,128]{1,0:T(8,128)(2,1)S(1)}, u32[]{:S(2)}, u32[]{:S(2)}) collective-permute-start(bf16[256,128]{1,0:T(8,128)(2,1)S(1)} %get-tuple-element.38), channel_id=1, source_target_pairs={{0,2},{1,3},{2,0},{3,1},{4,6},{5,7},{6,4},{7,5},{8,10},{9,11},{10,... | collective-permute-start | bytes 196616 | tf_op jit(solution)/shard_map/ppermute | solution.py:51
  16.0 14.1 %collective-permute-start.2 = (bf16[256,128]{1,0:T(8,128)(2,1)S(1)}, bf16[256,128]{1,0:T(8,128)(2,1)S(1)}, u32[]{:S(2)}, u32[]{:S(2)}) collective-permute-start(bf16[256,128]{1,0:T(8,128)(2,1)S(1)} %get-tuple-element.39), channel_id=1, source_target_pairs={{0,3},{1,2},{2,1},{3,0},{4,7},{5,6},{6,5},{7,4},{8,11},{9,10},{10,... | collective-permute-start | bytes 196616 | tf_op jit(solution)/shard_map/ppermute | solution.py:51
  25.7 9.0 %collective-permute-start.6 = (bf16[256,128]{1,0:T(8,128)(2,1)S(1)}, bf16[256,128]{1,0:T(8,128)(2,1)S(1)}, u32[]{:S(2)}, u32[]{:S(2)}) collective-permute-start(bf16[256,128]{1,0:T(8,128)(2,1)S(1)} %get-tuple-element.43), channel_id=1, source_target_pairs={{0,1},{1,0},{2,3},{3,2},{4,5},{5,4},{6,7},{7,6},{8,9},{9,8},{10,11... | collective-permute-start | bytes 196616 | tf_op jit(solution)/shard_map/ppermute | solution.py:51
  26.6 8.0 %collective-permute-start.7 = (bf16[256,128]{1,0:T(8,128)(2,1)S(1)}, bf16[256,128]{1,0:T(8,128)(2,1)S(1)}, u32[]{:S(2)}, u32[]{:S(2)}) collective-permute-start(bf16[256,128]{1,0:T(8,128)(2,1)S(1)} %get-tuple-element.44), channel_id=1, source_target_pairs={{0,2},{1,3},{2,0},{3,1},{4,6},{5,7},{6,4},{7,5},{8,10},{9,11},{10,... | collective-permute-start | bytes 196616 | tf_op jit(solution)/shard_map/ppermute | solution.py:51
  30.1 6.1 %collective-permute-start.8 = (bf16[256,128]{1,0:T(8,128)(2,1)S(1)}, bf16[256,128]{1,0:T(8,128)(2,1)S(1)}, u32[]{:S(2)}, u32[]{:S(2)}) collective-permute-start(bf16[256,128]{1,0:T(8,128)(2,1)S(1)} %get-tuple-element.45), channel_id=1, source_target_pairs={{0,3},{1,2},{2,1},{3,0},{4,7},{5,6},{6,5},{7,4},{8,11},{9,10},{10,... | collective-permute-start | bytes 196616 | tf_op jit(solution)/shard_map/ppermute | solution.py:51
  30.2 11.7 %collective-permute-start.3 = (bf16[256,128]{1,0:T(8,128)(2,1)S(1)}, bf16[256,128]{1,0:T(8,128)(2,1)S(1)}, u32[]{:S(2)}, u32[]{:S(2)}) collective-permute-start(bf16[256,128]{1,0:T(8,128)(2,1)S(1)} %share_sum.2.rest_0_.refs_0_), channel_id=1, source_target_pairs={{0,1},{1,0},{2,3},{3,2},{4,5},{5,4},{6,7},{7,6},{8,9},{9,8},{10,11... | collective-permute-start | bytes 196616 | tf_op jit(solution)/shard_map/ppermute | solution.py:51
  30.8 11.7 %collective-permute-start.4 = (bf16[256,128]{1,0:T(8,128)(2,1)S(1)}, bf16[256,128]{1,0:T(8,128)(2,1)S(1)}, u32[]{:S(2)}, u32[]{:S(2)}) collective-permute-start(bf16[256,128]{1,0:T(8,128)(2,1)S(1)} %share_sum.2.rest_0_.refs_0_), channel_id=1, source_target_pairs={{0,2},{1,3},{2,0},{3,1},{4,6},{5,7},{6,4},{7,5},{8,10},{9,11},{10,... | collective-permute-start | bytes 196616 | tf_op jit(solution)/shard_map/ppermute | solution.py:51
  34.6 7.9 %collective-permute-start.5 = (bf16[256,128]{1,0:T(8,128)(2,1)S(1)}, bf16[256,128]{1,0:T(8,128)(2,1)S(1)}, u32[]{:S(2)}, u32[]{:S(2)}) collective-permute-start(bf16[256,128]{1,0:T(8,128)(2,1)S(1)} %share_sum.2.rest_0_.refs_0_), channel_id=1, source_target_pairs={{0,3},{1,2},{2,1},{3,0},{4,7},{5,6},{6,5},{7,4},{8,11},{9,10},{10,... | collective-permute-start | bytes 196616 | tf_op jit(solution)/shard_map/ppermute | solution.py:51
  36.2 9.6 %collective-permute-start.10 = (bf16[256,128]{1,0:T(8,128)(2,1)S(1)}, bf16[256,128]{1,0:T(8,128)(2,1)S(1)}, u32[]{:S(2)}, u32[]{:S(2)}) collective-permute-start(bf16[256,128]{1,0:T(8,128)(2,1)S(1)} %share_sum.3.rest_0_.refs_4_), channel_id=1, source_target_pairs={{0,2},{1,3},{2,0},{3,1},{4,6},{5,7},{6,4},{7,5},{8,10},{9,11},{10,... | collective-permute-start | bytes 196616 | tf_op jit(solution)/shard_map/ppermute | solution.py:51
  41.8 6.1 %collective-permute-start.11 = (bf16[256,128]{1,0:T(8,128)(2,1)S(1)}, bf16[256,128]{1,0:T(8,128)(2,1)S(1)}, u32[]{:S(2)}, u32[]{:S(2)}) collective-permute-start(bf16[256,128]{1,0:T(8,128)(2,1)S(1)} %share_sum.3.rest_0_.refs_4_), channel_id=1, source_target_pairs={{0,3},{1,2},{2,1},{3,0},{4,7},{5,6},{6,5},{7,4},{8,11},{9,10},{10,... | collective-permute-start | bytes 196616 | tf_op jit(solution)/shard_map/ppermute | solution.py:51
  41.9 6.0 %collective-permute-start.9 = (bf16[256,128]{1,0:T(8,128)(2,1)S(1)}, bf16[256,128]{1,0:T(8,128)(2,1)S(1)}, u32[]{:S(2)}, u32[]{:S(2)}) collective-permute-start(bf16[256,128]{1,0:T(8,128)(2,1)S(1)} %share_sum.3.rest_0_.refs_4_), channel_id=1, source_target_pairs={{0,1},{1,0},{2,3},{3,2},{4,5},{5,4},{6,7},{7,6},{8,9},{9,8},{10,11... | collective-permute-start | bytes 196616 | tf_op jit(solution)/shard_map/ppermute | solution.py:51
  49.8 9.0 %collective-permute-start.17 = (bf16[256,3072]{1,0:T(8,128)(2,1)S(1)}, bf16[256,3072]{1,0:T(8,128)(2,1)S(1)}, u32[]{:S(2)}, u32[]{:S(2)}) collective-permute-start(bf16[256,3072]{1,0:T(8,128)(2,1)S(1)} %get-tuple-element.49.rest_4_), channel_id=1, source_target_pairs={{0,4},{4,0},{8,12},{12,8},{16,20},{20,16},{24,28},{28,24},{1,5},{5... | collective-permute-start | bytes 4718600 | tf_op jit(solution)/shard_map/ppermute | solution.py:51
  49.9 3.6 %collective-permute-start.12 = (f32[128,256]{1,0:T(8,128)S(1)}, f32[128,256]{1,0:T(8,128)S(1)}, u32[]{:S(2)}, u32[]{:S(2)}) collective-permute-start(f32[128,256]{1,0:T(8,128)S(1)} %get-tuple-element.47), channel_id=1, source_target_pairs={{0,4},{4,0},{8,12},{12,8},{16,20},{20,16},{24,28},{28,24},{1,5},{5... | collective-permute-start | bytes 393224 | tf_op jit(solution)/shard_map/ppermute | solution.py:51
  53.5 8.7 %collective-permute-start.13 = (f32[128,256]{1,0:T(8,128)S(1)}, f32[128,256]{1,0:T(8,128)S(1)}, u32[]{:S(2)}, u32[]{:S(2)}) collective-permute-start(f32[128,256]{1,0:T(8,128)S(1)} %add.33._), channel_id=1, source_target_pairs={{0,8},{4,12},{8,0},{12,4},{16,24},{20,28},{24,16},{28,20},{1,9},{5... | collective-permute-start | bytes 393224 | tf_op jit(solution)/shard_map/ppermute | solution.py:51
  55.0 7.7 %collective-permute-start.14 = (f32[128,256]{1,0:T(8,128)S(1)}, f32[128,256]{1,0:T(8,128)S(1)}, u32[]{:S(2)}, u32[]{:S(2)}) collective-permute-start(f32[128,256]{1,0:T(8,128)S(1)} %add.33._), channel_id=1, source_target_pairs={{0,16},{4,20},{8,24},{12,28},{16,0},{20,4},{24,8},{28,12},{1,17},{... | collective-permute-start | bytes 393224 | tf_op jit(solution)/shard_map/ppermute | solution.py:51
  56.5 7.2 %collective-permute-start.15 = (f32[128,256]{1,0:T(8,128)S(1)}, f32[128,256]{1,0:T(8,128)S(1)}, u32[]{:S(2)}, u32[]{:S(2)}) collective-permute-start(f32[128,256]{1,0:T(8,128)S(1)} %add.33._), channel_id=1, source_target_pairs={{0,24},{4,28},{8,16},{12,20},{16,8},{20,12},{24,0},{28,4},{1,25},{... | collective-permute-start | bytes 393224 | tf_op jit(solution)/shard_map/ppermute | solution.py:51
  59.2 15.2 %collective-permute-start.18 = (bf16[256,768]{1,0:T(8,128)(2,1)S(1)}, bf16[256,768]{1,0:T(8,128)(2,1)S(1)}, u32[]{:S(2)}, u32[]{:S(2)}) collective-permute-start(bf16[256,768]{1,0:T(8,128)(2,1)S(1)} %get-tuple-element.51), channel_id=1, source_target_pairs={{0,8},{4,12},{8,0},{12,4},{16,24},{20,28},{24,16},{28,20},{1,9},{5... | collective-permute-start | bytes 1179656 | tf_op jit(solution)/shard_map/ppermute | solution.py:51
  60.7 19.2 %collective-permute-start.19 = (bf16[256,768]{1,0:T(8,128)(2,1)S(1)}, bf16[256,768]{1,0:T(8,128)(2,1)S(1)}, u32[]{:S(2)}, u32[]{:S(2)}) collective-permute-start(bf16[256,768]{1,0:T(8,128)(2,1)S(1)} %get-tuple-element.52), channel_id=1, source_target_pairs={{0,16},{4,20},{8,24},{12,28},{16,0},{20,4},{24,8},{28,12},{1,17},{... | collective-permute-start | bytes 1179656 | tf_op jit(solution)/shard_map/ppermute | solution.py:51
  62.2 17.8 %collective-permute-start.20 = (bf16[256,768]{1,0:T(8,128)(2,1)S(1)}, bf16[256,768]{1,0:T(8,128)(2,1)S(1)}, u32[]{:S(2)}, u32[]{:S(2)}) collective-permute-start(bf16[256,768]{1,0:T(8,128)(2,1)S(1)} %get-tuple-element.53), channel_id=1, source_target_pairs={{0,24},{4,28},{8,16},{12,20},{16,8},{20,12},{24,0},{28,4},{1,25},{... | collective-permute-start | bytes 1179656 | tf_op jit(solution)/shard_map/ppermute | solution.py:51
  63.7 1.4 collective-permute-start.16
  80.5 20.2 %collective-permute-start.32 = (bf16[256,768]{1,0:T(8,128)(2,1)S(1)}, bf16[256,768]{1,0:T(8,128)(2,1)S(1)}, u32[]{:S(2)}, u32[]{:S(2)}) collective-permute-start(bf16[256,768]{1,0:T(8,128)(2,1)S(1)} %get-tuple-element.55.block0), channel_id=1, source_target_pairs={{0,8},{4,12},{8,0},{12,4},{16,24},{20,28},{24,16},{28,20},{1,9},{5... | collective-permute-start | bytes 1179656 | tf_op jit(solution)/shard_map/ppermute | solution.py:51
  81.8 19.4 %collective-permute-start.30 = (bf16[256,768]{1,0:T(8,128)(2,1)S(1)}, bf16[256,768]{1,0:T(8,128)(2,1)S(1)}, u32[]{:S(2)}, u32[]{:S(2)}) collective-permute-start(bf16[256,768]{1,0:T(8,128)(2,1)S(1)} %get-tuple-element.55.block0), channel_id=1, source_target_pairs={{0,16},{4,20},{8,24},{12,28},{16,0},{20,4},{24,8},{28,12},{1,17},{... | collective-permute-start | bytes 1179656 | tf_op jit(solution)/shard_map/ppermute | solution.py:51
  82.6 18.7 %collective-permute-start.28 = (bf16[256,768]{1,0:T(8,128)(2,1)S(1)}, bf16[256,768]{1,0:T(8,128)(2,1)S(1)}, u32[]{:S(2)}, u32[]{:S(2)}) collective-permute-start(bf16[256,768]{1,0:T(8,128)(2,1)S(1)} %get-tuple-element.55.block0), channel_id=1, source_target_pairs={{0,24},{4,28},{8,16},{12,20},{16,8},{20,12},{24,0},{28,4},{1,25},{... | collective-permute-start | bytes 1179656 | tf_op jit(solution)/shard_map/ppermute | solution.py:51
  84.1 1.2 collective-permute-start.21
  85.2 14.0 %collective-permute-start.22 = (f32[8,256]{1,0:T(8,128)S(1)}, f32[8,256]{1,0:T(8,128)S(1)}, u32[]{:S(2)}, u32[]{:S(2)}) collective-permute-start(f32[8,256]{1,0:T(8,128)S(1)} %add.37), channel_id=1, source_target_pairs={{0,8},{4,12},{8,0},{12,4},{16,24},{20,28},{24,16},{28,20},{1,9},{5... | collective-permute-start | bytes 24584 | tf_op jit(solution)/shard_map/ppermute | solution.py:51
  86.5 14.2 %collective-permute-start.23 = (f32[8,256]{1,0:T(8,128)S(1)}, f32[8,256]{1,0:T(8,128)S(1)}, u32[]{:S(2)}, u32[]{:S(2)}) collective-permute-start(f32[8,256]{1,0:T(8,128)S(1)} %add.37), channel_id=1, source_target_pairs={{0,16},{4,20},{8,24},{12,28},{16,0},{20,4},{24,8},{28,12},{1,17},{... | collective-permute-start | bytes 24584 | tf_op jit(solution)/shard_map/ppermute | solution.py:51
  99.3 4.5 %collective-permute-start.24 = (f32[8,256]{1,0:T(8,128)S(1)}, f32[8,256]{1,0:T(8,128)S(1)}, u32[]{:S(2)}, u32[]{:S(2)}) collective-permute-start(f32[8,256]{1,0:T(8,128)S(1)} %add.37), channel_id=1, source_target_pairs={{0,24},{4,28},{8,16},{12,20},{16,8},{20,12},{24,0},{28,4},{1,25},{... | collective-permute-start | bytes 24584 | tf_op jit(solution)/shard_map/ppermute | solution.py:51
  100.7 16.8 %collective-permute-start.34 = (bf16[256,768]{1,0:T(8,128)(2,1)S(1)}, bf16[256,768]{1,0:T(8,128)(2,1)S(1)}, u32[]{:S(2)}, u32[]{:S(2)}) collective-permute-start(bf16[256,768]{1,0:T(8,128)(2,1)S(1)} %get-tuple-element.55.block0), channel_id=1, source_target_pairs={{0,4},{4,0},{8,12},{12,8},{16,20},{20,16},{24,28},{28,24},{1,5},{5... | collective-permute-start | bytes 1179656 | tf_op jit(solution)/shard_map/ppermute | solution.py:51
  100.7 23.7 %collective-permute-start.33 = (bf16[256,768]{1,0:T(8,128)(2,1)S(1)}, bf16[256,768]{1,0:T(8,128)(2,1)S(1)}, u32[]{:S(2)}, u32[]{:S(2)}) collective-permute-start(bf16[256,768]{1,0:T(8,128)(2,1)S(1)} %collective-permute-done.32.block0), channel_id=1, source_target_pairs={{0,4},{4,0},{8,12},{12,8},{16,20},{20,16},{24,28},{28,24},{1,5},{5... | collective-permute-start | bytes 1179656 | tf_op jit(solution)/shard_map/ppermute | solution.py:51
  101.2 30.2 %collective-permute-start.31 = (bf16[256,768]{1,0:T(8,128)(2,1)S(1)}, bf16[256,768]{1,0:T(8,128)(2,1)S(1)}, u32[]{:S(2)}, u32[]{:S(2)}) collective-permute-start(bf16[256,768]{1,0:T(8,128)(2,1)S(1)} %collective-permute-done.30.block0), channel_id=1, source_target_pairs={{0,4},{4,0},{8,12},{12,8},{16,20},{20,16},{24,28},{28,24},{1,5},{5... | collective-permute-start | bytes 1179656 | tf_op jit(solution)/shard_map/ppermute | solution.py:51
  101.3 37.0 %collective-permute-start.29 = (bf16[256,768]{1,0:T(8,128)(2,1)S(1)}, bf16[256,768]{1,0:T(8,128)(2,1)S(1)}, u32[]{:S(2)}, u32[]{:S(2)}) collective-permute-start(bf16[256,768]{1,0:T(8,128)(2,1)S(1)} %collective-permute-done.28.block0), channel_id=1, source_target_pairs={{0,4},{4,0},{8,12},{12,8},{16,20},{20,16},{24,28},{28,24},{1,5},{5... | collective-permute-start | bytes 1179656 | tf_op jit(solution)/shard_map/ppermute | solution.py:51
  103.8 3.7 %collective-permute-start.25 = (f32[8,256]{1,0:T(8,128)S(1)}, f32[8,256]{1,0:T(8,128)S(1)}, u32[]{:S(2)}, u32[]{:S(2)}) collective-permute-start(f32[8,256]{1,0:T(8,128)S(1)} %add_add_fusion.2), channel_id=1, source_target_pairs={{0,1},{1,0},{2,3},{3,2},{4,5},{5,4},{6,7},{7,6},{8,9},{9,8},{10,11... | collective-permute-start | bytes 24584 | tf_op jit(solution)/shard_map/ppermute | solution.py:51
  107.5 4.5 %collective-permute-start.26 = (f32[8,256]{1,0:T(8,128)S(1)}, f32[8,256]{1,0:T(8,128)S(1)}, u32[]{:S(2)}, u32[]{:S(2)}) collective-permute-start(f32[8,256]{1,0:T(8,128)S(1)} %add_add_fusion.2), channel_id=1, source_target_pairs={{0,2},{1,3},{2,0},{3,1},{4,6},{5,7},{6,4},{7,5},{8,10},{9,11},{10,... | collective-permute-start | bytes 24584 | tf_op jit(solution)/shard_map/ppermute | solution.py:51
  112.0 5.4 %collective-permute-start.27 = (f32[8,256]{1,0:T(8,128)S(1)}, f32[8,256]{1,0:T(8,128)S(1)}, u32[]{:S(2)}, u32[]{:S(2)}) collective-permute-start(f32[8,256]{1,0:T(8,128)S(1)} %add_add_fusion.2), channel_id=1, source_target_pairs={{0,3},{1,2},{2,1},{3,0},{4,7},{5,6},{6,5},{7,4},{8,11},{9,10},{10,... | collective-permute-start | bytes 24584 | tf_op jit(solution)/shard_map/ppermute | solution.py:51

commit v3 on v2

--- a/solution.py
+++ b/solution.py
@@ -51,66 +51,73 @@
     return lax.ppermute(x, axis, [(i, i ^ d) for i in range(lax.axis_size(axis))])
 
 
+def block_copies(part, d, mom, grad, buf, gbuf, slot, sems):
+    half = gbuf.shape[1]
+    block = flip(lax.axis_index("col"), d)
+    there = pl.ds(pl.multiple_of((2 * block + part) * half, half), half)
+    here = pl.ds(pl.multiple_of(block * half, half), half)
+    return (
+        pltpu.make_async_copy(mom.at[there, :], buf.at[here, :], sems.at[0, d]),
+        pltpu.make_async_copy(grad.at[there, :], gbuf.at[slot], sems.at[1, d]),
+    )
+
+
+def project_block(d, buf, gref, basis, left):
+    half, n = gref.shape
+    rows = pl.ds(pl.multiple_of(flip(lax.axis_index("col"), d) * half, half), half)
+    chunk = 1536 if n % 1536 == 0 else n
+
+    def step(k, acc):
+        cols = pl.ds(pl.multiple_of(k * chunk, 128), chunk)
+        total = buf[rows, cols] + gref[:, cols].astype(f32)
+        buf[rows, cols] = total
+        return acc + dot(basis[:, cols], total.astype(bf16), ((1,), (1,)))
+
+    acc = lax.fori_loop(0, n // chunk, step, jnp.zeros((basis.shape[0], half), f32))
+    left[...] = acc.astype(left.dtype)
+
+
 def project_kernel(part, depth, mom, grad, basis, *rest):
-    rest = rest[-(depth + 5) :]
-    buf, lefts, gbuf, bbuf, sems, bsem = rest[0], rest[1 : depth + 1], *rest[depth + 1 :]
-    m, n = buf.shape
-    half = m // depth
-    me = lax.axis_index("col")
-    chunk = 1536 if n % 1536 == 0 else n
-
-    def copies(d):
-        block = flip(me, d)
-        there = pl.ds(pl.multiple_of((2 * block + part) * half, half), half)
-        here = pl.ds(pl.multiple_of(block * half, half), half)
-        return (
-            pltpu.make_async_copy(mom.at[there, :], buf.at[here, :], sems.at[0, d]),
-            pltpu.make_async_copy(grad.at[there, :], gbuf.at[here, :], sems.at[1, d]),
-        )
-
-    load_basis = pltpu.make_async_copy(basis, bbuf, bsem)
+    if part == 0:
+        (buf, kept), rest = rest[:2], rest[2:]
+    else:
+        kept, buf, rest = basis, rest[1], rest[2:]
+    lefts, (gbuf, sems, basis_sem) = rest[:depth], rest[depth:]
     order = list(reversed(range(depth)))
+    copies = [block_copies(part, d, mom, grad, buf, gbuf, d, sems) for d in range(depth)]
+    load_basis = pltpu.make_async_copy(basis, kept, basis_sem) if part == 0 else None
     for k, d in enumerate(order):
-        for copy in copies(d):
+        for copy in copies[d]:
             copy.start()
-        if k == 0:
+        if k == 0 and part == 0:
             load_basis.start()
     for k, d in enumerate(order):
-        for copy in copies(d):
+        for copy in copies[d]:
             copy.wait()
-        if k == 0:
+        if k == 0 and part == 0:
             load_basis.wait()
-        rows = pl.ds(pl.multiple_of(flip(me, d) * half, half), half)
-
-        def step(k, acc):
-            cols = pl.ds(pl.multiple_of(k * chunk, 128), chunk)
-            total = buf[rows, cols] + gbuf[rows, cols].astype(f32)
-            buf[rows, cols] = total
-            return acc + dot(bbuf[:, cols], total.astype(bf16), ((1,), (1,)))
-
-        acc = lax.fori_loop(0, n // chunk, step, jnp.zeros((bbuf.shape[0], half), f32))
-        lefts[d][...] = acc.astype(lefts[d].dtype)
+        project_block(d, buf, gbuf.at[d], kept, lefts[d])
 
 
 def project(momentum, gradient, basis, depth, part, after=()):
     m, n = momentum.shape
-    m = m // 2
     r = basis.shape[0]
+    half = m // 2 // depth
     kinds = [f32] + [bf16] * (depth - 1)
+    kept = [] if part else [pltpu.VMEM((r, n), bf16)]
     return pl.pallas_call(
         functools.partial(project_kernel, part, depth),
-        out_shape=(pltpu.VMEM((m, n), f32), *[shape((r, m // depth), k) for k in kinds]),
-        in_specs=[ANY] * (3 + len(after)),
-        out_specs=(VMEM,) * (depth + 1),
+        out_shape=(pltpu.VMEM((m // 2, n), f32), *kept, *[shape((r, half), k) for k in kinds]),
+        in_specs=[ANY, ANY] + [VMEM if part else ANY] + [ANY] * len(after),
+        out_specs=(VMEM,) * (depth + 1 + len(kept)),
         scratch_shapes=[
-            pltpu.VMEM((m, n), bf16),
-            pltpu.VMEM((r, n), bf16),
+            pltpu.VMEM((depth, half, n), bf16),
             pltpu.SemaphoreType.DMA((2, depth)),
             pltpu.SemaphoreType.DMA,
         ],
-        compiler_params=params(12),
+        compiler_params=params(10),
         name="project",
-    )(stay(momentum), stay(gradient), stay(basis), *after)
+    )(stay(momentum), stay(gradient), keep(basis) if part else stay(basis), *after)
 
 
 def keep(x):
@@ -129,16 +136,33 @@
     return whole
 
 
-def self_product(whole):
-    return dot(whole[...], whole[...], ((1,), (1,)))
+def gram_kernel(*refs):
+    lefts, (g_mine, g_other, total) = refs[:-3], refs[-3:]
+    core = lax.bitwise_and(lax.axis_index("row"), jnp.int32(1))
+    total[...] = sum(dot(ref[...], ref[...], ((1,), (1,))) for ref in lefts)
+    h = g_mine.shape[0]
+    g_mine[...] = total[pl.ds(pl.multiple_of(core * h, h), h), :]
+    g_other[...] = total[pl.ds(pl.multiple_of((1 - core) * h, h), h), :]
+
+
+def gram(lefts):
+    r = lefts[0].shape[0]
+    return pl.pallas_call(
+        gram_kernel,
+        out_shape=[shape((r // 2, r), f32)] * 2,
+        in_specs=[VMEM] * len(lefts),
+        out_specs=[VMEM] * 2,
+        scratch_shapes=[pltpu.VMEM((r, r), f32)],
+        compiler_params=params(8),
+        name="gram",
+    )(*lefts)
 
 
 def first_kernel(depth, width, buf, *rest):
-    lefts, (other, mine, gram, whole) = rest[:depth], rest[depth:]
+    lefts, (other, mine, whole) = rest[:depth], rest[depth:]
     core = lax.bitwise_and(lax.axis_index("row"), jnp.int32(1))
     size = other.shape[1]
     gather_left(lefts, whole)
-    gram[...] = self_product(whole)
     for out, half in ((other, 1 - core), (mine, core)):
 
         def step(k, carry, out=out, half=half):
@@ -154,24 +178,20 @@
     r = lefts[0].shape[0]
     return pl.pallas_call(
         functools.partial(first_kernel, len(lefts), width),
-        out_shape=(shape((r, n // 2), f32), shape((r, n // 2), f32), shape((r, r), f32)),
+        out_shape=(shape((r, n // 2), f32), shape((r, n // 2), f32)),
         in_specs=[VMEM] * (1 + len(lefts)),
-        out_specs=[VMEM] * 3,
+        out_specs=[VMEM] * 2,
         scratch_shapes=[pltpu.VMEM((r, m), bf16)],
         compiler_params=params(8),
         name="first_product",
     )(keep(buf), *lefts)
 
 
-def other_kernel(depth, width, buf, sums, gram, *rest):
-    lefts, (out, g_mine, g_other, whole, total) = rest[:depth], rest[depth:]
+def other_kernel(depth, width, buf, sums, *rest):
+    lefts, (out, whole) = rest[:depth], rest[-2:]
     core = lax.bitwise_and(lax.axis_index("row"), jnp.int32(1))
     size = out.shape[1]
     gather_left(lefts, whole)
-    total[...] = gram[...] + self_product(whole)
-    h = g_mine.shape[0]
-    g_mine[...] = total[pl.ds(pl.multiple_of(core * h, h), h), :]
-    g_other[...] = total[pl.ds(pl.multiple_of((1 - core) * h, h), h), :]
 
     def step(k, carry):
         cols = pl.ds(pl.multiple_of((1 - core) * size + k * width, 128), width)
@@ -182,18 +202,18 @@
     lax.fori_loop(0, size // width, step, 0)
 
 
-def other_product(buf, sums, gram, lefts, width):
+def other_product(buf, sums, lefts, width, after):
     m, n = buf.shape
     r = lefts[0].shape[0]
     return pl.pallas_call(
         functools.partial(other_kernel, len(lefts), width),
-        out_shape=(shape((r, n // 2), bf16), shape((r // 2, r), f32), shape((r // 2, r), f32)),
-        in_specs=[VMEM] * (3 + len(lefts)),
-        out_specs=[VMEM] * 3,
-        scratch_shapes=[pltpu.VMEM((r, m), bf16), pltpu.VMEM((r, r), f32)],
+        out_shape=shape((r, n // 2), bf16),
+        in_specs=[VMEM] * (2 + len(lefts)) + [ANY],
+        out_specs=VMEM,
+        scratch_shapes=[pltpu.VMEM((r, m), bf16)],
         compiler_params=params(8),
         name="other_product",
-    )(keep(buf), sums, gram, *lefts)
+    )(keep(buf), sums, *lefts, after)
 
 
 def mine_kernel(depth, width, buf, sums, *rest):
@@ -341,6 +361,18 @@
     )(inverse, *lefts)
 
 
+def hand_on(x, *earlier):
+    return pl.pallas_call(
+        lambda *refs: None,
+        out_shape=shape(x.shape, x.dtype),
+        in_specs=[ANY] * (1 + len(earlier)),
+        out_specs=ANY,
+        input_output_aliases={0: 0},
+        compiler_params=params(1),
+        name="hand_on",
+    )(x, *earlier)
+
+
 def apply_inverse(parts, block):
     return sum(dot(x, block) for x in reversed(parts))
 
@@ -366,9 +398,10 @@
 
 
 def result_kernel(d, factor, buf0, buf1, ortho_ref, inverse, squares, block0, block1, weight, *rest):
-    new_weight, new_momentum, basis, mbuf, wbuf, vbuf, nbuf, in_sems, out_sems = rest[-9:]
-    m = ortho_ref.shape[0]
+    new_weight, new_momentum, basis, mbuf, wbuf, vbuf, nbuf, lbuf, in_sems, out_sems, basis_sems = rest[-11:]
     r, width = block0.shape
+    tile = 256
+    tiles = width // tile
     half = width * (lax.axis_size("row") // 2)
     row = lax.axis_index("row")
     core = lax.bitwise_and(row, jnp.int32(1))
@@ -376,41 +409,51 @@
     starts = [core * half + chip * width, (1 - core) * half + chip * width]
     cols = [pl.ds(pl.multiple_of(start, 128), width) for start in starts]
     loads = [pltpu.make_async_copy(weight.at[:, cols[b]], wbuf.at[b], in_sems.at[b]) for b in range(2)]
-    stores = [
-        pltpu.make_async_copy(src.at[b], dst.at[:, cols[b]], out_sems.at[k, b])
-        for b in range(2)
-        for k, (src, dst) in enumerate(((mbuf, new_momentum), (vbuf, new_weight), (nbuf, basis)))
-    ]
+    basis_stores = [pltpu.make_async_copy(nbuf.at[b], basis.at[:, cols[b]], basis_sems.at[b]) for b in range(2)]
+
+    def stores(b, t):
+        at = pl.ds(pl.multiple_of(t * tile, tile), tile)
+        there = pl.ds(pl.multiple_of(starts[b] + t * tile, 128), tile)
+        return (
+            pltpu.make_async_copy(mbuf.at[b, :, at], new_momentum.at[:, there], out_sems.at[0, b, t]),
+            pltpu.make_async_copy(vbuf.at[b, :, at], new_weight.at[:, there], out_sems.at[1, b, t]),
+        )
+
     for load in loads:
         load.start()
     scale = lax.rsqrt(squares[...] / FF + epsilon)
     scale = jnp.transpose(jnp.concatenate([scale] * 16, axis=0))[:, :1]
     parts = split(inverse[...], 2)
-    lows = []
+    depth = lax.axis_size("col")
+    size = buf0.shape[0] // depth
     for b, block in enumerate((block0, block1)):
         right = apply_inverse(parts, block[...])
-        lows.append(right.astype(bf16))
+        lbuf[b] = right.astype(bf16)
         nbuf[b] = (right * scale).astype(bf16)
-    depth = lax.axis_size("col")
-    size = m // (2 * depth)
+        basis_stores[b].start()
+        loads[b].wait()
+
+        def step(t, carry, b=b):
+            at = pl.ds(pl.multiple_of(t * tile, tile), tile)
+            there = pl.ds(pl.multiple_of(starts[b] + t * tile, 128), tile)
+            correction = dot(ortho_ref[...], lbuf[b, :, at])
+            for k in range(2 * depth):
+                rows = slice(k * size, (k + 1) * size)
+                here = slice(k // 2 * size, (k // 2 + 1) * size)
+                old = (buf0, buf1)[k % 2][here, there]
+                mbuf[b, rows, at] = old - (1.0 - momentum_decay) * correction[rows]
+            change = dot(ortho_ref[...], nbuf[b, :, at])
+            vbuf[b, :, at] = (wbuf[b, :, at].astype(f32) - factor * change).astype(bf16)
+            for store in stores(b, t):
+                store.start()
+            return carry
+
+        lax.fori_loop(0, tiles, step, 0)
     for b in range(2):
-        loads[b].wait()
-
-        def step(k, carry, b=b):
-            for part, buf in enumerate((buf0, buf1)):
-                here = pl.ds(pl.multiple_of(k * size, size), size)
-                rows = pl.ds(pl.multiple_of((2 * k + part) * size, size), size)
-                correction = dot(ortho_ref[rows, :], lows[b])
-                mbuf[b, rows, :] = buf[here, cols[b]] - (1.0 - momentum_decay) * correction
-                change = dot(ortho_ref[rows, :], nbuf[b])
-                vbuf[b, rows, :] = (wbuf[b, rows, :].astype(f32) - factor * change).astype(bf16)
-            return carry
-
-        lax.fori_loop(0, depth, step, 0, unroll=2)
-        for store in stores[3 * b : 3 * b + 3]:
-            store.start()
-    for store in stores:
-        store.wait()
+        basis_stores[b].wait()
+        for t in range(tiles):
+            for store in stores(b, t):
+                store.wait()
 
 
 def results(d, factor, bufs, ortho_bf, inverse, squares, blocks, weight, before):
@@ -428,18 +471,22 @@
             pltpu.VMEM((2, m, width), bf16),
             pltpu.VMEM((2, m, width), bf16),
             pltpu.VMEM((2, r, width), bf16),
+            pltpu.VMEM((2, r, width), bf16),
             pltpu.SemaphoreType.DMA((2,)),
-            pltpu.SemaphoreType.DMA((3, 2)),
+            pltpu.SemaphoreType.DMA((2, 2, width // 256)),
+            pltpu.SemaphoreType.DMA((2,)),
         ],
         compiler_params=params(20),
         name="results",
     )(*ins)
 
 
-def pair_up(terms):
-    while len(terms) > 1:
-        terms = [terms[2 * i] + terms[2 * i + 1] for i in range(len(terms) // 2)]
-    return terms[0]
+def sum_over(x, axis, least=1):
+    d = least
+    while d < lax.axis_size(axis):
+        x = x + swap(x, axis, d)
+        d *= 2
+    return x
 
 
 def exchange(x, axis, count, unit=1):
@@ -452,34 +499,41 @@
     m, n = momentum.shape
     width = n // rows
 
-    bufs, lefts, after = [], [], ()
-    for part in range(2):
-        buf, own, *sent = project(momentum, gradient, old_basis, depth, part, after)
-        after = (sent[0],)
+    def sum_over_col(own, *sent):
         low = share_sum(own, [swap(x, "col", d + 1) for d, x in enumerate(sent)])
-        bufs.append(buf)
-        lefts.append(exchange(low, "col", depth))
-
-    other, mine, gram = first_product(bufs[0], lefts[0], width)
-    other, g_mine, g_other = other_product(bufs[1], other, gram, lefts[1], width)
+        return exchange(low, "col", depth)
+
+    buf0, kept, *outs = project(momentum, gradient, old_basis, depth, 0)
+    left0 = sum_over_col(*outs)
+    buf1, *outs = project(momentum, gradient, kept, depth, 1, (outs[1],))
+    left1 = sum_over_col(*outs)
+    bufs = (buf0, buf1)
+
+    other, mine = first_product(buf0, left0, width)
+    g_mine, g_other = gram(left0 + left1)
+    other = other_product(buf1, other, left1, width, g_mine)
+    g_mine = g_mine + swap(g_other, "row", 1)
     received = swap(other, "row", 1)
-    g_mine = g_mine + swap(g_other, "row", 1)
-    mine = mine_product(bufs[1], mine, lefts[1], width, other)
+    mine = mine_product(buf1, mine, left1, width, other)
     own, *sent = pair_sum(mine, received, chips, g_mine)
-    g_mine = pair_up(exchange(g_mine, "row", chips, 2))
+    g_mine = sum_over(g_mine, "row", 2)
     got = [swap(x, "row", 2 * (d + 1)) for d, x in enumerate(sent)]
-
     inverse = chol_inverse(g_mine, swap(g_mine, "row", 1))
-    ortho_bf = ortho(inverse, lefts[0] + lefts[1])
 
     share, squares = share_of(inverse, own, got)
-    blocks = exchange(share, "row", chips, 2)
-    squares = squares + swap(squares, "row", 1)
-    squares = pair_up(exchange(squares, "row", chips, 2))
-    squares = pair_up(exchange(squares, "col", depth))
+    ortho_bf = ortho(inverse, left0 + left1)
+    squares = sum_over(squares, "row", 2)
+    share = hand_on(share, squares)
+    squares = sum_over(squares + swap(squares, "row", 1), "col")
+
     factor = step_rate * math.sqrt(D / RANK)
-    outs = ()
+    outs, blocks = (), [share]
+    for d in range(1, chips):
+        source = share if d < 3 else hand_on(share, blocks[d - 2])
+        blocks.append(swap(source, "row", 2 * d))
     for d, block in enumerate(blocks):
+        if d > 2:
+            block = hand_on(block, outs[2])
         pair = (block, swap(block, "row", 1))
         outs = results(d, factor, bufs, ortho_bf, inverse, squares, pair, weight, outs)
     return tuple(outs)

time: 146 us -> 138 us (0.945)
  Pallas kernels: 65.4 us -> 61 us
  starting transfers between devices: 40.3 us -> 36.9 us
  waiting for transfers between devices: 38.7 us -> 36.4 us
  local copies, waits for them, and re-layouts: 0 us -> 1.88 us
    ppermute x35 -> x32, starting transfers between devices: 40.3 us -> 36.9 us  [swap(): lax.ppermute(x, axis, [(i, i ^ d) for i in range(lax.axis_size(axis))])]
    pallas_call x4, Pallas kernels: 27.7 us -> 24.4 us  [results(): pl.pallas_call(functools.partial(result_kernel, d, factor), out_shape=(sh...]
    ppermute x35 -> x32, waiting for transfers between devices: 38.7 us -> 36.4 us  [swap(): lax.ppermute(x, axis, [(i, i ^ d) for i in range(lax.axis_size(axis))])]
    unnamed x0 -> x2, local copies, waits for them, and re-layouts: none -> 1.88 us
  transfers between devices with their start and end apart: 35 -> 32, of which waited for: 12 -> 12; matrix products, arithmetic and copies ran while one was open for 0% -> 0% of each run, Pallas kernels for 32% -> 31%
where the time goes in v3:
time: 138 us; the launch traced here: 137 us
  Pallas kernels  61 us (44%)
  starting transfers between devices  36.9 us (27%)
  waiting for transfers between devices  36.4 us (26%)
  local copies, waits for them, and re-layouts  1.88 us (1%)
    ppermute x32, starting transfers between devices, swap(): lax.ppermute(x, axis, [(i, i ^ d) for i in range(lax.axis_size(axis))])  36.9 us
    ppermute x32, waiting for transfers between devices, swap(): lax.ppermute(x, axis, [(i, i ^ d) for i in range(lax.axis_size(axis))])  36.4 us
    pallas_call x4, Pallas kernels, results(): pl.pallas_call(functools.partial(result_kernel, d, factor), out_shape=(sh...  24.4 us
    pallas_call x2, Pallas kernels, project(): pl.pallas_call(functools.partial(project_kernel, part, depth), out_shape=...  18.4 us
    pallas_call x1, Pallas kernels, chol_inverse(): pl.pallas_call(chol_inverse_kernel, out_shape=shape((n, n), f32), in_spec...  9.14 us
    pallas_call x1, Pallas kernels, first_product(): pl.pallas_call(functools.partial(first_kernel, len(lefts), width), out_sh...  3.1 us
  transfers between devices with their start and end apart: 32, of which 12 were waited for; matrix products, arithmetic and copies ran while one was open for 0% of the time, Pallas kernels for 31%

profile of v3, /device:TPU:0, one launch (start us, length us, event | category | flops | bytes accessed | tf_op | source)
XLA Modules:
  0.0 137.4 jit_solution(1224561013117080113)
XLA Ops:
  0.6 9.7 %project.2 = (f32[512,6144]{1,0:T(8,128)S(1)}, bf16[256,6144]{1,0:T(8,128)(2,1)S(1)}, f32[256,128]{1,0:T(8,128)S(1)}, bf16[256,128]{1,0:T(8,128)(2,1)S(1)}, bf16...) custom-call(f32[1024,6144]{1,0:T(8,128)} %mom.3, bf16[1024,6144]{1,0:T(8,128)(2,1)} %grad.3, bf16[256,6144]{1,0:T(8,128)(2,1)} %basis.1), custom_call_target="tpu_custom_call" | custom-call | tf_op jit(solution)/shard_map/project/pallas_call | solution.py:108
  10.3 3.1 %collective-permute-start = (bf16[256,128]{1,0:T(8,128)(2,1)S(1)}, bf16[256,128]{1,0:T(8,128)(2,1)S(1)}, u32[]{:S(2)}, u32[]{:S(2)}) collective-permute-start(bf16[256,128]{1,0:T(8,128)(2,1)S(1)} %get-tuple-element.35.rest_0_), channel_id=1, source_target_pairs={{0,1},{1,0},{2,3},{3,2},{4,5},{5,4},{6,7},{7,6},{8,9},{9,8},{10,11... | collective-permute-start | bytes 196616 | tf_op jit(solution)/shard_map/ppermute | solution.py:51
  13.4 2.6 %collective-permute-start.1 = (bf16[256,128]{1,0:T(8,128)(2,1)S(1)}, bf16[256,128]{1,0:T(8,128)(2,1)S(1)}, u32[]{:S(2)}, u32[]{:S(2)}) collective-permute-start(bf16[256,128]{1,0:T(8,128)(2,1)S(1)} %get-tuple-element.38), channel_id=1, source_target_pairs={{0,2},{1,3},{2,0},{3,1},{4,6},{5,7},{6,4},{7,5},{8,10},{9,11},{10,... | collective-permute-start | bytes 196616 | tf_op jit(solution)/shard_map/ppermute | solution.py:51
  16.0 8.8 %project.3 = (f32[512,6144]{1,0:T(8,128)S(1)}, f32[256,128]{1,0:T(8,128)S(1)}, bf16[256,128]{1,0:T(8,128)(2,1)S(1)}, bf16[256,128]{1,0:T(8,128)(2,1)S(1)}, bf16[256,128]{1,0:T(8,128)(2,1)S(1)}) custom-call(f32[1024,6144]{1,0:T(8,128)} %mom.3, bf16[1024,6144]{1,0:T(8,128)(2,1)} %grad.3, bf16[256,6144]{1,0:T(8,128)(2,1)S(1)} %get-tuple-element.34.basis, ...), custom_call_target="tpu_custom_call" | custom-call | tf_op jit(solution)/shard_map/project/pallas_call | solution.py:108
  24.8 1.0 collective-permute-start.6
  25.7 3.5 %collective-permute-start.7 = (bf16[256,128]{1,0:T(8,128)(2,1)S(1)}, bf16[256,128]{1,0:T(8,128)(2,1)S(1)}, u32[]{:S(2)}, u32[]{:S(2)}) collective-permute-start(bf16[256,128]{1,0:T(8,128)(2,1)S(1)} %get-tuple-element.42), channel_id=1, source_target_pairs={{0,2},{1,3},{2,0},{3,1},{4,6},{5,7},{6,4},{7,5},{8,10},{9,11},{10,... | collective-permute-start | bytes 196616 | tf_op jit(solution)/shard_map/ppermute | solution.py:51
  29.3 0.6 collective-permute-start.3
  29.9 3.8 %collective-permute-start.4 = (bf16[256,128]{1,0:T(8,128)(2,1)S(1)}, bf16[256,128]{1,0:T(8,128)(2,1)S(1)}, u32[]{:S(2)}, u32[]{:S(2)}) collective-permute-start(bf16[256,128]{1,0:T(8,128)(2,1)S(1)} %share_sum.2.refs_0_.rest_0_), channel_id=1, source_target_pairs={{0,2},{1,3},{2,0},{3,1},{4,6},{5,7},{6,4},{7,5},{8,10},{9,11},{10,... | collective-permute-start | bytes 196616 | tf_op jit(solution)/shard_map/ppermute | solution.py:51
  33.7 1.5 %collective-permute-done.8.refs_2_ = bf16[256,128]{1,0:T(8,128)(2,1)S(1)} collective-permute-done((bf16[256,128]{1,0:T(8,128)(2,1)S(1)}, bf16[256,128]{1,0:T(8,128)(2,1)S(1)}, u32[]{:S(2)}, u32[]{:S(2)}) %collective-permute-start.8) | collective-permute-done | bytes 65568 | tf_op jit(solution)/shard_map/ppermute | solution.py:51
  35.3 5.6 %collective-permute-start.10 = (bf16[256,128]{1,0:T(8,128)(2,1)S(1)}, bf16[256,128]{1,0:T(8,128)(2,1)S(1)}, u32[]{:S(2)}, u32[]{:S(2)}) collective-permute-start(bf16[256,128]{1,0:T(8,128)(2,1)S(1)} %share_sum.3.refs_4_.rest_0_), channel_id=1, source_target_pairs={{0,2},{1,3},{2,0},{3,1},{4,6},{5,7},{6,4},{7,5},{8,10},{9,11},{10,... | collective-permute-start | bytes 196616 | tf_op jit(solution)/shard_map/ppermute | solution.py:51
  41.0 0.6 collective-permute-start.9
  41.6 3.1 %first_product.1 = (f32[256,3072]{1,0:T(8,128)S(1)}, f32[256,3072]{1,0:T(8,128)S(1)}) custom-call(f32[512,6144]{1,0:T(8,128)S(1)} %get-tuple-element.33.buf.buf0, bf16[256,128]{1,0:T(8,128)(2,1)S(1)} %share_sum.2.refs_0_.rest_0_, bf16[256,128]{1,0:T(8,128)(2,1)S(1)} %collective-permute-done.3.refs_1_.rest_1_, ...), custom_call_target="tpu_custom_call" | custom-call | tf_op jit(solution)/shard_map/first_product/pallas_call | solution.py:179
  44.7 2.3 %collective-permute-done.11.refs_7_.rest_3_ = bf16[256,128]{1,0:T(8,128)(2,1)S(1)} collective-permute-done((bf16[256,128]{1,0:T(8,128)(2,1)S(1)}, bf16[256,128]{1,0:T(8,128)(2,1)S(1)}, u32[]{:S(2)}, u32[]{:S(2)}) %collective-permute-start.11) | collective-permute-done | bytes 65568 | tf_op jit(solution)/shard_map/ppermute | solution.py:51
  47.0 0.5 gram.1
  47.5 1.6 %other_product.1.rest_4_ = bf16[256,3072]{1,0:T(8,128)(2,1)S(1)} custom-call(f32[512,6144]{1,0:T(8,128)S(1)} %get-tuple-element.36.buf.buf1, f32[256,3072]{1,0:T(8,128)S(1)} %get-tuple-element.47.sums, bf16[256,128]{1,0:T(8,128)(2,1)S(1)} %share_sum.3.refs_4_.rest_0_, bf16[256,128]{1,0:T(8,128)(2,1)S(1)} %collective-permute-done.9.refs_5_.rest_1_, ...), custom_call_target="tpu_custom_call" | custom-call | tf_op jit(solution)/shard_map/other_product/pallas_call | solution.py:208
  49.1 0.5 collective-permute-start.12
  49.6 1.8 %mine_product.1.mine = f32[256,3072]{1,0:T(8,128)S(1)} custom-call(f32[512,6144]{1,0:T(8,128)S(1)} %get-tuple-element.36.buf.buf1, f32[256,3072]{1,0:T(8,128)S(1)} %get-tuple-element.46.sums, bf16[256,128]{1,0:T(8,128)(2,1)S(1)} %share_sum.3.refs_4_.rest_0_, bf16[256,128]{1,0:T(8,128)(2,1)S(1)} %collective-permute-done.9.refs_5_.rest_1_, ...), custom_call_target="tpu_custom_call" | custom-call | tf_op jit(solution)/shard_map/mine_product/pallas_call | solution.py:237
  51.4 1.3 collective-permute-done.12
  52.7 1.6 %collective-permute-start.13 = (f32[128,256]{1,0:T(8,128)S(1)}, f32[128,256]{1,0:T(8,128)S(1)}, u32[]{:S(2)}, u32[]{:S(2)}) collective-permute-start(f32[128,256]{1,0:T(8,128)S(1)} %add.24._), channel_id=1, source_target_pairs={{0,8},{4,12},{8,0},{12,4},{16,24},{20,28},{24,16},{28,20},{1,9},{5... | collective-permute-start | bytes 393224 | tf_op jit(solution)/shard_map/ppermute | solution.py:51
  54.3 0.3 pair_sum.1
  54.6 0.6 collective-permute-start.17
  55.2 1.5 %collective-permute-start.18 = (bf16[256,768]{1,0:T(8,128)(2,1)S(1)}, bf16[256,768]{1,0:T(8,128)(2,1)S(1)}, u32[]{:S(2)}, u32[]{:S(2)}) collective-permute-start(bf16[256,768]{1,0:T(8,128)(2,1)S(1)} %get-tuple-element.50), channel_id=1, source_target_pairs={{0,16},{4,20},{8,24},{12,28},{16,0},{20,4},{24,8},{28,12},{1,17},{... | collective-permute-start | bytes 1179656 | tf_op jit(solution)/shard_map/ppermute | solution.py:51
  56.7 1.5 %collective-permute-start.19 = (bf16[256,768]{1,0:T(8,128)(2,1)S(1)}, bf16[256,768]{1,0:T(8,128)(2,1)S(1)}, u32[]{:S(2)}, u32[]{:S(2)}) collective-permute-start(bf16[256,768]{1,0:T(8,128)(2,1)S(1)} %get-tuple-element.51), channel_id=1, source_target_pairs={{0,24},{4,28},{8,16},{12,20},{16,8},{20,12},{24,0},{28,4},{1,25},{... | collective-permute-start | bytes 1179656 | tf_op jit(solution)/shard_map/ppermute | solution.py:51
  58.2 1.0 collective-permute-done.13
  59.2 1.6 %collective-permute-start.14 = (f32[128,256]{1,0:T(8,128)S(1)}, f32[128,256]{1,0:T(8,128)S(1)}, u32[]{:S(2)}, u32[]{:S(2)}) collective-permute-start(f32[128,256]{1,0:T(8,128)S(1)} %add.25), channel_id=1, source_target_pairs={{0,16},{4,20},{8,24},{12,28},{16,0},{20,4},{24,8},{28,12},{1,17},{... | collective-permute-start | bytes 393224 | tf_op jit(solution)/shard_map/ppermute | solution.py:51
  60.8 16.3 %collective-permute-done.14 = f32[128,256]{1,0:T(8,128)S(1)} collective-permute-done((f32[128,256]{1,0:T(8,128)S(1)}, f32[128,256]{1,0:T(8,128)S(1)}, u32[]{:S(2)}, u32[]{:S(2)}) %collective-permute-start.14) | collective-permute-done | bytes 131104 | tf_op jit(solution)/shard_map/ppermute | solution.py:51
  77.2 1.3 collective-permute-done.15.other
  78.5 9.1 %chol_inverse.1.inverse = f32[256,256]{1,0:T(8,128)S(1)} custom-call(f32[128,256]{1,0:T(8,128)S(1)} %add.26.mine, f32[128,256]{1,0:T(8,128)S(1)} %collective-permute-done.15.other), custom_call_target="tpu_custom_call" | custom-call | tf_op jit(solution)/shard_map/chol_inverse/pallas_call | solution.py:330
  87.7 0.6 share.1
  88.3 1.5 %collective-permute-start.20 = (f32[8,256]{1,0:T(8,128)S(1)}, f32[8,256]{1,0:T(8,128)S(1)}, u32[]{:S(2)}, u32[]{:S(2)}) collective-permute-start(f32[8,256]{1,0:T(8,128)S(1)} %get-tuple-element.52), channel_id=1, source_target_pairs={{0,8},{4,12},{8,0},{12,4},{16,24},{20,28},{24,16},{28,20},{1,9},{5... | collective-permute-start | bytes 24584 | tf_op jit(solution)/shard_map/ppermute | solution.py:51
  89.8 2.2 %collective-permute-done.20 = f32[8,256]{1,0:T(8,128)S(1)} collective-permute-done((f32[8,256]{1,0:T(8,128)S(1)}, f32[8,256]{1,0:T(8,128)S(1)}, u32[]{:S(2)}, u32[]{:S(2)}) %collective-permute-start.20) | collective-permute-done | bytes 8224 | tf_op jit(solution)/shard_map/ppermute | solution.py:51
  92.0 1.5 %collective-permute-start.21 = (f32[8,256]{1,0:T(8,128)S(1)}, f32[8,256]{1,0:T(8,128)S(1)}, u32[]{:S(2)}, u32[]{:S(2)}) collective-permute-start(f32[8,256]{1,0:T(8,128)S(1)} %add.27), channel_id=1, source_target_pairs={{0,16},{4,20},{8,24},{12,28},{16,0},{20,4},{24,8},{28,12},{1,17},{... | collective-permute-start | bytes 24584 | tf_op jit(solution)/shard_map/ppermute | solution.py:51
  93.5 2.2 %collective-permute-done.21 = f32[8,256]{1,0:T(8,128)S(1)} collective-permute-done((f32[8,256]{1,0:T(8,128)S(1)}, f32[8,256]{1,0:T(8,128)S(1)}, u32[]{:S(2)}, u32[]{:S(2)}) %collective-permute-start.21) | collective-permute-done | bytes 8224 | tf_op jit(solution)/shard_map/ppermute | solution.py:51
  95.6 1.5 %collective-permute-start.25 = (bf16[256,768]{1,0:T(8,128)(2,1)S(1)}, bf16[256,768]{1,0:T(8,128)(2,1)S(1)}, u32[]{:S(2)}, u32[]{:S(2)}) collective-permute-start(bf16[256,768]{1,0:T(8,128)(2,1)S(1)} %hand_on.3.refs_0_.block0), channel_id=1, source_target_pairs={{0,8},{4,12},{8,0},{12,4},{16,24},{20,28},{24,16},{28,20},{1,9},{5... | collective-permute-start | bytes 1179656 | tf_op jit(solution)/shard_map/ppermute | solution.py:51
  97.1 1.5 %collective-permute-start.27 = (bf16[256,768]{1,0:T(8,128)(2,1)S(1)}, bf16[256,768]{1,0:T(8,128)(2,1)S(1)}, u32[]{:S(2)}, u32[]{:S(2)}) collective-permute-start(bf16[256,768]{1,0:T(8,128)(2,1)S(1)} %hand_on.3.refs_0_.block0), channel_id=1, source_target_pairs={{0,16},{4,20},{8,24},{12,28},{16,0},{20,4},{24,8},{28,12},{1,17},{... | collective-permute-start | bytes 1179656 | tf_op jit(solution)/shard_map/ppermute | solution.py:51
  98.6 0.5 collective-permute-start.22
  99.1 1.2 collective-permute-done.22
  100.4 3.6 %collective-permute-done.23 = f32[8,256]{1,0:T(8,128)S(1)} collective-permute-done((f32[8,256]{1,0:T(8,128)S(1)}, f32[8,256]{1,0:T(8,128)S(1)}, u32[]{:S(2)}, u32[]{:S(2)}) %collective-permute-start.23) | collective-permute-done | bytes 8224 | tf_op jit(solution)/shard_map/ppermute | solution.py:51
  104.0 1.5 %collective-permute-start.24 = (f32[8,256]{1,0:T(8,128)S(1)}, f32[8,256]{1,0:T(8,128)S(1)}, u32[]{:S(2)}, u32[]{:S(2)}) collective-permute-start(f32[8,256]{1,0:T(8,128)S(1)} %add.30), channel_id=1, source_target_pairs={{0,2},{1,3},{2,0},{3,1},{4,6},{5,7},{6,4},{7,5},{8,10},{9,11},{10,... | collective-permute-start | bytes 24584 | tf_op jit(solution)/shard_map/ppermute | solution.py:51
  105.5 1.2 ortho.1.ortho_ref
  106.7 1.9 %collective-permute-done.24 = f32[8,256]{1,0:T(8,128)S(1)} collective-permute-done((f32[8,256]{1,0:T(8,128)S(1)}, f32[8,256]{1,0:T(8,128)S(1)}, u32[]{:S(2)}, u32[]{:S(2)}) %collective-permute-start.24) | collective-permute-done | bytes 8224 | tf_op jit(solution)/shard_map/ppermute | solution.py:51
  108.6 6.1 %results.4 = (bf16[1024,6144]{1,0:T(8,128)(2,1)}, f32[1024,6144]{1,0:T(8,128)}, bf16[256,6144]{1,0:T(8,128)(2,1)}) custom-call(f32[512,6144]{1,0:T(8,128)S(1)} %get-tuple-element.33.buf.buf0, f32[512,6144]{1,0:T(8,128)S(1)} %get-tuple-element.36.buf.buf1, bf16[1024,256]{1,0:T(8,128)(2,1)S(1)} %ortho.1.ortho_ref, f32[256,256]{1,0:T(8,128)S(1)} %chol_inverse.1.inverse, ...), custom_call_target="tpu_custom_call" | custom-call | tf_op jit(solution)/shard_map/results/pallas_call | solution.py:463
  114.7 0.6 collective-permute-start.26
  115.3 6.1 %results.5 = (bf16[1024,6144]{1,0:T(8,128)(2,1)}, f32[1024,6144]{1,0:T(8,128)}, bf16[256,6144]{1,0:T(8,128)(2,1)}) custom-call(f32[512,6144]{1,0:T(8,128)S(1)} %get-tuple-element.33.buf.buf0, f32[512,6144]{1,0:T(8,128)S(1)} %get-tuple-element.36.buf.buf1, ...), custom_call_target="tpu_custom_call", output_to_operand_aliasing={{0}: (8, {}), {1}: (9, {}), {2}: (10, {})} | custom-call | tf_op jit(solution)/shard_map/results/pallas_call | solution.py:463
  121.4 6.1 %results.6 = (bf16[1024,6144]{1,0:T(8,128)(2,1)}, f32[1024,6144]{1,0:T(8,128)}, bf16[256,6144]{1,0:T(8,128)(2,1)}) custom-call(f32[512,6144]{1,0:T(8,128)S(1)} %get-tuple-element.33.buf.buf0, f32[512,6144]{1,0:T(8,128)S(1)} %get-tuple-element.36.buf.buf1, ...), custom_call_target="tpu_custom_call", output_to_operand_aliasing={{0}: (8, {}), {1}: (9, {}), {2}: (10, {})} | custom-call | tf_op jit(solution)/shard_map/results/pallas_call | solution.py:463
  127.5 1.9 %copy-done = bf16[256,6144]{1,0:T(8,128)(2,1)S(1)} copy-done((bf16[256,6144]{1,0:T(8,128)(2,1)S(1)}, bf16[256,6144]{1,0:T(8,128)(2,1)}, u32[]{:S(2)}) %copy-start) | copy-done | bytes 3145752
  129.6 1.5 %collective-permute-done.31.block1 = bf16[256,768]{1,0:T(8,128)(2,1)S(1)} collective-permute-done((bf16[256,768]{1,0:T(8,128)(2,1)S(1)}, bf16[256,768]{1,0:T(8,128)(2,1)S(1)}, u32[]{:S(2)}, u32[]{:S(2)}) %collective-permute-start.31) | collective-permute-done | bytes 393248 | tf_op jit(solution)/shard_map/ppermute | solution.py:51
  131.1 6.1 %results.7 = (bf16[1024,6144]{1,0:T(8,128)(2,1)}, f32[1024,6144]{1,0:T(8,128)}, bf16[256,6144]{1,0:T(8,128)(2,1)}) custom-call(f32[512,6144]{1,0:T(8,128)S(1)} %get-tuple-element.33.buf.buf0, f32[512,6144]{1,0:T(8,128)S(1)} %get-tuple-element.36.buf.buf1, ...), custom_call_target="tpu_custom_call", output_to_operand_aliasing={{0}: (8, {}), {1}: (9, {}), {2}: (10, {})} | custom-call | tf_op jit(solution)/shard_map/results/pallas_call | solution.py:463
  (45 shorter events, 0.6 us)
Async XLA Ops:
  10.3 18.9 %collective-permute-start = (bf16[256,128]{1,0:T(8,128)(2,1)S(1)}, bf16[256,128]{1,0:T(8,128)(2,1)S(1)}, u32[]{:S(2)}, u32[]{:S(2)}) collective-permute-start(bf16[256,128]{1,0:T(8,128)(2,1)S(1)} %get-tuple-element.35.rest_0_), channel_id=1, source_target_pairs={{0,1},{1,0},{2,3},{3,2},{4,5},{5,4},{6,7},{7,6},{8,9},{9,8},{10,11... | collective-permute-start | bytes 196616 | tf_op jit(solution)/shard_map/ppermute | solution.py:51
  13.4 15.8 %collective-permute-start.1 = (bf16[256,128]{1,0:T(8,128)(2,1)S(1)}, bf16[256,128]{1,0:T(8,128)(2,1)S(1)}, u32[]{:S(2)}, u32[]{:S(2)}) collective-permute-start(bf16[256,128]{1,0:T(8,128)(2,1)S(1)} %get-tuple-element.38), channel_id=1, source_target_pairs={{0,2},{1,3},{2,0},{3,1},{4,6},{5,7},{6,4},{7,5},{8,10},{9,11},{10,... | collective-permute-start | bytes 196616 | tf_op jit(solution)/shard_map/ppermute | solution.py:51
  16.0 13.2 %collective-permute-start.2 = (bf16[256,128]{1,0:T(8,128)(2,1)S(1)}, bf16[256,128]{1,0:T(8,128)(2,1)S(1)}, u32[]{:S(2)}, u32[]{:S(2)}) collective-permute-start(bf16[256,128]{1,0:T(8,128)(2,1)S(1)} %get-tuple-element.39), channel_id=1, source_target_pairs={{0,3},{1,2},{2,1},{3,0},{4,7},{5,6},{6,5},{7,4},{8,11},{9,10},{10,... | collective-permute-start | bytes 196616 | tf_op jit(solution)/shard_map/ppermute | solution.py:51
  24.8 9.0 %collective-permute-start.6 = (bf16[256,128]{1,0:T(8,128)(2,1)S(1)}, bf16[256,128]{1,0:T(8,128)(2,1)S(1)}, u32[]{:S(2)}, u32[]{:S(2)}) collective-permute-start(bf16[256,128]{1,0:T(8,128)(2,1)S(1)} %get-tuple-element.41), channel_id=1, source_target_pairs={{0,1},{1,0},{2,3},{3,2},{4,5},{5,4},{6,7},{7,6},{8,9},{9,8},{10,11... | collective-permute-start | bytes 196616 | tf_op jit(solution)/shard_map/ppermute | solution.py:51
  25.7 8.0 %collective-permute-start.7 = (bf16[256,128]{1,0:T(8,128)(2,1)S(1)}, bf16[256,128]{1,0:T(8,128)(2,1)S(1)}, u32[]{:S(2)}, u32[]{:S(2)}) collective-permute-start(bf16[256,128]{1,0:T(8,128)(2,1)S(1)} %get-tuple-element.42), channel_id=1, source_target_pairs={{0,2},{1,3},{2,0},{3,1},{4,6},{5,7},{6,4},{7,5},{8,10},{9,11},{10,... | collective-permute-start | bytes 196616 | tf_op jit(solution)/shard_map/ppermute | solution.py:51
  29.2 6.1 %collective-permute-start.8 = (bf16[256,128]{1,0:T(8,128)(2,1)S(1)}, bf16[256,128]{1,0:T(8,128)(2,1)S(1)}, u32[]{:S(2)}, u32[]{:S(2)}) collective-permute-start(bf16[256,128]{1,0:T(8,128)(2,1)S(1)} %get-tuple-element.43), channel_id=1, source_target_pairs={{0,3},{1,2},{2,1},{3,0},{4,7},{5,6},{6,5},{7,4},{8,11},{9,10},{10,... | collective-permute-start | bytes 196616 | tf_op jit(solution)/shard_map/ppermute | solution.py:51
  29.3 11.7 %collective-permute-start.3 = (bf16[256,128]{1,0:T(8,128)(2,1)S(1)}, bf16[256,128]{1,0:T(8,128)(2,1)S(1)}, u32[]{:S(2)}, u32[]{:S(2)}) collective-permute-start(bf16[256,128]{1,0:T(8,128)(2,1)S(1)} %share_sum.2.refs_0_.rest_0_), channel_id=1, source_target_pairs={{0,1},{1,0},{2,3},{3,2},{4,5},{5,4},{6,7},{7,6},{8,9},{9,8},{10,11... | collective-permute-start | bytes 196616 | tf_op jit(solution)/shard_map/ppermute | solution.py:51
  29.9 11.7 %collective-permute-start.4 = (bf16[256,128]{1,0:T(8,128)(2,1)S(1)}, bf16[256,128]{1,0:T(8,128)(2,1)S(1)}, u32[]{:S(2)}, u32[]{:S(2)}) collective-permute-start(bf16[256,128]{1,0:T(8,128)(2,1)S(1)} %share_sum.2.refs_0_.rest_0_), channel_id=1, source_target_pairs={{0,2},{1,3},{2,0},{3,1},{4,6},{5,7},{6,4},{7,5},{8,10},{9,11},{10,... | collective-permute-start | bytes 196616 | tf_op jit(solution)/shard_map/ppermute | solution.py:51
  33.7 7.9 %collective-permute-start.5 = (bf16[256,128]{1,0:T(8,128)(2,1)S(1)}, bf16[256,128]{1,0:T(8,128)(2,1)S(1)}, u32[]{:S(2)}, u32[]{:S(2)}) collective-permute-start(bf16[256,128]{1,0:T(8,128)(2,1)S(1)} %share_sum.2.refs_0_.rest_0_), channel_id=1, source_target_pairs={{0,3},{1,2},{2,1},{3,0},{4,7},{5,6},{6,5},{7,4},{8,11},{9,10},{10,... | collective-permute-start | bytes 196616 | tf_op jit(solution)/shard_map/ppermute | solution.py:51
  35.3 9.4 %collective-permute-start.10 = (bf16[256,128]{1,0:T(8,128)(2,1)S(1)}, bf16[256,128]{1,0:T(8,128)(2,1)S(1)}, u32[]{:S(2)}, u32[]{:S(2)}) collective-permute-start(bf16[256,128]{1,0:T(8,128)(2,1)S(1)} %share_sum.3.refs_4_.rest_0_), channel_id=1, source_target_pairs={{0,2},{1,3},{2,0},{3,1},{4,6},{5,7},{6,4},{7,5},{8,10},{9,11},{10,... | collective-permute-start | bytes 196616 | tf_op jit(solution)/shard_map/ppermute | solution.py:51
  40.9 6.1 %collective-permute-start.11 = (bf16[256,128]{1,0:T(8,128)(2,1)S(1)}, bf16[256,128]{1,0:T(8,128)(2,1)S(1)}, u32[]{:S(2)}, u32[]{:S(2)}) collective-permute-start(bf16[256,128]{1,0:T(8,128)(2,1)S(1)} %share_sum.3.refs_4_.rest_0_), channel_id=1, source_target_pairs={{0,3},{1,2},{2,1},{3,0},{4,7},{5,6},{6,5},{7,4},{8,11},{9,10},{10,... | collective-permute-start | bytes 196616 | tf_op jit(solution)/shard_map/ppermute | solution.py:51
  41.0 6.0 %collective-permute-start.9 = (bf16[256,128]{1,0:T(8,128)(2,1)S(1)}, bf16[256,128]{1,0:T(8,128)(2,1)S(1)}, u32[]{:S(2)}, u32[]{:S(2)}) collective-permute-start(bf16[256,128]{1,0:T(8,128)(2,1)S(1)} %share_sum.3.refs_4_.rest_0_), channel_id=1, source_target_pairs={{0,1},{1,0},{2,3},{3,2},{4,5},{5,4},{6,7},{7,6},{8,9},{9,8},{10,11... | collective-permute-start | bytes 196616 | tf_op jit(solution)/shard_map/ppermute | solution.py:51
  49.1 5.2 %collective-permute-start.16 = (bf16[256,3072]{1,0:T(8,128)(2,1)S(1)}, bf16[256,3072]{1,0:T(8,128)(2,1)S(1)}, u32[]{:S(2)}, u32[]{:S(2)}) collective-permute-start(bf16[256,3072]{1,0:T(8,128)(2,1)S(1)} %other_product.1.rest_4_), channel_id=1, source_target_pairs={{0,4},{4,0},{8,12},{12,8},{16,20},{20,16},{24,28},{28,24},{1,5},{5... | collective-permute-start | bytes 4718600 | tf_op jit(solution)/shard_map/ppermute | solution.py:51
  49.1 3.6 %collective-permute-start.12 = (f32[128,256]{1,0:T(8,128)S(1)}, f32[128,256]{1,0:T(8,128)S(1)}, u32[]{:S(2)}, u32[]{:S(2)}) collective-permute-start(f32[128,256]{1,0:T(8,128)S(1)} %get-tuple-element.45), channel_id=1, source_target_pairs={{0,4},{4,0},{8,12},{12,8},{16,20},{20,16},{24,28},{28,24},{1,5},{5... | collective-permute-start | bytes 393224 | tf_op jit(solution)/shard_map/ppermute | solution.py:51
  52.7 6.4 %collective-permute-start.13 = (f32[128,256]{1,0:T(8,128)S(1)}, f32[128,256]{1,0:T(8,128)S(1)}, u32[]{:S(2)}, u32[]{:S(2)}) collective-permute-start(f32[128,256]{1,0:T(8,128)S(1)} %add.24._), channel_id=1, source_target_pairs={{0,8},{4,12},{8,0},{12,4},{16,24},{20,28},{24,16},{28,20},{1,9},{5... | collective-permute-start | bytes 393224 | tf_op jit(solution)/shard_map/ppermute | solution.py:51
  54.6 33.0 %collective-permute-start.17 = (bf16[256,768]{1,0:T(8,128)(2,1)S(1)}, bf16[256,768]{1,0:T(8,128)(2,1)S(1)}, u32[]{:S(2)}, u32[]{:S(2)}) collective-permute-start(bf16[256,768]{1,0:T(8,128)(2,1)S(1)} %get-tuple-element.49), channel_id=1, source_target_pairs={{0,8},{4,12},{8,0},{12,4},{16,24},{20,28},{24,16},{28,20},{1,9},{5... | collective-permute-start | bytes 1179656 | tf_op jit(solution)/shard_map/ppermute | solution.py:51
  55.2 32.4 %collective-permute-start.18 = (bf16[256,768]{1,0:T(8,128)(2,1)S(1)}, bf16[256,768]{1,0:T(8,128)(2,1)S(1)}, u32[]{:S(2)}, u32[]{:S(2)}) collective-permute-start(bf16[256,768]{1,0:T(8,128)(2,1)S(1)} %get-tuple-element.50), channel_id=1, source_target_pairs={{0,16},{4,20},{8,24},{12,28},{16,0},{20,4},{24,8},{28,12},{1,17},{... | collective-permute-start | bytes 1179656 | tf_op jit(solution)/shard_map/ppermute | solution.py:51
  56.7 30.9 %collective-permute-start.19 = (bf16[256,768]{1,0:T(8,128)(2,1)S(1)}, bf16[256,768]{1,0:T(8,128)(2,1)S(1)}, u32[]{:S(2)}, u32[]{:S(2)}) collective-permute-start(bf16[256,768]{1,0:T(8,128)(2,1)S(1)} %get-tuple-element.51), channel_id=1, source_target_pairs={{0,24},{4,28},{8,16},{12,20},{16,8},{20,12},{24,0},{28,4},{1,25},{... | collective-permute-start | bytes 1179656 | tf_op jit(solution)/shard_map/ppermute | solution.py:51
  59.2 17.9 %collective-permute-start.14 = (f32[128,256]{1,0:T(8,128)S(1)}, f32[128,256]{1,0:T(8,128)S(1)}, u32[]{:S(2)}, u32[]{:S(2)}) collective-permute-start(f32[128,256]{1,0:T(8,128)S(1)} %add.25), channel_id=1, source_target_pairs={{0,16},{4,20},{8,24},{12,28},{16,0},{20,4},{24,8},{28,12},{1,17},{... | collective-permute-start | bytes 393224 | tf_op jit(solution)/shard_map/ppermute | solution.py:51
  77.1 1.4 %collective-permute-start.15 = (f32[128,256]{1,0:T(8,128)S(1)}, f32[128,256]{1,0:T(8,128)S(1)}, u32[]{:S(2)}, u32[]{:S(2)}) collective-permute-start(f32[128,256]{1,0:T(8,128)S(1)} %add.26.mine), channel_id=1, source_target_pairs={{0,4},{4,0},{8,12},{12,8},{16,20},{20,16},{24,28},{28,24},{1,5},{5... | collective-permute-start | bytes 393224 | tf_op jit(solution)/shard_map/ppermute | solution.py:51
  88.3 3.7 %collective-permute-start.20 = (f32[8,256]{1,0:T(8,128)S(1)}, f32[8,256]{1,0:T(8,128)S(1)}, u32[]{:S(2)}, u32[]{:S(2)}) collective-permute-start(f32[8,256]{1,0:T(8,128)S(1)} %get-tuple-element.52), channel_id=1, source_target_pairs={{0,8},{4,12},{8,0},{12,4},{16,24},{20,28},{24,16},{28,20},{1,9},{5... | collective-permute-start | bytes 24584 | tf_op jit(solution)/shard_map/ppermute | solution.py:51
  92.0 3.7 %collective-permute-start.21 = (f32[8,256]{1,0:T(8,128)S(1)}, f32[8,256]{1,0:T(8,128)S(1)}, u32[]{:S(2)}, u32[]{:S(2)}) collective-permute-start(f32[8,256]{1,0:T(8,128)S(1)} %add.27), channel_id=1, source_target_pairs={{0,16},{4,20},{8,24},{12,28},{16,0},{20,4},{24,8},{28,12},{1,17},{... | collective-permute-start | bytes 24584 | tf_op jit(solution)/shard_map/ppermute | solution.py:51
  95.6 9.9 %collective-permute-start.25 = (bf16[256,768]{1,0:T(8,128)(2,1)S(1)}, bf16[256,768]{1,0:T(8,128)(2,1)S(1)}, u32[]{:S(2)}, u32[]{:S(2)}) collective-permute-start(bf16[256,768]{1,0:T(8,128)(2,1)S(1)} %hand_on.3.refs_0_.block0), channel_id=1, source_target_pairs={{0,8},{4,12},{8,0},{12,4},{16,24},{20,28},{24,16},{28,20},{1,9},{5... | collective-permute-start | bytes 1179656 | tf_op jit(solution)/shard_map/ppermute | solution.py:51
  97.1 11.5 %collective-permute-start.27 = (bf16[256,768]{1,0:T(8,128)(2,1)S(1)}, bf16[256,768]{1,0:T(8,128)(2,1)S(1)}, u32[]{:S(2)}, u32[]{:S(2)}) collective-permute-start(bf16[256,768]{1,0:T(8,128)(2,1)S(1)} %hand_on.3.refs_0_.block0), channel_id=1, source_target_pairs={{0,16},{4,20},{8,24},{12,28},{16,0},{20,4},{24,8},{28,12},{1,17},{... | collective-permute-start | bytes 1179656 | tf_op jit(solution)/shard_map/ppermute | solution.py:51
  98.6 10.0 %collective-permute-start.30 = (bf16[256,768]{1,0:T(8,128)(2,1)S(1)}, bf16[256,768]{1,0:T(8,128)(2,1)S(1)}, u32[]{:S(2)}, u32[]{:S(2)}) collective-permute-start(bf16[256,768]{1,0:T(8,128)(2,1)S(1)} %hand_on.3.refs_0_.block0), channel_id=1, source_target_pairs={{0,4},{4,0},{8,12},{12,8},{16,20},{20,16},{24,28},{28,24},{1,5},{5... | collective-permute-start | bytes 1179656 | tf_op jit(solution)/shard_map/ppermute | solution.py:51
  98.6 1.7 %collective-permute-start.22 = (f32[8,256]{1,0:T(8,128)S(1)}, f32[8,256]{1,0:T(8,128)S(1)}, u32[]{:S(2)}, u32[]{:S(2)}) collective-permute-start(f32[8,256]{1,0:T(8,128)S(1)} %add.28.refs_1_), channel_id=1, source_target_pairs={{0,4},{4,0},{8,12},{12,8},{16,20},{20,16},{24,28},{28,24},{1,5},{5... | collective-permute-start | bytes 24584 | tf_op jit(solution)/shard_map/ppermute | solution.py:51
  100.4 3.7 %collective-permute-start.23 = (f32[8,256]{1,0:T(8,128)S(1)}, f32[8,256]{1,0:T(8,128)S(1)}, u32[]{:S(2)}, u32[]{:S(2)}) collective-permute-start(f32[8,256]{1,0:T(8,128)S(1)} %add.29), channel_id=1, source_target_pairs={{0,1},{1,0},{2,3},{3,2},{4,5},{5,4},{6,7},{7,6},{8,9},{9,8},{10,11... | collective-permute-start | bytes 24584 | tf_op jit(solution)/shard_map/ppermute | solution.py:51
  104.0 4.5 %collective-permute-start.24 = (f32[8,256]{1,0:T(8,128)S(1)}, f32[8,256]{1,0:T(8,128)S(1)}, u32[]{:S(2)}, u32[]{:S(2)}) collective-permute-start(f32[8,256]{1,0:T(8,128)S(1)} %add.30), channel_id=1, source_target_pairs={{0,2},{1,3},{2,0},{3,1},{4,6},{5,7},{6,4},{7,5},{8,10},{9,11},{10,... | collective-permute-start | bytes 24584 | tf_op jit(solution)/shard_map/ppermute | solution.py:51
  105.5 9.8 %collective-permute-start.29 = (bf16[256,768]{1,0:T(8,128)(2,1)S(1)}, bf16[256,768]{1,0:T(8,128)(2,1)S(1)}, u32[]{:S(2)}, u32[]{:S(2)}) collective-permute-start(bf16[256,768]{1,0:T(8,128)(2,1)S(1)} %collective-permute-done.25.refs_1_.block0), channel_id=1, source_target_pairs={{0,4},{4,0},{8,12},{12,8},{16,20},{20,16},{24,28},{28,24},{1,5},{5... | collective-permute-start | bytes 1179656 | tf_op jit(solution)/shard_map/ppermute | solution.py:51
  108.6 12.8 %collective-permute-start.28 = (bf16[256,768]{1,0:T(8,128)(2,1)S(1)}, bf16[256,768]{1,0:T(8,128)(2,1)S(1)}, u32[]{:S(2)}, u32[]{:S(2)}) collective-permute-start(bf16[256,768]{1,0:T(8,128)(2,1)S(1)} %collective-permute-done.27.block0), channel_id=1, source_target_pairs={{0,4},{4,0},{8,12},{12,8},{16,20},{20,16},{24,28},{28,24},{1,5},{5... | collective-permute-start | bytes 1179656 | tf_op jit(solution)/shard_map/ppermute | solution.py:51
  114.7 12.8 %collective-permute-start.26 = (bf16[256,768]{1,0:T(8,128)(2,1)S(1)}, bf16[256,768]{1,0:T(8,128)(2,1)S(1)}, u32[]{:S(2)}, u32[]{:S(2)}) collective-permute-start(bf16[256,768]{1,0:T(8,128)(2,1)S(1)} %hand_on.4), channel_id=1, source_target_pairs={{0,24},{4,28},{8,16},{12,20},{16,8},{20,12},{24,0},{28,4},{1,25},{... | collective-permute-start | bytes 1179656 | tf_op jit(solution)/shard_map/ppermute | solution.py:51
  127.5 1.9 %copy-start = (bf16[256,6144]{1,0:T(8,128)(2,1)S(1)}, bf16[256,6144]{1,0:T(8,128)(2,1)}, u32[]{:S(2)}) copy-start(bf16[256,6144]{1,0:T(8,128)(2,1)} %get-tuple-element.60.refs_1_.rest_2_) | copy-start | bytes 9437188
  129.4 1.7 %collective-permute-start.31 = (bf16[256,768]{1,0:T(8,128)(2,1)S(1)}, bf16[256,768]{1,0:T(8,128)(2,1)S(1)}, u32[]{:S(2)}, u32[]{:S(2)}) collective-permute-start(bf16[256,768]{1,0:T(8,128)(2,1)S(1)} %hand_on.5.block0), channel_id=1, source_target_pairs={{0,4},{4,0},{8,12},{12,8},{16,20},{20,16},{24,28},{28,24},{1,5},{5... | collective-permute-start | bytes 1179656 | tf_op jit(solution)/shard_map/ppermute | solution.py:51

commit v4 on v3

--- a/solution.py
+++ b/solution.py
@@ -116,8 +116,14 @@
             pltpu.SemaphoreType.DMA,
         ],
         compiler_params=params(10),
+        cost_estimate=cost(momentum, gradient),
         name="project",
     )(stay(momentum), stay(gradient), keep(basis) if part else stay(basis), *after)
+
+
+def cost(*arrays):
+    size = sum(math.prod(x.shape) * x.dtype.itemsize for x in arrays)
+    return pl.CostEstimate(flops=0, bytes_accessed=size, transcendentals=0)
 
 
 def keep(x):
@@ -137,7 +143,7 @@
 
 
 def gram_kernel(*refs):
-    lefts, (g_mine, g_other, total) = refs[:-3], refs[-3:]
+    lefts, (_, g_mine, g_other, total) = refs[:-4], refs[-4:]
     core = lax.bitwise_and(lax.axis_index("row"), jnp.int32(1))
     total[...] = sum(dot(ref[...], ref[...], ((1,), (1,))) for ref in lefts)
     h = g_mine.shape[0]
@@ -145,17 +151,17 @@
     g_other[...] = total[pl.ds(pl.multiple_of((1 - core) * h, h), h), :]
 
 
-def gram(lefts):
+def gram(lefts, after):
     r = lefts[0].shape[0]
     return pl.pallas_call(
         gram_kernel,
         out_shape=[shape((r // 2, r), f32)] * 2,
-        in_specs=[VMEM] * len(lefts),
+        in_specs=[VMEM] * len(lefts) + [ANY],
         out_specs=[VMEM] * 2,
         scratch_shapes=[pltpu.VMEM((r, r), f32)],
         compiler_params=params(8),
         name="gram",
-    )(*lefts)
+    )(*lefts, after)
 
 
 def first_kernel(depth, width, buf, *rest):
@@ -183,6 +189,7 @@
         out_specs=[VMEM] * 2,
         scratch_shapes=[pltpu.VMEM((r, m), bf16)],
         compiler_params=params(8),
+        cost_estimate=cost(buf, shape((r, n), f32)),
         name="first_product",
     )(keep(buf), *lefts)
 
@@ -212,6 +219,7 @@
         out_specs=VMEM,
         scratch_shapes=[pltpu.VMEM((r, m), bf16)],
         compiler_params=params(8),
+        cost_estimate=cost(buf, sums),
         name="other_product",
     )(keep(buf), sums, *lefts, after)
 
@@ -231,18 +239,19 @@
     lax.fori_loop(0, size // width, step, 0)
 
 
-def mine_product(buf, sums, lefts, width, after):
+def mine_product(buf, sums, lefts, width, *after):
     m, n = buf.shape
     r = lefts[0].shape[0]
     return pl.pallas_call(
         functools.partial(mine_kernel, len(lefts), width),
         out_shape=shape((r, n // 2), f32),
-        in_specs=[VMEM] * (2 + len(lefts)) + [ANY],
+        in_specs=[VMEM] * (2 + len(lefts)) + [ANY] * len(after),
         out_specs=VMEM,
         scratch_shapes=[pltpu.VMEM((r, m), bf16)],
         compiler_params=params(8),
+        cost_estimate=cost(buf, sums),
         name="mine_product",
-    )(keep(buf), sums, *lefts, after)
+    )(keep(buf), sums, *lefts, *after)
 
 
 def pair_sum_kernel(chips, mine, received, _, *outs):
@@ -334,6 +343,7 @@
         out_specs=VMEM,
         scratch_shapes=[pltpu.VMEM((n, 2 * n), f32)],
         compiler_params=params(8),
+        cost_estimate=cost(*[mine] * 256),
         name="chol_inverse",
     )(mine, other)
 
@@ -357,6 +367,7 @@
         in_specs=[VMEM] * (1 + len(lefts)),
         out_specs=VMEM,
         compiler_params=params(8),
+        cost_estimate=cost(*[shape((half * len(lefts), r), bf16)] * 8),
         name="ortho",
     )(inverse, *lefts)
 
@@ -397,75 +408,90 @@
     )(inverse, own, *received)
 
 
-def result_kernel(d, factor, buf0, buf1, ortho_ref, inverse, squares, block0, block1, weight, *rest):
-    new_weight, new_momentum, basis, mbuf, wbuf, vbuf, nbuf, lbuf, in_sems, out_sems, basis_sems = rest[-11:]
-    r, width = block0.shape
+def result_kernel(pairs, factor, buf0, buf1, ortho_ref, inverse, squares, *refs):
+    blocks, (weight, *rest) = refs[: 2 * len(pairs)], refs[2 * len(pairs) :]
+    *_, new_weight, new_momentum, basis, token, mbuf, wbuf, vbuf, nbuf, lbuf, in_sems, out_sems, basis_sems = rest
+    r, width = blocks[0].shape
     tile = 256
     tiles = width // tile
+    count = len(blocks)
     half = width * (lax.axis_size("row") // 2)
     row = lax.axis_index("row")
     core = lax.bitwise_and(row, jnp.int32(1))
-    chip = flip(lax.div(row, jnp.int32(2)), d)
-    starts = [core * half + chip * width, (1 - core) * half + chip * width]
-    cols = [pl.ds(pl.multiple_of(start, 128), width) for start in starts]
-    loads = [pltpu.make_async_copy(weight.at[:, cols[b]], wbuf.at[b], in_sems.at[b]) for b in range(2)]
-    basis_stores = [pltpu.make_async_copy(nbuf.at[b], basis.at[:, cols[b]], basis_sems.at[b]) for b in range(2)]
+    chip = lax.div(row, jnp.int32(2))
+    starts = []
+    for d in pairs:
+        starts += [core * half + flip(chip, d) * width, (1 - core) * half + flip(chip, d) * width]
+
+    def cols(b):
+        return pl.ds(pl.multiple_of(starts[b], 128), width)
+
+    def load(b):
+        return pltpu.make_async_copy(weight.at[:, cols(b)], wbuf.at[b % 2], in_sems.at[b % 2])
+
+    def store_basis(b):
+        return pltpu.make_async_copy(nbuf.at[b % 2], basis.at[:, cols(b)], basis_sems.at[b % 2])
 
     def stores(b, t):
-        at = pl.ds(pl.multiple_of(t * tile, tile), tile)
+        at = pl.ds(t * tile, tile)
         there = pl.ds(pl.multiple_of(starts[b] + t * tile, 128), tile)
         return (
-            pltpu.make_async_copy(mbuf.at[b, :, at], new_momentum.at[:, there], out_sems.at[0, b, t]),
-            pltpu.make_async_copy(vbuf.at[b, :, at], new_weight.at[:, there], out_sems.at[1, b, t]),
+            pltpu.make_async_copy(mbuf.at[b % 2, :, at], new_momentum.at[:, there], out_sems.at[0, b % 2, t]),
+            pltpu.make_async_copy(vbuf.at[b % 2, :, at], new_weight.at[:, there], out_sems.at[1, b % 2, t]),
         )
 
-    for load in loads:
-        load.start()
+    def finish(b):
+        store_basis(b).wait()
+        for t in range(tiles):
+            for store in stores(b, t):
+                store.wait()
+
+    for b in range(2):
+        load(b).start()
     scale = lax.rsqrt(squares[...] / FF + epsilon)
     scale = jnp.transpose(jnp.concatenate([scale] * 16, axis=0))[:, :1]
+    token[...] = jnp.zeros_like(token)
     parts = split(inverse[...], 2)
     depth = lax.axis_size("col")
     size = buf0.shape[0] // depth
-    for b, block in enumerate((block0, block1)):
-        right = apply_inverse(parts, block[...])
-        lbuf[b] = right.astype(bf16)
-        nbuf[b] = (right * scale).astype(bf16)
-        basis_stores[b].start()
-        loads[b].wait()
-
-        def step(t, carry, b=b):
-            at = pl.ds(pl.multiple_of(t * tile, tile), tile)
+    for b in range(count):
+        k = b % 2
+        if b >= 2:
+            finish(b - 2)
+        right = apply_inverse(parts, blocks[b][...])
+        lbuf[k] = ((1.0 - momentum_decay) * right).astype(bf16)
+        nbuf[k] = (right * scale).astype(bf16)
+        store_basis(b).start()
+        load(b).wait()
+        for t in range(tiles):
+            at = slice(t * tile, (t + 1) * tile)
             there = pl.ds(pl.multiple_of(starts[b] + t * tile, 128), tile)
-            correction = dot(ortho_ref[...], lbuf[b, :, at])
-            for k in range(2 * depth):
-                rows = slice(k * size, (k + 1) * size)
-                here = slice(k // 2 * size, (k // 2 + 1) * size)
-                old = (buf0, buf1)[k % 2][here, there]
-                mbuf[b, rows, at] = old - (1.0 - momentum_decay) * correction[rows]
-            change = dot(ortho_ref[...], nbuf[b, :, at])
-            vbuf[b, :, at] = (wbuf[b, :, at].astype(f32) - factor * change).astype(bf16)
+            correction = dot(ortho_ref[...], lbuf[k, :, at])
+            for j in range(2 * depth):
+                rows = slice(j * size, (j + 1) * size)
+                here = slice(j // 2 * size, (j // 2 + 1) * size)
+                mbuf[k, rows, at] = (buf0, buf1)[j % 2][here, there] - correction[rows]
+            change = dot(ortho_ref[...], nbuf[k, :, at])
+            vbuf[k, :, at] = (wbuf[k, :, at].astype(f32) - factor * change).astype(bf16)
             for store in stores(b, t):
                 store.start()
-            return carry
-
-        lax.fori_loop(0, tiles, step, 0)
-    for b in range(2):
-        basis_stores[b].wait()
-        for t in range(tiles):
-            for store in stores(b, t):
-                store.wait()
-
-
-def results(d, factor, bufs, ortho_bf, inverse, squares, blocks, weight, before):
+        if b + 2 < count:
+            load(b + 2).start()
+    for b in range(count - 2, count):
+        finish(b)
+
+
+def results(pairs, factor, bufs, ortho_bf, inverse, squares, blocks, weight, outs):
     m, n = weight.shape
     r, width = blocks[0].shape
-    ins = [*map(keep, bufs), ortho_bf, inverse, squares, *blocks, stay(weight), *map(stay, before)]
-    return pl.pallas_call(
-        functools.partial(result_kernel, d, factor),
-        out_shape=(shape((m, n), bf16), shape((m, n), f32), shape((r, n), bf16)),
-        in_specs=[VMEM] * 7 + [ANY] * (1 + len(before)),
-        out_specs=[ANY] * 3,
-        input_output_aliases={8 + k: k for k in range(len(before))},
+    ins = [*map(keep, bufs), ortho_bf, inverse, squares, *blocks, stay(weight), *map(stay, outs)]
+    at = len(ins) - len(outs)
+    *outs, token = pl.pallas_call(
+        functools.partial(result_kernel, pairs, factor),
+        out_shape=[shape((m, n), bf16), shape((m, n), f32), shape((r, n), bf16), shape((8, 128), f32)],
+        in_specs=[VMEM] * (5 + len(blocks)) + [ANY] * (1 + len(outs)),
+        out_specs=[ANY] * 3 + [VMEM],
+        input_output_aliases={at + k: k for k in range(len(outs))},
         scratch_shapes=[
             pltpu.VMEM((2, m, width), f32),
             pltpu.VMEM((2, m, width), bf16),
@@ -477,8 +503,10 @@
             pltpu.SemaphoreType.DMA((2,)),
         ],
         compiler_params=params(20),
+        cost_estimate=cost(*[shape((m, width), f32)] * (2 * len(blocks))),
         name="results",
     )(*ins)
+    return outs, token
 
 
 def sum_over(x, axis, least=1):
@@ -493,6 +521,21 @@
     return [x] + [swap(x, axis, unit * d) for d in range(1, count)]
 
 
+def pair_up(terms):
+    while len(terms) > 1:
+        terms = [terms[2 * i] + terms[2 * i + 1] for i in range(len(terms) // 2)]
+    return terms[0]
+
+
+def gather(x, axis):
+    blocks = [x]
+    size = lax.axis_size(axis)
+    for d in range(1, size):
+        low = d & -d
+        blocks.append(swap(blocks[d - low] if d != low else x, axis, low))
+    return blocks
+
+
 def per_device(weight, gradient, momentum, old_basis):
     depth, rows = lax.axis_size("col"), lax.axis_size("row")
     chips = rows // 2
@@ -500,8 +543,7 @@
     width = n // rows
 
     def sum_over_col(own, *sent):
-        low = share_sum(own, [swap(x, "col", d + 1) for d, x in enumerate(sent)])
-        return exchange(low, "col", depth)
+        return gather(share_sum(own, [swap(x, "col", d + 1) for d, x in enumerate(sent)]), "col")
 
     buf0, kept, *outs = project(momentum, gradient, old_basis, depth, 0)
     left0 = sum_over_col(*outs)
@@ -510,32 +552,36 @@
     bufs = (buf0, buf1)
 
     other, mine = first_product(buf0, left0, width)
-    g_mine, g_other = gram(left0 + left1)
+    g_mine, g_other = gram(left0 + left1, other)
     other = other_product(buf1, other, left1, width, g_mine)
     g_mine = g_mine + swap(g_other, "row", 1)
-    received = swap(other, "row", 1)
-    mine = mine_product(buf1, mine, left1, width, other)
+    received = swap(hand_on(other, g_mine), "row", 1)
+    mine = mine_product(buf1, mine, left1, width, g_mine, other)
+    g_mine = sum_over(g_mine, "row", 2)
     own, *sent = pair_sum(mine, received, chips, g_mine)
-    g_mine = sum_over(g_mine, "row", 2)
     got = [swap(x, "row", 2 * (d + 1)) for d, x in enumerate(sent)]
     inverse = chol_inverse(g_mine, swap(g_mine, "row", 1))
 
     share, squares = share_of(inverse, own, got)
     ortho_bf = ortho(inverse, left0 + left1)
-    squares = sum_over(squares, "row", 2)
+    squares = pair_up(exchange(squares, "row", chips, 2))
     share = hand_on(share, squares)
-    squares = sum_over(squares + swap(squares, "row", 1), "col")
+    squares = pair_up(exchange(squares + swap(squares, "row", 1), "col", depth))
 
     factor = step_rate * math.sqrt(D / RANK)
-    outs, blocks = (), [share]
-    for d in range(1, chips):
-        source = share if d < 3 else hand_on(share, blocks[d - 2])
-        blocks.append(swap(source, "row", 2 * d))
-    for d, block in enumerate(blocks):
-        if d > 2:
-            block = hand_on(block, outs[2])
-        pair = (block, swap(block, "row", 1))
-        outs = results(d, factor, bufs, ortho_bf, inverse, squares, pair, weight, outs)
+    near = min(3, chips)
+    blocks = [share] + [swap(share, "row", 2 * d) for d in range(1, near)]
+    blocks = [share] + [hand_on(x, squares) for x in blocks[1:]]
+    for d in range(near, chips):
+        share = hand_on(share, blocks[d - 2])
+        blocks.append(swap(share, "row", 2 * d))
+    blocks[0] = share
+    pairs = [x for block in blocks[:near] for x in (block, swap(block, "row", 1))]
+    common = (factor, bufs, ortho_bf, inverse, squares)
+    outs, token = results(tuple(range(near)), *common, pairs, weight, [])
+    for d in range(near, chips):
+        block = hand_on(blocks[d], token)
+        outs, token = results((d,), *common, (block, swap(block, "row", 1)), weight, outs)
     return tuple(outs)
 
 

time: 138 us -> 124 us (0.90)
  waiting for transfers between devices: 36.4 us -> 27.6 us
  Pallas kernels: 61 us -> 57.6 us
  local copies, waits for them, and re-layouts: 1.88 us -> 0 us
    ppermute x32 -> x34, waiting for transfers between devices: 36.4 us -> 27.6 us  [swap(): lax.ppermute(x, axis, [(i, i ^ d) for i in range(lax.axis_size(axis))])]
    pallas_call x4 -> x2, Pallas kernels: 24.4 us -> 20.8 us  [results(): pl.pallas_call(functools.partial(result_kernel, pairs, factor), out_shape...]
    unnamed x2 -> x0, local copies, waits for them, and re-layouts: 1.88 us -> none
    ppermute x32 -> x34, starting transfers between devices: 36.9 us -> 38 us  [swap(): lax.ppermute(x, axis, [(i, i ^ d) for i in range(lax.axis_size(axis))])]
  transfers between devices with their start and end apart: 32 -> 34, of which waited for: 12 -> 15; matrix products, arithmetic and copies ran while one was open for 0% -> 0% of each run, Pallas kernels for 31% -> 31%
where the time goes in v4:
time: 124 us
  Pallas kernels  57.6 us (46%)
  starting transfers between devices  38 us (31%)
  waiting for transfers between devices  27.6 us (22%)
    ppermute x34, starting transfers between devices, swap(): lax.ppermute(x, axis, [(i, i ^ d) for i in range(lax.axis_size(axis))])  38 us
    ppermute x34, waiting for transfers between devices, swap(): lax.ppermute(x, axis, [(i, i ^ d) for i in range(lax.axis_size(axis))])  27.6 us
    pallas_call x2, Pallas kernels, results(): pl.pallas_call(functools.partial(result_kernel, pairs, factor), out_shape...  20.8 us
    pallas_call x2, Pallas kernels, project(): pl.pallas_call(functools.partial(project_kernel, part, depth), out_shape=...  18.5 us
    pallas_call x1, Pallas kernels, chol_inverse(): pl.pallas_call(chol_inverse_kernel, out_shape=shape((n, n), f32), in_spec...  9.14 us
    pallas_call x1, Pallas kernels, first_product(): pl.pallas_call(functools.partial(first_kernel, len(lefts), width), out_sh...  3.09 us
  transfers between devices with their start and end apart: 34, of which 15 were waited for; matrix products, arithmetic and copies ran while one was open for 0% of the time, Pallas kernels for 31%

profile of v4, /device:TPU:0, one launch (start us, length us, event | category | flops | bytes accessed | tf_op | source)
XLA Modules:
  0.0 124.3 jit_solution(17388637552448092347)
XLA Ops:
  0.6 9.7 %project.2 = (f32[512,6144]{1,0:T(8,128)S(1)}, bf16[256,6144]{1,0:T(8,128)(2,1)S(1)}, f32[256,128]{1,0:T(8,128)S(1)}, bf16[256,128]{1,0:T(8,128)(2,1)S(1)}, bf16...) custom-call(f32[1024,6144]{1,0:T(8,128)} %mom.3, bf16[1024,6144]{1,0:T(8,128)(2,1)} %grad.3, bf16[256,6144]{1,0:T(8,128)(2,1)} %basis.1), custom_call_target="tpu_custom_call" | custom-call | bytes 37748736 | tf_op jit(solution)/shard_map/project/pallas_call | solution.py:108
  10.3 4.1 %collective-permute-start.1 = (bf16[256,128]{1,0:T(8,128)(2,1)S(1)}, bf16[256,128]{1,0:T(8,128)(2,1)S(1)}, u32[]{:S(2)}, u32[]{:S(2)}) collective-permute-start(bf16[256,128]{1,0:T(8,128)(2,1)S(1)} %get-tuple-element.36), channel_id=1, source_target_pairs={{0,2},{1,3},{2,0},{3,1},{4,6},{5,7},{6,4},{7,5},{8,10},{9,11},{10,... | collective-permute-start | bytes 196616 | tf_op jit(solution)/shard_map/ppermute | solution.py:51
  14.4 1.3 %collective-permute-start.2 = (bf16[256,128]{1,0:T(8,128)(2,1)S(1)}, bf16[256,128]{1,0:T(8,128)(2,1)S(1)}, u32[]{:S(2)}, u32[]{:S(2)}) collective-permute-start(bf16[256,128]{1,0:T(8,128)(2,1)S(1)} %get-tuple-element.37), channel_id=1, source_target_pairs={{0,3},{1,2},{2,1},{3,0},{4,7},{5,6},{6,5},{7,4},{8,11},{9,10},{10,... | collective-permute-start | bytes 196616 | tf_op jit(solution)/shard_map/ppermute | solution.py:51
  16.0 8.8 %project.3 = (f32[512,6144]{1,0:T(8,128)S(1)}, f32[256,128]{1,0:T(8,128)S(1)}, bf16[256,128]{1,0:T(8,128)(2,1)S(1)}, bf16[256,128]{1,0:T(8,128)(2,1)S(1)}, bf16[256,128]{1,0:T(8,128)(2,1)S(1)}) custom-call(f32[1024,6144]{1,0:T(8,128)} %mom.3, bf16[1024,6144]{1,0:T(8,128)(2,1)} %grad.3, bf16[256,6144]{1,0:T(8,128)(2,1)S(1)} %get-tuple-element.32.basis, ...), custom_call_target="tpu_custom_call" | custom-call | bytes 37748736 | tf_op jit(solution)/shard_map/project/pallas_call | solution.py:108
  24.8 1.9 %collective-permute-start.6 = (bf16[256,128]{1,0:T(8,128)(2,1)S(1)}, bf16[256,128]{1,0:T(8,128)(2,1)S(1)}, u32[]{:S(2)}, u32[]{:S(2)}) collective-permute-start(bf16[256,128]{1,0:T(8,128)(2,1)S(1)} %get-tuple-element.39), channel_id=1, source_target_pairs={{0,1},{1,0},{2,3},{3,2},{4,5},{5,4},{6,7},{7,6},{8,9},{9,8},{10,11... | collective-permute-start | bytes 196616 | tf_op jit(solution)/shard_map/ppermute | solution.py:51
  26.7 1.7 %collective-permute-start.7 = (bf16[256,128]{1,0:T(8,128)(2,1)S(1)}, bf16[256,128]{1,0:T(8,128)(2,1)S(1)}, u32[]{:S(2)}, u32[]{:S(2)}) collective-permute-start(bf16[256,128]{1,0:T(8,128)(2,1)S(1)} %get-tuple-element.40), channel_id=1, source_target_pairs={{0,2},{1,3},{2,0},{3,1},{4,6},{5,7},{6,4},{7,5},{8,10},{9,11},{10,... | collective-permute-start | bytes 196616 | tf_op jit(solution)/shard_map/ppermute | solution.py:51
  28.4 0.9 collective-permute-start.8
  29.3 2.0 %collective-permute-start.4 = (bf16[256,128]{1,0:T(8,128)(2,1)S(1)}, bf16[256,128]{1,0:T(8,128)(2,1)S(1)}, u32[]{:S(2)}, u32[]{:S(2)}) collective-permute-start(bf16[256,128]{1,0:T(8,128)(2,1)S(1)} %share_sum.2.rest_0_.refs_0_), channel_id=1, source_target_pairs={{0,2},{1,3},{2,0},{3,1},{4,6},{5,7},{6,4},{7,5},{8,10},{9,11},{10,... | collective-permute-start | bytes 196616 | tf_op jit(solution)/shard_map/ppermute | solution.py:51
  31.3 4.6 %collective-permute-done.7.refs_1_ = bf16[256,128]{1,0:T(8,128)(2,1)S(1)} collective-permute-done((bf16[256,128]{1,0:T(8,128)(2,1)S(1)}, bf16[256,128]{1,0:T(8,128)(2,1)S(1)}, u32[]{:S(2)}, u32[]{:S(2)}) %collective-permute-start.7) | collective-permute-done | bytes 65568 | tf_op jit(solution)/shard_map/ppermute | solution.py:51
  36.0 2.6 %collective-permute-start.10 = (bf16[256,128]{1,0:T(8,128)(2,1)S(1)}, bf16[256,128]{1,0:T(8,128)(2,1)S(1)}, u32[]{:S(2)}, u32[]{:S(2)}) collective-permute-start(bf16[256,128]{1,0:T(8,128)(2,1)S(1)} %share_sum.3.refs_4_.rest_0_), channel_id=1, source_target_pairs={{0,2},{1,3},{2,0},{3,1},{4,6},{5,7},{6,4},{7,5},{8,10},{9,11},{10,... | collective-permute-start | bytes 196616 | tf_op jit(solution)/shard_map/ppermute | solution.py:51
  38.6 2.0 %collective-permute-start.5 = (bf16[256,128]{1,0:T(8,128)(2,1)S(1)}, bf16[256,128]{1,0:T(8,128)(2,1)S(1)}, u32[]{:S(2)}, u32[]{:S(2)}) collective-permute-start(bf16[256,128]{1,0:T(8,128)(2,1)S(1)} %collective-permute-done.4.rest_2_.refs_2_), channel_id=1, source_target_pairs={{0,1},{1,0},{2,3},{3,2},{4,5},{5,4},{6,7},{7,6},{8,9},{9,8},{10,11... | collective-permute-start | bytes 196616 | tf_op jit(solution)/shard_map/ppermute | solution.py:51
  40.6 0.7 collective-permute-done.10.refs_6_.rest_2_
  41.3 1.7 %collective-permute-start.11 = (bf16[256,128]{1,0:T(8,128)(2,1)S(1)}, bf16[256,128]{1,0:T(8,128)(2,1)S(1)}, u32[]{:S(2)}, u32[]{:S(2)}) collective-permute-start(bf16[256,128]{1,0:T(8,128)(2,1)S(1)} %collective-permute-done.10.refs_6_.rest_2_), channel_id=1, source_target_pairs={{0,1},{1,0},{2,3},{3,2},{4,5},{5,4},{6,7},{7,6},{8,9},{9,8},{10,11... | collective-permute-start | bytes 196616 | tf_op jit(solution)/shard_map/ppermute | solution.py:51
  43.3 0.7 collective-permute-done.5.rest_3_.refs_3_
  44.0 3.1 %first_product.1 = (f32[256,3072]{1,0:T(8,128)S(1)}, f32[256,3072]{1,0:T(8,128)S(1)}) custom-call(f32[512,6144]{1,0:T(8,128)S(1)} %get-tuple-element.31.buf.buf0, bf16[256,128]{1,0:T(8,128)(2,1)S(1)} %share_sum.2.rest_0_.refs_0_, bf16[256,128]{1,0:T(8,128)(2,1)S(1)} %collective-permute-done.3.rest_1_.refs_1_, ...), custom_call_target="tpu_custom_call" | custom-call | bytes 18874368 | tf_op jit(solution)/shard_map/first_product/pallas_call | solution.py:185
  47.7 1.6 %other_product.1.rest_5_.refs_0_ = bf16[256,3072]{1,0:T(8,128)(2,1)S(1)} custom-call(f32[512,6144]{1,0:T(8,128)S(1)} %get-tuple-element.34.buf.buf1, f32[256,3072]{1,0:T(8,128)S(1)} %get-tuple-element.42.refs_8_.sums, bf16[256,128]{1,0:T(8,128)(2,1)S(1)} %share_sum.3.refs_4_.rest_0_, bf16[256,128]{1,0:T(8,128)(2,1)S(1)} %collective-permute-done.9.refs_5_.rest_1_, ...), custom_call_target="tpu_custom_call" | custom-call | bytes 15728640 | tf_op jit(solution)/shard_map/other_product/pallas_call | solution.py:215
  49.3 1.8 %mine_product.1.mine = f32[256,3072]{1,0:T(8,128)S(1)} custom-call(f32[512,6144]{1,0:T(8,128)S(1)} %get-tuple-element.34.buf.buf1, f32[256,3072]{1,0:T(8,128)S(1)} %get-tuple-element.45.sums, bf16[256,128]{1,0:T(8,128)(2,1)S(1)} %share_sum.3.refs_4_.rest_0_, bf16[256,128]{1,0:T(8,128)(2,1)S(1)} %collective-permute-done.9.refs_5_.rest_1_, ...), custom_call_target="tpu_custom_call" | custom-call | bytes 15728640 | tf_op jit(solution)/shard_map/mine_product/pallas_call | solution.py:245
  51.2 0.6 collective-permute-start.16
  51.7 1.5 %collective-permute-start.13 = (f32[128,256]{1,0:T(8,128)S(1)}, f32[128,256]{1,0:T(8,128)S(1)}, u32[]{:S(2)}, u32[]{:S(2)}) collective-permute-start(f32[128,256]{1,0:T(8,128)S(1)} %add.30.rest_4_.refs_1_), channel_id=1, source_target_pairs={{0,8},{4,12},{8,0},{12,4},{16,24},{20,28},{24,16},{28,20},{1,9},{5... | collective-permute-start | bytes 393224 | tf_op jit(solution)/shard_map/ppermute | solution.py:51
  53.2 4.0 %collective-permute-done.13 = f32[128,256]{1,0:T(8,128)S(1)} collective-permute-done((f32[128,256]{1,0:T(8,128)S(1)}, f32[128,256]{1,0:T(8,128)S(1)}, u32[]{:S(2)}, u32[]{:S(2)}) %collective-permute-start.13) | collective-permute-done | bytes 131104 | tf_op jit(solution)/shard_map/ppermute | solution.py:51
  57.2 1.6 %collective-permute-start.14 = (f32[128,256]{1,0:T(8,128)S(1)}, f32[128,256]{1,0:T(8,128)S(1)}, u32[]{:S(2)}, u32[]{:S(2)}) collective-permute-start(f32[128,256]{1,0:T(8,128)S(1)} %add.31), channel_id=1, source_target_pairs={{0,16},{4,20},{8,24},{12,28},{16,0},{20,4},{24,8},{28,12},{1,17},{... | collective-permute-start | bytes 393224 | tf_op jit(solution)/shard_map/ppermute | solution.py:51
  58.8 3.4 %collective-permute-done.14 = f32[128,256]{1,0:T(8,128)S(1)} collective-permute-done((f32[128,256]{1,0:T(8,128)S(1)}, f32[128,256]{1,0:T(8,128)S(1)}, u32[]{:S(2)}, u32[]{:S(2)}) %collective-permute-start.14) | collective-permute-done | bytes 131104 | tf_op jit(solution)/shard_map/ppermute | solution.py:51
  62.6 1.6 %collective-permute-start.17 = (bf16[256,768]{1,0:T(8,128)(2,1)S(1)}, bf16[256,768]{1,0:T(8,128)(2,1)S(1)}, u32[]{:S(2)}, u32[]{:S(2)}) collective-permute-start(bf16[256,768]{1,0:T(8,128)(2,1)S(1)} %get-tuple-element.47), channel_id=1, source_target_pairs={{0,8},{4,12},{8,0},{12,4},{16,24},{20,28},{24,16},{28,20},{1,9},{5... | collective-permute-start | bytes 1179656 | tf_op jit(solution)/shard_map/ppermute | solution.py:51
  64.2 1.5 %collective-permute-start.18 = (bf16[256,768]{1,0:T(8,128)(2,1)S(1)}, bf16[256,768]{1,0:T(8,128)(2,1)S(1)}, u32[]{:S(2)}, u32[]{:S(2)}) collective-permute-start(bf16[256,768]{1,0:T(8,128)(2,1)S(1)} %get-tuple-element.48), channel_id=1, source_target_pairs={{0,16},{4,20},{8,24},{12,28},{16,0},{20,4},{24,8},{28,12},{1,17},{... | collective-permute-start | bytes 1179656 | tf_op jit(solution)/shard_map/ppermute | solution.py:51
  65.7 0.5 collective-permute-start.19
  66.2 1.3 %collective-permute-done.15.other = f32[128,256]{1,0:T(8,128)S(1)} collective-permute-done((f32[128,256]{1,0:T(8,128)S(1)}, f32[128,256]{1,0:T(8,128)S(1)}, u32[]{:S(2)}, u32[]{:S(2)}) %collective-permute-start.15) | collective-permute-done | bytes 131104 | tf_op jit(solution)/shard_map/ppermute | solution.py:51
  67.5 9.1 %chol_inverse.1.inverse = f32[256,256]{1,0:T(8,128)S(1)} custom-call(f32[128,256]{1,0:T(8,128)S(1)} %add.32.mine._, f32[128,256]{1,0:T(8,128)S(1)} %collective-permute-done.15.other), custom_call_target="tpu_custom_call" | custom-call | bytes 33554432 | tf_op jit(solution)/shard_map/chol_inverse/pallas_call | solution.py:339
  76.7 4.7 %collective-permute-done.18.refs_1_ = bf16[256,768]{1,0:T(8,128)(2,1)S(1)} collective-permute-done((bf16[256,768]{1,0:T(8,128)(2,1)S(1)}, bf16[256,768]{1,0:T(8,128)(2,1)S(1)}, u32[]{:S(2)}, u32[]{:S(2)}) %collective-permute-start.18) | collective-permute-done | bytes 393248 | tf_op jit(solution)/shard_map/ppermute | solution.py:51
  81.5 0.6 share.1
  82.0 1.5 %collective-permute-start.22 = (f32[8,256]{1,0:T(8,128)S(1)}, f32[8,256]{1,0:T(8,128)S(1)}, u32[]{:S(2)}, u32[]{:S(2)}) collective-permute-start(f32[8,256]{1,0:T(8,128)S(1)} %get-tuple-element.50), channel_id=1, source_target_pairs={{0,24},{4,28},{8,16},{12,20},{16,8},{20,12},{24,0},{28,4},{1,25},{... | collective-permute-start | bytes 24584 | tf_op jit(solution)/shard_map/ppermute | solution.py:51
  83.6 1.2 collective-permute-start.21
  84.7 0.8 collective-permute-start.20
  85.6 1.2 collective-permute-done.22
  86.7 0.5 collective-permute-done.21
  87.2 1.3 %collective-permute-done.20 = f32[8,256]{1,0:T(8,128)S(1)} collective-permute-done((f32[8,256]{1,0:T(8,128)S(1)}, f32[8,256]{1,0:T(8,128)S(1)}, u32[]{:S(2)}, u32[]{:S(2)}) %collective-permute-start.20) | collective-permute-done | bytes 8224 | tf_op jit(solution)/shard_map/ppermute | solution.py:51
  88.6 0.8 collective-permute-start.31
  89.3 1.6 %collective-permute-start.27 = (bf16[256,768]{1,0:T(8,128)(2,1)S(1)}, bf16[256,768]{1,0:T(8,128)(2,1)S(1)}, u32[]{:S(2)}, u32[]{:S(2)}) collective-permute-start(bf16[256,768]{1,0:T(8,128)(2,1)S(1)} %hand_on.7.refs_0_), channel_id=1, source_target_pairs={{0,8},{4,12},{8,0},{12,4},{16,24},{20,28},{24,16},{28,20},{1,9},{5... | collective-permute-start | bytes 1179656 | tf_op jit(solution)/shard_map/ppermute | solution.py:51
  90.9 1.2 collective-permute-done.23
  92.0 1.9 %collective-permute-start.26 = (f32[8,256]{1,0:T(8,128)S(1)}, f32[8,256]{1,0:T(8,128)S(1)}, u32[]{:S(2)}, u32[]{:S(2)}) collective-permute-start(f32[8,256]{1,0:T(8,128)S(1)} %add.36), channel_id=1, source_target_pairs={{0,3},{1,2},{2,1},{3,0},{4,7},{5,6},{6,5},{7,4},{8,11},{9,10},{10,... | collective-permute-start | bytes 24584 | tf_op jit(solution)/shard_map/ppermute | solution.py:51
  93.9 0.6 collective-permute-start.25
  94.5 1.9 %collective-permute-start.24 = (f32[8,256]{1,0:T(8,128)S(1)}, f32[8,256]{1,0:T(8,128)S(1)}, u32[]{:S(2)}, u32[]{:S(2)}) collective-permute-start(f32[8,256]{1,0:T(8,128)S(1)} %add.36), channel_id=1, source_target_pairs={{0,1},{1,0},{2,3},{3,2},{4,5},{5,4},{6,7},{7,6},{8,9},{9,8},{10,11... | collective-permute-start | bytes 24584 | tf_op jit(solution)/shard_map/ppermute | solution.py:51
  96.4 1.1 collective-permute-done.26
  97.5 1.0 collective-permute-done.25
  99.2 1.2 collective-permute-start.28
  100.4 1.2 ortho.1.ortho_ref
  101.6 14.1 %results.2 = (bf16[1024,6144]{1,0:T(8,128)(2,1)}, f32[1024,6144]{1,0:T(8,128)}, bf16[256,6144]{1,0:T(8,128)(2,1)}, f32[8,128]{1,0:T(8,128)S(1)}) custom-call(f32[512,6144]{1,0:T(8,128)S(1)} %get-tuple-element.31.buf.buf0, f32[512,6144]{1,0:T(8,128)S(1)} %get-tuple-element.34.buf.buf1, bf16[1024,256]{1,0:T(8,128)(2,1)S(1)} %ortho.1.ortho_ref, ...), custom_call_target="tpu_custom_call" | custom-call | bytes 37748736 | tf_op jit(solution)/shard_map/results/pallas_call | solution.py:489
  115.9 1.6 %collective-permute-done.33.refs_1_ = bf16[256,768]{1,0:T(8,128)(2,1)S(1)} collective-permute-done((bf16[256,768]{1,0:T(8,128)(2,1)S(1)}, bf16[256,768]{1,0:T(8,128)(2,1)S(1)}, u32[]{:S(2)}, u32[]{:S(2)}) %collective-permute-start.33) | collective-permute-done | bytes 393248 | tf_op jit(solution)/shard_map/ppermute | solution.py:51
  117.5 6.7 %results.3 = (bf16[1024,6144]{1,0:T(8,128)(2,1)}, f32[1024,6144]{1,0:T(8,128)}, bf16[256,6144]{1,0:T(8,128)(2,1)}, f32[8,128]{1,0:T(8,128)}) custom-call(f32[512,6144]{1,0:T(8,128)S(1)} %get-tuple-element.31.buf.buf0, f32[512,6144]{1,0:T(8,128)S(1)} %get-tuple-element.34.buf.buf1, ...), custom_call_target="tpu_custom_call", output_to_operand_aliasing={{0}: (8, {}), {1}: (9, {}), {2}: (10, {})} | custom-call | bytes 12582912 | tf_op jit(solution)/shard_map/results/pallas_call | solution.py:489
  (46 shorter events, 2.6 us)
Async XLA Ops:
  10.3 18.1 %collective-permute-start.1 = (bf16[256,128]{1,0:T(8,128)(2,1)S(1)}, bf16[256,128]{1,0:T(8,128)(2,1)S(1)}, u32[]{:S(2)}, u32[]{:S(2)}) collective-permute-start(bf16[256,128]{1,0:T(8,128)(2,1)S(1)} %get-tuple-element.36), channel_id=1, source_target_pairs={{0,2},{1,3},{2,0},{3,1},{4,6},{5,7},{6,4},{7,5},{8,10},{9,11},{10,... | collective-permute-start | bytes 196616 | tf_op jit(solution)/shard_map/ppermute | solution.py:51
  14.4 14.9 %collective-permute-start.2 = (bf16[256,128]{1,0:T(8,128)(2,1)S(1)}, bf16[256,128]{1,0:T(8,128)(2,1)S(1)}, u32[]{:S(2)}, u32[]{:S(2)}) collective-permute-start(bf16[256,128]{1,0:T(8,128)(2,1)S(1)} %get-tuple-element.37), channel_id=1, source_target_pairs={{0,3},{1,2},{2,1},{3,0},{4,7},{5,6},{6,5},{7,4},{8,11},{9,10},{10,... | collective-permute-start | bytes 196616 | tf_op jit(solution)/shard_map/ppermute | solution.py:51
  15.8 13.5 %collective-permute-start = (bf16[256,128]{1,0:T(8,128)(2,1)S(1)}, bf16[256,128]{1,0:T(8,128)(2,1)S(1)}, u32[]{:S(2)}, u32[]{:S(2)}) collective-permute-start(bf16[256,128]{1,0:T(8,128)(2,1)S(1)} %get-tuple-element.33.rest_0_), channel_id=1, source_target_pairs={{0,1},{1,0},{2,3},{3,2},{4,5},{5,4},{6,7},{7,6},{8,9},{9,8},{10,11... | collective-permute-start | bytes 196616 | tf_op jit(solution)/shard_map/ppermute | solution.py:51
  24.8 6.5 %collective-permute-start.6 = (bf16[256,128]{1,0:T(8,128)(2,1)S(1)}, bf16[256,128]{1,0:T(8,128)(2,1)S(1)}, u32[]{:S(2)}, u32[]{:S(2)}) collective-permute-start(bf16[256,128]{1,0:T(8,128)(2,1)S(1)} %get-tuple-element.39), channel_id=1, source_target_pairs={{0,1},{1,0},{2,3},{3,2},{4,5},{5,4},{6,7},{7,6},{8,9},{9,8},{10,11... | collective-permute-start | bytes 196616 | tf_op jit(solution)/shard_map/ppermute | solution.py:51
  26.7 9.2 %collective-permute-start.7 = (bf16[256,128]{1,0:T(8,128)(2,1)S(1)}, bf16[256,128]{1,0:T(8,128)(2,1)S(1)}, u32[]{:S(2)}, u32[]{:S(2)}) collective-permute-start(bf16[256,128]{1,0:T(8,128)(2,1)S(1)} %get-tuple-element.40), channel_id=1, source_target_pairs={{0,2},{1,3},{2,0},{3,1},{4,6},{5,7},{6,4},{7,5},{8,10},{9,11},{10,... | collective-permute-start | bytes 196616 | tf_op jit(solution)/shard_map/ppermute | solution.py:51
  28.4 7.5 %collective-permute-start.8 = (bf16[256,128]{1,0:T(8,128)(2,1)S(1)}, bf16[256,128]{1,0:T(8,128)(2,1)S(1)}, u32[]{:S(2)}, u32[]{:S(2)}) collective-permute-start(bf16[256,128]{1,0:T(8,128)(2,1)S(1)} %get-tuple-element.41), channel_id=1, source_target_pairs={{0,3},{1,2},{2,1},{3,0},{4,7},{5,6},{6,5},{7,4},{8,11},{9,10},{10,... | collective-permute-start | bytes 196616 | tf_op jit(solution)/shard_map/ppermute | solution.py:51
  29.3 9.3 %collective-permute-start.4 = (bf16[256,128]{1,0:T(8,128)(2,1)S(1)}, bf16[256,128]{1,0:T(8,128)(2,1)S(1)}, u32[]{:S(2)}, u32[]{:S(2)}) collective-permute-start(bf16[256,128]{1,0:T(8,128)(2,1)S(1)} %share_sum.2.rest_0_.refs_0_), channel_id=1, source_target_pairs={{0,2},{1,3},{2,0},{3,1},{4,6},{5,7},{6,4},{7,5},{8,10},{9,11},{10,... | collective-permute-start | bytes 196616 | tf_op jit(solution)/shard_map/ppermute | solution.py:51
  36.0 5.3 %collective-permute-start.10 = (bf16[256,128]{1,0:T(8,128)(2,1)S(1)}, bf16[256,128]{1,0:T(8,128)(2,1)S(1)}, u32[]{:S(2)}, u32[]{:S(2)}) collective-permute-start(bf16[256,128]{1,0:T(8,128)(2,1)S(1)} %share_sum.3.refs_4_.rest_0_), channel_id=1, source_target_pairs={{0,2},{1,3},{2,0},{3,1},{4,6},{5,7},{6,4},{7,5},{8,10},{9,11},{10,... | collective-permute-start | bytes 196616 | tf_op jit(solution)/shard_map/ppermute | solution.py:51
  38.5 4.8 %collective-permute-start.3 = (bf16[256,128]{1,0:T(8,128)(2,1)S(1)}, bf16[256,128]{1,0:T(8,128)(2,1)S(1)}, u32[]{:S(2)}, u32[]{:S(2)}) collective-permute-start(bf16[256,128]{1,0:T(8,128)(2,1)S(1)} %share_sum.2.rest_0_.refs_0_), channel_id=1, source_target_pairs={{0,1},{1,0},{2,3},{3,2},{4,5},{5,4},{6,7},{7,6},{8,9},{9,8},{10,11... | collective-permute-start | bytes 196616 | tf_op jit(solution)/shard_map/ppermute | solution.py:51
  38.6 5.4 %collective-permute-start.5 = (bf16[256,128]{1,0:T(8,128)(2,1)S(1)}, bf16[256,128]{1,0:T(8,128)(2,1)S(1)}, u32[]{:S(2)}, u32[]{:S(2)}) collective-permute-start(bf16[256,128]{1,0:T(8,128)(2,1)S(1)} %collective-permute-done.4.rest_2_.refs_2_), channel_id=1, source_target_pairs={{0,1},{1,0},{2,3},{3,2},{4,5},{5,4},{6,7},{7,6},{8,9},{9,8},{10,11... | collective-permute-start | bytes 196616 | tf_op jit(solution)/shard_map/ppermute | solution.py:51
  40.6 6.5 %collective-permute-start.9 = (bf16[256,128]{1,0:T(8,128)(2,1)S(1)}, bf16[256,128]{1,0:T(8,128)(2,1)S(1)}, u32[]{:S(2)}, u32[]{:S(2)}) collective-permute-start(bf16[256,128]{1,0:T(8,128)(2,1)S(1)} %share_sum.3.refs_4_.rest_0_), channel_id=1, source_target_pairs={{0,1},{1,0},{2,3},{3,2},{4,5},{5,4},{6,7},{7,6},{8,9},{9,8},{10,11... | collective-permute-start | bytes 196616 | tf_op jit(solution)/shard_map/ppermute | solution.py:51
  41.3 5.8 %collective-permute-start.11 = (bf16[256,128]{1,0:T(8,128)(2,1)S(1)}, bf16[256,128]{1,0:T(8,128)(2,1)S(1)}, u32[]{:S(2)}, u32[]{:S(2)}) collective-permute-start(bf16[256,128]{1,0:T(8,128)(2,1)S(1)} %collective-permute-done.10.refs_6_.rest_2_), channel_id=1, source_target_pairs={{0,1},{1,0},{2,3},{3,2},{4,5},{5,4},{6,7},{7,6},{8,9},{9,8},{10,11... | collective-permute-start | bytes 196616 | tf_op jit(solution)/shard_map/ppermute | solution.py:51
  47.6 1.7 %collective-permute-start.12 = (f32[128,256]{1,0:T(8,128)S(1)}, f32[128,256]{1,0:T(8,128)S(1)}, u32[]{:S(2)}, u32[]{:S(2)}) collective-permute-start(f32[128,256]{1,0:T(8,128)S(1)} %get-tuple-element.44), channel_id=1, source_target_pairs={{0,4},{4,0},{8,12},{12,8},{16,20},{20,16},{24,28},{28,24},{1,5},{5... | collective-permute-start | bytes 393224 | tf_op jit(solution)/shard_map/ppermute | solution.py:51
  51.2 11.1 %collective-permute-start.16 = (bf16[256,3072]{1,0:T(8,128)(2,1)S(1)}, bf16[256,3072]{1,0:T(8,128)(2,1)S(1)}, u32[]{:S(2)}, u32[]{:S(2)}) collective-permute-start(bf16[256,3072]{1,0:T(8,128)(2,1)S(1)} %hand_on.6), channel_id=1, source_target_pairs={{0,4},{4,0},{8,12},{12,8},{16,20},{20,16},{24,28},{28,24},{1,5},{5... | collective-permute-start | bytes 4718600 | tf_op jit(solution)/shard_map/ppermute | solution.py:51
  51.7 5.5 %collective-permute-start.13 = (f32[128,256]{1,0:T(8,128)S(1)}, f32[128,256]{1,0:T(8,128)S(1)}, u32[]{:S(2)}, u32[]{:S(2)}) collective-permute-start(f32[128,256]{1,0:T(8,128)S(1)} %add.30.rest_4_.refs_1_), channel_id=1, source_target_pairs={{0,8},{4,12},{8,0},{12,4},{16,24},{20,28},{24,16},{28,20},{1,9},{5... | collective-permute-start | bytes 393224 | tf_op jit(solution)/shard_map/ppermute | solution.py:51
  57.2 5.0 %collective-permute-start.14 = (f32[128,256]{1,0:T(8,128)S(1)}, f32[128,256]{1,0:T(8,128)S(1)}, u32[]{:S(2)}, u32[]{:S(2)}) collective-permute-start(f32[128,256]{1,0:T(8,128)S(1)} %add.31), channel_id=1, source_target_pairs={{0,16},{4,20},{8,24},{12,28},{16,0},{20,4},{24,8},{28,12},{1,17},{... | collective-permute-start | bytes 393224 | tf_op jit(solution)/shard_map/ppermute | solution.py:51
  62.6 14.1 %collective-permute-start.17 = (bf16[256,768]{1,0:T(8,128)(2,1)S(1)}, bf16[256,768]{1,0:T(8,128)(2,1)S(1)}, u32[]{:S(2)}, u32[]{:S(2)}) collective-permute-start(bf16[256,768]{1,0:T(8,128)(2,1)S(1)} %get-tuple-element.47), channel_id=1, source_target_pairs={{0,8},{4,12},{8,0},{12,4},{16,24},{20,28},{24,16},{28,20},{1,9},{5... | collective-permute-start | bytes 1179656 | tf_op jit(solution)/shard_map/ppermute | solution.py:51
  64.2 17.3 %collective-permute-start.18 = (bf16[256,768]{1,0:T(8,128)(2,1)S(1)}, bf16[256,768]{1,0:T(8,128)(2,1)S(1)}, u32[]{:S(2)}, u32[]{:S(2)}) collective-permute-start(bf16[256,768]{1,0:T(8,128)(2,1)S(1)} %get-tuple-element.48), channel_id=1, source_target_pairs={{0,16},{4,20},{8,24},{12,28},{16,0},{20,4},{24,8},{28,12},{1,17},{... | collective-permute-start | bytes 1179656 | tf_op jit(solution)/shard_map/ppermute | solution.py:51
  65.7 15.8 %collective-permute-start.19 = (bf16[256,768]{1,0:T(8,128)(2,1)S(1)}, bf16[256,768]{1,0:T(8,128)(2,1)S(1)}, u32[]{:S(2)}, u32[]{:S(2)}) collective-permute-start(bf16[256,768]{1,0:T(8,128)(2,1)S(1)} %get-tuple-element.49), channel_id=1, source_target_pairs={{0,24},{4,28},{8,16},{12,20},{16,8},{20,12},{24,0},{28,4},{1,25},{... | collective-permute-start | bytes 1179656 | tf_op jit(solution)/shard_map/ppermute | solution.py:51
  66.2 1.3 %collective-permute-start.15 = (f32[128,256]{1,0:T(8,128)S(1)}, f32[128,256]{1,0:T(8,128)S(1)}, u32[]{:S(2)}, u32[]{:S(2)}) collective-permute-start(f32[128,256]{1,0:T(8,128)S(1)} %add.32.mine._), channel_id=1, source_target_pairs={{0,4},{4,0},{8,12},{12,8},{16,20},{20,16},{24,28},{28,24},{1,5},{5... | collective-permute-start | bytes 393224 | tf_op jit(solution)/shard_map/ppermute | solution.py:51
  82.0 4.7 %collective-permute-start.22 = (f32[8,256]{1,0:T(8,128)S(1)}, f32[8,256]{1,0:T(8,128)S(1)}, u32[]{:S(2)}, u32[]{:S(2)}) collective-permute-start(f32[8,256]{1,0:T(8,128)S(1)} %get-tuple-element.50), channel_id=1, source_target_pairs={{0,24},{4,28},{8,16},{12,20},{16,8},{20,12},{24,0},{28,4},{1,25},{... | collective-permute-start | bytes 24584 | tf_op jit(solution)/shard_map/ppermute | solution.py:51
  83.6 3.7 %collective-permute-start.21 = (f32[8,256]{1,0:T(8,128)S(1)}, f32[8,256]{1,0:T(8,128)S(1)}, u32[]{:S(2)}, u32[]{:S(2)}) collective-permute-start(f32[8,256]{1,0:T(8,128)S(1)} %get-tuple-element.50), channel_id=1, source_target_pairs={{0,16},{4,20},{8,24},{12,28},{16,0},{20,4},{24,8},{28,12},{1,17},{... | collective-permute-start | bytes 24584 | tf_op jit(solution)/shard_map/ppermute | solution.py:51
  84.7 3.8 %collective-permute-start.20 = (f32[8,256]{1,0:T(8,128)S(1)}, f32[8,256]{1,0:T(8,128)S(1)}, u32[]{:S(2)}, u32[]{:S(2)}) collective-permute-start(f32[8,256]{1,0:T(8,128)S(1)} %get-tuple-element.50), channel_id=1, source_target_pairs={{0,8},{4,12},{8,0},{12,4},{16,24},{20,28},{24,16},{28,20},{1,9},{5... | collective-permute-start | bytes 24584 | tf_op jit(solution)/shard_map/ppermute | solution.py:51
  88.6 9.9 %collective-permute-start.31 = (bf16[256,768]{1,0:T(8,128)(2,1)S(1)}, bf16[256,768]{1,0:T(8,128)(2,1)S(1)}, u32[]{:S(2)}, u32[]{:S(2)}) collective-permute-start(bf16[256,768]{1,0:T(8,128)(2,1)S(1)} %hand_on.7.refs_0_), channel_id=1, source_target_pairs={{0,16},{4,20},{8,24},{12,28},{16,0},{20,4},{24,8},{28,12},{1,17},{... | collective-permute-start | bytes 1179656 | tf_op jit(solution)/shard_map/ppermute | solution.py:51
  89.3 9.3 %collective-permute-start.27 = (bf16[256,768]{1,0:T(8,128)(2,1)S(1)}, bf16[256,768]{1,0:T(8,128)(2,1)S(1)}, u32[]{:S(2)}, u32[]{:S(2)}) collective-permute-start(bf16[256,768]{1,0:T(8,128)(2,1)S(1)} %hand_on.7.refs_0_), channel_id=1, source_target_pairs={{0,8},{4,12},{8,0},{12,4},{16,24},{20,28},{24,16},{28,20},{1,9},{5... | collective-permute-start | bytes 1179656 | tf_op jit(solution)/shard_map/ppermute | solution.py:51
  90.9 1.2 collective-permute-start.23
  92.0 5.4 %collective-permute-start.26 = (f32[8,256]{1,0:T(8,128)S(1)}, f32[8,256]{1,0:T(8,128)S(1)}, u32[]{:S(2)}, u32[]{:S(2)}) collective-permute-start(f32[8,256]{1,0:T(8,128)S(1)} %add.36), channel_id=1, source_target_pairs={{0,3},{1,2},{2,1},{3,0},{4,7},{5,6},{6,5},{7,4},{8,11},{9,10},{10,... | collective-permute-start | bytes 24584 | tf_op jit(solution)/shard_map/ppermute | solution.py:51
  93.9 4.5 %collective-permute-start.25 = (f32[8,256]{1,0:T(8,128)S(1)}, f32[8,256]{1,0:T(8,128)S(1)}, u32[]{:S(2)}, u32[]{:S(2)}) collective-permute-start(f32[8,256]{1,0:T(8,128)S(1)} %add.36), channel_id=1, source_target_pairs={{0,2},{1,3},{2,0},{3,1},{4,6},{5,7},{6,4},{7,5},{8,10},{9,11},{10,... | collective-permute-start | bytes 24584 | tf_op jit(solution)/shard_map/ppermute | solution.py:51
  94.5 4.0 %collective-permute-start.24 = (f32[8,256]{1,0:T(8,128)S(1)}, f32[8,256]{1,0:T(8,128)S(1)}, u32[]{:S(2)}, u32[]{:S(2)}) collective-permute-start(f32[8,256]{1,0:T(8,128)S(1)} %add.36), channel_id=1, source_target_pairs={{0,1},{1,0},{2,3},{3,2},{4,5},{5,4},{6,7},{7,6},{8,9},{9,8},{10,11... | collective-permute-start | bytes 24584 | tf_op jit(solution)/shard_map/ppermute | solution.py:51
  98.5 3.0 %collective-permute-start.32 = (bf16[256,768]{1,0:T(8,128)(2,1)S(1)}, bf16[256,768]{1,0:T(8,128)(2,1)S(1)}, u32[]{:S(2)}, u32[]{:S(2)}) collective-permute-start(bf16[256,768]{1,0:T(8,128)(2,1)S(1)} %hand_on.10.refs_4_), channel_id=1, source_target_pairs={{0,4},{4,0},{8,12},{12,8},{16,20},{20,16},{24,28},{28,24},{1,5},{5... | collective-permute-start | bytes 1179656 | tf_op jit(solution)/shard_map/ppermute | solution.py:51
  98.6 2.9 %collective-permute-start.29 = (bf16[256,768]{1,0:T(8,128)(2,1)S(1)}, bf16[256,768]{1,0:T(8,128)(2,1)S(1)}, u32[]{:S(2)}, u32[]{:S(2)}) collective-permute-start(bf16[256,768]{1,0:T(8,128)(2,1)S(1)} %hand_on.9.refs_0_), channel_id=1, source_target_pairs={{0,4},{4,0},{8,12},{12,8},{16,20},{20,16},{24,28},{28,24},{1,5},{5... | collective-permute-start | bytes 1179656 | tf_op jit(solution)/shard_map/ppermute | solution.py:51
  99.1 2.5 %collective-permute-start.30 = (bf16[256,768]{1,0:T(8,128)(2,1)S(1)}, bf16[256,768]{1,0:T(8,128)(2,1)S(1)}, u32[]{:S(2)}, u32[]{:S(2)}) collective-permute-start(bf16[256,768]{1,0:T(8,128)(2,1)S(1)} %hand_on.8.refs_1_.refs_2_), channel_id=1, source_target_pairs={{0,4},{4,0},{8,12},{12,8},{16,20},{20,16},{24,28},{28,24},{1,5},{5... | collective-permute-start | bytes 1179656 | tf_op jit(solution)/shard_map/ppermute | solution.py:51
  99.2 16.5 %collective-permute-start.28 = (bf16[256,768]{1,0:T(8,128)(2,1)S(1)}, bf16[256,768]{1,0:T(8,128)(2,1)S(1)}, u32[]{:S(2)}, u32[]{:S(2)}) collective-permute-start(bf16[256,768]{1,0:T(8,128)(2,1)S(1)} %hand_on.9.refs_0_), channel_id=1, source_target_pairs={{0,24},{4,28},{8,16},{12,20},{16,8},{20,12},{24,0},{28,4},{1,25},{... | collective-permute-start | bytes 1179656 | tf_op jit(solution)/shard_map/ppermute | solution.py:51
  115.7 1.8 %collective-permute-start.33 = (bf16[256,768]{1,0:T(8,128)(2,1)S(1)}, bf16[256,768]{1,0:T(8,128)(2,1)S(1)}, u32[]{:S(2)}, u32[]{:S(2)}) collective-permute-start(bf16[256,768]{1,0:T(8,128)(2,1)S(1)} %hand_on.11.refs_0_), channel_id=1, source_target_pairs={{0,4},{4,0},{8,12},{12,8},{16,20},{20,16},{24,28},{28,24},{1,5},{5... | collective-permute-start | bytes 1179656 | tf_op jit(solution)/shard_map/ppermute | solution.py:51

commit v5 on v4

v5 whole, which is shorter than its diff:
```python
import functools
import math

import jax
import jax.numpy as jnp
from jax import lax
from jax.experimental import pallas as pl
from jax.experimental.pallas import tpu as pltpu
from jax.sharding import PartitionSpec as P

D = 8192
FF = 24576
RANK = 256

epsilon = 1e-06
momentum_decay = 0.6
step_rate = 0.5

bf16, f32 = jnp.bfloat16, jnp.float32
VMEM = pl.BlockSpec(memory_space=pltpu.VMEM)
ANY = pl.BlockSpec(memory_space=pl.ANY)
MIB = 1 << 20


def shape(dims, kind):
    return jax.ShapeDtypeStruct(dims, kind)


def params(mib):
    return pltpu.CompilerParams(vmem_limit_bytes=mib * MIB)


def dot(a, b, dims=((1,), (0,))):
    return lax.dot_general(a, b, (dims, ((), ())), preferred_element_type=f32)


def split(x, terms):
    parts = []
    for _ in range(terms):
        part = x.astype(bf16)
        parts.append(part)
        x = x - part.astype(f32)
    return parts


def flip(i, d):
    return lax.bitwise_xor(i, jnp.int32(d))


def swap(x, axis, d):
    return lax.ppermute(x, axis, [(i, i ^ d) for i in range(lax.axis_size(axis))])


def project_kernel(part, depth, width, mom, grad, basis, *rest):
    if part == 0:
        (buf, kept), rest = rest[:2], rest[2:]
    else:
        kept, buf, rest = basis, rest[1], rest[2:]
    held, sent, gbuf, total, sems, basis_sem = rest
    m, n = buf.shape
    half = m // depth

    def copies(c):
        cols = pl.ds(pl.multiple_of(c * width, 128), width)
        pairs = []
        for k in range(depth):
            there = pl.ds((2 * k + part) * half, half)
            here = pl.ds(k * half, half)
            pairs.append(pltpu.make_async_copy(mom.at[there, cols], buf.at[here, cols], sems.at[0, k, c]))
            pairs.append(pltpu.make_async_copy(grad.at[there, cols], gbuf.at[here, cols], sems.at[1, k, c]))
        if part == 0:
            pairs.append(pltpu.make_async_copy(basis.at[:, cols], kept.at[:, cols], basis_sem.at[c]))
        return pairs

    def start(c, carry):
        for copy in copies(c):
            copy.start()
        return carry

    def step(c, carry):
        for copy in copies(c):
            copy.wait()
        cols = pl.ds(pl.multiple_of(c * width, 128), width)
        added = buf[:, cols] + gbuf[:, cols].astype(f32)
        buf[:, cols] = added
        total[...] += dot(added.astype(bf16), kept[:, cols], ((1,), (1,)))
        return carry

    total[...] = jnp.zeros_like(total)
    lax.fori_loop(0, n // width, start, 0)
    lax.fori_loop(0, n // width, step, 0)
    me = lax.axis_index("col")
    for out, odd in ((held, 0), (sent, 1)):
        for j in range(depth // 2):
            rows = pl.ds(pl.multiple_of(flip(me, 2 * j + odd) * half, half), half)
            out[:, j * half : (j + 1) * half] = jnp.transpose(total[rows, :]).astype(out.dtype)


def project(momentum, gradient, basis, depth, width, part, after=()):
    m, n = momentum.shape
    m = m // 2
    r = basis.shape[0]
    kept = [] if part else [pltpu.VMEM((r, n), bf16)]
    return pl.pallas_call(
        functools.partial(project_kernel, part, depth, width),
        out_shape=(pltpu.VMEM((m, n), f32), *kept, shape((r, m // 2), f32), shape((r, m // 2), bf16)),
        in_specs=[ANY, ANY] + [VMEM if part else ANY] + [ANY] * len(after),
        out_specs=(VMEM,) * (3 + len(kept)),
        scratch_shapes=[
            pltpu.VMEM((m, n), bf16),
            pltpu.VMEM((m, r), f32),
            pltpu.SemaphoreType.DMA((2, depth, n // width)),
            pltpu.SemaphoreType.DMA((n // width,)),
        ],
        compiler_params=params(14),
        cost_estimate=cost(momentum, gradient),
        name="project",
    )(stay(momentum), stay(gradient), keep(basis) if part else stay(basis), *after)


def fold_kernel(half, held, received, held_out, sent_out):
    added = held[...] + received[...].astype(f32)
    for j in range(held_out.shape[1] // half):
        at = slice(j * half, (j + 1) * half)
        held_out[:, at] = added[:, 2 * j * half : (2 * j + 1) * half]
        sent_out[:, at] = added[:, (2 * j + 1) * half : (2 * j + 2) * half].astype(bf16)


def fold(held, received, half):
    r, size = held.shape
    return pl.pallas_call(
        functools.partial(fold_kernel, half),
        out_shape=(shape((r, size // 2), f32), shape((r, size // 2), bf16)),
        in_specs=[VMEM, VMEM],
        out_specs=(VMEM, VMEM),
        compiler_params=params(8),
        name="fold",
    )(held, received)


def fold_last_kernel(held, received, *rest):
    before, out = rest[:-1], rest[-1]
    half = held.shape[1]
    for k, ref in enumerate(before):
        out[:, k * half : (k + 1) * half] = ref[...]
    out[:, len(before) * half :] = (held[...] + received[...].astype(f32)).astype(bf16)


def fold_last(held, received, *before):
    r, half = held.shape
    return pl.pallas_call(
        fold_last_kernel,
        out_shape=shape((r, half * (1 + len(before))), bf16),
        in_specs=[VMEM] * (2 + len(before)),
        out_specs=VMEM,
        compiler_params=params(8),
        name="fold_last",
    )(held, received, *before)


def cost(*arrays):
    size = sum(math.prod(x.shape) * x.dtype.itemsize for x in arrays)
    return pl.CostEstimate(flops=0, bytes_accessed=size, transcendentals=0)


def keep(x):
    return pltpu.with_memory_space_constraint(x, pltpu.VMEM)


def stay(x):
    return pltpu.with_memory_space_constraint(x, pltpu.HBM)


def buffer_rows(bufs, ds, depth, cols):
    half = bufs[0].shape[0] // depth
    me = lax.axis_index("col")
    rows = [pl.ds(pl.multiple_of(flip(me, d) * half, half), half) for d in ds]
    return jnp.concatenate([buf[at, cols].astype(bf16) for at in rows for buf in bufs], axis=0)


def first_kernel(depth, width, buf0, buf1, *rest):
    lefts, (other, mine, gram, whole) = rest[:-4], rest[-4:]
    core = lax.bitwise_and(lax.axis_index("row"), jnp.int32(1))
    size = other.shape[1]
    block = lefts[0].shape[1]
    for d, ref in enumerate(lefts):
        whole[:, d * block : (d + 1) * block] = ref[...]
    gram[...] = dot(whole[...], whole[...], ((1,), (1,)))
    for out, half in ((other, 1 - core), (mine, core)):

        def step(k, carry, out=out, half=half):
            cols = pl.ds(pl.multiple_of(half * size + k * width, 128), width)
            b = buffer_rows((buf0, buf1), range(len(lefts)), depth, cols)
            out[:, pl.ds(pl.multiple_of(k * width, 128), width)] = dot(whole[...], b)
            return carry

        lax.fori_loop(0, size // width, step, 0)


def first_product(bufs, lefts, depth, width):
    m, n = bufs[0].shape
    r, block = lefts[0].shape
    return pl.pallas_call(
        functools.partial(first_kernel, depth, width),
        out_shape=(shape((r, n // 2), f32), shape((r, n // 2), f32), shape((r, r), f32)),
        in_specs=[VMEM] * (2 + len(lefts)),
        out_specs=[VMEM] * 3,
        scratch_shapes=[pltpu.VMEM((r, block * len(lefts)), bf16)],
        compiler_params=params(10),
        cost_estimate=cost(*bufs, shape((r, n), f32)),
        name="first_product",
    )(*map(keep, bufs), *lefts)


def gram_kernel(left, sums, g_mine, g_other, total):
    core = lax.bitwise_and(lax.axis_index("row"), jnp.int32(1))
    total[...] = sums[...] + dot(left[...], left[...], ((1,), (1,)))
    h = g_mine.shape[0]
    g_mine[...] = total[pl.ds(pl.multiple_of(core * h, h), h), :]
    g_other[...] = total[pl.ds(pl.multiple_of((1 - core) * h, h), h), :]


def gram(left, sums):
    r = left.shape[0]
    return pl.pallas_call(
        gram_kernel,
        out_shape=[shape((r // 2, r), f32)] * 2,
        in_specs=[VMEM, VMEM],
        out_specs=[VMEM] * 2,
        scratch_shapes=[pltpu.VMEM((r, r), f32)],
        compiler_params=params(8),
        name="gram",
    )(left, sums)


def last_kernel(depth, width, mine, buf0, buf1, sums, left, *rest):
    out = rest[-1]
    core = lax.bitwise_and(lax.axis_index("row"), jnp.int32(1))
    half = core if mine else 1 - core
    size = out.shape[1]

    def step(k, carry):
        cols = pl.ds(pl.multiple_of(half * size + k * width, 128), width)
        at = pl.ds(pl.multiple_of(k * width, 128), width)
        b = buffer_rows((buf0, buf1), [depth - 1], depth, cols)
        out[:, at] = (sums[:, at] + dot(left[...], b)).astype(out.dtype)
        return carry

    lax.fori_loop(0, size // width, step, 0)


def last_product(bufs, sums, left, depth, width, mine, *after):
    return pl.pallas_call(
        functools.partial(last_kernel, depth, width, mine),
        out_shape=shape(sums.shape, f32 if mine else bf16),
        in_specs=[VMEM] * 4 + [ANY] * len(after),
        out_specs=VMEM,
        compiler_params=params(8),
        cost_estimate=cost(*bufs[:1], sums),
        name="mine_product" if mine else "other_product",
    )(*map(keep, bufs), sums, left, *after)


def pair_sum_kernel(chips, mine, received, _, *outs):
    me = lax.div(lax.axis_index("row"), jnp.int32(2))
    width = outs[0].shape[1]
    for d in range(chips):
        cols = pl.ds(pl.multiple_of(flip(me, d) * width, 128), width)
        outs[d][...] = (mine[:, cols] + received[:, cols].astype(f32)).astype(outs[d].dtype)


def pair_sum(mine, received, chips, after):
    r, n = mine.shape
    kinds = [f32] + [bf16] * (chips - 1)
    return pl.pallas_call(
        functools.partial(pair_sum_kernel, chips),
        out_shape=[shape((r, n // chips), k) for k in kinds],
        in_specs=[VMEM, VMEM, ANY],
        out_specs=[VMEM] * chips,
        compiler_params=params(8),
        name="pair_sum",
    )(mine, received, after)


def eliminate(tiles, at, nb, group):
    sub = lax.broadcasted_iota(jnp.int32, (nb, 128), 0)
    scale = jnp.zeros((nb, 128), f32)
    for g in range(0, nb, group):
        cols = [
            jnp.broadcast_to(tiles[0][:, at + g + j : at + g + j + 1], (nb, 128)) for j in range(group)
        ]
        for j in range(group):
            t = g + j
            pivot = cols[j][t : t + 1, :]
            factor = jnp.where(sub > t, cols[j], 0.0) * (1.0 / pivot)
            scale = jnp.where(sub == t, lax.rsqrt(pivot), scale)
            for l in range(j + 1, group):
                cols[l] = cols[l] - factor * cols[l][t : t + 1, :]
            tiles = [x - factor * x[t : t + 1, :] for x in tiles]
    return [x * scale for x in tiles]


def chol_inverse_kernel(mine, other, out, work):
    n = out.shape[0]
    h = n // 2
    core = lax.bitwise_and(lax.axis_index("row"), jnp.int32(1))
    work[pl.ds(pl.multiple_of(core * h, h), h), :n] = mine[...]
    work[pl.ds(pl.multiple_of((1 - core) * h, h), h), :n] = other[...]
    r_id = lax.broadcasted_iota(jnp.int32, (n, n), 0)
    c_id = lax.broadcasted_iota(jnp.int32, (n, n), 1)
    work[:, n:] = jnp.where(r_id == c_id, 1.0, 0.0).astype(f32)
    nb = 32
    for p in range(n // nb):
        lo = p * nb
        left = (lo // 128) * 128
        right = n + ((lo + nb + 127) // 128) * 128
        tiles = [work[lo : lo + nb, c : c + 128] for c in range(left, right, 128)]
        s = jnp.concatenate(eliminate(tiles, lo - left, nb, 8), axis=1)
        work[lo : lo + nb, left:right] = s
        if lo + nb < n:
            lead = s[:, lo + nb - left : n - left]
            work[lo + nb :, left:right] -= lax.dot_general(
                lead, s, (((0,), (0,)), ((), ())), precision=lax.Precision.HIGHEST, preferred_element_type=f32
            )
    out[...] = jnp.where(r_id >= c_id, work[:, n:], 0.0)


def chol_inverse(mine, other):
    n = mine.shape[1]
    return pl.pallas_call(
        chol_inverse_kernel,
        out_shape=shape((n, n), f32),
        in_specs=[VMEM, VMEM],
        out_specs=VMEM,
        scratch_shapes=[pltpu.VMEM((n, 2 * n), f32)],
        compiler_params=params(8),
        cost_estimate=cost(*[mine] * 256),
        name="chol_inverse",
    )(mine, other)


def ortho_kernel(inverse, *refs):
    lefts, out = refs[:-1], refs[-1]
    block = lefts[0].shape[1]
    me = lax.axis_index("col")
    parts = split(inverse[...], 3)
    for d, ref in enumerate(lefts):
        rows = pl.ds(pl.multiple_of(flip(me, d) * block, block), block)
        out[rows, :] = sum(dot(ref[...], x, ((0,), (1,))) for x in reversed(parts)).astype(bf16)


def ortho(inverse, lefts):
    r, block = lefts[0].shape
    return pl.pallas_call(
        ortho_kernel,
        out_shape=shape((block * len(lefts), r), bf16),
        in_specs=[VMEM] * (1 + len(lefts)),
        out_specs=VMEM,
        compiler_params=params(8),
        cost_estimate=cost(*[shape((block * len(lefts), r), bf16)] * 8),
        name="ortho",
    )(inverse, *lefts)


def hand_on(x, *earlier):
    return pl.pallas_call(
        lambda *refs: None,
        out_shape=shape(x.shape, x.dtype),
        in_specs=[ANY] * (1 + len(earlier)),
        out_specs=ANY,
        input_output_aliases={0: 0},
        compiler_params=params(1),
        name="hand_on",
    )(x, *earlier)


def apply_inverse(parts, block):
    return sum(dot(x, block) for x in reversed(parts))


def share_kernel(inverse, own, *refs):
    received, (out, squares) = refs[:-2], refs[-2:]
    out[...] = (own[...] + sum(ref[...].astype(f32) for ref in received)).astype(bf16)
    value = apply_inverse(split(inverse[...], 2), out[...])
    total = jnp.sum(value * value, axis=1, keepdims=True)
    squares[...] = jnp.transpose(jnp.broadcast_to(total, (total.shape[0], 128)))[:8, :]


def share_of(inverse, own, received):
    r = own.shape[0]
    return pl.pallas_call(
        share_kernel,
        out_shape=(shape(own.shape, bf16), shape((8, r), f32)),
        in_specs=[VMEM] * (2 + len(received)),
        out_specs=(VMEM, VMEM),
        compiler_params=params(8),
        name="share",
    )(inverse, own, *received)


def result_kernel(pairs, factor, buf0, buf1, ortho_ref, inverse, squares, weight, *refs):
    blocks, rest = refs[: 2 * len(pairs)], refs[2 * len(pairs) :]
    *_, new_weight, new_momentum, basis, token, mbuf, wbuf, vbuf, nbuf, lbuf, in_sems, out_sems, basis_sems = rest
    r, width = blocks[0].shape
    tile = 256
    tiles = width // tile
    count = len(blocks)
    half = width * (lax.axis_size("row") // 2)
    row = lax.axis_index("row")
    core = lax.bitwise_and(row, jnp.int32(1))
    chip = lax.div(row, jnp.int32(2))
    starts = []
    for d in pairs:
        starts += [core * half + flip(chip, d) * width, (1 - core) * half + flip(chip, d) * width]

    def load(b):
        cols = pl.ds(pl.multiple_of(starts[b], 128), width)
        return pltpu.make_async_copy(weight.at[:, cols], wbuf.at[b % 2], in_sems.at[b % 2])

    def store_basis(b):
        cols = pl.ds(pl.multiple_of(starts[b], 128), width)
        return pltpu.make_async_copy(nbuf.at[b % 2], basis.at[:, cols], basis_sems.at[b % 2])

    def place(b, t):
        return pl.ds(t * tile, tile), pl.ds(pl.multiple_of(starts[b] + t * tile, 128), tile)

    def store_momentum(b, t):
        at, there = place(b, t)
        return pltpu.make_async_copy(mbuf.at[b % 2, :, at], new_momentum.at[:, there], out_sems.at[0, b % 2, t])

    def store_weight(b, t):
        at, there = place(b, t)
        return pltpu.make_async_copy(vbuf.at[b % 2, :, at], new_weight.at[:, there], out_sems.at[1, b % 2, t])

    def finish(b):
        store_basis(b).wait()
        for t in range(tiles):
            store_momentum(b, t).wait()
            store_weight(b, t).wait()

    for b in range(2):
        load(b).start()
    scale = lax.rsqrt(squares[...] / FF + epsilon)
    scale = jnp.transpose(jnp.concatenate([scale] * 16, axis=0))[:, :1]
    token[...] = jnp.zeros_like(token)
    parts = split(inverse[...], 2)
    depth = lax.axis_size("col")
    size = buf0.shape[0] // depth
    for b in range(count):
        k = b % 2
        if b >= 2:
            finish(b - 2)
        right = apply_inverse(parts, blocks[b][...])
        lbuf[k] = ((1.0 - momentum_decay) * right).astype(bf16)
        nbuf[k] = (right * scale).astype(bf16)
        store_basis(b).start()
        for t in range(tiles):
            at, there = place(b, t)
            correction = dot(ortho_ref[...], lbuf[k, :, at])
            for j in range(2 * depth):
                rows = slice(j * size, (j + 1) * size)
                here = slice(j // 2 * size, (j // 2 + 1) * size)
                mbuf[k, rows, at] = (buf0, buf1)[j % 2][here, there] - correction[rows]
            store_momentum(b, t).start()
        load(b).wait()
        for t in range(tiles):
            at, there = place(b, t)
            change = dot(ortho_ref[...], nbuf[k, :, at])
            vbuf[k, :, at] = (wbuf[k, :, at].astype(f32) - factor * change).astype(bf16)
            store_weight(b, t).start()
        if b + 2 < count:
            load(b + 2).start()
    for b in range(count - 2, count):
        finish(b)


def results(pairs, factor, bufs, ortho_bf, inverse, squares, weight, blocks, outs):
    m, n = weight.shape
    r, width = blocks[0].shape
    ins = [*map(keep, bufs), ortho_bf, inverse, squares, stay(weight), *blocks, *map(stay, outs)]
    at = len(ins) - len(outs)
    *outs, token = pl.pallas_call(
        functools.partial(result_kernel, pairs, factor),
        out_shape=[shape((m, n), bf16), shape((m, n), f32), shape((r, n), bf16), shape((8, 128), f32)],
        in_specs=[VMEM] * 5 + [ANY] + [VMEM] * len(blocks) + [ANY] * len(outs),
        out_specs=[ANY] * 3 + [VMEM],
        input_output_aliases={at + k: k for k in range(len(outs))},
        scratch_shapes=[
            pltpu.VMEM((2, m, width), f32),
            pltpu.VMEM((2, m, width), bf16),
            pltpu.VMEM((2, m, width), bf16),
            pltpu.VMEM((2, r, width), bf16),
            pltpu.VMEM((2, r, width), bf16),
            pltpu.SemaphoreType.DMA((2,)),
            pltpu.SemaphoreType.DMA((2, 2, width // 256)),
            pltpu.SemaphoreType.DMA((2,)),
        ],
        compiler_params=params(15),
        cost_estimate=cost(*[shape((m, width), f32)] * (2 * len(blocks))),
        name="results",
    )(*ins)
    return outs, token


def sum_over(x, axis, least=1):
    d = least
    while d < lax.axis_size(axis):
        x = x + swap(x, axis, d)
        d *= 2
    return x


def exchange(x, axis, count, unit=1):
    return [x] + [swap(x, axis, unit * d) for d in range(1, count)]


def pair_up(terms):
    while len(terms) > 1:
        terms = [terms[2 * i] + terms[2 * i + 1] for i in range(len(terms) // 2)]
    return terms[0]


def gather(x, axis):
    blocks = [x]
    size = lax.axis_size(axis)
    for d in range(1, size):
        low = d & -d
        blocks.append(swap(blocks[d - low] if d != low else x, axis, low))
    return blocks


def per_device(weight, gradient, momentum, old_basis):
    depth, rows = lax.axis_size("col"), lax.axis_size("row")
    chips = rows // 2
    m, n = momentum.shape
    width = n // rows

    def sum_over_col(held, sent, *before):
        half = m // 2 // depth
        d = 1
        while held.shape[1] > half:
            held, sent = fold(held, swap(sent, "col", d), half)
            d *= 2
        return fold_last(held, swap(sent, "col", d), *before)

    buf0, kept, *outs = project(momentum, gradient, old_basis, depth, width, 0)
    low = sum_over_col(*outs)
    buf1, *outs = project(momentum, gradient, kept, depth, width, 1, (outs[1],))
    lefts = gather(sum_over_col(*outs, low), "col")
    bufs = (buf0, buf1)

    other, mine, g_sums = first_product(bufs, lefts[:-1], depth, width)
    g_mine, g_other = gram(lefts[-1], g_sums)
    other = last_product(bufs, other, lefts[-1], depth, width, False, g_mine)
    g_mine = g_mine + swap(g_other, "row", 1)
    other = hand_on(other, g_mine)
    received = swap(other, "row", 1)
    mine = last_product(bufs, mine, lefts[-1], depth, width, True, g_mine, other)
    own, *sent = pair_sum(mine, received, chips, g_mine)
    g_mine = pair_up(exchange(g_mine, "row", chips, 2))
    got = [swap(x, "row", 2 * (d + 1)) for d, x in enumerate(sent)]
    inverse = chol_inverse(g_mine, swap(g_mine, "row", 1))

    share, squares = share_of(inverse, own, got)
    ortho_bf = ortho(inverse, lefts)
    squares = pair_up(exchange(squares, "row", chips, 2))
    share = hand_on(share, squares)
    squares = pair_up(exchange(squares + swap(squares, "row", 1), "col", depth))

    factor = step_rate * math.sqrt(D / RANK)
    near = min(3, chips)
    blocks = [share] + [swap(share, "row", 2 * d) for d in range(1, near)]
    blocks = [share] + [hand_on(x, squares) for x in blocks[1:]]
    for d in range(near, chips):
        share = hand_on(share, blocks[d - 2])
        blocks.append(swap(share, "row", 2 * d))
    blocks[0] = share
    pairs = [x for block in blocks[:near] for x in (block, swap(block, "row", 1))]
    common = (factor, bufs, ortho_bf, inverse, squares, weight)
    outs, token = results(tuple(range(near)), *common, pairs, [])
    for d in range(near, chips):
        block = hand_on(blocks[d], token)
        outs, token = results((d,), *common, (block, swap(block, "row", 1)), outs)
    return tuple(outs)


def plain_per_device(weight, gradient, momentum, old_basis):
    buffer = momentum + gradient.astype(f32)
    buffer_low = buffer.astype(bf16)
    left_factor = lax.psum(dot(buffer_low, old_basis, ((1,), (1,))), "col")
    gram_share = lax.dot_general(
        left_factor,
        left_factor,
        (((0,), (0,)), ((), ())),
        precision=lax.Precision.HIGHEST,
        preferred_element_type=f32,
    )
    chol_factor = jnp.linalg.cholesky(lax.psum(gram_share, "row"))
    orthonormal = lax.linalg.triangular_solve(
        chol_factor, left_factor, left_side=False, lower=True, transpose_a=True
    ).astype(bf16)
    right_share = lax.psum_scatter(
        dot(orthonormal, buffer_low, ((0,), (0,))), "row", scatter_dimension=0, tiled=True
    )
    sum_squares = lax.psum(jnp.sum(right_share * right_share, axis=1), "col")
    scale_share = jnp.sqrt(sum_squares / FF + epsilon)
    basis_share = (right_share / scale_share[:, None]).astype(bf16)
    new_basis = lax.all_gather(basis_share, "row", axis=0, tiled=True)
    col_scale = lax.all_gather(scale_share, "row", axis=0, tiled=True)
    scaled = (orthonormal.astype(f32) * col_scale[None, :]).astype(bf16)
    new_momentum = buffer - (1.0 - momentum_decay) * dot(scaled, new_basis)
    factor = step_rate * math.sqrt(D / RANK)
    new_weight = (weight.astype(f32) - factor * dot(orthonormal, new_basis)).astype(bf16)
    return (new_weight, new_momentum, new_basis)


def power_of_two(k):
    return k > 1 and k & (k - 1) == 0


def solution(mesh):
    rows, depth = mesh.shape["row"], mesh.shape["col"]
    tiled = (
        power_of_two(rows)
        and power_of_two(depth)
        and D % (rows * depth * 128) == 0
        and FF % (rows * depth * 256) == 0
    )
    return jax.shard_map(
        per_device if tiled else plain_per_device,
        mesh=mesh,
        in_specs=(P("row", "col"), P("row", "col"), P("row", "col"), P(None, "col")),
        out_specs=(P("row", "col"), P("row", "col"), P(None, "col")),
        check_vma=False,
    )
```

time: 124 us -> 119 us (0.960)
  starting transfers between devices: 38 us -> 31.3 us
  waiting for transfers between devices: 27.6 us -> 29.2 us
    ppermute x34 -> x30, starting transfers between devices: 38 us -> 31.3 us  [swap(): lax.ppermute(x, axis, [(i, i ^ d) for i in range(lax.axis_size(axis))])]
    pallas_call x2, Pallas kernels: 20.8 us -> 23.1 us  [results(): pl.pallas_call(functools.partial(result_kernel, pairs, factor), out_shape...]
    pallas_call x8 -> x10, Pallas kernels: 26.3 us -> 23.9 us  [the longest x2 16.5 us: project(): pl.pallas_call(functools.partial(project_kernel, part, depth, width), out...]
    ppermute x34 -> x30, waiting for transfers between devices: 27.6 us -> 29.2 us  [swap(): lax.ppermute(x, axis, [(i, i ^ d) for i in range(lax.axis_size(axis))])]
  transfers between devices with their start and end apart: 34 -> 30, of which waited for: 15 -> 17; matrix products, arithmetic and copies ran while one was open for 0% -> 0% of each run, Pallas kernels for 31% -> 34%
where the time goes in v5:
time: 119 us
  Pallas kernels  57.4 us (48%)
  starting transfers between devices  31.3 us (26%)
  waiting for transfers between devices  29.2 us (25%)
    ppermute x30, starting transfers between devices, swap(): lax.ppermute(x, axis, [(i, i ^ d) for i in range(lax.axis_size(axis))])  31.3 us
    ppermute x30, waiting for transfers between devices, swap(): lax.ppermute(x, axis, [(i, i ^ d) for i in range(lax.axis_size(axis))])  29.2 us
    pallas_call x2, Pallas kernels, results(): pl.pallas_call(functools.partial(result_kernel, pairs, factor), out_shape...  23.1 us
    pallas_call x2, Pallas kernels, project(): pl.pallas_call(functools.partial(project_kernel, part, depth, width), out...  16.5 us
    pallas_call x1, Pallas kernels, chol_inverse(): pl.pallas_call(chol_inverse_kernel, out_shape=shape((n, n), f32), in_spec...  9.14 us
    pallas_call x1, Pallas kernels, first_product(): pl.pallas_call(functools.partial(first_kernel, depth, width), out_shape=(...  4.29 us
    pallas_call x2, Pallas kernels, last_product(): pl.pallas_call(functools.partial(last_kernel, depth, width, mine), out_sh...  2.41 us
  transfers between devices with their start and end apart: 30, of which 17 were waited for; matrix products, arithmetic and copies ran while one was open for 0% of the time, Pallas kernels for 34%

profile of v5, /device:TPU:0, one launch (start us, length us, event | category | flops | bytes accessed | tf_op | source)
XLA Modules:
  0.0 119.0 jit_solution(17768834093452655800)
XLA Ops:
  0.6 8.7 %project.2 = (f32[512,6144]{1,0:T(8,128)S(1)}, bf16[256,6144]{1,0:T(8,128)(2,1)S(1)}, f32[256,256]{1,0:T(8,128)S(1)}, bf16[256,256]{1,0:T(8,128)(2,1)S(1)}) custom-call(f32[1024,6144]{1,0:T(8,128)} %mom.3, bf16[1024,6144]{1,0:T(8,128)(2,1)} %grad.3, bf16[256,6144]{1,0:T(8,128)(2,1)} %basis.1), custom_call_target="tpu_custom_call" | custom-call | bytes 37748736 | tf_op jit(solution)/shard_map/project/pallas_call | solution.py:104
  9.3 3.1 %collective-permute-start.2 = (bf16[256,256]{1,0:T(8,128)(2,1)S(1)}, bf16[256,256]{1,0:T(8,128)(2,1)S(1)}, u32[]{:S(2)}, u32[]{:S(2)}) collective-permute-start(bf16[256,256]{1,0:T(8,128)(2,1)S(1)} %get-tuple-element.34.rest_0_), channel_id=1, source_target_pairs={{0,1},{1,0},{2,3},{3,2},{4,5},{5,4},{6,7},{7,6},{8,9},{9,8},{10,11... | collective-permute-start | bytes 393224 | tf_op jit(solution)/shard_map/ppermute | solution.py:51
  12.4 7.8 %project.3 = (f32[512,6144]{1,0:T(8,128)S(1)}, f32[256,256]{1,0:T(8,128)S(1)}, bf16[256,256]{1,0:T(8,128)(2,1)S(1)}) custom-call(f32[1024,6144]{1,0:T(8,128)} %mom.3, bf16[1024,6144]{1,0:T(8,128)(2,1)} %grad.3, bf16[256,6144]{1,0:T(8,128)(2,1)S(1)} %get-tuple-element.33.basis, bf16[256,256]{1,0:T(8,128)(2,1)S(1)} %get-tuple-element.34.rest_0_), custom_call_target="tpu_custom_call" | custom-call | bytes 37748736 | tf_op jit(solution)/shard_map/project/pallas_call | solution.py:104
  20.4 3.1 %collective-permute-start.3 = (bf16[256,128]{1,0:T(8,128)(2,1)S(1)}, bf16[256,128]{1,0:T(8,128)(2,1)S(1)}, u32[]{:S(2)}, u32[]{:S(2)}) collective-permute-start(bf16[256,128]{1,0:T(8,128)(2,1)S(1)} %get-tuple-element.42), channel_id=1, source_target_pairs={{0,2},{1,3},{2,0},{3,1},{4,6},{5,7},{6,4},{7,5},{8,10},{9,11},{10,... | collective-permute-start | bytes 196616 | tf_op jit(solution)/shard_map/ppermute | solution.py:51
  23.4 3.2 %collective-permute-done.received = bf16[256,256]{1,0:T(8,128)(2,1)S(1)} collective-permute-done((bf16[256,256]{1,0:T(8,128)(2,1)S(1)}, bf16[256,256]{1,0:T(8,128)(2,1)S(1)}, u32[]{:S(2)}, u32[]{:S(2)}) %collective-permute-start) | collective-permute-done | bytes 131104 | tf_op jit(solution)/shard_map/ppermute | solution.py:51
  26.7 2.3 %collective-permute-start.1 = (bf16[256,128]{1,0:T(8,128)(2,1)S(1)}, bf16[256,128]{1,0:T(8,128)(2,1)S(1)}, u32[]{:S(2)}, u32[]{:S(2)}) collective-permute-start(bf16[256,128]{1,0:T(8,128)(2,1)S(1)} %get-tuple-element.39), channel_id=1, source_target_pairs={{0,2},{1,3},{2,0},{3,1},{4,6},{5,7},{6,4},{7,5},{8,10},{9,11},{10,... | collective-permute-start | bytes 196616 | tf_op jit(solution)/shard_map/ppermute | solution.py:51
  29.0 2.9 %collective-permute-done.1.received = bf16[256,128]{1,0:T(8,128)(2,1)S(1)} collective-permute-done((bf16[256,128]{1,0:T(8,128)(2,1)S(1)}, bf16[256,128]{1,0:T(8,128)(2,1)S(1)}, u32[]{:S(2)}, u32[]{:S(2)}) %collective-permute-start.1) | collective-permute-done | bytes 65568 | tf_op jit(solution)/shard_map/ppermute | solution.py:51
  31.9 2.5 %collective-permute-start.4 = (bf16[256,256]{1,0:T(8,128)(2,1)S(1)}, bf16[256,256]{1,0:T(8,128)(2,1)S(1)}, u32[]{:S(2)}, u32[]{:S(2)}) collective-permute-start(bf16[256,256]{1,0:T(8,128)(2,1)S(1)} %fold_last.3.rest_0_.refs_0_), channel_id=1, source_target_pairs={{0,2},{1,3},{2,0},{3,1},{4,6},{5,7},{6,4},{7,5},{8,10},{9,11},{10,... | collective-permute-start | bytes 393224 | tf_op jit(solution)/shard_map/ppermute | solution.py:51
  34.5 4.4 %collective-permute-done.4.rest_2_.refs_2_ = bf16[256,256]{1,0:T(8,128)(2,1)S(1)} collective-permute-done((bf16[256,256]{1,0:T(8,128)(2,1)S(1)}, bf16[256,256]{1,0:T(8,128)(2,1)S(1)}, u32[]{:S(2)}, u32[]{:S(2)}) %collective-permute-start.4) | collective-permute-done | bytes 131104 | tf_op jit(solution)/shard_map/ppermute | solution.py:51
  38.8 2.7 %collective-permute-done.6.rest_1_.refs_1_ = bf16[256,256]{1,0:T(8,128)(2,1)S(1)} collective-permute-done((bf16[256,256]{1,0:T(8,128)(2,1)S(1)}, bf16[256,256]{1,0:T(8,128)(2,1)S(1)}, u32[]{:S(2)}, u32[]{:S(2)}) %collective-permute-start.6) | collective-permute-done | bytes 131104 | tf_op jit(solution)/shard_map/ppermute | solution.py:51
  41.6 4.3 %first_product.1 = (f32[256,3072]{1,0:T(8,128)S(1)}, f32[256,3072]{1,0:T(8,128)S(1)}, f32[256,256]{1,0:T(8,128)S(1)}) custom-call(f32[512,6144]{1,0:T(8,128)S(1)} %get-tuple-element.32.buf0, f32[512,6144]{1,0:T(8,128)S(1)} %get-tuple-element.35.buf1, bf16[256,256]{1,0:T(8,128)(2,1)S(1)} %fold_last.3.rest_0_.refs_0_, ...), custom_call_target="tpu_custom_call" | custom-call | bytes 31457280 | tf_op jit(solution)/shard_map/first_product/pallas_call | solution.py:203
  45.9 0.3 gram.1
  46.2 1.1 other_product.1.refs_0_
  47.6 0.4 collective-permute-start.12
  48.0 2.4 %collective-permute-start.10 = (f32[128,256]{1,0:T(8,128)S(1)}, f32[128,256]{1,0:T(8,128)S(1)}, u32[]{:S(2)}, u32[]{:S(2)}) collective-permute-start(f32[128,256]{1,0:T(8,128)S(1)} %add.33.refs_1_.rest_0_._), channel_id=1, source_target_pairs={{0,24},{4,28},{8,16},{12,20},{16,8},{20,12},{24,0},{28,4},{1,25},{... | collective-permute-start | bytes 393224 | tf_op jit(solution)/shard_map/ppermute | solution.py:51
  50.3 0.5 collective-permute-start.9
  50.8 0.6 collective-permute-start.8
  51.4 1.3 %mine_product.1.mine = f32[256,3072]{1,0:T(8,128)S(1)} custom-call(f32[512,6144]{1,0:T(8,128)S(1)} %get-tuple-element.32.buf0, f32[512,6144]{1,0:T(8,128)S(1)} %get-tuple-element.35.buf1, f32[256,3072]{1,0:T(8,128)S(1)} %get-tuple-element.46.sums, bf16[256,256]{1,0:T(8,128)(2,1)S(1)} %collective-permute-done.5.left.refs_3_, ...), custom_call_target="tpu_custom_call" | custom-call | bytes 15728640 | tf_op jit(solution)/shard_map/mine_product/pallas_call | solution.py:253
  52.7 0.3 pair_sum.1
  53.1 1.5 %collective-permute-start.13 = (bf16[256,768]{1,0:T(8,128)(2,1)S(1)}, bf16[256,768]{1,0:T(8,128)(2,1)S(1)}, u32[]{:S(2)}, u32[]{:S(2)}) collective-permute-start(bf16[256,768]{1,0:T(8,128)(2,1)S(1)} %get-tuple-element.49), channel_id=1, source_target_pairs={{0,8},{4,12},{8,0},{12,4},{16,24},{20,28},{24,16},{28,20},{1,9},{5... | collective-permute-start | bytes 1179656 | tf_op jit(solution)/shard_map/ppermute | solution.py:51
  54.6 1.5 %collective-permute-start.14 = (bf16[256,768]{1,0:T(8,128)(2,1)S(1)}, bf16[256,768]{1,0:T(8,128)(2,1)S(1)}, u32[]{:S(2)}, u32[]{:S(2)}) collective-permute-start(bf16[256,768]{1,0:T(8,128)(2,1)S(1)} %get-tuple-element.50), channel_id=1, source_target_pairs={{0,16},{4,20},{8,24},{12,28},{16,0},{20,4},{24,8},{28,12},{1,17},{... | collective-permute-start | bytes 1179656 | tf_op jit(solution)/shard_map/ppermute | solution.py:51
  56.1 1.5 %collective-permute-start.15 = (bf16[256,768]{1,0:T(8,128)(2,1)S(1)}, bf16[256,768]{1,0:T(8,128)(2,1)S(1)}, u32[]{:S(2)}, u32[]{:S(2)}) collective-permute-start(bf16[256,768]{1,0:T(8,128)(2,1)S(1)} %get-tuple-element.51), channel_id=1, source_target_pairs={{0,24},{4,28},{8,16},{12,20},{16,8},{20,12},{24,0},{28,4},{1,25},{... | collective-permute-start | bytes 1179656 | tf_op jit(solution)/shard_map/ppermute | solution.py:51
  57.6 0.4 collective-permute-done.8
  58.1 1.3 %collective-permute-done.11.other = f32[128,256]{1,0:T(8,128)S(1)} collective-permute-done((f32[128,256]{1,0:T(8,128)S(1)}, f32[128,256]{1,0:T(8,128)S(1)}, u32[]{:S(2)}, u32[]{:S(2)}) %collective-permute-start.11) | collective-permute-done | bytes 131104 | tf_op jit(solution)/shard_map/ppermute | solution.py:51
  59.5 9.1 %chol_inverse.1.inverse = f32[256,256]{1,0:T(8,128)S(1)} custom-call(f32[128,256]{1,0:T(8,128)S(1)} %add_add_fusion.mine, f32[128,256]{1,0:T(8,128)S(1)} %collective-permute-done.11.other), custom_call_target="tpu_custom_call" | custom-call | bytes 33554432 | tf_op jit(solution)/shard_map/chol_inverse/pallas_call | solution.py:330
  68.6 5.5 %collective-permute-done.15.refs_2_ = bf16[256,768]{1,0:T(8,128)(2,1)S(1)} collective-permute-done((bf16[256,768]{1,0:T(8,128)(2,1)S(1)}, bf16[256,768]{1,0:T(8,128)(2,1)S(1)}, u32[]{:S(2)}, u32[]{:S(2)}) %collective-permute-start.15) | collective-permute-done | bytes 393248 | tf_op jit(solution)/shard_map/ppermute | solution.py:51
  74.1 0.6 share.1
  74.7 2.5 %collective-permute-start.18 = (f32[8,256]{1,0:T(8,128)S(1)}, f32[8,256]{1,0:T(8,128)S(1)}, u32[]{:S(2)}, u32[]{:S(2)}) collective-permute-start(f32[8,256]{1,0:T(8,128)S(1)} %get-tuple-element.52), channel_id=1, source_target_pairs={{0,24},{4,28},{8,16},{12,20},{16,8},{20,12},{24,0},{28,4},{1,25},{... | collective-permute-start | bytes 24584 | tf_op jit(solution)/shard_map/ppermute | solution.py:51
  77.2 0.5 collective-permute-start.17
  77.7 0.6 collective-permute-start.16
  78.2 1.1 collective-permute-done.18
  79.3 1.5 %collective-permute-done.17 = f32[8,256]{1,0:T(8,128)S(1)} collective-permute-done((f32[8,256]{1,0:T(8,128)S(1)}, f32[8,256]{1,0:T(8,128)S(1)}, u32[]{:S(2)}, u32[]{:S(2)}) %collective-permute-start.17) | collective-permute-done | bytes 8224 | tf_op jit(solution)/shard_map/ppermute | solution.py:51
  80.8 0.5 collective-permute-done.16
  81.3 1.5 %collective-permute-start.27 = (bf16[256,768]{1,0:T(8,128)(2,1)S(1)}, bf16[256,768]{1,0:T(8,128)(2,1)S(1)}, u32[]{:S(2)}, u32[]{:S(2)}) collective-permute-start(bf16[256,768]{1,0:T(8,128)(2,1)S(1)} %hand_on.7.refs_0_), channel_id=1, source_target_pairs={{0,16},{4,20},{8,24},{12,28},{16,0},{20,4},{24,8},{28,12},{1,17},{... | collective-permute-start | bytes 1179656 | tf_op jit(solution)/shard_map/ppermute | solution.py:51
  82.9 0.5 collective-permute-start.23
  83.4 1.2 collective-permute-done.19
  84.5 1.8 %collective-permute-start.22 = (f32[8,256]{1,0:T(8,128)S(1)}, f32[8,256]{1,0:T(8,128)S(1)}, u32[]{:S(2)}, u32[]{:S(2)}) collective-permute-start(f32[8,256]{1,0:T(8,128)S(1)} %add.40), channel_id=1, source_target_pairs={{0,3},{1,2},{2,1},{3,0},{4,7},{5,6},{6,5},{7,4},{8,11},{9,10},{10,... | collective-permute-start | bytes 24584 | tf_op jit(solution)/shard_map/ppermute | solution.py:51
  86.3 0.5 collective-permute-start.21
  86.8 2.1 %collective-permute-start.20 = (f32[8,256]{1,0:T(8,128)S(1)}, f32[8,256]{1,0:T(8,128)S(1)}, u32[]{:S(2)}, u32[]{:S(2)}) collective-permute-start(f32[8,256]{1,0:T(8,128)S(1)} %add.40), channel_id=1, source_target_pairs={{0,1},{1,0},{2,3},{3,2},{4,5},{5,4},{6,7},{7,6},{8,9},{9,8},{10,11... | collective-permute-start | bytes 24584 | tf_op jit(solution)/shard_map/ppermute | solution.py:51
  88.9 1.1 collective-permute-done.22
  90.0 0.9 collective-permute-done.21
  91.0 0.6 collective-permute-done.23.refs_0_
  91.6 0.5 collective-permute-start.26
  92.1 1.0 collective-permute-start.24
  93.0 0.6 ortho.1.ortho_ref
  93.9 15.4 %results.2 = (bf16[1024,6144]{1,0:T(8,128)(2,1)}, f32[1024,6144]{1,0:T(8,128)}, bf16[256,6144]{1,0:T(8,128)(2,1)}, f32[8,128]{1,0:T(8,128)S(1)}) custom-call(f32[512,6144]{1,0:T(8,128)S(1)} %get-tuple-element.32.buf0, f32[512,6144]{1,0:T(8,128)S(1)} %get-tuple-element.35.buf1, bf16[1024,256]{1,0:T(8,128)(2,1)S(1)} %ortho.1.ortho_ref, ...), custom_call_target="tpu_custom_call" | custom-call | bytes 37748736 | tf_op jit(solution)/shard_map/results/pallas_call | solution.py:482
  109.5 1.6 %collective-permute-done.29.refs_1_ = bf16[256,768]{1,0:T(8,128)(2,1)S(1)} collective-permute-done((bf16[256,768]{1,0:T(8,128)(2,1)S(1)}, bf16[256,768]{1,0:T(8,128)(2,1)S(1)}, u32[]{:S(2)}, u32[]{:S(2)}) %collective-permute-start.29) | collective-permute-done | bytes 393248 | tf_op jit(solution)/shard_map/ppermute | solution.py:51
  111.1 7.7 %results.3 = (bf16[1024,6144]{1,0:T(8,128)(2,1)}, f32[1024,6144]{1,0:T(8,128)}, bf16[256,6144]{1,0:T(8,128)(2,1)}, f32[8,128]{1,0:T(8,128)}) custom-call(f32[512,6144]{1,0:T(8,128)S(1)} %get-tuple-element.32.buf0, f32[512,6144]{1,0:T(8,128)S(1)} %get-tuple-element.35.buf1, ...), custom_call_target="tpu_custom_call", output_to_operand_aliasing={{0}: (8, {}), {1}: (9, {}), {2}: (10, {})} | custom-call | bytes 12582912 | tf_op jit(solution)/shard_map/results/pallas_call | solution.py:482
  (39 shorter events, 1.1 us)
Async XLA Ops:
  9.3 11.0 %collective-permute-start.2 = (bf16[256,256]{1,0:T(8,128)(2,1)S(1)}, bf16[256,256]{1,0:T(8,128)(2,1)S(1)}, u32[]{:S(2)}, u32[]{:S(2)}) collective-permute-start(bf16[256,256]{1,0:T(8,128)(2,1)S(1)} %get-tuple-element.34.rest_0_), channel_id=1, source_target_pairs={{0,1},{1,0},{2,3},{3,2},{4,5},{5,4},{6,7},{7,6},{8,9},{9,8},{10,11... | collective-permute-start | bytes 393224 | tf_op jit(solution)/shard_map/ppermute | solution.py:51
  20.2 6.4 %collective-permute-start = (bf16[256,256]{1,0:T(8,128)(2,1)S(1)}, bf16[256,256]{1,0:T(8,128)(2,1)S(1)}, u32[]{:S(2)}, u32[]{:S(2)}) collective-permute-start(bf16[256,256]{1,0:T(8,128)(2,1)S(1)} %get-tuple-element.37), channel_id=1, source_target_pairs={{0,1},{1,0},{2,3},{3,2},{4,5},{5,4},{6,7},{7,6},{8,9},{9,8},{10,11... | collective-permute-start | bytes 393224 | tf_op jit(solution)/shard_map/ppermute | solution.py:51
  20.4 8.7 %collective-permute-start.3 = (bf16[256,128]{1,0:T(8,128)(2,1)S(1)}, bf16[256,128]{1,0:T(8,128)(2,1)S(1)}, u32[]{:S(2)}, u32[]{:S(2)}) collective-permute-start(bf16[256,128]{1,0:T(8,128)(2,1)S(1)} %get-tuple-element.42), channel_id=1, source_target_pairs={{0,2},{1,3},{2,0},{3,1},{4,6},{5,7},{6,4},{7,5},{8,10},{9,11},{10,... | collective-permute-start | bytes 196616 | tf_op jit(solution)/shard_map/ppermute | solution.py:51
  26.7 5.2 %collective-permute-start.1 = (bf16[256,128]{1,0:T(8,128)(2,1)S(1)}, bf16[256,128]{1,0:T(8,128)(2,1)S(1)}, u32[]{:S(2)}, u32[]{:S(2)}) collective-permute-start(bf16[256,128]{1,0:T(8,128)(2,1)S(1)} %get-tuple-element.39), channel_id=1, source_target_pairs={{0,2},{1,3},{2,0},{3,1},{4,6},{5,7},{6,4},{7,5},{8,10},{9,11},{10,... | collective-permute-start | bytes 196616 | tf_op jit(solution)/shard_map/ppermute | solution.py:51
  31.9 6.9 %collective-permute-start.4 = (bf16[256,256]{1,0:T(8,128)(2,1)S(1)}, bf16[256,256]{1,0:T(8,128)(2,1)S(1)}, u32[]{:S(2)}, u32[]{:S(2)}) collective-permute-start(bf16[256,256]{1,0:T(8,128)(2,1)S(1)} %fold_last.3.rest_0_.refs_0_), channel_id=1, source_target_pairs={{0,2},{1,3},{2,0},{3,1},{4,6},{5,7},{6,4},{7,5},{8,10},{9,11},{10,... | collective-permute-start | bytes 393224 | tf_op jit(solution)/shard_map/ppermute | solution.py:51
  34.5 7.1 %collective-permute-start.6 = (bf16[256,256]{1,0:T(8,128)(2,1)S(1)}, bf16[256,256]{1,0:T(8,128)(2,1)S(1)}, u32[]{:S(2)}, u32[]{:S(2)}) collective-permute-start(bf16[256,256]{1,0:T(8,128)(2,1)S(1)} %fold_last.3.rest_0_.refs_0_), channel_id=1, source_target_pairs={{0,1},{1,0},{2,3},{3,2},{4,5},{5,4},{6,7},{7,6},{8,9},{9,8},{10,11... | collective-permute-start | bytes 393224 | tf_op jit(solution)/shard_map/ppermute | solution.py:51
  38.8 7.0 %collective-permute-start.5 = (bf16[256,256]{1,0:T(8,128)(2,1)S(1)}, bf16[256,256]{1,0:T(8,128)(2,1)S(1)}, u32[]{:S(2)}, u32[]{:S(2)}) collective-permute-start(bf16[256,256]{1,0:T(8,128)(2,1)S(1)} %collective-permute-done.4.rest_2_.refs_2_), channel_id=1, source_target_pairs={{0,1},{1,0},{2,3},{3,2},{4,5},{5,4},{6,7},{7,6},{8,9},{9,8},{10,11... | collective-permute-start | bytes 393224 | tf_op jit(solution)/shard_map/ppermute | solution.py:51
  46.1 1.4 %collective-permute-start.7 = (f32[128,256]{1,0:T(8,128)S(1)}, f32[128,256]{1,0:T(8,128)S(1)}, u32[]{:S(2)}, u32[]{:S(2)}) collective-permute-start(f32[128,256]{1,0:T(8,128)S(1)} %get-tuple-element.45), channel_id=1, source_target_pairs={{0,4},{4,0},{8,12},{12,8},{16,20},{20,16},{24,28},{28,24},{1,5},{5... | collective-permute-start | bytes 393224 | tf_op jit(solution)/shard_map/ppermute | solution.py:51
  47.6 5.2 %collective-permute-start.12 = (bf16[256,3072]{1,0:T(8,128)(2,1)S(1)}, bf16[256,3072]{1,0:T(8,128)(2,1)S(1)}, u32[]{:S(2)}, u32[]{:S(2)}) collective-permute-start(bf16[256,3072]{1,0:T(8,128)(2,1)S(1)} %hand_on.6.rest_1_), channel_id=1, source_target_pairs={{0,4},{4,0},{8,12},{12,8},{16,20},{20,16},{24,28},{28,24},{1,5},{5... | collective-permute-start | bytes 4718600 | tf_op jit(solution)/shard_map/ppermute | solution.py:51
  48.0 8.1 %collective-permute-start.10 = (f32[128,256]{1,0:T(8,128)S(1)}, f32[128,256]{1,0:T(8,128)S(1)}, u32[]{:S(2)}, u32[]{:S(2)}) collective-permute-start(f32[128,256]{1,0:T(8,128)S(1)} %add.33.refs_1_.rest_0_._), channel_id=1, source_target_pairs={{0,24},{4,28},{8,16},{12,20},{16,8},{20,12},{24,0},{28,4},{1,25},{... | collective-permute-start | bytes 393224 | tf_op jit(solution)/shard_map/ppermute | solution.py:51
  50.3 7.3 %collective-permute-start.9 = (f32[128,256]{1,0:T(8,128)S(1)}, f32[128,256]{1,0:T(8,128)S(1)}, u32[]{:S(2)}, u32[]{:S(2)}) collective-permute-start(f32[128,256]{1,0:T(8,128)S(1)} %add.33.refs_1_.rest_0_._), channel_id=1, source_target_pairs={{0,16},{4,20},{8,24},{12,28},{16,0},{20,4},{24,8},{28,12},{1,17},{... | collective-permute-start | bytes 393224 | tf_op jit(solution)/shard_map/ppermute | solution.py:51
  50.8 7.2 %collective-permute-start.8 = (f32[128,256]{1,0:T(8,128)S(1)}, f32[128,256]{1,0:T(8,128)S(1)}, u32[]{:S(2)}, u32[]{:S(2)}) collective-permute-start(f32[128,256]{1,0:T(8,128)S(1)} %add.33.refs_1_.rest_0_._), channel_id=1, source_target_pairs={{0,8},{4,12},{8,0},{12,4},{16,24},{20,28},{24,16},{28,20},{1,9},{5... | collective-permute-start | bytes 393224 | tf_op jit(solution)/shard_map/ppermute | solution.py:51
  53.1 15.5 %collective-permute-start.13 = (bf16[256,768]{1,0:T(8,128)(2,1)S(1)}, bf16[256,768]{1,0:T(8,128)(2,1)S(1)}, u32[]{:S(2)}, u32[]{:S(2)}) collective-permute-start(bf16[256,768]{1,0:T(8,128)(2,1)S(1)} %get-tuple-element.49), channel_id=1, source_target_pairs={{0,8},{4,12},{8,0},{12,4},{16,24},{20,28},{24,16},{28,20},{1,9},{5... | collective-permute-start | bytes 1179656 | tf_op jit(solution)/shard_map/ppermute | solution.py:51
  54.6 14.0 %collective-permute-start.14 = (bf16[256,768]{1,0:T(8,128)(2,1)S(1)}, bf16[256,768]{1,0:T(8,128)(2,1)S(1)}, u32[]{:S(2)}, u32[]{:S(2)}) collective-permute-start(bf16[256,768]{1,0:T(8,128)(2,1)S(1)} %get-tuple-element.50), channel_id=1, source_target_pairs={{0,16},{4,20},{8,24},{12,28},{16,0},{20,4},{24,8},{28,12},{1,17},{... | collective-permute-start | bytes 1179656 | tf_op jit(solution)/shard_map/ppermute | solution.py:51
  56.1 18.0 %collective-permute-start.15 = (bf16[256,768]{1,0:T(8,128)(2,1)S(1)}, bf16[256,768]{1,0:T(8,128)(2,1)S(1)}, u32[]{:S(2)}, u32[]{:S(2)}) collective-permute-start(bf16[256,768]{1,0:T(8,128)(2,1)S(1)} %get-tuple-element.51), channel_id=1, source_target_pairs={{0,24},{4,28},{8,16},{12,20},{16,8},{20,12},{24,0},{28,4},{1,25},{... | collective-permute-start | bytes 1179656 | tf_op jit(solution)/shard_map/ppermute | solution.py:51
  58.1 1.4 %collective-permute-start.11 = (f32[128,256]{1,0:T(8,128)S(1)}, f32[128,256]{1,0:T(8,128)S(1)}, u32[]{:S(2)}, u32[]{:S(2)}) collective-permute-start(f32[128,256]{1,0:T(8,128)S(1)} %add_add_fusion.mine), channel_id=1, source_target_pairs={{0,4},{4,0},{8,12},{12,8},{16,20},{20,16},{24,28},{28,24},{1,5},{5... | collective-permute-start | bytes 393224 | tf_op jit(solution)/shard_map/ppermute | solution.py:51
  74.7 4.6 %collective-permute-start.18 = (f32[8,256]{1,0:T(8,128)S(1)}, f32[8,256]{1,0:T(8,128)S(1)}, u32[]{:S(2)}, u32[]{:S(2)}) collective-permute-start(f32[8,256]{1,0:T(8,128)S(1)} %get-tuple-element.52), channel_id=1, source_target_pairs={{0,24},{4,28},{8,16},{12,20},{16,8},{20,12},{24,0},{28,4},{1,25},{... | collective-permute-start | bytes 24584 | tf_op jit(solution)/shard_map/ppermute | solution.py:51
  77.2 3.7 %collective-permute-start.17 = (f32[8,256]{1,0:T(8,128)S(1)}, f32[8,256]{1,0:T(8,128)S(1)}, u32[]{:S(2)}, u32[]{:S(2)}) collective-permute-start(f32[8,256]{1,0:T(8,128)S(1)} %get-tuple-element.52), channel_id=1, source_target_pairs={{0,16},{4,20},{8,24},{12,28},{16,0},{20,4},{24,8},{28,12},{1,17},{... | collective-permute-start | bytes 24584 | tf_op jit(solution)/shard_map/ppermute | solution.py:51
  77.7 3.7 %collective-permute-start.16 = (f32[8,256]{1,0:T(8,128)S(1)}, f32[8,256]{1,0:T(8,128)S(1)}, u32[]{:S(2)}, u32[]{:S(2)}) collective-permute-start(f32[8,256]{1,0:T(8,128)S(1)} %get-tuple-element.52), channel_id=1, source_target_pairs={{0,8},{4,12},{8,0},{12,4},{16,24},{20,28},{24,16},{28,20},{1,9},{5... | collective-permute-start | bytes 24584 | tf_op jit(solution)/shard_map/ppermute | solution.py:51
  81.3 9.6 %collective-permute-start.27 = (bf16[256,768]{1,0:T(8,128)(2,1)S(1)}, bf16[256,768]{1,0:T(8,128)(2,1)S(1)}, u32[]{:S(2)}, u32[]{:S(2)}) collective-permute-start(bf16[256,768]{1,0:T(8,128)(2,1)S(1)} %hand_on.7.refs_0_), channel_id=1, source_target_pairs={{0,16},{4,20},{8,24},{12,28},{16,0},{20,4},{24,8},{28,12},{1,17},{... | collective-permute-start | bytes 1179656 | tf_op jit(solution)/shard_map/ppermute | solution.py:51
  82.9 8.7 %collective-permute-start.23 = (bf16[256,768]{1,0:T(8,128)(2,1)S(1)}, bf16[256,768]{1,0:T(8,128)(2,1)S(1)}, u32[]{:S(2)}, u32[]{:S(2)}) collective-permute-start(bf16[256,768]{1,0:T(8,128)(2,1)S(1)} %hand_on.7.refs_0_), channel_id=1, source_target_pairs={{0,8},{4,12},{8,0},{12,4},{16,24},{20,28},{24,16},{28,20},{1,9},{5... | collective-permute-start | bytes 1179656 | tf_op jit(solution)/shard_map/ppermute | solution.py:51
  83.4 1.2 collective-permute-start.19
  84.5 5.4 %collective-permute-start.22 = (f32[8,256]{1,0:T(8,128)S(1)}, f32[8,256]{1,0:T(8,128)S(1)}, u32[]{:S(2)}, u32[]{:S(2)}) collective-permute-start(f32[8,256]{1,0:T(8,128)S(1)} %add.40), channel_id=1, source_target_pairs={{0,3},{1,2},{2,1},{3,0},{4,7},{5,6},{6,5},{7,4},{8,11},{9,10},{10,... | collective-permute-start | bytes 24584 | tf_op jit(solution)/shard_map/ppermute | solution.py:51
  86.3 4.5 %collective-permute-start.21 = (f32[8,256]{1,0:T(8,128)S(1)}, f32[8,256]{1,0:T(8,128)S(1)}, u32[]{:S(2)}, u32[]{:S(2)}) collective-permute-start(f32[8,256]{1,0:T(8,128)S(1)} %add.40), channel_id=1, source_target_pairs={{0,2},{1,3},{2,0},{3,1},{4,6},{5,7},{6,4},{7,5},{8,10},{9,11},{10,... | collective-permute-start | bytes 24584 | tf_op jit(solution)/shard_map/ppermute | solution.py:51
  86.8 4.1 %collective-permute-start.20 = (f32[8,256]{1,0:T(8,128)S(1)}, f32[8,256]{1,0:T(8,128)S(1)}, u32[]{:S(2)}, u32[]{:S(2)}) collective-permute-start(f32[8,256]{1,0:T(8,128)S(1)} %add.40), channel_id=1, source_target_pairs={{0,1},{1,0},{2,3},{3,2},{4,5},{5,4},{6,7},{7,6},{8,9},{9,8},{10,11... | collective-permute-start | bytes 24584 | tf_op jit(solution)/shard_map/ppermute | solution.py:51
  90.9 2.8 %collective-permute-start.28 = (bf16[256,768]{1,0:T(8,128)(2,1)S(1)}, bf16[256,768]{1,0:T(8,128)(2,1)S(1)}, u32[]{:S(2)}, u32[]{:S(2)}) collective-permute-start(bf16[256,768]{1,0:T(8,128)(2,1)S(1)} %hand_on.10.refs_4_), channel_id=1, source_target_pairs={{0,4},{4,0},{8,12},{12,8},{16,20},{20,16},{24,28},{28,24},{1,5},{5... | collective-permute-start | bytes 1179656 | tf_op jit(solution)/shard_map/ppermute | solution.py:51
  91.6 2.1 %collective-permute-start.25 = (bf16[256,768]{1,0:T(8,128)(2,1)S(1)}, bf16[256,768]{1,0:T(8,128)(2,1)S(1)}, u32[]{:S(2)}, u32[]{:S(2)}) collective-permute-start(bf16[256,768]{1,0:T(8,128)(2,1)S(1)} %hand_on.9.refs_0_), channel_id=1, source_target_pairs={{0,4},{4,0},{8,12},{12,8},{16,20},{20,16},{24,28},{28,24},{1,5},{5... | collective-permute-start | bytes 1179656 | tf_op jit(solution)/shard_map/ppermute | solution.py:51
  91.6 2.3 %collective-permute-start.26 = (bf16[256,768]{1,0:T(8,128)(2,1)S(1)}, bf16[256,768]{1,0:T(8,128)(2,1)S(1)}, u32[]{:S(2)}, u32[]{:S(2)}) collective-permute-start(bf16[256,768]{1,0:T(8,128)(2,1)S(1)} %hand_on.8.refs_1_.refs_2_), channel_id=1, source_target_pairs={{0,4},{4,0},{8,12},{12,8},{16,20},{20,16},{24,28},{28,24},{1,5},{5... | collective-permute-start | bytes 1179656 | tf_op jit(solution)/shard_map/ppermute | solution.py:51
  92.1 17.2 %collective-permute-start.24 = (bf16[256,768]{1,0:T(8,128)(2,1)S(1)}, bf16[256,768]{1,0:T(8,128)(2,1)S(1)}, u32[]{:S(2)}, u32[]{:S(2)}) collective-permute-start(bf16[256,768]{1,0:T(8,128)(2,1)S(1)} %hand_on.9.refs_0_), channel_id=1, source_target_pairs={{0,24},{4,28},{8,16},{12,20},{16,8},{20,12},{24,0},{28,4},{1,25},{... | collective-permute-start | bytes 1179656 | tf_op jit(solution)/shard_map/ppermute | solution.py:51
  109.3 1.8 %collective-permute-start.29 = (bf16[256,768]{1,0:T(8,128)(2,1)S(1)}, bf16[256,768]{1,0:T(8,128)(2,1)S(1)}, u32[]{:S(2)}, u32[]{:S(2)}) collective-permute-start(bf16[256,768]{1,0:T(8,128)(2,1)S(1)} %hand_on.11.refs_0_), channel_id=1, source_target_pairs={{0,4},{4,0},{8,12},{12,8},{16,20},{20,16},{24,28},{28,24},{1,5},{5... | collective-permute-start | bytes 1179656 | tf_op jit(solution)/shard_map/ppermute | solution.py:51

commit v6 on v5

--- a/solution.py
+++ b/solution.py
@@ -378,29 +378,28 @@
     return sum(dot(x, block) for x in reversed(parts))
 
 
-def share_kernel(inverse, own, *refs):
-    received, (out, squares) = refs[:-2], refs[-2:]
+def share_kernel(own, *refs):
+    received, (_, out) = refs[:-2], refs[-2:]
     out[...] = (own[...] + sum(ref[...].astype(f32) for ref in received)).astype(bf16)
-    value = apply_inverse(split(inverse[...], 2), out[...])
-    total = jnp.sum(value * value, axis=1, keepdims=True)
-    squares[...] = jnp.transpose(jnp.broadcast_to(total, (total.shape[0], 128)))[:8, :]
-
-
-def share_of(inverse, own, received):
-    r = own.shape[0]
+
+
+def share_of(own, received, after):
     return pl.pallas_call(
         share_kernel,
-        out_shape=(shape(own.shape, bf16), shape((8, r), f32)),
-        in_specs=[VMEM] * (2 + len(received)),
-        out_specs=(VMEM, VMEM),
+        out_shape=shape(own.shape, bf16),
+        in_specs=[VMEM] * (1 + len(received)) + [ANY],
+        out_specs=VMEM,
         compiler_params=params(8),
         name="share",
-    )(inverse, own, *received)
-
-
-def result_kernel(pairs, factor, buf0, buf1, ortho_ref, inverse, squares, weight, *refs):
+    )(own, *received, after)
+
+
+def result_kernel(pairs, factor, momentum_too, weight_too, terms, buf0, buf1, ortho_ref, inverse, weight, *refs):
+    squares, refs = refs[:terms], refs[terms:]
     blocks, rest = refs[: 2 * len(pairs)], refs[2 * len(pairs) :]
-    *_, new_weight, new_momentum, basis, token, mbuf, wbuf, vbuf, nbuf, lbuf, in_sems, out_sems, basis_sems = rest
+    *outs, sums, mbuf, wbuf, vbuf, nbuf, lbuf, in_sems, out_sems, basis_sems = rest
+    new_momentum = outs[-1] if momentum_too else None
+    new_weight, basis = outs[-2 - momentum_too : len(outs) - momentum_too] if weight_too else (None, None)
     r, width = blocks[0].shape
     tile = 256
     tiles = width // tile
@@ -433,16 +432,22 @@
         return pltpu.make_async_copy(vbuf.at[b % 2, :, at], new_weight.at[:, there], out_sems.at[1, b % 2, t])
 
     def finish(b):
-        store_basis(b).wait()
+        if weight_too:
+            store_basis(b).wait()
         for t in range(tiles):
-            store_momentum(b, t).wait()
-            store_weight(b, t).wait()
-
-    for b in range(2):
-        load(b).start()
-    scale = lax.rsqrt(squares[...] / FF + epsilon)
-    scale = jnp.transpose(jnp.concatenate([scale] * 16, axis=0))[:, :1]
-    token[...] = jnp.zeros_like(token)
+            if momentum_too:
+                store_momentum(b, t).wait()
+            if weight_too:
+                store_weight(b, t).wait()
+
+    if weight_too:
+        for b in range(2):
+            load(b).start()
+        total = jnp.sum(pair_up([ref[...] for ref in squares]), axis=0, keepdims=True)
+        scale = lax.rsqrt(total / FF + epsilon)
+        scale = jnp.transpose(jnp.broadcast_to(scale, (128, r)))[:, :1]
+    sums[...] = jnp.zeros_like(sums)
+    block_id = lax.broadcasted_iota(jnp.int32, sums.shape, 0)
     parts = split(inverse[...], 2)
     depth = lax.axis_size("col")
     size = buf0.shape[0] // depth
@@ -451,44 +456,56 @@
         if b >= 2:
             finish(b - 2)
         right = apply_inverse(parts, blocks[b][...])
-        lbuf[k] = ((1.0 - momentum_decay) * right).astype(bf16)
-        nbuf[k] = (right * scale).astype(bf16)
-        store_basis(b).start()
+        if momentum_too:
+            lbuf[k] = ((1.0 - momentum_decay) * right).astype(bf16)
+            total = jnp.sum(right * right, axis=1, keepdims=True)
+            total = jnp.transpose(jnp.broadcast_to(total, (r, 128)))[: sums.shape[0], :]
+            sums[...] += jnp.where(block_id == lax.div(starts[b], jnp.int32(width)), total, 0.0)
+        if weight_too:
+            nbuf[k] = (right * scale).astype(bf16)
+            store_basis(b).start()
+            load(b).wait()
         for t in range(tiles):
             at, there = place(b, t)
-            correction = dot(ortho_ref[...], lbuf[k, :, at])
-            for j in range(2 * depth):
-                rows = slice(j * size, (j + 1) * size)
-                here = slice(j // 2 * size, (j // 2 + 1) * size)
-                mbuf[k, rows, at] = (buf0, buf1)[j % 2][here, there] - correction[rows]
-            store_momentum(b, t).start()
-        load(b).wait()
-        for t in range(tiles):
-            at, there = place(b, t)
-            change = dot(ortho_ref[...], nbuf[k, :, at])
-            vbuf[k, :, at] = (wbuf[k, :, at].astype(f32) - factor * change).astype(bf16)
-            store_weight(b, t).start()
-        if b + 2 < count:
+            if momentum_too:
+                correction = dot(ortho_ref[...], lbuf[k, :, at])
+                for j in range(2 * depth):
+                    rows = slice(j * size, (j + 1) * size)
+                    here = slice(j // 2 * size, (j // 2 + 1) * size)
+                    mbuf[k, rows, at] = (buf0, buf1)[j % 2][here, there] - correction[rows]
+                store_momentum(b, t).start()
+            if weight_too:
+                change = dot(ortho_ref[...], nbuf[k, :, at])
+                vbuf[k, :, at] = (wbuf[k, :, at].astype(f32) - factor * change).astype(bf16)
+                store_weight(b, t).start()
+        if weight_too and b + 2 < count:
             load(b + 2).start()
     for b in range(count - 2, count):
         finish(b)
 
 
-def results(pairs, factor, bufs, ortho_bf, inverse, squares, weight, blocks, outs):
+def results(pairs, kinds, factor, bufs, ortho_bf, inverse, weight, squares, blocks, outs=(), after=()):
+    momentum_too, weight_too = kinds
     m, n = weight.shape
     r, width = blocks[0].shape
-    ins = [*map(keep, bufs), ortho_bf, inverse, squares, stay(weight), *blocks, *map(stay, outs)]
+    ins = [*map(keep, bufs), ortho_bf, inverse, stay(weight), *squares, *blocks, *after, *map(stay, outs)]
     at = len(ins) - len(outs)
-    *outs, token = pl.pallas_call(
-        functools.partial(result_kernel, pairs, factor),
-        out_shape=[shape((m, n), bf16), shape((m, n), f32), shape((r, n), bf16), shape((8, 128), f32)],
-        in_specs=[VMEM] * 5 + [ANY] + [VMEM] * len(blocks) + [ANY] * len(outs),
-        out_specs=[ANY] * 3 + [VMEM],
+    out_shape = []
+    if weight_too:
+        out_shape += [shape((m, n), bf16), shape((r, n), bf16)]
+    if momentum_too:
+        out_shape += [shape((m, n), f32)]
+    m_slots, w_slots = (m if momentum_too else 8), (m if weight_too else 16)
+    return pl.pallas_call(
+        functools.partial(result_kernel, pairs, factor, momentum_too, weight_too, len(squares)),
+        out_shape=[*out_shape, shape((max(8, n // width), r), f32)],
+        in_specs=[VMEM] * 4 + [ANY] + [VMEM] * (len(squares) + len(blocks)) + [ANY] * (len(after) + len(outs)),
+        out_specs=[ANY] * len(out_shape) + [VMEM],
         input_output_aliases={at + k: k for k in range(len(outs))},
         scratch_shapes=[
-            pltpu.VMEM((2, m, width), f32),
-            pltpu.VMEM((2, m, width), bf16),
-            pltpu.VMEM((2, m, width), bf16),
+            pltpu.VMEM((2, m_slots, width), f32),
+            pltpu.VMEM((2, w_slots, width), bf16),
+            pltpu.VMEM((2, w_slots, width), bf16),
             pltpu.VMEM((2, r, width), bf16),
             pltpu.VMEM((2, r, width), bf16),
             pltpu.SemaphoreType.DMA((2,)),
@@ -496,10 +513,9 @@
             pltpu.SemaphoreType.DMA((2,)),
         ],
         compiler_params=params(15),
-        cost_estimate=cost(*[shape((m, width), f32)] * (2 * len(blocks))),
+        cost_estimate=cost(*[shape((m, width), f32)] * len(blocks) * (momentum_too + weight_too)),
         name="results",
     )(*ins)
-    return outs, token
 
 
 def sum_over(x, axis, least=1):
@@ -561,27 +577,46 @@
     got = [swap(x, "row", 2 * (d + 1)) for d, x in enumerate(sent)]
     inverse = chol_inverse(g_mine, swap(g_mine, "row", 1))
 
-    share, squares = share_of(inverse, own, got)
+    share = share_of(own, got, inverse)
     ortho_bf = ortho(inverse, lefts)
-    squares = pair_up(exchange(squares, "row", chips, 2))
-    share = hand_on(share, squares)
-    squares = pair_up(exchange(squares + swap(squares, "row", 1), "col", depth))
 
     factor = step_rate * math.sqrt(D / RANK)
-    near = min(3, chips)
-    blocks = [share] + [swap(share, "row", 2 * d) for d in range(1, near)]
-    blocks = [share] + [hand_on(x, squares) for x in blocks[1:]]
-    for d in range(near, chips):
-        share = hand_on(share, blocks[d - 2])
-        blocks.append(swap(share, "row", 2 * d))
-    blocks[0] = share
-    pairs = [x for block in blocks[:near] for x in (block, swap(block, "row", 1))]
-    common = (factor, bufs, ortho_bf, inverse, squares, weight)
-    outs, token = results(tuple(range(near)), *common, pairs, [])
-    for d in range(near, chips):
-        block = hand_on(blocks[d], token)
-        outs, token = results((d,), *common, (block, swap(block, "row", 1)), outs)
-    return tuple(outs)
+    common = (factor, bufs, ortho_bf, inverse, weight)
+    blocks = {0: share}
+    for d in range(1, chips):
+        if d & (d - 1) == 0:
+            blocks[d] = swap(share, "row", 2 * d)
+    near = sorted(blocks)
+    pairs = {0: (share, swap(share, "row", 1))}
+    momentum, sums = results((0,), (True, False), *common, (), pairs[0])
+    for d in near[1:]:
+        blocks[d] = hand_on(blocks[d], sums)
+        pairs[d] = (blocks[d], swap(blocks[d], "row", 1))
+    far = [d for d in range(chips) if d not in blocks]
+    h = share.shape[0] // 2
+    halves = {}
+    for d in far:
+        least, most = d & -d, 1 << (d.bit_length() - 1)
+        halves[d] = (
+            swap(blocks[d ^ most][:h], "row", 2 * most),
+            swap(blocks[d ^ least][h:], "row", 2 * least),
+        )
+        blocks[d] = jnp.concatenate(halves[d], axis=0)
+    squares = [sums]
+    rest = [x for d in near[1:] for x in pairs[d]]
+    momentum, sums = results(tuple(near[1:]), (True, False), *common, (), rest, [momentum])
+    squares.append(sums)
+    for d in far:
+        top, bottom = halves[d]
+        block = jnp.concatenate([hand_on(top, sums), bottom], axis=0)
+        pairs[d] = (block, swap(block, "row", 1))
+        momentum, sums = results((d,), (True, False), *common, (), pairs[d], [momentum])
+        squares.append(sums)
+    scales = exchange(sum(squares), "col", depth)
+    order = near + far
+    rest = [x for d in order for x in pairs[d]]
+    new_weight, new_basis, _ = results(tuple(order), (False, True), *common, scales, rest)
+    return (new_weight, momentum, new_basis)
 
 
 def plain_per_device(weight, gradient, momentum, old_basis):
@@ -621,7 +656,7 @@
 def solution(mesh):
     rows, depth = mesh.shape["row"], mesh.shape["col"]
     tiled = (
-        power_of_two(rows)
+        power_of_two(rows // 2)
         and power_of_two(depth)
         and D % (rows * depth * 128) == 0
         and FF % (rows * depth * 256) == 0

time: 119 us -> 122 us (1.025)
  Pallas kernels: 57.4 us -> 61.5 us
  starting transfers between devices: 31.3 us -> 29.7 us
    pallas_call x3 -> x5, Pallas kernels: 23.7 us -> 27.8 us  [the longest x4 27.6 us: results(): pl.pallas_call(functools.partial(result_kernel, pairs, factor, momentum_t...]
    ppermute x30 -> x27, starting transfers between devices: 31.3 us -> 29.7 us  [swap(): lax.ppermute(x, axis, [(i, i ^ d) for i in range(lax.axis_size(axis))])]
    ppermute x30 -> x27, waiting for transfers between devices: 29.2 us -> 29.7 us  [swap(): lax.ppermute(x, axis, [(i, i ^ d) for i in range(lax.axis_size(axis))])]
  transfers between devices with their start and end apart: 30 -> 27, of which waited for: 17 -> 13; matrix products, arithmetic and copies ran while one was open for 0% -> 0% of each run, Pallas kernels for 34% -> 29%
where the time goes in v6:
time: 122 us
  Pallas kernels  61.5 us (50%)
  starting transfers between devices  29.7 us (24%)
  waiting for transfers between devices  29.7 us (24%)
    ppermute x27, starting transfers between devices, swap(): lax.ppermute(x, axis, [(i, i ^ d) for i in range(lax.axis_size(axis))])  29.7 us
    ppermute x27, waiting for transfers between devices, swap(): lax.ppermute(x, axis, [(i, i ^ d) for i in range(lax.axis_size(axis))])  29.7 us
    pallas_call x4, Pallas kernels, results(): pl.pallas_call(functools.partial(result_kernel, pairs, factor, momentum_t...  27.6 us
    pallas_call x2, Pallas kernels, project(): pl.pallas_call(functools.partial(project_kernel, part, depth, width), out...  16.5 us
    pallas_call x1, Pallas kernels, chol_inverse(): pl.pallas_call(chol_inverse_kernel, out_shape=shape((n, n), f32), in_spec...  9.15 us
    pallas_call x1, Pallas kernels, first_product(): pl.pallas_call(functools.partial(first_kernel, depth, width), out_shape=(...  4.29 us
    pallas_call x2, Pallas kernels, last_product(): pl.pallas_call(functools.partial(last_kernel, depth, width, mine), out_sh...  2.45 us
  transfers between devices with their start and end apart: 27, of which 13 were waited for; matrix products, arithmetic and copies ran while one was open for 0% of the time, Pallas kernels for 29%

profile of v6, /device:TPU:0, one launch (start us, length us, event | category | flops | bytes accessed | tf_op | source)
XLA Modules:
  0.0 122.1 jit_solution(8668136172246914190)
XLA Ops:
  0.6 8.7 %project.2 = (f32[512,6144]{1,0:T(8,128)S(1)}, bf16[256,6144]{1,0:T(8,128)(2,1)S(1)}, f32[256,256]{1,0:T(8,128)S(1)}, bf16[256,256]{1,0:T(8,128)(2,1)S(1)}) custom-call(f32[1024,6144]{1,0:T(8,128)} %mom.3, bf16[1024,6144]{1,0:T(8,128)(2,1)} %grad.3, bf16[256,6144]{1,0:T(8,128)(2,1)} %basis.1), custom_call_target="tpu_custom_call" | custom-call | bytes 37748736 | tf_op jit(solution)/shard_map/project/pallas_call | solution.py:104
  9.4 3.1 %collective-permute-start.2 = (bf16[256,256]{1,0:T(8,128)(2,1)S(1)}, bf16[256,256]{1,0:T(8,128)(2,1)S(1)}, u32[]{:S(2)}, u32[]{:S(2)}) collective-permute-start(bf16[256,256]{1,0:T(8,128)(2,1)S(1)} %get-tuple-element.33.rest_0_), channel_id=1, source_target_pairs={{0,1},{1,0},{2,3},{3,2},{4,5},{5,4},{6,7},{7,6},{8,9},{9,8},{10,11... | collective-permute-start | bytes 393224 | tf_op jit(solution)/shard_map/ppermute | solution.py:51
  12.4 7.8 %project.3 = (f32[512,6144]{1,0:T(8,128)S(1)}, f32[256,256]{1,0:T(8,128)S(1)}, bf16[256,256]{1,0:T(8,128)(2,1)S(1)}) custom-call(f32[1024,6144]{1,0:T(8,128)} %mom.3, bf16[1024,6144]{1,0:T(8,128)(2,1)} %grad.3, bf16[256,6144]{1,0:T(8,128)(2,1)S(1)} %get-tuple-element.32.basis, bf16[256,256]{1,0:T(8,128)(2,1)S(1)} %get-tuple-element.33.rest_0_), custom_call_target="tpu_custom_call" | custom-call | bytes 37748736 | tf_op jit(solution)/shard_map/project/pallas_call | solution.py:104
  20.2 0.1 collective-permute-start
  20.4 3.1 %collective-permute-start.3 = (bf16[256,128]{1,0:T(8,128)(2,1)S(1)}, bf16[256,128]{1,0:T(8,128)(2,1)S(1)}, u32[]{:S(2)}, u32[]{:S(2)}) collective-permute-start(bf16[256,128]{1,0:T(8,128)(2,1)S(1)} %get-tuple-element.41), channel_id=1, source_target_pairs={{0,2},{1,3},{2,0},{3,1},{4,6},{5,7},{6,4},{7,5},{8,10},{9,11},{10,... | collective-permute-start | bytes 196616 | tf_op jit(solution)/shard_map/ppermute | solution.py:51
  23.4 3.2 %collective-permute-done.received = bf16[256,256]{1,0:T(8,128)(2,1)S(1)} collective-permute-done((bf16[256,256]{1,0:T(8,128)(2,1)S(1)}, bf16[256,256]{1,0:T(8,128)(2,1)S(1)}, u32[]{:S(2)}, u32[]{:S(2)}) %collective-permute-start) | collective-permute-done | bytes 131104 | tf_op jit(solution)/shard_map/ppermute | solution.py:51
  26.7 2.3 %collective-permute-start.1 = (bf16[256,128]{1,0:T(8,128)(2,1)S(1)}, bf16[256,128]{1,0:T(8,128)(2,1)S(1)}, u32[]{:S(2)}, u32[]{:S(2)}) collective-permute-start(bf16[256,128]{1,0:T(8,128)(2,1)S(1)} %get-tuple-element.38), channel_id=1, source_target_pairs={{0,2},{1,3},{2,0},{3,1},{4,6},{5,7},{6,4},{7,5},{8,10},{9,11},{10,... | collective-permute-start | bytes 196616 | tf_op jit(solution)/shard_map/ppermute | solution.py:51
  29.0 2.9 %collective-permute-done.1.received = bf16[256,128]{1,0:T(8,128)(2,1)S(1)} collective-permute-done((bf16[256,128]{1,0:T(8,128)(2,1)S(1)}, bf16[256,128]{1,0:T(8,128)(2,1)S(1)}, u32[]{:S(2)}, u32[]{:S(2)}) %collective-permute-start.1) | collective-permute-done | bytes 65568 | tf_op jit(solution)/shard_map/ppermute | solution.py:51
  32.0 2.5 %collective-permute-start.4 = (bf16[256,256]{1,0:T(8,128)(2,1)S(1)}, bf16[256,256]{1,0:T(8,128)(2,1)S(1)}, u32[]{:S(2)}, u32[]{:S(2)}) collective-permute-start(bf16[256,256]{1,0:T(8,128)(2,1)S(1)} %fold_last.3.rest_0_.refs_0_), channel_id=1, source_target_pairs={{0,2},{1,3},{2,0},{3,1},{4,6},{5,7},{6,4},{7,5},{8,10},{9,11},{10,... | collective-permute-start | bytes 393224 | tf_op jit(solution)/shard_map/ppermute | solution.py:51
  34.5 4.4 %collective-permute-done.4.rest_2_.refs_2_ = bf16[256,256]{1,0:T(8,128)(2,1)S(1)} collective-permute-done((bf16[256,256]{1,0:T(8,128)(2,1)S(1)}, bf16[256,256]{1,0:T(8,128)(2,1)S(1)}, u32[]{:S(2)}, u32[]{:S(2)}) %collective-permute-start.4) | collective-permute-done | bytes 131104 | tf_op jit(solution)/shard_map/ppermute | solution.py:51
  38.9 2.7 %collective-permute-done.6.rest_1_.refs_1_ = bf16[256,256]{1,0:T(8,128)(2,1)S(1)} collective-permute-done((bf16[256,256]{1,0:T(8,128)(2,1)S(1)}, bf16[256,256]{1,0:T(8,128)(2,1)S(1)}, u32[]{:S(2)}, u32[]{:S(2)}) %collective-permute-start.6) | collective-permute-done | bytes 131104 | tf_op jit(solution)/shard_map/ppermute | solution.py:51
  41.6 4.3 %first_product.1 = (f32[256,3072]{1,0:T(8,128)S(1)}, f32[256,3072]{1,0:T(8,128)S(1)}, f32[256,256]{1,0:T(8,128)S(1)}) custom-call(f32[512,6144]{1,0:T(8,128)S(1)} %get-tuple-element.31.buf0, f32[512,6144]{1,0:T(8,128)S(1)} %get-tuple-element.34.buf1, bf16[256,256]{1,0:T(8,128)(2,1)S(1)} %fold_last.3.rest_0_.refs_0_, ...), custom_call_target="tpu_custom_call" | custom-call | bytes 31457280 | tf_op jit(solution)/shard_map/first_product/pallas_call | solution.py:203
  45.9 0.3 gram.1
  46.2 0.1 collective-permute-start.7
  46.2 1.1 other_product.1.refs_0_
  47.4 0.2 collective-permute-done.7
  47.6 0.4 collective-permute-start.12
  48.0 2.4 %collective-permute-start.10 = (f32[128,256]{1,0:T(8,128)S(1)}, f32[128,256]{1,0:T(8,128)S(1)}, u32[]{:S(2)}, u32[]{:S(2)}) collective-permute-start(f32[128,256]{1,0:T(8,128)S(1)} %add.18.refs_1_.rest_0_._), channel_id=1, source_target_pairs={{0,24},{4,28},{8,16},{12,20},{16,8},{20,12},{24,0},{28,4},{1,25},{... | collective-permute-start | bytes 393224 | tf_op jit(solution)/shard_map/ppermute | solution.py:51
  50.4 0.5 collective-permute-start.9
  50.9 0.6 collective-permute-start.8
  51.5 1.3 %mine_product.1.mine = f32[256,3072]{1,0:T(8,128)S(1)} custom-call(f32[512,6144]{1,0:T(8,128)S(1)} %get-tuple-element.31.buf0, f32[512,6144]{1,0:T(8,128)S(1)} %get-tuple-element.34.buf1, f32[256,3072]{1,0:T(8,128)S(1)} %get-tuple-element.45.sums, bf16[256,256]{1,0:T(8,128)(2,1)S(1)} %collective-permute-done.5.left.refs_3_, ...), custom_call_target="tpu_custom_call" | custom-call | bytes 15728640 | tf_op jit(solution)/shard_map/mine_product/pallas_call | solution.py:253
  52.8 0.3 pair_sum.1
  53.1 1.5 %collective-permute-start.13 = (bf16[256,768]{1,0:T(8,128)(2,1)S(1)}, bf16[256,768]{1,0:T(8,128)(2,1)S(1)}, u32[]{:S(2)}, u32[]{:S(2)}) collective-permute-start(bf16[256,768]{1,0:T(8,128)(2,1)S(1)} %get-tuple-element.48), channel_id=1, source_target_pairs={{0,8},{4,12},{8,0},{12,4},{16,24},{20,28},{24,16},{28,20},{1,9},{5... | collective-permute-start | bytes 1179656 | tf_op jit(solution)/shard_map/ppermute | solution.py:51
  54.6 1.5 %collective-permute-start.14 = (bf16[256,768]{1,0:T(8,128)(2,1)S(1)}, bf16[256,768]{1,0:T(8,128)(2,1)S(1)}, u32[]{:S(2)}, u32[]{:S(2)}) collective-permute-start(bf16[256,768]{1,0:T(8,128)(2,1)S(1)} %get-tuple-element.49), channel_id=1, source_target_pairs={{0,16},{4,20},{8,24},{12,28},{16,0},{20,4},{24,8},{28,12},{1,17},{... | collective-permute-start | bytes 1179656 | tf_op jit(solution)/shard_map/ppermute | solution.py:51
  56.1 1.5 %collective-permute-start.15 = (bf16[256,768]{1,0:T(8,128)(2,1)S(1)}, bf16[256,768]{1,0:T(8,128)(2,1)S(1)}, u32[]{:S(2)}, u32[]{:S(2)}) collective-permute-start(bf16[256,768]{1,0:T(8,128)(2,1)S(1)} %get-tuple-element.50), channel_id=1, source_target_pairs={{0,24},{4,28},{8,16},{12,20},{16,8},{20,12},{24,0},{28,4},{1,25},{... | collective-permute-start | bytes 1179656 | tf_op jit(solution)/shard_map/ppermute | solution.py:51
  57.6 0.4 collective-permute-done.8
  58.2 1.3 %collective-permute-done.11.other = f32[128,256]{1,0:T(8,128)S(1)} collective-permute-done((f32[128,256]{1,0:T(8,128)S(1)}, f32[128,256]{1,0:T(8,128)S(1)}, u32[]{:S(2)}, u32[]{:S(2)}) %collective-permute-start.11) | collective-permute-done | bytes 131104 | tf_op jit(solution)/shard_map/ppermute | solution.py:51
  59.5 9.1 %chol_inverse.1.inverse.refs_3_ = f32[256,256]{1,0:T(8,128)S(1)} custom-call(f32[128,256]{1,0:T(8,128)S(1)} %add_add_fusion.mine, f32[128,256]{1,0:T(8,128)S(1)} %collective-permute-done.11.other), custom_call_target="tpu_custom_call" | custom-call | bytes 33554432 | tf_op jit(solution)/shard_map/chol_inverse/pallas_call | solution.py:330
  68.7 5.5 %collective-permute-done.15.refs_2_ = bf16[256,768]{1,0:T(8,128)(2,1)S(1)} collective-permute-done((bf16[256,768]{1,0:T(8,128)(2,1)S(1)}, bf16[256,768]{1,0:T(8,128)(2,1)S(1)}, u32[]{:S(2)}, u32[]{:S(2)}) %collective-permute-start.15) | collective-permute-done | bytes 393248 | tf_op jit(solution)/shard_map/ppermute | solution.py:51
  74.1 0.2 share.1.refs_0_.refs_4_
  74.3 0.1 collective-permute-start.16
  74.4 1.5 %collective-permute-start.17 = (bf16[256,768]{1,0:T(8,128)(2,1)S(1)}, bf16[256,768]{1,0:T(8,128)(2,1)S(1)}, u32[]{:S(2)}, u32[]{:S(2)}) collective-permute-start(bf16[256,768]{1,0:T(8,128)(2,1)S(1)} %share.1.refs_0_.refs_4_), channel_id=1, source_target_pairs={{0,8},{4,12},{8,0},{12,4},{16,24},{20,28},{24,16},{28,20},{1,9},{5... | collective-permute-start | bytes 1179656 | tf_op jit(solution)/shard_map/ppermute | solution.py:51
  75.9 1.5 %collective-permute-start.19 = (bf16[256,768]{1,0:T(8,128)(2,1)S(1)}, bf16[256,768]{1,0:T(8,128)(2,1)S(1)}, u32[]{:S(2)}, u32[]{:S(2)}) collective-permute-start(bf16[256,768]{1,0:T(8,128)(2,1)S(1)} %share.1.refs_0_.refs_4_), channel_id=1, source_target_pairs={{0,16},{4,20},{8,24},{12,28},{16,0},{20,4},{24,8},{28,12},{1,17},{... | collective-permute-start | bytes 1179656 | tf_op jit(solution)/shard_map/ppermute | solution.py:51
  77.4 0.6 ortho.1.ortho_ref
  78.1 3.6 %results.4 = (f32[1024,6144]{1,0:T(8,128)}, f32[8,256]{1,0:T(8,128)S(1)}) custom-call(f32[512,6144]{1,0:T(8,128)S(1)} %get-tuple-element.31.buf0, f32[512,6144]{1,0:T(8,128)S(1)} %get-tuple-element.34.buf1, bf16[1024,256]{1,0:T(8,128)(2,1)S(1)} %ortho.1.ortho_ref, f32[256,256]{1,0:T(8,128)S(1)} %chol_inverse.1.inverse.refs_3_, bf16[1024,6144]{1,0:T(8,128)(2,1)} %weight.7, ...), custom_call_target="tpu_custom_call" | custom-call | bytes 6291456 | tf_op jit(solution)/shard_map/results/pallas_call | solution.py:499
  81.7 4.2 %collective-permute-done.17.refs_0_ = bf16[256,768]{1,0:T(8,128)(2,1)S(1)} collective-permute-done((bf16[256,768]{1,0:T(8,128)(2,1)S(1)}, bf16[256,768]{1,0:T(8,128)(2,1)S(1)}, u32[]{:S(2)}, u32[]{:S(2)}) %collective-permute-start.17) | collective-permute-done | bytes 393248 | tf_op jit(solution)/shard_map/ppermute | solution.py:51
  85.9 1.2 collective-permute-done.19.refs_0_
  87.1 1.6 %collective-permute-start.21 = (bf16[128,768]{1,0:T(8,128)(2,1)S(1)}, bf16[128,768]{1,0:T(8,128)(2,1)S(1)}, u32[]{:S(2)}, u32[]{:S(2)}) collective-permute-start(bf16[128,768]{1,0:T(8,128)(2,1)S(1)} %slice.8), channel_id=1, source_target_pairs={{0,16},{4,20},{8,24},{12,28},{16,0},{20,4},{24,8},{28,12},{1,17},{... | collective-permute-start | bytes 589832 | tf_op jit(solution)/shard_map/ppermute | solution.py:51
  88.7 0.9 collective-permute-start.22
  89.6 6.5 %results.5 = (f32[1024,6144]{1,0:T(8,128)}, f32[8,256]{1,0:T(8,128)S(1)}) custom-call(f32[512,6144]{1,0:T(8,128)S(1)} %get-tuple-element.31.buf0, f32[512,6144]{1,0:T(8,128)S(1)} %get-tuple-element.34.buf1, bf16[1024,256]{1,0:T(8,128)(2,1)S(1)} %ortho.1.ortho_ref, f32[256,256]{1,0:T(8,128)S(1)} %chol_inverse.1.inverse.refs_3_, ...), custom_call_target="tpu_custom_call", output_to_operand_aliasing={{0}: (9, {})} | custom-call | bytes 12582912 | tf_op jit(solution)/shard_map/results/pallas_call | solution.py:499
  96.2 1.7 %collective-permute-done.23.refs_1_.refs_11_ = bf16[256,768]{1,0:T(8,128)(2,1)S(1)} collective-permute-done((bf16[256,768]{1,0:T(8,128)(2,1)S(1)}, bf16[256,768]{1,0:T(8,128)(2,1)S(1)}, u32[]{:S(2)}, u32[]{:S(2)}) %collective-permute-start.23) | collective-permute-done | bytes 393248 | tf_op jit(solution)/shard_map/ppermute | solution.py:51
  97.9 3.6 %results.6 = (f32[1024,6144]{1,0:T(8,128)}, f32[8,256]{1,0:T(8,128)S(1)}) custom-call(f32[512,6144]{1,0:T(8,128)S(1)} %get-tuple-element.31.buf0, f32[512,6144]{1,0:T(8,128)S(1)} %get-tuple-element.34.buf1, bf16[1024,256]{1,0:T(8,128)(2,1)S(1)} %ortho.1.ortho_ref, f32[256,256]{1,0:T(8,128)S(1)} %chol_inverse.1.inverse.refs_3_, ...), custom_call_target="tpu_custom_call", output_to_operand_aliasing={{0}: (7, {})} | custom-call | bytes 6291456 | tf_op jit(solution)/shard_map/results/pallas_call | solution.py:499
  101.6 1.9 %collective-permute-start.26 = (f32[8,256]{1,0:T(8,128)S(1)}, f32[8,256]{1,0:T(8,128)S(1)}, u32[]{:S(2)}, u32[]{:S(2)}) collective-permute-start(f32[8,256]{1,0:T(8,128)S(1)} %add_add_fusion.1.refs_0_), channel_id=1, source_target_pairs={{0,3},{1,2},{2,1},{3,0},{4,7},{5,6},{6,5},{7,4},{8,11},{9,10},{10,... | collective-permute-start | bytes 24584 | tf_op jit(solution)/shard_map/ppermute | solution.py:51
  103.4 0.5 collective-permute-start.25
  103.9 2.1 %collective-permute-start.24 = (f32[8,256]{1,0:T(8,128)S(1)}, f32[8,256]{1,0:T(8,128)S(1)}, u32[]{:S(2)}, u32[]{:S(2)}) collective-permute-start(f32[8,256]{1,0:T(8,128)S(1)} %add_add_fusion.1.refs_0_), channel_id=1, source_target_pairs={{0,1},{1,0},{2,3},{3,2},{4,5},{5,4},{6,7},{7,6},{8,9},{9,8},{10,11... | collective-permute-start | bytes 24584 | tf_op jit(solution)/shard_map/ppermute | solution.py:51
  106.0 1.1 collective-permute-done.26.refs_3_
  107.1 0.9 collective-permute-done.25.refs_2_
  108.0 13.9 %results.7 = (bf16[1024,6144]{1,0:T(8,128)(2,1)}, bf16[256,6144]{1,0:T(8,128)(2,1)}, f32[8,256]{1,0:T(8,128)}) custom-call(f32[512,6144]{1,0:T(8,128)S(1)} %get-tuple-element.31.buf0, f32[512,6144]{1,0:T(8,128)S(1)} %get-tuple-element.34.buf1, bf16[1024,256]{1,0:T(8,128)(2,1)S(1)} %ortho.1.ortho_ref, f32[256,256]{1,0:T(8,128)S(1)} %chol_inverse.1.inverse.refs_3_, ...), custom_call_target="tpu_custom_call" | custom-call | bytes 25165824 | tf_op jit(solution)/shard_map/results/pallas_call | solution.py:499
  (34 shorter events, 0.4 us)
Async XLA Ops:
  9.4 11.0 %collective-permute-start.2 = (bf16[256,256]{1,0:T(8,128)(2,1)S(1)}, bf16[256,256]{1,0:T(8,128)(2,1)S(1)}, u32[]{:S(2)}, u32[]{:S(2)}) collective-permute-start(bf16[256,256]{1,0:T(8,128)(2,1)S(1)} %get-tuple-element.33.rest_0_), channel_id=1, source_target_pairs={{0,1},{1,0},{2,3},{3,2},{4,5},{5,4},{6,7},{7,6},{8,9},{9,8},{10,11... | collective-permute-start | bytes 393224 | tf_op jit(solution)/shard_map/ppermute | solution.py:51
  20.2 6.4 %collective-permute-start = (bf16[256,256]{1,0:T(8,128)(2,1)S(1)}, bf16[256,256]{1,0:T(8,128)(2,1)S(1)}, u32[]{:S(2)}, u32[]{:S(2)}) collective-permute-start(bf16[256,256]{1,0:T(8,128)(2,1)S(1)} %get-tuple-element.36), channel_id=1, source_target_pairs={{0,1},{1,0},{2,3},{3,2},{4,5},{5,4},{6,7},{7,6},{8,9},{9,8},{10,11... | collective-permute-start | bytes 393224 | tf_op jit(solution)/shard_map/ppermute | solution.py:51
  20.4 8.7 %collective-permute-start.3 = (bf16[256,128]{1,0:T(8,128)(2,1)S(1)}, bf16[256,128]{1,0:T(8,128)(2,1)S(1)}, u32[]{:S(2)}, u32[]{:S(2)}) collective-permute-start(bf16[256,128]{1,0:T(8,128)(2,1)S(1)} %get-tuple-element.41), channel_id=1, source_target_pairs={{0,2},{1,3},{2,0},{3,1},{4,6},{5,7},{6,4},{7,5},{8,10},{9,11},{10,... | collective-permute-start | bytes 196616 | tf_op jit(solution)/shard_map/ppermute | solution.py:51
  26.7 5.2 %collective-permute-start.1 = (bf16[256,128]{1,0:T(8,128)(2,1)S(1)}, bf16[256,128]{1,0:T(8,128)(2,1)S(1)}, u32[]{:S(2)}, u32[]{:S(2)}) collective-permute-start(bf16[256,128]{1,0:T(8,128)(2,1)S(1)} %get-tuple-element.38), channel_id=1, source_target_pairs={{0,2},{1,3},{2,0},{3,1},{4,6},{5,7},{6,4},{7,5},{8,10},{9,11},{10,... | collective-permute-start | bytes 196616 | tf_op jit(solution)/shard_map/ppermute | solution.py:51
  32.0 6.9 %collective-permute-start.4 = (bf16[256,256]{1,0:T(8,128)(2,1)S(1)}, bf16[256,256]{1,0:T(8,128)(2,1)S(1)}, u32[]{:S(2)}, u32[]{:S(2)}) collective-permute-start(bf16[256,256]{1,0:T(8,128)(2,1)S(1)} %fold_last.3.rest_0_.refs_0_), channel_id=1, source_target_pairs={{0,2},{1,3},{2,0},{3,1},{4,6},{5,7},{6,4},{7,5},{8,10},{9,11},{10,... | collective-permute-start | bytes 393224 | tf_op jit(solution)/shard_map/ppermute | solution.py:51
  34.5 7.1 %collective-permute-start.6 = (bf16[256,256]{1,0:T(8,128)(2,1)S(1)}, bf16[256,256]{1,0:T(8,128)(2,1)S(1)}, u32[]{:S(2)}, u32[]{:S(2)}) collective-permute-start(bf16[256,256]{1,0:T(8,128)(2,1)S(1)} %fold_last.3.rest_0_.refs_0_), channel_id=1, source_target_pairs={{0,1},{1,0},{2,3},{3,2},{4,5},{5,4},{6,7},{7,6},{8,9},{9,8},{10,11... | collective-permute-start | bytes 393224 | tf_op jit(solution)/shard_map/ppermute | solution.py:51
  38.8 7.0 %collective-permute-start.5 = (bf16[256,256]{1,0:T(8,128)(2,1)S(1)}, bf16[256,256]{1,0:T(8,128)(2,1)S(1)}, u32[]{:S(2)}, u32[]{:S(2)}) collective-permute-start(bf16[256,256]{1,0:T(8,128)(2,1)S(1)} %collective-permute-done.4.rest_2_.refs_2_), channel_id=1, source_target_pairs={{0,1},{1,0},{2,3},{3,2},{4,5},{5,4},{6,7},{7,6},{8,9},{9,8},{10,11... | collective-permute-start | bytes 393224 | tf_op jit(solution)/shard_map/ppermute | solution.py:51
  46.2 1.4 %collective-permute-start.7 = (f32[128,256]{1,0:T(8,128)S(1)}, f32[128,256]{1,0:T(8,128)S(1)}, u32[]{:S(2)}, u32[]{:S(2)}) collective-permute-start(f32[128,256]{1,0:T(8,128)S(1)} %get-tuple-element.44), channel_id=1, source_target_pairs={{0,4},{4,0},{8,12},{12,8},{16,20},{20,16},{24,28},{28,24},{1,5},{5... | collective-permute-start | bytes 393224 | tf_op jit(solution)/shard_map/ppermute | solution.py:51
  47.6 5.2 %collective-permute-start.12 = (bf16[256,3072]{1,0:T(8,128)(2,1)S(1)}, bf16[256,3072]{1,0:T(8,128)(2,1)S(1)}, u32[]{:S(2)}, u32[]{:S(2)}) collective-permute-start(bf16[256,3072]{1,0:T(8,128)(2,1)S(1)} %hand_on.4.rest_1_), channel_id=1, source_target_pairs={{0,4},{4,0},{8,12},{12,8},{16,20},{20,16},{24,28},{28,24},{1,5},{5... | collective-permute-start | bytes 4718600 | tf_op jit(solution)/shard_map/ppermute | solution.py:51
  48.0 8.2 %collective-permute-start.10 = (f32[128,256]{1,0:T(8,128)S(1)}, f32[128,256]{1,0:T(8,128)S(1)}, u32[]{:S(2)}, u32[]{:S(2)}) collective-permute-start(f32[128,256]{1,0:T(8,128)S(1)} %add.18.refs_1_.rest_0_._), channel_id=1, source_target_pairs={{0,24},{4,28},{8,16},{12,20},{16,8},{20,12},{24,0},{28,4},{1,25},{... | collective-permute-start | bytes 393224 | tf_op jit(solution)/shard_map/ppermute | solution.py:51
  50.4 7.3 %collective-permute-start.9 = (f32[128,256]{1,0:T(8,128)S(1)}, f32[128,256]{1,0:T(8,128)S(1)}, u32[]{:S(2)}, u32[]{:S(2)}) collective-permute-start(f32[128,256]{1,0:T(8,128)S(1)} %add.18.refs_1_.rest_0_._), channel_id=1, source_target_pairs={{0,16},{4,20},{8,24},{12,28},{16,0},{20,4},{24,8},{28,12},{1,17},{... | collective-permute-start | bytes 393224 | tf_op jit(solution)/shard_map/ppermute | solution.py:51
  50.9 7.2 %collective-permute-start.8 = (f32[128,256]{1,0:T(8,128)S(1)}, f32[128,256]{1,0:T(8,128)S(1)}, u32[]{:S(2)}, u32[]{:S(2)}) collective-permute-start(f32[128,256]{1,0:T(8,128)S(1)} %add.18.refs_1_.rest_0_._), channel_id=1, source_target_pairs={{0,8},{4,12},{8,0},{12,4},{16,24},{20,28},{24,16},{28,20},{1,9},{5... | collective-permute-start | bytes 393224 | tf_op jit(solution)/shard_map/ppermute | solution.py:51
  53.1 15.5 %collective-permute-start.13 = (bf16[256,768]{1,0:T(8,128)(2,1)S(1)}, bf16[256,768]{1,0:T(8,128)(2,1)S(1)}, u32[]{:S(2)}, u32[]{:S(2)}) collective-permute-start(bf16[256,768]{1,0:T(8,128)(2,1)S(1)} %get-tuple-element.48), channel_id=1, source_target_pairs={{0,8},{4,12},{8,0},{12,4},{16,24},{20,28},{24,16},{28,20},{1,9},{5... | collective-permute-start | bytes 1179656 | tf_op jit(solution)/shard_map/ppermute | solution.py:51
  54.6 14.0 %collective-permute-start.14 = (bf16[256,768]{1,0:T(8,128)(2,1)S(1)}, bf16[256,768]{1,0:T(8,128)(2,1)S(1)}, u32[]{:S(2)}, u32[]{:S(2)}) collective-permute-start(bf16[256,768]{1,0:T(8,128)(2,1)S(1)} %get-tuple-element.49), channel_id=1, source_target_pairs={{0,16},{4,20},{8,24},{12,28},{16,0},{20,4},{24,8},{28,12},{1,17},{... | collective-permute-start | bytes 1179656 | tf_op jit(solution)/shard_map/ppermute | solution.py:51
  56.1 18.0 %collective-permute-start.15 = (bf16[256,768]{1,0:T(8,128)(2,1)S(1)}, bf16[256,768]{1,0:T(8,128)(2,1)S(1)}, u32[]{:S(2)}, u32[]{:S(2)}) collective-permute-start(bf16[256,768]{1,0:T(8,128)(2,1)S(1)} %get-tuple-element.50), channel_id=1, source_target_pairs={{0,24},{4,28},{8,16},{12,20},{16,8},{20,12},{24,0},{28,4},{1,25},{... | collective-permute-start | bytes 1179656 | tf_op jit(solution)/shard_map/ppermute | solution.py:51
  58.1 1.4 %collective-permute-start.11 = (f32[128,256]{1,0:T(8,128)S(1)}, f32[128,256]{1,0:T(8,128)S(1)}, u32[]{:S(2)}, u32[]{:S(2)}) collective-permute-start(f32[128,256]{1,0:T(8,128)S(1)} %add_add_fusion.mine), channel_id=1, source_target_pairs={{0,4},{4,0},{8,12},{12,8},{16,20},{20,16},{24,28},{28,24},{1,5},{5... | collective-permute-start | bytes 393224 | tf_op jit(solution)/shard_map/ppermute | solution.py:51
  74.3 3.8 %collective-permute-start.16 = (bf16[256,768]{1,0:T(8,128)(2,1)S(1)}, bf16[256,768]{1,0:T(8,128)(2,1)S(1)}, u32[]{:S(2)}, u32[]{:S(2)}) collective-permute-start(bf16[256,768]{1,0:T(8,128)(2,1)S(1)} %share.1.refs_0_.refs_4_), channel_id=1, source_target_pairs={{0,4},{4,0},{8,12},{12,8},{16,20},{20,16},{24,28},{28,24},{1,5},{5... | collective-permute-start | bytes 1179656 | tf_op jit(solution)/shard_map/ppermute | solution.py:51
  74.4 11.5 %collective-permute-start.17 = (bf16[256,768]{1,0:T(8,128)(2,1)S(1)}, bf16[256,768]{1,0:T(8,128)(2,1)S(1)}, u32[]{:S(2)}, u32[]{:S(2)}) collective-permute-start(bf16[256,768]{1,0:T(8,128)(2,1)S(1)} %share.1.refs_0_.refs_4_), channel_id=1, source_target_pairs={{0,8},{4,12},{8,0},{12,4},{16,24},{20,28},{24,16},{28,20},{1,9},{5... | collective-permute-start | bytes 1179656 | tf_op jit(solution)/shard_map/ppermute | solution.py:51
  75.9 11.2 %collective-permute-start.19 = (bf16[256,768]{1,0:T(8,128)(2,1)S(1)}, bf16[256,768]{1,0:T(8,128)(2,1)S(1)}, u32[]{:S(2)}, u32[]{:S(2)}) collective-permute-start(bf16[256,768]{1,0:T(8,128)(2,1)S(1)} %share.1.refs_0_.refs_4_), channel_id=1, source_target_pairs={{0,16},{4,20},{8,24},{12,28},{16,0},{20,4},{24,8},{28,12},{1,17},{... | collective-permute-start | bytes 1179656 | tf_op jit(solution)/shard_map/ppermute | solution.py:51
  85.9 3.7 %collective-permute-start.18 = (bf16[256,768]{1,0:T(8,128)(2,1)S(1)}, bf16[256,768]{1,0:T(8,128)(2,1)S(1)}, u32[]{:S(2)}, u32[]{:S(2)}) collective-permute-start(bf16[256,768]{1,0:T(8,128)(2,1)S(1)} %hand_on.5.refs_0_.refs_6_), channel_id=1, source_target_pairs={{0,4},{4,0},{8,12},{12,8},{16,20},{20,16},{24,28},{28,24},{1,5},{5... | collective-permute-start | bytes 1179656 | tf_op jit(solution)/shard_map/ppermute | solution.py:51
  87.1 2.5 %collective-permute-start.20 = (bf16[256,768]{1,0:T(8,128)(2,1)S(1)}, bf16[256,768]{1,0:T(8,128)(2,1)S(1)}, u32[]{:S(2)}, u32[]{:S(2)}) collective-permute-start(bf16[256,768]{1,0:T(8,128)(2,1)S(1)} %hand_on.6.refs_2_.refs_8_), channel_id=1, source_target_pairs={{0,4},{4,0},{8,12},{12,8},{16,20},{20,16},{24,28},{28,24},{1,5},{5... | collective-permute-start | bytes 1179656 | tf_op jit(solution)/shard_map/ppermute | solution.py:51
  87.1 9.0 %collective-permute-start.21 = (bf16[128,768]{1,0:T(8,128)(2,1)S(1)}, bf16[128,768]{1,0:T(8,128)(2,1)S(1)}, u32[]{:S(2)}, u32[]{:S(2)}) collective-permute-start(bf16[128,768]{1,0:T(8,128)(2,1)S(1)} %slice.8), channel_id=1, source_target_pairs={{0,16},{4,20},{8,24},{12,28},{16,0},{20,4},{24,8},{28,12},{1,17},{... | collective-permute-start | bytes 589832 | tf_op jit(solution)/shard_map/ppermute | solution.py:51
  88.7 7.4 %collective-permute-start.22 = (bf16[128,768]{1,0:T(8,128)(2,1)S(1)}, bf16[128,768]{1,0:T(8,128)(2,1)S(1)}, u32[]{:S(2)}, u32[]{:S(2)}) collective-permute-start(bf16[128,768]{1,0:T(8,128)(2,1)S(1)} %slice.9), channel_id=1, source_target_pairs={{0,8},{4,12},{8,0},{12,4},{16,24},{20,28},{24,16},{28,20},{1,9},{5... | collective-permute-start | bytes 589832 | tf_op jit(solution)/shard_map/ppermute | solution.py:51
  96.1 1.8 %collective-permute-start.23 = (bf16[256,768]{1,0:T(8,128)(2,1)S(1)}, bf16[256,768]{1,0:T(8,128)(2,1)S(1)}, u32[]{:S(2)}, u32[]{:S(2)}) collective-permute-start(bf16[256,768]{1,0:T(8,128)(2,1)S(1)} %pad_maximum_fusion.refs_0_.refs_10_), channel_id=1, source_target_pairs={{0,4},{4,0},{8,12},{12,8},{16,20},{20,16},{24,28},{28,24},{1,5},{5... | collective-permute-start | bytes 1179656 | tf_op jit(solution)/shard_map/ppermute | solution.py:51
  101.6 5.5 %collective-permute-start.26 = (f32[8,256]{1,0:T(8,128)S(1)}, f32[8,256]{1,0:T(8,128)S(1)}, u32[]{:S(2)}, u32[]{:S(2)}) collective-permute-start(f32[8,256]{1,0:T(8,128)S(1)} %add_add_fusion.1.refs_0_), channel_id=1, source_target_pairs={{0,3},{1,2},{2,1},{3,0},{4,7},{5,6},{6,5},{7,4},{8,11},{9,10},{10,... | collective-permute-start | bytes 24584 | tf_op jit(solution)/shard_map/ppermute | solution.py:51
  103.4 4.5 %collective-permute-start.25 = (f32[8,256]{1,0:T(8,128)S(1)}, f32[8,256]{1,0:T(8,128)S(1)}, u32[]{:S(2)}, u32[]{:S(2)}) collective-permute-start(f32[8,256]{1,0:T(8,128)S(1)} %add_add_fusion.1.refs_0_), channel_id=1, source_target_pairs={{0,2},{1,3},{2,0},{3,1},{4,6},{5,7},{6,4},{7,5},{8,10},{9,11},{10,... | collective-permute-start | bytes 24584 | tf_op jit(solution)/shard_map/ppermute | solution.py:51
  103.9 4.1 %collective-permute-start.24 = (f32[8,256]{1,0:T(8,128)S(1)}, f32[8,256]{1,0:T(8,128)S(1)}, u32[]{:S(2)}, u32[]{:S(2)}) collective-permute-start(f32[8,256]{1,0:T(8,128)S(1)} %add_add_fusion.1.refs_0_), channel_id=1, source_target_pairs={{0,1},{1,0},{2,3},{3,2},{4,5},{5,4},{6,7},{7,6},{8,9},{9,8},{10,11... | collective-permute-start | bytes 24584 | tf_op jit(solution)/shard_map/ppermute | solution.py:51

commit v7 on v6

--- a/solution.py
+++ b/solution.py
@@ -374,71 +374,85 @@
     )(x, *earlier)
 
 
-def apply_inverse(parts, block):
-    return sum(dot(x, block) for x in reversed(parts))
-
-
-def share_kernel(own, *refs):
-    received, (_, out) = refs[:-2], refs[-2:]
-    out[...] = (own[...] + sum(ref[...].astype(f32) for ref in received)).astype(bf16)
-
-
-def share_of(own, received, after):
+def share_kernel(inverse, own, *refs):
+    received, out = refs[:-1], refs[-1]
+    total = own[...] + sum(ref[...].astype(f32) for ref in received)
+    x_high, x_low = split(inverse[...], 2)
+    high, low = split(total, 2)
+    out[...] = (dot(x_high, low) + dot(x_low, high) + dot(x_high, high)).astype(bf16)
+
+
+def share_of(inverse, own, received):
     return pl.pallas_call(
         share_kernel,
         out_shape=shape(own.shape, bf16),
-        in_specs=[VMEM] * (1 + len(received)) + [ANY],
+        in_specs=[VMEM] * (2 + len(received)),
         out_specs=VMEM,
         compiler_params=params(8),
         name="share",
-    )(own, *received, after)
-
-
-def result_kernel(pairs, factor, momentum_too, weight_too, terms, buf0, buf1, ortho_ref, inverse, weight, *refs):
+    )(inverse, own, *received)
+
+
+def square_rows(blocks, ids, out_shape):
+    rows, r = out_shape
+    block_id = lax.broadcasted_iota(jnp.int32, out_shape, 0)
+    sums = jnp.zeros(out_shape, f32)
+    for block, i in zip(blocks, ids):
+        value = block[...].astype(f32)
+        total = jnp.sum(value * value, axis=1, keepdims=True)
+        total = jnp.transpose(jnp.broadcast_to(total, (r, 128)))[:rows, :]
+        sums = sums + jnp.where(block_id == i, total, 0.0)
+    return sums
+
+
+def block_ids(pairs):
+    row = lax.axis_index("row")
+    core = lax.bitwise_and(row, jnp.int32(1))
+    chip = lax.div(row, jnp.int32(2))
+    chips = lax.axis_size("row") // 2
+    return [half * chips + flip(chip, d) for d in pairs for half in (core, 1 - core)]
+
+
+def squares_kernel(pairs, before, *refs):
+    blocks, earlier, out = refs[: 2 * len(pairs)], refs[2 * len(pairs) : -1], refs[-1]
+    out[...] = square_rows(blocks, block_ids(pairs), out.shape) + sum(ref[...] for ref in earlier)
+
+
+def squares_of(pairs, blocks, earlier):
+    return pl.pallas_call(
+        functools.partial(squares_kernel, pairs, len(earlier)),
+        out_shape=shape(earlier[0].shape, f32),
+        in_specs=[VMEM] * (len(blocks) + len(earlier)),
+        out_specs=VMEM,
+        compiler_params=params(8),
+        name="squares",
+    )(*blocks, *earlier)
+
+
+def result_kernel(pairs, factor, momentum_too, weight_too, terms, buf0, buf1, ortho_ref, weight, *refs):
     squares, refs = refs[:terms], refs[terms:]
     blocks, rest = refs[: 2 * len(pairs)], refs[2 * len(pairs) :]
-    *outs, sums, mbuf, wbuf, vbuf, nbuf, lbuf, in_sems, out_sems, basis_sems = rest
+    *outs, sums, mbuf, wbuf, vbuf, nbuf, in_sems, out_sems = rest
     new_momentum = outs[-1] if momentum_too else None
     new_weight, basis = outs[-2 - momentum_too : len(outs) - momentum_too] if weight_too else (None, None)
     r, width = blocks[0].shape
-    tile = 256
-    tiles = width // tile
     count = len(blocks)
-    half = width * (lax.axis_size("row") // 2)
-    row = lax.axis_index("row")
-    core = lax.bitwise_and(row, jnp.int32(1))
-    chip = lax.div(row, jnp.int32(2))
-    starts = []
-    for d in pairs:
-        starts += [core * half + flip(chip, d) * width, (1 - core) * half + flip(chip, d) * width]
+    ids = block_ids(pairs)
+    cols = [pl.ds(pl.multiple_of(i * width, 128), width) for i in ids]
 
     def load(b):
-        cols = pl.ds(pl.multiple_of(starts[b], 128), width)
-        return pltpu.make_async_copy(weight.at[:, cols], wbuf.at[b % 2], in_sems.at[b % 2])
-
-    def store_basis(b):
-        cols = pl.ds(pl.multiple_of(starts[b], 128), width)
-        return pltpu.make_async_copy(nbuf.at[b % 2], basis.at[:, cols], basis_sems.at[b % 2])
-
-    def place(b, t):
-        return pl.ds(t * tile, tile), pl.ds(pl.multiple_of(starts[b] + t * tile, 128), tile)
-
-    def store_momentum(b, t):
-        at, there = place(b, t)
-        return pltpu.make_async_copy(mbuf.at[b % 2, :, at], new_momentum.at[:, there], out_sems.at[0, b % 2, t])
-
-    def store_weight(b, t):
-        at, there = place(b, t)
-        return pltpu.make_async_copy(vbuf.at[b % 2, :, at], new_weight.at[:, there], out_sems.at[1, b % 2, t])
-
-    def finish(b):
+        return pltpu.make_async_copy(weight.at[:, cols[b]], wbuf.at[b % 2], in_sems.at[b % 2])
+
+    def stores(b):
+        copies = []
+        if momentum_too:
+            copies.append((mbuf, new_momentum))
         if weight_too:
-            store_basis(b).wait()
-        for t in range(tiles):
-            if momentum_too:
-                store_momentum(b, t).wait()
-            if weight_too:
-                store_weight(b, t).wait()
+            copies += [(vbuf, new_weight), (nbuf, basis)]
+        return [
+            pltpu.make_async_copy(src.at[b % 2], dst.at[:, cols[b]], out_sems.at[k, b % 2])
+            for k, (src, dst) in enumerate(copies)
+        ]
 
     if weight_too:
         for b in range(2):
@@ -446,49 +460,46 @@
         total = jnp.sum(pair_up([ref[...] for ref in squares]), axis=0, keepdims=True)
         scale = lax.rsqrt(total / FF + epsilon)
         scale = jnp.transpose(jnp.broadcast_to(scale, (128, r)))[:, :1]
-    sums[...] = jnp.zeros_like(sums)
-    block_id = lax.broadcasted_iota(jnp.int32, sums.shape, 0)
-    parts = split(inverse[...], 2)
     depth = lax.axis_size("col")
     size = buf0.shape[0] // depth
+    m = ortho_ref.shape[0]
+    step = m // 2
     for b in range(count):
         k = b % 2
         if b >= 2:
-            finish(b - 2)
-        right = apply_inverse(parts, blocks[b][...])
+            for store in stores(b - 2):
+                store.wait()
+        if weight_too:
+            nbuf[k] = (blocks[b][...].astype(f32) * scale).astype(bf16)
         if momentum_too:
-            lbuf[k] = ((1.0 - momentum_decay) * right).astype(bf16)
-            total = jnp.sum(right * right, axis=1, keepdims=True)
-            total = jnp.transpose(jnp.broadcast_to(total, (r, 128)))[: sums.shape[0], :]
-            sums[...] += jnp.where(block_id == lax.div(starts[b], jnp.int32(width)), total, 0.0)
+            for lo in range(0, m, step):
+                correction = dot(ortho_ref[lo : lo + step, :], blocks[b][...])
+                for j in range(lo // size, (lo + step) // size):
+                    here = slice(j // 2 * size, (j // 2 + 1) * size)
+                    part = correction[j * size - lo : (j + 1) * size - lo]
+                    old = (buf0, buf1)[j % 2][here, cols[b]]
+                    mbuf[k, j * size : (j + 1) * size, :] = old - (1.0 - momentum_decay) * part
         if weight_too:
-            nbuf[k] = (right * scale).astype(bf16)
-            store_basis(b).start()
             load(b).wait()
-        for t in range(tiles):
-            at, there = place(b, t)
-            if momentum_too:
-                correction = dot(ortho_ref[...], lbuf[k, :, at])
-                for j in range(2 * depth):
-                    rows = slice(j * size, (j + 1) * size)
-                    here = slice(j // 2 * size, (j // 2 + 1) * size)
-                    mbuf[k, rows, at] = (buf0, buf1)[j % 2][here, there] - correction[rows]
-                store_momentum(b, t).start()
-            if weight_too:
-                change = dot(ortho_ref[...], nbuf[k, :, at])
-                vbuf[k, :, at] = (wbuf[k, :, at].astype(f32) - factor * change).astype(bf16)
-                store_weight(b, t).start()
+            for lo in range(0, m, step):
+                at = slice(lo, lo + step)
+                change = dot(ortho_ref[at, :], nbuf[k])
+                vbuf[k, at, :] = (wbuf[k, at, :].astype(f32) - factor * change).astype(bf16)
+        for store in stores(b):
+            store.start()
         if weight_too and b + 2 < count:
             load(b + 2).start()
+    sums[...] = square_rows(blocks, ids, sums.shape) if momentum_too else jnp.zeros_like(sums)
     for b in range(count - 2, count):
-        finish(b)
-
-
-def results(pairs, kinds, factor, bufs, ortho_bf, inverse, weight, squares, blocks, outs=(), after=()):
+        for store in stores(b):
+            store.wait()
+
+
+def results(pairs, kinds, factor, bufs, ortho_bf, weight, squares, blocks, outs=(), after=()):
     momentum_too, weight_too = kinds
     m, n = weight.shape
     r, width = blocks[0].shape
-    ins = [*map(keep, bufs), ortho_bf, inverse, stay(weight), *squares, *blocks, *after, *map(stay, outs)]
+    ins = [*map(keep, bufs), ortho_bf, stay(weight), *squares, *blocks, *after, *map(stay, outs)]
     at = len(ins) - len(outs)
     out_shape = []
     if weight_too:
@@ -499,7 +510,7 @@
     return pl.pallas_call(
         functools.partial(result_kernel, pairs, factor, momentum_too, weight_too, len(squares)),
         out_shape=[*out_shape, shape((max(8, n // width), r), f32)],
-        in_specs=[VMEM] * 4 + [ANY] + [VMEM] * (len(squares) + len(blocks)) + [ANY] * (len(after) + len(outs)),
+        in_specs=[VMEM] * 3 + [ANY] + [VMEM] * (len(squares) + len(blocks)) + [ANY] * (len(after) + len(outs)),
         out_specs=[ANY] * len(out_shape) + [VMEM],
         input_output_aliases={at + k: k for k in range(len(outs))},
         scratch_shapes=[
@@ -507,10 +518,8 @@
             pltpu.VMEM((2, w_slots, width), bf16),
             pltpu.VMEM((2, w_slots, width), bf16),
             pltpu.VMEM((2, r, width), bf16),
-            pltpu.VMEM((2, r, width), bf16),
             pltpu.SemaphoreType.DMA((2,)),
-            pltpu.SemaphoreType.DMA((2, 2, width // 256)),
-            pltpu.SemaphoreType.DMA((2,)),
+            pltpu.SemaphoreType.DMA((3, 2)),
         ],
         compiler_params=params(15),
         cost_estimate=cost(*[shape((m, width), f32)] * len(blocks) * (momentum_too + weight_too)),
@@ -577,11 +586,11 @@
     got = [swap(x, "row", 2 * (d + 1)) for d, x in enumerate(sent)]
     inverse = chol_inverse(g_mine, swap(g_mine, "row", 1))
 
-    share = share_of(own, got, inverse)
+    share = share_of(inverse, own, got)
     ortho_bf = ortho(inverse, lefts)
 
     factor = step_rate * math.sqrt(D / RANK)
-    common = (factor, bufs, ortho_bf, inverse, weight)
+    common = (factor, bufs, ortho_bf, weight)
     blocks = {0: share}
     for d in range(1, chips):
         if d & (d - 1) == 0:
@@ -610,9 +619,13 @@
         top, bottom = halves[d]
         block = jnp.concatenate([hand_on(top, sums), bottom], axis=0)
         pairs[d] = (block, swap(block, "row", 1))
-        momentum, sums = results((d,), (True, False), *common, (), pairs[d], [momentum])
-        squares.append(sums)
-    scales = exchange(sum(squares), "col", depth)
+    if far:
+        rest = [x for d in far for x in pairs[d]]
+        total = squares_of(tuple(far), rest, squares)
+        momentum, _ = results(tuple(far), (True, False), *common, (), rest, [momentum], [total])
+    else:
+        total = sum(squares)
+    scales = exchange(total, "col", depth)
     order = near + far
     rest = [x for d in order for x in pairs[d]]
     new_weight, new_basis, _ = results(tuple(order), (False, True), *common, scales, rest)

time: 122 us -> 121 us (level)
  waiting for transfers between devices: 29.7 us -> 28.3 us
    ppermute x27, waiting for transfers between devices: 29.7 us -> 28.3 us  [swap(): lax.ppermute(x, axis, [(i, i ^ d) for i in range(lax.axis_size(axis))])]
  transfers between devices with their start and end apart: 27 -> 27, of which waited for: 13 -> 12; matrix products, arithmetic and copies ran while one was open for 0% -> 0% of each run, Pallas kernels for 29% -> 31%
where the time goes in v7:
time: 121 us
  Pallas kernels  61.5 us (51%)
  starting transfers between devices  29.7 us (25%)
  waiting for transfers between devices  28.3 us (23%)
    ppermute x27, starting transfers between devices, swap(): lax.ppermute(x, axis, [(i, i ^ d) for i in range(lax.axis_size(axis))])  29.7 us
    ppermute x27, waiting for transfers between devices, swap(): lax.ppermute(x, axis, [(i, i ^ d) for i in range(lax.axis_size(axis))])  28.3 us
    pallas_call x4, Pallas kernels, results(): pl.pallas_call(functools.partial(result_kernel, pairs, factor, momentum_t...  26.9 us
    pallas_call x2, Pallas kernels, project(): pl.pallas_call(functools.partial(project_kernel, part, depth, width), out...  16.5 us
    pallas_call x1, Pallas kernels, chol_inverse(): pl.pallas_call(chol_inverse_kernel, out_shape=shape((n, n), f32), in_spec...  9.15 us
    pallas_call x1, Pallas kernels, first_product(): pl.pallas_call(functools.partial(first_kernel, depth, width), out_shape=(...  4.29 us
    pallas_call x2, Pallas kernels, last_product(): pl.pallas_call(functools.partial(last_kernel, depth, width, mine), out_sh...  2.45 us
  transfers between devices with their start and end apart: 27, of which 12 were waited for; matrix products, arithmetic and copies ran while one was open for 0% of the time, Pallas kernels for 31%

profile of v7, /device:TPU:0, one launch (start us, length us, event | category | flops | bytes accessed | tf_op | source)
XLA Modules:
  0.0 120.7 jit_solution(6032331703139562093)
XLA Ops:
  0.6 8.7 %project.2 = (f32[512,6144]{1,0:T(8,128)S(1)}, bf16[256,6144]{1,0:T(8,128)(2,1)S(1)}, f32[256,256]{1,0:T(8,128)S(1)}, bf16[256,256]{1,0:T(8,128)(2,1)S(1)}) custom-call(f32[1024,6144]{1,0:T(8,128)} %mom.3, bf16[1024,6144]{1,0:T(8,128)(2,1)} %grad.3, bf16[256,6144]{1,0:T(8,128)(2,1)} %basis.1), custom_call_target="tpu_custom_call" | custom-call | bytes 37748736 | tf_op jit(solution)/shard_map/project/pallas_call | solution.py:104
  9.4 3.1 %collective-permute-start.2 = (bf16[256,256]{1,0:T(8,128)(2,1)S(1)}, bf16[256,256]{1,0:T(8,128)(2,1)S(1)}, u32[]{:S(2)}, u32[]{:S(2)}) collective-permute-start(bf16[256,256]{1,0:T(8,128)(2,1)S(1)} %get-tuple-element.32.rest_0_), channel_id=1, source_target_pairs={{0,1},{1,0},{2,3},{3,2},{4,5},{5,4},{6,7},{7,6},{8,9},{9,8},{10,11... | collective-permute-start | bytes 393224 | tf_op jit(solution)/shard_map/ppermute | solution.py:51
  12.4 7.8 %project.3 = (f32[512,6144]{1,0:T(8,128)S(1)}, f32[256,256]{1,0:T(8,128)S(1)}, bf16[256,256]{1,0:T(8,128)(2,1)S(1)}) custom-call(f32[1024,6144]{1,0:T(8,128)} %mom.3, bf16[1024,6144]{1,0:T(8,128)(2,1)} %grad.3, bf16[256,6144]{1,0:T(8,128)(2,1)S(1)} %get-tuple-element.31.basis, bf16[256,256]{1,0:T(8,128)(2,1)S(1)} %get-tuple-element.32.rest_0_), custom_call_target="tpu_custom_call" | custom-call | bytes 37748736 | tf_op jit(solution)/shard_map/project/pallas_call | solution.py:104
  20.2 0.1 collective-permute-start
  20.4 3.1 %collective-permute-start.3 = (bf16[256,128]{1,0:T(8,128)(2,1)S(1)}, bf16[256,128]{1,0:T(8,128)(2,1)S(1)}, u32[]{:S(2)}, u32[]{:S(2)}) collective-permute-start(bf16[256,128]{1,0:T(8,128)(2,1)S(1)} %get-tuple-element.40), channel_id=1, source_target_pairs={{0,2},{1,3},{2,0},{3,1},{4,6},{5,7},{6,4},{7,5},{8,10},{9,11},{10,... | collective-permute-start | bytes 196616 | tf_op jit(solution)/shard_map/ppermute | solution.py:51
  23.4 3.2 %collective-permute-done.received = bf16[256,256]{1,0:T(8,128)(2,1)S(1)} collective-permute-done((bf16[256,256]{1,0:T(8,128)(2,1)S(1)}, bf16[256,256]{1,0:T(8,128)(2,1)S(1)}, u32[]{:S(2)}, u32[]{:S(2)}) %collective-permute-start) | collective-permute-done | bytes 131104 | tf_op jit(solution)/shard_map/ppermute | solution.py:51
  26.7 2.3 %collective-permute-start.1 = (bf16[256,128]{1,0:T(8,128)(2,1)S(1)}, bf16[256,128]{1,0:T(8,128)(2,1)S(1)}, u32[]{:S(2)}, u32[]{:S(2)}) collective-permute-start(bf16[256,128]{1,0:T(8,128)(2,1)S(1)} %get-tuple-element.37), channel_id=1, source_target_pairs={{0,2},{1,3},{2,0},{3,1},{4,6},{5,7},{6,4},{7,5},{8,10},{9,11},{10,... | collective-permute-start | bytes 196616 | tf_op jit(solution)/shard_map/ppermute | solution.py:51
  29.0 2.9 %collective-permute-done.1.received = bf16[256,128]{1,0:T(8,128)(2,1)S(1)} collective-permute-done((bf16[256,128]{1,0:T(8,128)(2,1)S(1)}, bf16[256,128]{1,0:T(8,128)(2,1)S(1)}, u32[]{:S(2)}, u32[]{:S(2)}) %collective-permute-start.1) | collective-permute-done | bytes 65568 | tf_op jit(solution)/shard_map/ppermute | solution.py:51
  32.0 2.5 %collective-permute-start.4 = (bf16[256,256]{1,0:T(8,128)(2,1)S(1)}, bf16[256,256]{1,0:T(8,128)(2,1)S(1)}, u32[]{:S(2)}, u32[]{:S(2)}) collective-permute-start(bf16[256,256]{1,0:T(8,128)(2,1)S(1)} %fold_last.3.rest_0_.refs_0_), channel_id=1, source_target_pairs={{0,2},{1,3},{2,0},{3,1},{4,6},{5,7},{6,4},{7,5},{8,10},{9,11},{10,... | collective-permute-start | bytes 393224 | tf_op jit(solution)/shard_map/ppermute | solution.py:51
  34.5 4.4 %collective-permute-done.4.rest_2_.refs_2_ = bf16[256,256]{1,0:T(8,128)(2,1)S(1)} collective-permute-done((bf16[256,256]{1,0:T(8,128)(2,1)S(1)}, bf16[256,256]{1,0:T(8,128)(2,1)S(1)}, u32[]{:S(2)}, u32[]{:S(2)}) %collective-permute-start.4) | collective-permute-done | bytes 131104 | tf_op jit(solution)/shard_map/ppermute | solution.py:51
  38.9 2.7 %collective-permute-done.6.rest_1_.refs_1_ = bf16[256,256]{1,0:T(8,128)(2,1)S(1)} collective-permute-done((bf16[256,256]{1,0:T(8,128)(2,1)S(1)}, bf16[256,256]{1,0:T(8,128)(2,1)S(1)}, u32[]{:S(2)}, u32[]{:S(2)}) %collective-permute-start.6) | collective-permute-done | bytes 131104 | tf_op jit(solution)/shard_map/ppermute | solution.py:51
  41.6 4.3 %first_product.1 = (f32[256,3072]{1,0:T(8,128)S(1)}, f32[256,3072]{1,0:T(8,128)S(1)}, f32[256,256]{1,0:T(8,128)S(1)}) custom-call(f32[512,6144]{1,0:T(8,128)S(1)} %get-tuple-element.30.buf0, f32[512,6144]{1,0:T(8,128)S(1)} %get-tuple-element.33.buf1, bf16[256,256]{1,0:T(8,128)(2,1)S(1)} %fold_last.3.rest_0_.refs_0_, ...), custom_call_target="tpu_custom_call" | custom-call | bytes 31457280 | tf_op jit(solution)/shard_map/first_product/pallas_call | solution.py:203
  45.9 0.3 gram.1
  46.2 0.1 collective-permute-start.7
  46.2 1.1 other_product.1.refs_0_
  47.4 0.2 collective-permute-done.7
  47.6 0.4 collective-permute-start.12
  48.0 2.4 %collective-permute-start.10 = (f32[128,256]{1,0:T(8,128)S(1)}, f32[128,256]{1,0:T(8,128)S(1)}, u32[]{:S(2)}, u32[]{:S(2)}) collective-permute-start(f32[128,256]{1,0:T(8,128)S(1)} %add.12.refs_1_.rest_0_._), channel_id=1, source_target_pairs={{0,24},{4,28},{8,16},{12,20},{16,8},{20,12},{24,0},{28,4},{1,25},{... | collective-permute-start | bytes 393224 | tf_op jit(solution)/shard_map/ppermute | solution.py:51
  50.4 0.5 collective-permute-start.9
  50.9 0.6 collective-permute-start.8
  51.5 1.3 %mine_product.1.mine = f32[256,3072]{1,0:T(8,128)S(1)} custom-call(f32[512,6144]{1,0:T(8,128)S(1)} %get-tuple-element.30.buf0, f32[512,6144]{1,0:T(8,128)S(1)} %get-tuple-element.33.buf1, f32[256,3072]{1,0:T(8,128)S(1)} %get-tuple-element.44.sums, bf16[256,256]{1,0:T(8,128)(2,1)S(1)} %collective-permute-done.5.left.refs_3_, ...), custom_call_target="tpu_custom_call" | custom-call | bytes 15728640 | tf_op jit(solution)/shard_map/mine_product/pallas_call | solution.py:253
  52.8 0.3 pair_sum.1
  53.1 1.5 %collective-permute-start.13 = (bf16[256,768]{1,0:T(8,128)(2,1)S(1)}, bf16[256,768]{1,0:T(8,128)(2,1)S(1)}, u32[]{:S(2)}, u32[]{:S(2)}) collective-permute-start(bf16[256,768]{1,0:T(8,128)(2,1)S(1)} %get-tuple-element.47), channel_id=1, source_target_pairs={{0,8},{4,12},{8,0},{12,4},{16,24},{20,28},{24,16},{28,20},{1,9},{5... | collective-permute-start | bytes 1179656 | tf_op jit(solution)/shard_map/ppermute | solution.py:51
  54.6 1.5 %collective-permute-start.14 = (bf16[256,768]{1,0:T(8,128)(2,1)S(1)}, bf16[256,768]{1,0:T(8,128)(2,1)S(1)}, u32[]{:S(2)}, u32[]{:S(2)}) collective-permute-start(bf16[256,768]{1,0:T(8,128)(2,1)S(1)} %get-tuple-element.48), channel_id=1, source_target_pairs={{0,16},{4,20},{8,24},{12,28},{16,0},{20,4},{24,8},{28,12},{1,17},{... | collective-permute-start | bytes 1179656 | tf_op jit(solution)/shard_map/ppermute | solution.py:51
  56.1 1.5 %collective-permute-start.15 = (bf16[256,768]{1,0:T(8,128)(2,1)S(1)}, bf16[256,768]{1,0:T(8,128)(2,1)S(1)}, u32[]{:S(2)}, u32[]{:S(2)}) collective-permute-start(bf16[256,768]{1,0:T(8,128)(2,1)S(1)} %get-tuple-element.49), channel_id=1, source_target_pairs={{0,24},{4,28},{8,16},{12,20},{16,8},{20,12},{24,0},{28,4},{1,25},{... | collective-permute-start | bytes 1179656 | tf_op jit(solution)/shard_map/ppermute | solution.py:51
  57.6 0.4 collective-permute-done.8
  58.1 0.1 collective-permute-start.11
  58.2 1.3 %collective-permute-done.11.other = f32[128,256]{1,0:T(8,128)S(1)} collective-permute-done((f32[128,256]{1,0:T(8,128)S(1)}, f32[128,256]{1,0:T(8,128)S(1)}, u32[]{:S(2)}, u32[]{:S(2)}) %collective-permute-start.11) | collective-permute-done | bytes 131104 | tf_op jit(solution)/shard_map/ppermute | solution.py:51
  59.5 9.1 %chol_inverse.1.inverse = f32[256,256]{1,0:T(8,128)S(1)} custom-call(f32[128,256]{1,0:T(8,128)S(1)} %add_add_fusion.mine, f32[128,256]{1,0:T(8,128)S(1)} %collective-permute-done.11.other), custom_call_target="tpu_custom_call" | custom-call | bytes 33554432 | tf_op jit(solution)/shard_map/chol_inverse/pallas_call | solution.py:330
  68.7 5.5 %collective-permute-done.15.refs_2_ = bf16[256,768]{1,0:T(8,128)(2,1)S(1)} collective-permute-done((bf16[256,768]{1,0:T(8,128)(2,1)S(1)}, bf16[256,768]{1,0:T(8,128)(2,1)S(1)}, u32[]{:S(2)}, u32[]{:S(2)}) %collective-permute-start.15) | collective-permute-done | bytes 393248 | tf_op jit(solution)/shard_map/ppermute | solution.py:51
  74.1 0.6 share.1.refs_0_.refs_4_
  74.8 1.5 %collective-permute-start.16 = (bf16[256,768]{1,0:T(8,128)(2,1)S(1)}, bf16[256,768]{1,0:T(8,128)(2,1)S(1)}, u32[]{:S(2)}, u32[]{:S(2)}) collective-permute-start(bf16[256,768]{1,0:T(8,128)(2,1)S(1)} %share.1.refs_0_.refs_4_), channel_id=1, source_target_pairs={{0,8},{4,12},{8,0},{12,4},{16,24},{20,28},{24,16},{28,20},{1,9},{5... | collective-permute-start | bytes 1179656 | tf_op jit(solution)/shard_map/ppermute | solution.py:51
  76.3 1.5 %collective-permute-start.20 = (bf16[256,768]{1,0:T(8,128)(2,1)S(1)}, bf16[256,768]{1,0:T(8,128)(2,1)S(1)}, u32[]{:S(2)}, u32[]{:S(2)}) collective-permute-start(bf16[256,768]{1,0:T(8,128)(2,1)S(1)} %share.1.refs_0_.refs_4_), channel_id=1, source_target_pairs={{0,16},{4,20},{8,24},{12,28},{16,0},{20,4},{24,8},{28,12},{1,17},{... | collective-permute-start | bytes 1179656 | tf_op jit(solution)/shard_map/ppermute | solution.py:51
  77.9 0.6 ortho.1.ortho_ref
  78.5 3.4 %results.4 = (f32[1024,6144]{1,0:T(8,128)}, f32[8,256]{1,0:T(8,128)S(1)}) custom-call(f32[512,6144]{1,0:T(8,128)S(1)} %get-tuple-element.30.buf0, f32[512,6144]{1,0:T(8,128)S(1)} %get-tuple-element.33.buf1, bf16[1024,256]{1,0:T(8,128)(2,1)S(1)} %ortho.1.ortho_ref, bf16[1024,6144]{1,0:T(8,128)(2,1)} %weight.7, bf16[256,768]{1,0:T(8,128)(2,1)S(1)} %share.1.refs_0_.refs_4_, ...), custom_call_target="tpu_custom_call" | custom-call | bytes 6291456 | tf_op jit(solution)/shard_map/results/pallas_call | solution.py:510
  81.9 4.4 %collective-permute-done.16.refs_0_ = bf16[256,768]{1,0:T(8,128)(2,1)S(1)} collective-permute-done((bf16[256,768]{1,0:T(8,128)(2,1)S(1)}, bf16[256,768]{1,0:T(8,128)(2,1)S(1)}, u32[]{:S(2)}, u32[]{:S(2)}) %collective-permute-start.16) | collective-permute-done | bytes 393248 | tf_op jit(solution)/shard_map/ppermute | solution.py:51
  86.3 1.2 collective-permute-done.20.refs_0_
  87.5 1.6 %collective-permute-start.18 = (bf16[128,768]{1,0:T(8,128)(2,1)S(1)}, bf16[128,768]{1,0:T(8,128)(2,1)S(1)}, u32[]{:S(2)}, u32[]{:S(2)}) collective-permute-start(bf16[128,768]{1,0:T(8,128)(2,1)S(1)} %slice.8), channel_id=1, source_target_pairs={{0,16},{4,20},{8,24},{12,28},{16,0},{20,4},{24,8},{28,12},{1,17},{... | collective-permute-start | bytes 589832 | tf_op jit(solution)/shard_map/ppermute | solution.py:51
  89.2 0.9 collective-permute-start.22
  90.0 5.9 %results.5 = (f32[1024,6144]{1,0:T(8,128)}, f32[8,256]{1,0:T(8,128)S(1)}) custom-call(f32[512,6144]{1,0:T(8,128)S(1)} %get-tuple-element.30.buf0, f32[512,6144]{1,0:T(8,128)S(1)} %get-tuple-element.33.buf1, bf16[1024,256]{1,0:T(8,128)(2,1)S(1)} %ortho.1.ortho_ref, bf16[1024,6144]{1,0:T(8,128)(2,1)} %weight.7, ...), custom_call_target="tpu_custom_call", output_to_operand_aliasing={{0}: (8, {})} | custom-call | bytes 12582912 | tf_op jit(solution)/shard_map/results/pallas_call | solution.py:510
  95.9 0.3 collective-permute-done.22
  96.4 1.7 %collective-permute-done.23.refs_1_.refs_11_ = bf16[256,768]{1,0:T(8,128)(2,1)S(1)} collective-permute-done((bf16[256,768]{1,0:T(8,128)(2,1)S(1)}, bf16[256,768]{1,0:T(8,128)(2,1)S(1)}, u32[]{:S(2)}, u32[]{:S(2)}) %collective-permute-start.23) | collective-permute-done | bytes 393248 | tf_op jit(solution)/shard_map/ppermute | solution.py:51
  98.1 0.3 squares.1.refs_0_.refs_2_
  98.3 1.8 %collective-permute-start.26 = (f32[8,256]{1,0:T(8,128)S(1)}, f32[8,256]{1,0:T(8,128)S(1)}, u32[]{:S(2)}, u32[]{:S(2)}) collective-permute-start(f32[8,256]{1,0:T(8,128)S(1)} %squares.1.refs_0_.refs_2_), channel_id=1, source_target_pairs={{0,3},{1,2},{2,1},{3,0},{4,7},{5,6},{6,5},{7,4},{8,11},{9,10},{10,... | collective-permute-start | bytes 24584 | tf_op jit(solution)/shard_map/ppermute | solution.py:51
  100.2 0.5 collective-permute-start.25
  100.7 2.1 %collective-permute-start.24 = (f32[8,256]{1,0:T(8,128)S(1)}, f32[8,256]{1,0:T(8,128)S(1)}, u32[]{:S(2)}, u32[]{:S(2)}) collective-permute-start(f32[8,256]{1,0:T(8,128)S(1)} %squares.1.refs_0_.refs_2_), channel_id=1, source_target_pairs={{0,1},{1,0},{2,3},{3,2},{4,5},{5,4},{6,7},{7,6},{8,9},{9,8},{10,11... | collective-permute-start | bytes 24584 | tf_op jit(solution)/shard_map/ppermute | solution.py:51
  102.8 4.0 %results.7 = (f32[1024,6144]{1,0:T(8,128)}, f32[8,256]{1,0:T(8,128)}) custom-call(f32[512,6144]{1,0:T(8,128)S(1)} %get-tuple-element.30.buf0, f32[512,6144]{1,0:T(8,128)S(1)} %get-tuple-element.33.buf1, bf16[1024,256]{1,0:T(8,128)(2,1)S(1)} %ortho.1.ortho_ref, bf16[1024,6144]{1,0:T(8,128)(2,1)} %weight.7, ...), custom_call_target="tpu_custom_call", output_to_operand_aliasing={{0}: (7, {})} | custom-call | bytes 6291456 | tf_op jit(solution)/shard_map/results/pallas_call | solution.py:510
  106.8 13.7 %results.6 = (bf16[1024,6144]{1,0:T(8,128)(2,1)}, bf16[256,6144]{1,0:T(8,128)(2,1)}, f32[8,256]{1,0:T(8,128)}) custom-call(f32[512,6144]{1,0:T(8,128)S(1)} %get-tuple-element.30.buf0, f32[512,6144]{1,0:T(8,128)S(1)} %get-tuple-element.33.buf1, bf16[1024,256]{1,0:T(8,128)(2,1)S(1)} %ortho.1.ortho_ref, bf16[1024,6144]{1,0:T(8,128)(2,1)} %weight.7, ...), custom_call_target="tpu_custom_call" | custom-call | bytes 25165824 | tf_op jit(solution)/shard_map/results/pallas_call | solution.py:510
  (34 shorter events, 0.4 us)
Async XLA Ops:
  9.4 11.0 %collective-permute-start.2 = (bf16[256,256]{1,0:T(8,128)(2,1)S(1)}, bf16[256,256]{1,0:T(8,128)(2,1)S(1)}, u32[]{:S(2)}, u32[]{:S(2)}) collective-permute-start(bf16[256,256]{1,0:T(8,128)(2,1)S(1)} %get-tuple-element.32.rest_0_), channel_id=1, source_target_pairs={{0,1},{1,0},{2,3},{3,2},{4,5},{5,4},{6,7},{7,6},{8,9},{9,8},{10,11... | collective-permute-start | bytes 393224 | tf_op jit(solution)/shard_map/ppermute | solution.py:51
  20.2 6.4 %collective-permute-start = (bf16[256,256]{1,0:T(8,128)(2,1)S(1)}, bf16[256,256]{1,0:T(8,128)(2,1)S(1)}, u32[]{:S(2)}, u32[]{:S(2)}) collective-permute-start(bf16[256,256]{1,0:T(8,128)(2,1)S(1)} %get-tuple-element.35), channel_id=1, source_target_pairs={{0,1},{1,0},{2,3},{3,2},{4,5},{5,4},{6,7},{7,6},{8,9},{9,8},{10,11... | collective-permute-start | bytes 393224 | tf_op jit(solution)/shard_map/ppermute | solution.py:51
  20.4 8.7 %collective-permute-start.3 = (bf16[256,128]{1,0:T(8,128)(2,1)S(1)}, bf16[256,128]{1,0:T(8,128)(2,1)S(1)}, u32[]{:S(2)}, u32[]{:S(2)}) collective-permute-start(bf16[256,128]{1,0:T(8,128)(2,1)S(1)} %get-tuple-element.40), channel_id=1, source_target_pairs={{0,2},{1,3},{2,0},{3,1},{4,6},{5,7},{6,4},{7,5},{8,10},{9,11},{10,... | collective-permute-start | bytes 196616 | tf_op jit(solution)/shard_map/ppermute | solution.py:51
  26.7 5.2 %collective-permute-start.1 = (bf16[256,128]{1,0:T(8,128)(2,1)S(1)}, bf16[256,128]{1,0:T(8,128)(2,1)S(1)}, u32[]{:S(2)}, u32[]{:S(2)}) collective-permute-start(bf16[256,128]{1,0:T(8,128)(2,1)S(1)} %get-tuple-element.37), channel_id=1, source_target_pairs={{0,2},{1,3},{2,0},{3,1},{4,6},{5,7},{6,4},{7,5},{8,10},{9,11},{10,... | collective-permute-start | bytes 196616 | tf_op jit(solution)/shard_map/ppermute | solution.py:51
  32.0 6.9 %collective-permute-start.4 = (bf16[256,256]{1,0:T(8,128)(2,1)S(1)}, bf16[256,256]{1,0:T(8,128)(2,1)S(1)}, u32[]{:S(2)}, u32[]{:S(2)}) collective-permute-start(bf16[256,256]{1,0:T(8,128)(2,1)S(1)} %fold_last.3.rest_0_.refs_0_), channel_id=1, source_target_pairs={{0,2},{1,3},{2,0},{3,1},{4,6},{5,7},{6,4},{7,5},{8,10},{9,11},{10,... | collective-permute-start | bytes 393224 | tf_op jit(solution)/shard_map/ppermute | solution.py:51
  34.5 7.1 %collective-permute-start.6 = (bf16[256,256]{1,0:T(8,128)(2,1)S(1)}, bf16[256,256]{1,0:T(8,128)(2,1)S(1)}, u32[]{:S(2)}, u32[]{:S(2)}) collective-permute-start(bf16[256,256]{1,0:T(8,128)(2,1)S(1)} %fold_last.3.rest_0_.refs_0_), channel_id=1, source_target_pairs={{0,1},{1,0},{2,3},{3,2},{4,5},{5,4},{6,7},{7,6},{8,9},{9,8},{10,11... | collective-permute-start | bytes 393224 | tf_op jit(solution)/shard_map/ppermute | solution.py:51
  38.8 7.0 %collective-permute-start.5 = (bf16[256,256]{1,0:T(8,128)(2,1)S(1)}, bf16[256,256]{1,0:T(8,128)(2,1)S(1)}, u32[]{:S(2)}, u32[]{:S(2)}) collective-permute-start(bf16[256,256]{1,0:T(8,128)(2,1)S(1)} %collective-permute-done.4.rest_2_.refs_2_), channel_id=1, source_target_pairs={{0,1},{1,0},{2,3},{3,2},{4,5},{5,4},{6,7},{7,6},{8,9},{9,8},{10,11... | collective-permute-start | bytes 393224 | tf_op jit(solution)/shard_map/ppermute | solution.py:51
  46.2 1.4 %collective-permute-start.7 = (f32[128,256]{1,0:T(8,128)S(1)}, f32[128,256]{1,0:T(8,128)S(1)}, u32[]{:S(2)}, u32[]{:S(2)}) collective-permute-start(f32[128,256]{1,0:T(8,128)S(1)} %get-tuple-element.43), channel_id=1, source_target_pairs={{0,4},{4,0},{8,12},{12,8},{16,20},{20,16},{24,28},{28,24},{1,5},{5... | collective-permute-start | bytes 393224 | tf_op jit(solution)/shard_map/ppermute | solution.py:51
  47.6 5.2 %collective-permute-start.12 = (bf16[256,3072]{1,0:T(8,128)(2,1)S(1)}, bf16[256,3072]{1,0:T(8,128)(2,1)S(1)}, u32[]{:S(2)}, u32[]{:S(2)}) collective-permute-start(bf16[256,3072]{1,0:T(8,128)(2,1)S(1)} %hand_on.4.rest_1_), channel_id=1, source_target_pairs={{0,4},{4,0},{8,12},{12,8},{16,20},{20,16},{24,28},{28,24},{1,5},{5... | collective-permute-start | bytes 4718600 | tf_op jit(solution)/shard_map/ppermute | solution.py:51
  48.0 8.2 %collective-permute-start.10 = (f32[128,256]{1,0:T(8,128)S(1)}, f32[128,256]{1,0:T(8,128)S(1)}, u32[]{:S(2)}, u32[]{:S(2)}) collective-permute-start(f32[128,256]{1,0:T(8,128)S(1)} %add.12.refs_1_.rest_0_._), channel_id=1, source_target_pairs={{0,24},{4,28},{8,16},{12,20},{16,8},{20,12},{24,0},{28,4},{1,25},{... | collective-permute-start | bytes 393224 | tf_op jit(solution)/shard_map/ppermute | solution.py:51
  50.4 7.3 %collective-permute-start.9 = (f32[128,256]{1,0:T(8,128)S(1)}, f32[128,256]{1,0:T(8,128)S(1)}, u32[]{:S(2)}, u32[]{:S(2)}) collective-permute-start(f32[128,256]{1,0:T(8,128)S(1)} %add.12.refs_1_.rest_0_._), channel_id=1, source_target_pairs={{0,16},{4,20},{8,24},{12,28},{16,0},{20,4},{24,8},{28,12},{1,17},{... | collective-permute-start | bytes 393224 | tf_op jit(solution)/shard_map/ppermute | solution.py:51
  50.9 7.2 %collective-permute-start.8 = (f32[128,256]{1,0:T(8,128)S(1)}, f32[128,256]{1,0:T(8,128)S(1)}, u32[]{:S(2)}, u32[]{:S(2)}) collective-permute-start(f32[128,256]{1,0:T(8,128)S(1)} %add.12.refs_1_.rest_0_._), channel_id=1, source_target_pairs={{0,8},{4,12},{8,0},{12,4},{16,24},{20,28},{24,16},{28,20},{1,9},{5... | collective-permute-start | bytes 393224 | tf_op jit(solution)/shard_map/ppermute | solution.py:51
  53.1 15.5 %collective-permute-start.13 = (bf16[256,768]{1,0:T(8,128)(2,1)S(1)}, bf16[256,768]{1,0:T(8,128)(2,1)S(1)}, u32[]{:S(2)}, u32[]{:S(2)}) collective-permute-start(bf16[256,768]{1,0:T(8,128)(2,1)S(1)} %get-tuple-element.47), channel_id=1, source_target_pairs={{0,8},{4,12},{8,0},{12,4},{16,24},{20,28},{24,16},{28,20},{1,9},{5... | collective-permute-start | bytes 1179656 | tf_op jit(solution)/shard_map/ppermute | solution.py:51
  54.6 14.0 %collective-permute-start.14 = (bf16[256,768]{1,0:T(8,128)(2,1)S(1)}, bf16[256,768]{1,0:T(8,128)(2,1)S(1)}, u32[]{:S(2)}, u32[]{:S(2)}) collective-permute-start(bf16[256,768]{1,0:T(8,128)(2,1)S(1)} %get-tuple-element.48), channel_id=1, source_target_pairs={{0,16},{4,20},{8,24},{12,28},{16,0},{20,4},{24,8},{28,12},{1,17},{... | collective-permute-start | bytes 1179656 | tf_op jit(solution)/shard_map/ppermute | solution.py:51
  56.1 18.0 %collective-permute-start.15 = (bf16[256,768]{1,0:T(8,128)(2,1)S(1)}, bf16[256,768]{1,0:T(8,128)(2,1)S(1)}, u32[]{:S(2)}, u32[]{:S(2)}) collective-permute-start(bf16[256,768]{1,0:T(8,128)(2,1)S(1)} %get-tuple-element.49), channel_id=1, source_target_pairs={{0,24},{4,28},{8,16},{12,20},{16,8},{20,12},{24,0},{28,4},{1,25},{... | collective-permute-start | bytes 1179656 | tf_op jit(solution)/shard_map/ppermute | solution.py:51
  58.1 1.4 %collective-permute-start.11 = (f32[128,256]{1,0:T(8,128)S(1)}, f32[128,256]{1,0:T(8,128)S(1)}, u32[]{:S(2)}, u32[]{:S(2)}) collective-permute-start(f32[128,256]{1,0:T(8,128)S(1)} %add_add_fusion.mine), channel_id=1, source_target_pairs={{0,4},{4,0},{8,12},{12,8},{16,20},{20,16},{24,28},{28,24},{1,5},{5... | collective-permute-start | bytes 393224 | tf_op jit(solution)/shard_map/ppermute | solution.py:51
  74.7 3.8 %collective-permute-start.17 = (bf16[256,768]{1,0:T(8,128)(2,1)S(1)}, bf16[256,768]{1,0:T(8,128)(2,1)S(1)}, u32[]{:S(2)}, u32[]{:S(2)}) collective-permute-start(bf16[256,768]{1,0:T(8,128)(2,1)S(1)} %share.1.refs_0_.refs_4_), channel_id=1, source_target_pairs={{0,4},{4,0},{8,12},{12,8},{16,20},{20,16},{24,28},{28,24},{1,5},{5... | collective-permute-start | bytes 1179656 | tf_op jit(solution)/shard_map/ppermute | solution.py:51
  74.8 11.5 %collective-permute-start.16 = (bf16[256,768]{1,0:T(8,128)(2,1)S(1)}, bf16[256,768]{1,0:T(8,128)(2,1)S(1)}, u32[]{:S(2)}, u32[]{:S(2)}) collective-permute-start(bf16[256,768]{1,0:T(8,128)(2,1)S(1)} %share.1.refs_0_.refs_4_), channel_id=1, source_target_pairs={{0,8},{4,12},{8,0},{12,4},{16,24},{20,28},{24,16},{28,20},{1,9},{5... | collective-permute-start | bytes 1179656 | tf_op jit(solution)/shard_map/ppermute | solution.py:51
  76.3 11.2 %collective-permute-start.20 = (bf16[256,768]{1,0:T(8,128)(2,1)S(1)}, bf16[256,768]{1,0:T(8,128)(2,1)S(1)}, u32[]{:S(2)}, u32[]{:S(2)}) collective-permute-start(bf16[256,768]{1,0:T(8,128)(2,1)S(1)} %share.1.refs_0_.refs_4_), channel_id=1, source_target_pairs={{0,16},{4,20},{8,24},{12,28},{16,0},{20,4},{24,8},{28,12},{1,17},{... | collective-permute-start | bytes 1179656 | tf_op jit(solution)/shard_map/ppermute | solution.py:51
  86.3 3.7 %collective-permute-start.19 = (bf16[256,768]{1,0:T(8,128)(2,1)S(1)}, bf16[256,768]{1,0:T(8,128)(2,1)S(1)}, u32[]{:S(2)}, u32[]{:S(2)}) collective-permute-start(bf16[256,768]{1,0:T(8,128)(2,1)S(1)} %hand_on.5.refs_0_.refs_6_), channel_id=1, source_target_pairs={{0,4},{4,0},{8,12},{12,8},{16,20},{20,16},{24,28},{28,24},{1,5},{5... | collective-permute-start | bytes 1179656 | tf_op jit(solution)/shard_map/ppermute | solution.py:51
  87.5 2.5 %collective-permute-start.21 = (bf16[256,768]{1,0:T(8,128)(2,1)S(1)}, bf16[256,768]{1,0:T(8,128)(2,1)S(1)}, u32[]{:S(2)}, u32[]{:S(2)}) collective-permute-start(bf16[256,768]{1,0:T(8,128)(2,1)S(1)} %hand_on.6.refs_2_.refs_8_), channel_id=1, source_target_pairs={{0,4},{4,0},{8,12},{12,8},{16,20},{20,16},{24,28},{28,24},{1,5},{5... | collective-permute-start | bytes 1179656 | tf_op jit(solution)/shard_map/ppermute | solution.py:51
  87.5 8.4 %collective-permute-start.18 = (bf16[128,768]{1,0:T(8,128)(2,1)S(1)}, bf16[128,768]{1,0:T(8,128)(2,1)S(1)}, u32[]{:S(2)}, u32[]{:S(2)}) collective-permute-start(bf16[128,768]{1,0:T(8,128)(2,1)S(1)} %slice.8), channel_id=1, source_target_pairs={{0,16},{4,20},{8,24},{12,28},{16,0},{20,4},{24,8},{28,12},{1,17},{... | collective-permute-start | bytes 589832 | tf_op jit(solution)/shard_map/ppermute | solution.py:51
  89.2 7.1 %collective-permute-start.22 = (bf16[128,768]{1,0:T(8,128)(2,1)S(1)}, bf16[128,768]{1,0:T(8,128)(2,1)S(1)}, u32[]{:S(2)}, u32[]{:S(2)}) collective-permute-start(bf16[128,768]{1,0:T(8,128)(2,1)S(1)} %slice.9), channel_id=1, source_target_pairs={{0,8},{4,12},{8,0},{12,4},{16,24},{20,28},{24,16},{28,20},{1,9},{5... | collective-permute-start | bytes 589832 | tf_op jit(solution)/shard_map/ppermute | solution.py:51
  96.3 1.8 %collective-permute-start.23 = (bf16[256,768]{1,0:T(8,128)(2,1)S(1)}, bf16[256,768]{1,0:T(8,128)(2,1)S(1)}, u32[]{:S(2)}, u32[]{:S(2)}) collective-permute-start(bf16[256,768]{1,0:T(8,128)(2,1)S(1)} %pad_maximum_fusion.refs_0_.refs_10_), channel_id=1, source_target_pairs={{0,4},{4,0},{8,12},{12,8},{16,20},{20,16},{24,28},{28,24},{1,5},{5... | collective-permute-start | bytes 1179656 | tf_op jit(solution)/shard_map/ppermute | solution.py:51
  98.3 8.4 %collective-permute-start.26 = (f32[8,256]{1,0:T(8,128)S(1)}, f32[8,256]{1,0:T(8,128)S(1)}, u32[]{:S(2)}, u32[]{:S(2)}) collective-permute-start(f32[8,256]{1,0:T(8,128)S(1)} %squares.1.refs_0_.refs_2_), channel_id=1, source_target_pairs={{0,3},{1,2},{2,1},{3,0},{4,7},{5,6},{6,5},{7,4},{8,11},{9,10},{10,... | collective-permute-start | bytes 24584 | tf_op jit(solution)/shard_map/ppermute | solution.py:51
  100.2 6.6 %collective-permute-start.25 = (f32[8,256]{1,0:T(8,128)S(1)}, f32[8,256]{1,0:T(8,128)S(1)}, u32[]{:S(2)}, u32[]{:S(2)}) collective-permute-start(f32[8,256]{1,0:T(8,128)S(1)} %squares.1.refs_0_.refs_2_), channel_id=1, source_target_pairs={{0,2},{1,3},{2,0},{3,1},{4,6},{5,7},{6,4},{7,5},{8,10},{9,11},{10,... | collective-permute-start | bytes 24584 | tf_op jit(solution)/shard_map/ppermute | solution.py:51
  100.7 6.1 %collective-permute-start.24 = (f32[8,256]{1,0:T(8,128)S(1)}, f32[8,256]{1,0:T(8,128)S(1)}, u32[]{:S(2)}, u32[]{:S(2)}) collective-permute-start(f32[8,256]{1,0:T(8,128)S(1)} %squares.1.refs_0_.refs_2_), channel_id=1, source_target_pairs={{0,1},{1,0},{2,3},{3,2},{4,5},{5,4},{6,7},{7,6},{8,9},{9,8},{10,11... | collective-permute-start | bytes 24584 | tf_op jit(solution)/shard_map/ppermute | solution.py:51

commit v8 on v5

--- a/solution.py
+++ b/solution.py
@@ -178,6 +178,14 @@
     return jnp.concatenate([buf[at, cols].astype(bf16) for at in rows for buf in bufs], axis=0)
 
 
+def early(depth):
+    return (0, depth // 2)
+
+
+def late(depth):
+    return tuple(d for d in range(depth) if d not in early(depth))
+
+
 def first_kernel(depth, width, buf0, buf1, *rest):
     lefts, (other, mine, gram, whole) = rest[:-4], rest[-4:]
     core = lax.bitwise_and(lax.axis_index("row"), jnp.int32(1))
@@ -190,7 +198,7 @@
 
         def step(k, carry, out=out, half=half):
             cols = pl.ds(pl.multiple_of(half * size + k * width, 128), width)
-            b = buffer_rows((buf0, buf1), range(len(lefts)), depth, cols)
+            b = buffer_rows((buf0, buf1), early(depth), depth, cols)
             out[:, pl.ds(pl.multiple_of(k * width, 128), width)] = dot(whole[...], b)
             return carry
 
@@ -212,53 +220,59 @@
     )(*map(keep, bufs), *lefts)
 
 
-def gram_kernel(left, sums, g_mine, g_other, total):
+def gram_kernel(sums, *rest):
+    lefts, (g_mine, g_other, total) = rest[:-3], rest[-3:]
     core = lax.bitwise_and(lax.axis_index("row"), jnp.int32(1))
-    total[...] = sums[...] + dot(left[...], left[...], ((1,), (1,)))
+    total[...] = sums[...] + sum(dot(ref[...], ref[...], ((1,), (1,))) for ref in lefts)
     h = g_mine.shape[0]
     g_mine[...] = total[pl.ds(pl.multiple_of(core * h, h), h), :]
     g_other[...] = total[pl.ds(pl.multiple_of((1 - core) * h, h), h), :]
 
 
-def gram(left, sums):
-    r = left.shape[0]
+def gram(lefts, sums):
+    r = lefts[0].shape[0]
     return pl.pallas_call(
         gram_kernel,
         out_shape=[shape((r // 2, r), f32)] * 2,
-        in_specs=[VMEM, VMEM],
+        in_specs=[VMEM] * (1 + len(lefts)),
         out_specs=[VMEM] * 2,
         scratch_shapes=[pltpu.VMEM((r, r), f32)],
         compiler_params=params(8),
         name="gram",
-    )(left, sums)
-
-
-def last_kernel(depth, width, mine, buf0, buf1, sums, left, *rest):
-    out = rest[-1]
+    )(sums, *lefts)
+
+
+def last_kernel(depth, width, mine, buf0, buf1, sums, *rest):
+    lefts, (*_, out, whole) = rest[: len(late(depth))], rest[len(late(depth)) :]
     core = lax.bitwise_and(lax.axis_index("row"), jnp.int32(1))
     half = core if mine else 1 - core
     size = out.shape[1]
+    block = lefts[0].shape[1]
+    for k, ref in enumerate(lefts):
+        whole[:, k * block : (k + 1) * block] = ref[...]
 
     def step(k, carry):
         cols = pl.ds(pl.multiple_of(half * size + k * width, 128), width)
         at = pl.ds(pl.multiple_of(k * width, 128), width)
-        b = buffer_rows((buf0, buf1), [depth - 1], depth, cols)
-        out[:, at] = (sums[:, at] + dot(left[...], b)).astype(out.dtype)
+        b = buffer_rows((buf0, buf1), late(depth), depth, cols)
+        out[:, at] = (sums[:, at] + dot(whole[...], b)).astype(out.dtype)
         return carry
 
     lax.fori_loop(0, size // width, step, 0)
 
 
-def last_product(bufs, sums, left, depth, width, mine, *after):
+def last_product(bufs, sums, lefts, depth, width, mine, *after):
+    r, block = lefts[0].shape
     return pl.pallas_call(
         functools.partial(last_kernel, depth, width, mine),
         out_shape=shape(sums.shape, f32 if mine else bf16),
-        in_specs=[VMEM] * 4 + [ANY] * len(after),
+        in_specs=[VMEM] * (3 + len(lefts)) + [ANY] * len(after),
         out_specs=VMEM,
+        scratch_shapes=[pltpu.VMEM((r, block * len(lefts)), bf16)],
         compiler_params=params(8),
         cost_estimate=cost(*bufs[:1], sums),
         name="mine_product" if mine else "other_product",
-    )(*map(keep, bufs), sums, left, *after)
+    )(*map(keep, bufs), sums, *lefts, *after)
 
 
 def pair_sum_kernel(chips, mine, received, _, *outs):
@@ -374,23 +388,34 @@
     )(x, *earlier)
 
 
-def apply_inverse(parts, block):
-    return sum(dot(x, block) for x in reversed(parts))
+def block_ids(pairs):
+    row = lax.axis_index("row")
+    core = lax.bitwise_and(row, jnp.int32(1))
+    chip = lax.div(row, jnp.int32(2))
+    chips = lax.axis_size("row") // 2
+    return [half * chips + flip(chip, d) for d in pairs for half in (core, 1 - core)]
 
 
 def share_kernel(inverse, own, *refs):
     received, (out, squares) = refs[:-2], refs[-2:]
-    out[...] = (own[...] + sum(ref[...].astype(f32) for ref in received)).astype(bf16)
-    value = apply_inverse(split(inverse[...], 2), out[...])
-    total = jnp.sum(value * value, axis=1, keepdims=True)
-    squares[...] = jnp.transpose(jnp.broadcast_to(total, (total.shape[0], 128)))[:8, :]
+    total = own[...] + sum(ref[...].astype(f32) for ref in received)
+    x_high, x_low = split(inverse[...], 2)
+    high, low = split(total, 2)
+    right = dot(x_high, low) + dot(x_low, high) + dot(x_high, high)
+    out[...] = right.astype(bf16)
+    r = out.shape[0]
+    sums = jnp.sum(right * right, axis=1, keepdims=True)
+    sums = jnp.transpose(jnp.broadcast_to(sums, (r, 128)))[: squares.shape[0], :]
+    block_id = lax.broadcasted_iota(jnp.int32, squares.shape, 0)
+    squares[...] = jnp.where(block_id == block_ids((0,))[0], sums, 0.0)
 
 
 def share_of(inverse, own, received):
-    r = own.shape[0]
+    r, width = own.shape
+    rows = max(8, lax.axis_size("row"))
     return pl.pallas_call(
         share_kernel,
-        out_shape=(shape(own.shape, bf16), shape((8, r), f32)),
+        out_shape=(shape((r, width), bf16), shape((rows, r), f32)),
         in_specs=[VMEM] * (2 + len(received)),
         out_specs=(VMEM, VMEM),
         compiler_params=params(8),
@@ -398,20 +423,14 @@
     )(inverse, own, *received)
 
 
-def result_kernel(pairs, factor, buf0, buf1, ortho_ref, inverse, squares, weight, *refs):
+def result_kernel(pairs, factor, buf0, buf1, ortho_ref, squares, weight, *refs):
     blocks, rest = refs[: 2 * len(pairs)], refs[2 * len(pairs) :]
-    *_, new_weight, new_momentum, basis, token, mbuf, wbuf, vbuf, nbuf, lbuf, in_sems, out_sems, basis_sems = rest
+    *_, new_weight, new_momentum, basis, token, mbuf, wbuf, vbuf, nbuf, in_sems, out_sems, basis_sems = rest
     r, width = blocks[0].shape
     tile = 256
     tiles = width // tile
     count = len(blocks)
-    half = width * (lax.axis_size("row") // 2)
-    row = lax.axis_index("row")
-    core = lax.bitwise_and(row, jnp.int32(1))
-    chip = lax.div(row, jnp.int32(2))
-    starts = []
-    for d in pairs:
-        starts += [core * half + flip(chip, d) * width, (1 - core) * half + flip(chip, d) * width]
+    starts = [i * width for i in block_ids(pairs)]
 
     def load(b):
         cols = pl.ds(pl.multiple_of(starts[b], 128), width)
@@ -424,72 +443,66 @@
     def place(b, t):
         return pl.ds(t * tile, tile), pl.ds(pl.multiple_of(starts[b] + t * tile, 128), tile)
 
-    def store_momentum(b, t):
+    def stores(b, t):
         at, there = place(b, t)
-        return pltpu.make_async_copy(mbuf.at[b % 2, :, at], new_momentum.at[:, there], out_sems.at[0, b % 2, t])
-
-    def store_weight(b, t):
-        at, there = place(b, t)
-        return pltpu.make_async_copy(vbuf.at[b % 2, :, at], new_weight.at[:, there], out_sems.at[1, b % 2, t])
+        return (
+            pltpu.make_async_copy(mbuf.at[b % 2, :, at], new_momentum.at[:, there], out_sems.at[0, b % 2, t]),
+            pltpu.make_async_copy(vbuf.at[b % 2, :, at], new_weight.at[:, there], out_sems.at[1, b % 2, t]),
+        )
 
     def finish(b):
         store_basis(b).wait()
         for t in range(tiles):
-            store_momentum(b, t).wait()
-            store_weight(b, t).wait()
+            for store in stores(b, t):
+                store.wait()
 
     for b in range(2):
         load(b).start()
-    scale = lax.rsqrt(squares[...] / FF + epsilon)
-    scale = jnp.transpose(jnp.concatenate([scale] * 16, axis=0))[:, :1]
+    scale = lax.rsqrt(jnp.sum(squares[...], axis=0, keepdims=True) / FF + epsilon)
+    scale = jnp.transpose(jnp.broadcast_to(scale, (128, r)))[:, :1]
     token[...] = jnp.zeros_like(token)
-    parts = split(inverse[...], 2)
     depth = lax.axis_size("col")
     size = buf0.shape[0] // depth
     for b in range(count):
         k = b % 2
         if b >= 2:
             finish(b - 2)
-        right = apply_inverse(parts, blocks[b][...])
-        lbuf[k] = ((1.0 - momentum_decay) * right).astype(bf16)
-        nbuf[k] = (right * scale).astype(bf16)
+        nbuf[k] = (blocks[b][...].astype(f32) * scale).astype(bf16)
         store_basis(b).start()
+        load(b).wait()
         for t in range(tiles):
             at, there = place(b, t)
-            correction = dot(ortho_ref[...], lbuf[k, :, at])
+            correction = dot(ortho_ref[...], blocks[b][:, at])
             for j in range(2 * depth):
                 rows = slice(j * size, (j + 1) * size)
                 here = slice(j // 2 * size, (j // 2 + 1) * size)
-                mbuf[k, rows, at] = (buf0, buf1)[j % 2][here, there] - correction[rows]
-            store_momentum(b, t).start()
-        load(b).wait()
-        for t in range(tiles):
-            at, there = place(b, t)
+                old = (buf0, buf1)[j % 2][here, there]
+                mbuf[k, rows, at] = old - (1.0 - momentum_decay) * correction[rows]
             change = dot(ortho_ref[...], nbuf[k, :, at])
             vbuf[k, :, at] = (wbuf[k, :, at].astype(f32) - factor * change).astype(bf16)
-            store_weight(b, t).start()
+            for store in stores(b, t):
+                store.start()
         if b + 2 < count:
             load(b + 2).start()
     for b in range(count - 2, count):
         finish(b)
 
 
-def results(pairs, factor, bufs, ortho_bf, inverse, squares, weight, blocks, outs):
+def results(pairs, factor, bufs, ortho_bf, squares, weight, blocks, outs=(), after=()):
     m, n = weight.shape
     r, width = blocks[0].shape
-    ins = [*map(keep, bufs), ortho_bf, inverse, squares, stay(weight), *blocks, *map(stay, outs)]
+    ins = [*map(keep, bufs), ortho_bf, squares, stay(weight), *blocks, *after, *map(stay, outs)]
     at = len(ins) - len(outs)
     *outs, token = pl.pallas_call(
         functools.partial(result_kernel, pairs, factor),
         out_shape=[shape((m, n), bf16), shape((m, n), f32), shape((r, n), bf16), shape((8, 128), f32)],
-        in_specs=[VMEM] * 5 + [ANY] + [VMEM] * len(blocks) + [ANY] * len(outs),
+        in_specs=[VMEM] * 4 + [ANY] + [VMEM] * len(blocks) + [ANY] * (len(after) + len(outs)),
         out_specs=[ANY] * 3 + [VMEM],
         input_output_aliases={at + k: k for k in range(len(outs))},
         scratch_shapes=[
             pltpu.VMEM((2, m, width), f32),
             pltpu.VMEM((2, m, width), bf16),
             pltpu.VMEM((2, m, width), bf16),
-            pltpu.VMEM((2, r, width), bf16),
             pltpu.VMEM((2, r, width), bf16),
             pltpu.SemaphoreType.DMA((2,)),
             pltpu.SemaphoreType.DMA((2, 2, width // 256)),
@@ -549,13 +562,14 @@
     lefts = gather(sum_over_col(*outs, low), "col")
     bufs = (buf0, buf1)
 
-    other, mine, g_sums = first_product(bufs, lefts[:-1], depth, width)
-    g_mine, g_other = gram(lefts[-1], g_sums)
-    other = last_product(bufs, other, lefts[-1], depth, width, False, g_mine)
+    other, mine, g_sums = first_product(bufs, [lefts[d] for d in early(depth)], depth, width)
+    lefts_late = [lefts[d] for d in late(depth)]
+    g_mine, g_other = gram(lefts_late, g_sums)
+    other = last_product(bufs, other, lefts_late, depth, width, False, g_mine)
     g_mine = g_mine + swap(g_other, "row", 1)
     other = hand_on(other, g_mine)
     received = swap(other, "row", 1)
-    mine = last_product(bufs, mine, lefts[-1], depth, width, True, g_mine, other)
+    mine = last_product(bufs, mine, lefts_late, depth, width, True, g_mine, other)
     own, *sent = pair_sum(mine, received, chips, g_mine)
     g_mine = pair_up(exchange(g_mine, "row", chips, 2))
     got = [swap(x, "row", 2 * (d + 1)) for d, x in enumerate(sent)]
@@ -563,25 +577,35 @@
 
     share, squares = share_of(inverse, own, got)
     ortho_bf = ortho(inverse, lefts)
+
+    near = [d for d in range(chips) if d & (d - 1) == 0]
+    blocks = {d: swap(share, "row", 2 * d) for d in near[1:]}
+    own_pair = swap(share, "row", 1)
+    squares = pair_up(exchange(hand_on(squares, own_pair), "col", depth))
+    squares = hand_on(squares, *blocks.values(), ortho_bf)
     squares = pair_up(exchange(squares, "row", chips, 2))
-    share = hand_on(share, squares)
-    squares = pair_up(exchange(squares + swap(squares, "row", 1), "col", depth))
+    pairs = {}
+    for d in near[1:]:
+        block = hand_on(blocks[d], squares)
+        pairs[d] = (block, swap(block, "row", 1))
+    squares = squares + swap(squares, "row", 1)
+    share = hand_on(share, *[pair[0] for pair in pairs.values()])
+    pairs[0] = (share, own_pair)
+    far = [d for d in range(chips) if d not in near]
+    blocks = {d: swap(share, "row", 2 * d) for d in far}
 
     factor = step_rate * math.sqrt(D / RANK)
-    near = min(3, chips)
-    blocks = [share] + [swap(share, "row", 2 * d) for d in range(1, near)]
-    blocks = [share] + [hand_on(x, squares) for x in blocks[1:]]
-    for d in range(near, chips):
-        share = hand_on(share, blocks[d - 2])
-        blocks.append(swap(share, "row", 2 * d))
-    blocks[0] = share
-    pairs = [x for block in blocks[:near] for x in (block, swap(block, "row", 1))]
-    common = (factor, bufs, ortho_bf, inverse, squares, weight)
-    outs, token = results(tuple(range(near)), *common, pairs, [])
-    for d in range(near, chips):
-        block = hand_on(blocks[d], token)
+    common = (factor, bufs, ortho_bf, squares, weight)
+    outs, token = (), share
+    if near[1:]:
+        rest = [x for d in near[1:] for x in pairs[d]]
+        outs, token = results(tuple(near[1:]), *common, rest, (), (share,))
+    blocks = {d: hand_on(block, token) for d, block in blocks.items()}
+    outs, token = results((0,), *common, pairs[0], outs)
+    for d, block in blocks.items():
         outs, token = results((d,), *common, (block, swap(block, "row", 1)), outs)
-    return tuple(outs)
+    new_weight, new_momentum, new_basis = outs
+    return (new_weight, new_momentum, new_basis)
 
 
 def plain_per_device(weight, gradient, momentum, old_basis):
@@ -621,8 +645,9 @@
 def solution(mesh):
     rows, depth = mesh.shape["row"], mesh.shape["col"]
     tiled = (
-        power_of_two(rows)
+        power_of_two(rows // 2)
         and power_of_two(depth)
+        and depth > 2
         and D % (rows * depth * 128) == 0
         and FF % (rows * depth * 256) == 0
     )

time: 119 us -> 119 us (level)
  starting transfers between devices: 31.3 us -> 32.6 us
  waiting for transfers between devices: 29.2 us -> 28 us
    ppermute x30, starting transfers between devices: 31.3 us -> 32.6 us  [swap(): lax.ppermute(x, axis, [(i, i ^ d) for i in range(lax.axis_size(axis))])]
    ppermute x30, waiting for transfers between devices: 29.2 us -> 28 us  [swap(): lax.ppermute(x, axis, [(i, i ^ d) for i in range(lax.axis_size(axis))])]
    pallas_call x2 -> x3, Pallas kernels: 23.1 us -> 22.4 us  [results(): pl.pallas_call(functools.partial(result_kernel, pairs, factor), out_shape...]
  transfers between devices with their start and end apart: 30 -> 30, of which waited for: 17 -> 13; matrix products, arithmetic and copies ran while one was open for 0% -> 0% of each run, Pallas kernels for 34% -> 34%
where the time goes in v8:
time: 119 us; the launch traced here: 118 us
  Pallas kernels  56.8 us (48%)
  starting transfers between devices  32.6 us (27%)
  waiting for transfers between devices  28 us (24%)
    ppermute x30, starting transfers between devices, swap(): lax.ppermute(x, axis, [(i, i ^ d) for i in range(lax.axis_size(axis))])  32.6 us
    ppermute x30, waiting for transfers between devices, swap(): lax.ppermute(x, axis, [(i, i ^ d) for i in range(lax.axis_size(axis))])  28 us
    pallas_call x3, Pallas kernels, results(): pl.pallas_call(functools.partial(result_kernel, pairs, factor), out_shape...  22.4 us
    pallas_call x2, Pallas kernels, project(): pl.pallas_call(functools.partial(project_kernel, part, depth, width), out...  16.5 us
    pallas_call x1, Pallas kernels, chol_inverse(): pl.pallas_call(chol_inverse_kernel, out_shape=shape((n, n), f32), in_spec...  9.14 us
    pallas_call x1, Pallas kernels, first_product(): pl.pallas_call(functools.partial(first_kernel, depth, width), out_shape=(...  3.36 us
    pallas_call x2, Pallas kernels, last_product(): pl.pallas_call(functools.partial(last_kernel, depth, width, mine), out_sh...  3.29 us
  transfers between devices with their start and end apart: 30, of which 13 were waited for; matrix products, arithmetic and copies ran while one was open for 0% of the time, Pallas kernels for 34%

profile of v8, /device:TPU:0, one launch (start us, length us, event | category | flops | bytes accessed | tf_op | source)
XLA Modules:
  0.0 118.5 jit_solution(15719772600764280937)
XLA Ops:
  0.6 8.7 %project.2 = (f32[512,6144]{1,0:T(8,128)S(1)}, bf16[256,6144]{1,0:T(8,128)(2,1)S(1)}, f32[256,256]{1,0:T(8,128)S(1)}, bf16[256,256]{1,0:T(8,128)(2,1)S(1)}) custom-call(f32[1024,6144]{1,0:T(8,128)} %mom.3, bf16[1024,6144]{1,0:T(8,128)(2,1)} %grad.3, bf16[256,6144]{1,0:T(8,128)(2,1)} %basis.1), custom_call_target="tpu_custom_call" | custom-call | bytes 37748736 | tf_op jit(solution)/shard_map/project/pallas_call | solution.py:104
  9.3 3.1 %collective-permute-start.2 = (bf16[256,256]{1,0:T(8,128)(2,1)S(1)}, bf16[256,256]{1,0:T(8,128)(2,1)S(1)}, u32[]{:S(2)}, u32[]{:S(2)}) collective-permute-start(bf16[256,256]{1,0:T(8,128)(2,1)S(1)} %get-tuple-element.37.rest_0_), channel_id=1, source_target_pairs={{0,1},{1,0},{2,3},{3,2},{4,5},{5,4},{6,7},{7,6},{8,9},{9,8},{10,11... | collective-permute-start | bytes 393224 | tf_op jit(solution)/shard_map/ppermute | solution.py:51
  12.4 7.8 %project.3 = (f32[512,6144]{1,0:T(8,128)S(1)}, f32[256,256]{1,0:T(8,128)S(1)}, bf16[256,256]{1,0:T(8,128)(2,1)S(1)}) custom-call(f32[1024,6144]{1,0:T(8,128)} %mom.3, bf16[1024,6144]{1,0:T(8,128)(2,1)} %grad.3, bf16[256,6144]{1,0:T(8,128)(2,1)S(1)} %get-tuple-element.36.basis, bf16[256,256]{1,0:T(8,128)(2,1)S(1)} %get-tuple-element.37.rest_0_), custom_call_target="tpu_custom_call" | custom-call | bytes 37748736 | tf_op jit(solution)/shard_map/project/pallas_call | solution.py:104
  20.4 3.1 %collective-permute-start.3 = (bf16[256,128]{1,0:T(8,128)(2,1)S(1)}, bf16[256,128]{1,0:T(8,128)(2,1)S(1)}, u32[]{:S(2)}, u32[]{:S(2)}) collective-permute-start(bf16[256,128]{1,0:T(8,128)(2,1)S(1)} %get-tuple-element.45), channel_id=1, source_target_pairs={{0,2},{1,3},{2,0},{3,1},{4,6},{5,7},{6,4},{7,5},{8,10},{9,11},{10,... | collective-permute-start | bytes 196616 | tf_op jit(solution)/shard_map/ppermute | solution.py:51
  23.4 3.2 %collective-permute-done.received = bf16[256,256]{1,0:T(8,128)(2,1)S(1)} collective-permute-done((bf16[256,256]{1,0:T(8,128)(2,1)S(1)}, bf16[256,256]{1,0:T(8,128)(2,1)S(1)}, u32[]{:S(2)}, u32[]{:S(2)}) %collective-permute-start) | collective-permute-done | bytes 131104 | tf_op jit(solution)/shard_map/ppermute | solution.py:51
  26.7 2.3 %collective-permute-start.1 = (bf16[256,128]{1,0:T(8,128)(2,1)S(1)}, bf16[256,128]{1,0:T(8,128)(2,1)S(1)}, u32[]{:S(2)}, u32[]{:S(2)}) collective-permute-start(bf16[256,128]{1,0:T(8,128)(2,1)S(1)} %get-tuple-element.42), channel_id=1, source_target_pairs={{0,2},{1,3},{2,0},{3,1},{4,6},{5,7},{6,4},{7,5},{8,10},{9,11},{10,... | collective-permute-start | bytes 196616 | tf_op jit(solution)/shard_map/ppermute | solution.py:51
  29.0 2.9 %collective-permute-done.1.received = bf16[256,128]{1,0:T(8,128)(2,1)S(1)} collective-permute-done((bf16[256,128]{1,0:T(8,128)(2,1)S(1)}, bf16[256,128]{1,0:T(8,128)(2,1)S(1)}, u32[]{:S(2)}, u32[]{:S(2)}) %collective-permute-start.1) | collective-permute-done | bytes 65568 | tf_op jit(solution)/shard_map/ppermute | solution.py:51
  31.9 2.5 %collective-permute-start.4 = (bf16[256,256]{1,0:T(8,128)(2,1)S(1)}, bf16[256,256]{1,0:T(8,128)(2,1)S(1)}, u32[]{:S(2)}, u32[]{:S(2)}) collective-permute-start(bf16[256,256]{1,0:T(8,128)(2,1)S(1)} %fold_last.3.rest_0_.refs_0_), channel_id=1, source_target_pairs={{0,2},{1,3},{2,0},{3,1},{4,6},{5,7},{6,4},{7,5},{8,10},{9,11},{10,... | collective-permute-start | bytes 393224 | tf_op jit(solution)/shard_map/ppermute | solution.py:51
  34.5 4.4 %collective-permute-done.4.rest_1_.refs_2_ = bf16[256,256]{1,0:T(8,128)(2,1)S(1)} collective-permute-done((bf16[256,256]{1,0:T(8,128)(2,1)S(1)}, bf16[256,256]{1,0:T(8,128)(2,1)S(1)}, u32[]{:S(2)}, u32[]{:S(2)}) %collective-permute-start.4) | collective-permute-done | bytes 131104 | tf_op jit(solution)/shard_map/ppermute | solution.py:51
  38.8 3.4 %first_product.1 = (f32[256,3072]{1,0:T(8,128)S(1)}, f32[256,3072]{1,0:T(8,128)S(1)}, f32[256,256]{1,0:T(8,128)S(1)}) custom-call(f32[512,6144]{1,0:T(8,128)S(1)} %get-tuple-element.35.buf0, f32[512,6144]{1,0:T(8,128)S(1)} %get-tuple-element.38.buf1, bf16[256,256]{1,0:T(8,128)(2,1)S(1)} %fold_last.3.rest_0_.refs_0_, ...), custom_call_target="tpu_custom_call" | custom-call | bytes 31457280 | tf_op jit(solution)/shard_map/first_product/pallas_call | solution.py:211
  42.2 1.6 %collective-permute-done.6.rest_1_.refs_3_ = bf16[256,256]{1,0:T(8,128)(2,1)S(1)} collective-permute-done((bf16[256,256]{1,0:T(8,128)(2,1)S(1)}, bf16[256,256]{1,0:T(8,128)(2,1)S(1)}, u32[]{:S(2)}, u32[]{:S(2)}) %collective-permute-start.6) | collective-permute-done | bytes 131104 | tf_op jit(solution)/shard_map/ppermute | solution.py:51
  43.8 0.3 gram.1
  44.2 1.6 %other_product.1.refs_0_ = bf16[256,3072]{1,0:T(8,128)(2,1)S(1)} custom-call(f32[512,6144]{1,0:T(8,128)S(1)} %get-tuple-element.35.buf0, f32[512,6144]{1,0:T(8,128)S(1)} %get-tuple-element.38.buf1, f32[256,3072]{1,0:T(8,128)S(1)} %get-tuple-element.50.sums, bf16[256,256]{1,0:T(8,128)(2,1)S(1)} %collective-permute-done.5.rest_0_.refs_1_, ...), custom_call_target="tpu_custom_call" | custom-call | bytes 15728640 | tf_op jit(solution)/shard_map/other_product/pallas_call | solution.py:266
  45.8 0.6 collective-permute-start.12
  46.4 2.4 %collective-permute-start.10 = (f32[128,256]{1,0:T(8,128)S(1)}, f32[128,256]{1,0:T(8,128)S(1)}, u32[]{:S(2)}, u32[]{:S(2)}) collective-permute-start(f32[128,256]{1,0:T(8,128)S(1)} %add.33.refs_1_.rest_2_._), channel_id=1, source_target_pairs={{0,24},{4,28},{8,16},{12,20},{16,8},{20,12},{24,0},{28,4},{1,25},{... | collective-permute-start | bytes 393224 | tf_op jit(solution)/shard_map/ppermute | solution.py:51
  48.8 0.5 collective-permute-start.8
  49.3 0.6 collective-permute-start.9
  49.8 1.7 %mine_product.1.mine = f32[256,3072]{1,0:T(8,128)S(1)} custom-call(f32[512,6144]{1,0:T(8,128)S(1)} %get-tuple-element.35.buf0, f32[512,6144]{1,0:T(8,128)S(1)} %get-tuple-element.38.buf1, f32[256,3072]{1,0:T(8,128)S(1)} %get-tuple-element.49.sums, bf16[256,256]{1,0:T(8,128)(2,1)S(1)} %collective-permute-done.5.rest_0_.refs_1_, ...), custom_call_target="tpu_custom_call" | custom-call | bytes 15728640 | tf_op jit(solution)/shard_map/mine_product/pallas_call | solution.py:266
  51.6 0.3 pair_sum.1
  51.9 1.5 %collective-permute-start.13 = (bf16[256,768]{1,0:T(8,128)(2,1)S(1)}, bf16[256,768]{1,0:T(8,128)(2,1)S(1)}, u32[]{:S(2)}, u32[]{:S(2)}) collective-permute-start(bf16[256,768]{1,0:T(8,128)(2,1)S(1)} %get-tuple-element.52), channel_id=1, source_target_pairs={{0,8},{4,12},{8,0},{12,4},{16,24},{20,28},{24,16},{28,20},{1,9},{5... | collective-permute-start | bytes 1179656 | tf_op jit(solution)/shard_map/ppermute | solution.py:51
  53.5 1.5 %collective-permute-start.14 = (bf16[256,768]{1,0:T(8,128)(2,1)S(1)}, bf16[256,768]{1,0:T(8,128)(2,1)S(1)}, u32[]{:S(2)}, u32[]{:S(2)}) collective-permute-start(bf16[256,768]{1,0:T(8,128)(2,1)S(1)} %get-tuple-element.53), channel_id=1, source_target_pairs={{0,16},{4,20},{8,24},{12,28},{16,0},{20,4},{24,8},{28,12},{1,17},{... | collective-permute-start | bytes 1179656 | tf_op jit(solution)/shard_map/ppermute | solution.py:51
  55.0 1.1 collective-permute-start.15
  56.0 0.4 collective-permute-done.8
  56.6 1.3 %collective-permute-done.11.other = f32[128,256]{1,0:T(8,128)S(1)} collective-permute-done((f32[128,256]{1,0:T(8,128)S(1)}, f32[128,256]{1,0:T(8,128)S(1)}, u32[]{:S(2)}, u32[]{:S(2)}) %collective-permute-start.11) | collective-permute-done | bytes 131104 | tf_op jit(solution)/shard_map/ppermute | solution.py:51
  57.9 9.1 %chol_inverse.1.inverse = f32[256,256]{1,0:T(8,128)S(1)} custom-call(f32[128,256]{1,0:T(8,128)S(1)} %add_add_fusion.mine, f32[128,256]{1,0:T(8,128)S(1)} %collective-permute-done.11.other), custom_call_target="tpu_custom_call" | custom-call | bytes 33554432 | tf_op jit(solution)/shard_map/chol_inverse/pallas_call | solution.py:344
  67.1 5.3 %collective-permute-done.15.refs_2_ = bf16[256,768]{1,0:T(8,128)(2,1)S(1)} collective-permute-done((bf16[256,768]{1,0:T(8,128)(2,1)S(1)}, bf16[256,768]{1,0:T(8,128)(2,1)S(1)}, u32[]{:S(2)}, u32[]{:S(2)}) %collective-permute-start.15) | collective-permute-done | bytes 393248 | tf_op jit(solution)/shard_map/ppermute | solution.py:51
  72.4 0.7 share.1
  73.1 1.5 %collective-permute-start.20 = (bf16[256,768]{1,0:T(8,128)(2,1)S(1)}, bf16[256,768]{1,0:T(8,128)(2,1)S(1)}, u32[]{:S(2)}, u32[]{:S(2)}) collective-permute-start(bf16[256,768]{1,0:T(8,128)(2,1)S(1)} %get-tuple-element.56.refs_0_), channel_id=1, source_target_pairs={{0,8},{4,12},{8,0},{12,4},{16,24},{20,28},{24,16},{28,20},{1,9},{5... | collective-permute-start | bytes 1179656 | tf_op jit(solution)/shard_map/ppermute | solution.py:51
  74.7 1.5 %collective-permute-start.21 = (bf16[256,768]{1,0:T(8,128)(2,1)S(1)}, bf16[256,768]{1,0:T(8,128)(2,1)S(1)}, u32[]{:S(2)}, u32[]{:S(2)}) collective-permute-start(bf16[256,768]{1,0:T(8,128)(2,1)S(1)} %get-tuple-element.56.refs_0_), channel_id=1, source_target_pairs={{0,16},{4,20},{8,24},{12,28},{16,0},{20,4},{24,8},{28,12},{1,17},{... | collective-permute-start | bytes 1179656 | tf_op jit(solution)/shard_map/ppermute | solution.py:51
  76.2 0.4 collective-permute-start.17
  76.6 3.0 %collective-permute-start.18 = (f32[8,256]{1,0:T(8,128)S(1)}, f32[8,256]{1,0:T(8,128)S(1)}, u32[]{:S(2)}, u32[]{:S(2)}) collective-permute-start(f32[8,256]{1,0:T(8,128)S(1)} %hand_on.8), channel_id=1, source_target_pairs={{0,2},{1,3},{2,0},{3,1},{4,6},{5,7},{6,4},{7,5},{8,10},{9,11},{10,... | collective-permute-start | bytes 24584 | tf_op jit(solution)/shard_map/ppermute | solution.py:51
  79.7 1.0 collective-permute-start.19
  80.7 0.6 ortho.1.refs_3_.ortho_ref
  81.3 3.8 %collective-permute-done.19 = f32[8,256]{1,0:T(8,128)S(1)} collective-permute-done((f32[8,256]{1,0:T(8,128)S(1)}, f32[8,256]{1,0:T(8,128)S(1)}, u32[]{:S(2)}, u32[]{:S(2)}) %collective-permute-start.19) | collective-permute-done | bytes 8224 | tf_op jit(solution)/shard_map/ppermute | solution.py:51
  85.1 0.7 collective-permute-done.21.refs_2_.refs_0_
  85.8 0.6 collective-permute-start.22
  86.4 1.5 %collective-permute-start.23 = (f32[8,256]{1,0:T(8,128)S(1)}, f32[8,256]{1,0:T(8,128)S(1)}, u32[]{:S(2)}, u32[]{:S(2)}) collective-permute-start(f32[8,256]{1,0:T(8,128)S(1)} %hand_on.9), channel_id=1, source_target_pairs={{0,16},{4,20},{8,24},{12,28},{16,0},{20,4},{24,8},{28,12},{1,17},{... | collective-permute-start | bytes 24584 | tf_op jit(solution)/shard_map/ppermute | solution.py:51
  87.9 1.4 %collective-permute-start.24 = (f32[8,256]{1,0:T(8,128)S(1)}, f32[8,256]{1,0:T(8,128)S(1)}, u32[]{:S(2)}, u32[]{:S(2)}) collective-permute-start(f32[8,256]{1,0:T(8,128)S(1)} %hand_on.9), channel_id=1, source_target_pairs={{0,24},{4,28},{8,16},{12,20},{16,8},{20,12},{24,0},{28,4},{1,25},{... | collective-permute-start | bytes 24584 | tf_op jit(solution)/shard_map/ppermute | solution.py:51
  89.3 0.2 collective-permute-done.22
  89.5 0.6 collective-permute-done.23
  90.1 2.4 %collective-permute-done.24 = f32[8,256]{1,0:T(8,128)S(1)} collective-permute-done((f32[8,256]{1,0:T(8,128)S(1)}, f32[8,256]{1,0:T(8,128)S(1)}, u32[]{:S(2)}, u32[]{:S(2)}) %collective-permute-start.24) | collective-permute-done | bytes 8224 | tf_op jit(solution)/shard_map/ppermute | solution.py:51
  92.5 0.5 collective-permute-start.27
  93.0 1.4 %collective-permute-start.26 = (bf16[256,768]{1,0:T(8,128)(2,1)S(1)}, bf16[256,768]{1,0:T(8,128)(2,1)S(1)}, u32[]{:S(2)}, u32[]{:S(2)}) collective-permute-start(bf16[256,768]{1,0:T(8,128)(2,1)S(1)} %hand_on.12.refs_4_.refs_0_), channel_id=1, source_target_pairs={{0,24},{4,28},{8,16},{12,20},{16,8},{20,12},{24,0},{28,4},{1,25},{... | collective-permute-start | bytes 1179656 | tf_op jit(solution)/shard_map/ppermute | solution.py:51
  94.4 1.2 collective-permute-done.25
  95.6 9.5 %results.3 = (bf16[1024,6144]{1,0:T(8,128)(2,1)}, f32[1024,6144]{1,0:T(8,128)}, bf16[256,6144]{1,0:T(8,128)(2,1)}, f32[8,128]{1,0:T(8,128)S(1)}) custom-call(f32[512,6144]{1,0:T(8,128)S(1)} %get-tuple-element.35.buf0, f32[512,6144]{1,0:T(8,128)S(1)} %get-tuple-element.38.buf1, bf16[1024,256]{1,0:T(8,128)(2,1)S(1)} %ortho.1.refs_3_.ortho_ref, ...), custom_call_target="tpu_custom_call" | custom-call | bytes 25165824 | tf_op jit(solution)/shard_map/results/pallas_call | solution.py:496
  105.1 0.2 collective-permute-start.29
  105.4 6.4 %results.4 = (bf16[1024,6144]{1,0:T(8,128)(2,1)}, f32[1024,6144]{1,0:T(8,128)}, bf16[256,6144]{1,0:T(8,128)(2,1)}, f32[8,128]{1,0:T(8,128)}) custom-call(f32[512,6144]{1,0:T(8,128)S(1)} %get-tuple-element.35.buf0, f32[512,6144]{1,0:T(8,128)S(1)} %get-tuple-element.38.buf1, ...), custom_call_target="tpu_custom_call", output_to_operand_aliasing={{0}: (7, {}), {1}: (8, {}), {2}: (9, {})} | custom-call | bytes 12582912 | tf_op jit(solution)/shard_map/results/pallas_call | solution.py:496
  111.8 6.5 %results.5 = (bf16[1024,6144]{1,0:T(8,128)(2,1)}, f32[1024,6144]{1,0:T(8,128)}, bf16[256,6144]{1,0:T(8,128)(2,1)}, f32[8,128]{1,0:T(8,128)}) custom-call(f32[512,6144]{1,0:T(8,128)S(1)} %get-tuple-element.35.buf0, f32[512,6144]{1,0:T(8,128)S(1)} %get-tuple-element.38.buf1, ...), custom_call_target="tpu_custom_call", output_to_operand_aliasing={{0}: (7, {}), {1}: (8, {}), {2}: (9, {})} | custom-call | bytes 12582912 | tf_op jit(solution)/shard_map/results/pallas_call | solution.py:496
  (41 shorter events, 0.5 us)
Async XLA Ops:
  9.3 11.0 %collective-permute-start.2 = (bf16[256,256]{1,0:T(8,128)(2,1)S(1)}, bf16[256,256]{1,0:T(8,128)(2,1)S(1)}, u32[]{:S(2)}, u32[]{:S(2)}) collective-permute-start(bf16[256,256]{1,0:T(8,128)(2,1)S(1)} %get-tuple-element.37.rest_0_), channel_id=1, source_target_pairs={{0,1},{1,0},{2,3},{3,2},{4,5},{5,4},{6,7},{7,6},{8,9},{9,8},{10,11... | collective-permute-start | bytes 393224 | tf_op jit(solution)/shard_map/ppermute | solution.py:51
  20.2 6.4 %collective-permute-start = (bf16[256,256]{1,0:T(8,128)(2,1)S(1)}, bf16[256,256]{1,0:T(8,128)(2,1)S(1)}, u32[]{:S(2)}, u32[]{:S(2)}) collective-permute-start(bf16[256,256]{1,0:T(8,128)(2,1)S(1)} %get-tuple-element.40), channel_id=1, source_target_pairs={{0,1},{1,0},{2,3},{3,2},{4,5},{5,4},{6,7},{7,6},{8,9},{9,8},{10,11... | collective-permute-start | bytes 393224 | tf_op jit(solution)/shard_map/ppermute | solution.py:51
  20.4 8.7 %collective-permute-start.3 = (bf16[256,128]{1,0:T(8,128)(2,1)S(1)}, bf16[256,128]{1,0:T(8,128)(2,1)S(1)}, u32[]{:S(2)}, u32[]{:S(2)}) collective-permute-start(bf16[256,128]{1,0:T(8,128)(2,1)S(1)} %get-tuple-element.45), channel_id=1, source_target_pairs={{0,2},{1,3},{2,0},{3,1},{4,6},{5,7},{6,4},{7,5},{8,10},{9,11},{10,... | collective-permute-start | bytes 196616 | tf_op jit(solution)/shard_map/ppermute | solution.py:51
  26.7 5.2 %collective-permute-start.1 = (bf16[256,128]{1,0:T(8,128)(2,1)S(1)}, bf16[256,128]{1,0:T(8,128)(2,1)S(1)}, u32[]{:S(2)}, u32[]{:S(2)}) collective-permute-start(bf16[256,128]{1,0:T(8,128)(2,1)S(1)} %get-tuple-element.42), channel_id=1, source_target_pairs={{0,2},{1,3},{2,0},{3,1},{4,6},{5,7},{6,4},{7,5},{8,10},{9,11},{10,... | collective-permute-start | bytes 196616 | tf_op jit(solution)/shard_map/ppermute | solution.py:51
  31.9 6.9 %collective-permute-start.4 = (bf16[256,256]{1,0:T(8,128)(2,1)S(1)}, bf16[256,256]{1,0:T(8,128)(2,1)S(1)}, u32[]{:S(2)}, u32[]{:S(2)}) collective-permute-start(bf16[256,256]{1,0:T(8,128)(2,1)S(1)} %fold_last.3.rest_0_.refs_0_), channel_id=1, source_target_pairs={{0,2},{1,3},{2,0},{3,1},{4,6},{5,7},{6,4},{7,5},{8,10},{9,11},{10,... | collective-permute-start | bytes 393224 | tf_op jit(solution)/shard_map/ppermute | solution.py:51
  34.5 7.7 %collective-permute-start.5 = (bf16[256,256]{1,0:T(8,128)(2,1)S(1)}, bf16[256,256]{1,0:T(8,128)(2,1)S(1)}, u32[]{:S(2)}, u32[]{:S(2)}) collective-permute-start(bf16[256,256]{1,0:T(8,128)(2,1)S(1)} %fold_last.3.rest_0_.refs_0_), channel_id=1, source_target_pairs={{0,1},{1,0},{2,3},{3,2},{4,5},{5,4},{6,7},{7,6},{8,9},{9,8},{10,11... | collective-permute-start | bytes 393224 | tf_op jit(solution)/shard_map/ppermute | solution.py:51
  38.8 5.0 %collective-permute-start.6 = (bf16[256,256]{1,0:T(8,128)(2,1)S(1)}, bf16[256,256]{1,0:T(8,128)(2,1)S(1)}, u32[]{:S(2)}, u32[]{:S(2)}) collective-permute-start(bf16[256,256]{1,0:T(8,128)(2,1)S(1)} %collective-permute-done.4.rest_1_.refs_2_), channel_id=1, source_target_pairs={{0,1},{1,0},{2,3},{3,2},{4,5},{5,4},{6,7},{7,6},{8,9},{9,8},{10,11... | collective-permute-start | bytes 393224 | tf_op jit(solution)/shard_map/ppermute | solution.py:51
  44.1 1.7 %collective-permute-start.7 = (f32[128,256]{1,0:T(8,128)S(1)}, f32[128,256]{1,0:T(8,128)S(1)}, u32[]{:S(2)}, u32[]{:S(2)}) collective-permute-start(f32[128,256]{1,0:T(8,128)S(1)} %get-tuple-element.48), channel_id=1, source_target_pairs={{0,4},{4,0},{8,12},{12,8},{16,20},{20,16},{24,28},{28,24},{1,5},{5... | collective-permute-start | bytes 393224 | tf_op jit(solution)/shard_map/ppermute | solution.py:51
  45.8 5.8 %collective-permute-start.12 = (bf16[256,3072]{1,0:T(8,128)(2,1)S(1)}, bf16[256,3072]{1,0:T(8,128)(2,1)S(1)}, u32[]{:S(2)}, u32[]{:S(2)}) collective-permute-start(bf16[256,3072]{1,0:T(8,128)(2,1)S(1)} %hand_on.7.rest_3_), channel_id=1, source_target_pairs={{0,4},{4,0},{8,12},{12,8},{16,20},{20,16},{24,28},{28,24},{1,5},{5... | collective-permute-start | bytes 4718600 | tf_op jit(solution)/shard_map/ppermute | solution.py:51
  46.4 8.6 %collective-permute-start.10 = (f32[128,256]{1,0:T(8,128)S(1)}, f32[128,256]{1,0:T(8,128)S(1)}, u32[]{:S(2)}, u32[]{:S(2)}) collective-permute-start(f32[128,256]{1,0:T(8,128)S(1)} %add.33.refs_1_.rest_2_._), channel_id=1, source_target_pairs={{0,24},{4,28},{8,16},{12,20},{16,8},{20,12},{24,0},{28,4},{1,25},{... | collective-permute-start | bytes 393224 | tf_op jit(solution)/shard_map/ppermute | solution.py:51
  48.8 7.7 %collective-permute-start.8 = (f32[128,256]{1,0:T(8,128)S(1)}, f32[128,256]{1,0:T(8,128)S(1)}, u32[]{:S(2)}, u32[]{:S(2)}) collective-permute-start(f32[128,256]{1,0:T(8,128)S(1)} %add.33.refs_1_.rest_2_._), channel_id=1, source_target_pairs={{0,8},{4,12},{8,0},{12,4},{16,24},{20,28},{24,16},{28,20},{1,9},{5... | collective-permute-start | bytes 393224 | tf_op jit(solution)/shard_map/ppermute | solution.py:51
  49.3 7.1 %collective-permute-start.9 = (f32[128,256]{1,0:T(8,128)S(1)}, f32[128,256]{1,0:T(8,128)S(1)}, u32[]{:S(2)}, u32[]{:S(2)}) collective-permute-start(f32[128,256]{1,0:T(8,128)S(1)} %add.33.refs_1_.rest_2_._), channel_id=1, source_target_pairs={{0,16},{4,20},{8,24},{12,28},{16,0},{20,4},{24,8},{28,12},{1,17},{... | collective-permute-start | bytes 393224 | tf_op jit(solution)/shard_map/ppermute | solution.py:51
  51.9 15.1 %collective-permute-start.13 = (bf16[256,768]{1,0:T(8,128)(2,1)S(1)}, bf16[256,768]{1,0:T(8,128)(2,1)S(1)}, u32[]{:S(2)}, u32[]{:S(2)}) collective-permute-start(bf16[256,768]{1,0:T(8,128)(2,1)S(1)} %get-tuple-element.52), channel_id=1, source_target_pairs={{0,8},{4,12},{8,0},{12,4},{16,24},{20,28},{24,16},{28,20},{1,9},{5... | collective-permute-start | bytes 1179656 | tf_op jit(solution)/shard_map/ppermute | solution.py:51
  53.5 13.6 %collective-permute-start.14 = (bf16[256,768]{1,0:T(8,128)(2,1)S(1)}, bf16[256,768]{1,0:T(8,128)(2,1)S(1)}, u32[]{:S(2)}, u32[]{:S(2)}) collective-permute-start(bf16[256,768]{1,0:T(8,128)(2,1)S(1)} %get-tuple-element.53), channel_id=1, source_target_pairs={{0,16},{4,20},{8,24},{12,28},{16,0},{20,4},{24,8},{28,12},{1,17},{... | collective-permute-start | bytes 1179656 | tf_op jit(solution)/shard_map/ppermute | solution.py:51
  55.0 17.4 %collective-permute-start.15 = (bf16[256,768]{1,0:T(8,128)(2,1)S(1)}, bf16[256,768]{1,0:T(8,128)(2,1)S(1)}, u32[]{:S(2)}, u32[]{:S(2)}) collective-permute-start(bf16[256,768]{1,0:T(8,128)(2,1)S(1)} %get-tuple-element.54), channel_id=1, source_target_pairs={{0,24},{4,28},{8,16},{12,20},{16,8},{20,12},{24,0},{28,4},{1,25},{... | collective-permute-start | bytes 1179656 | tf_op jit(solution)/shard_map/ppermute | solution.py:51
  56.5 1.4 %collective-permute-start.11 = (f32[128,256]{1,0:T(8,128)S(1)}, f32[128,256]{1,0:T(8,128)S(1)}, u32[]{:S(2)}, u32[]{:S(2)}) collective-permute-start(f32[128,256]{1,0:T(8,128)S(1)} %add_add_fusion.mine), channel_id=1, source_target_pairs={{0,4},{4,0},{8,12},{12,8},{16,20},{20,16},{24,28},{28,24},{1,5},{5... | collective-permute-start | bytes 393224 | tf_op jit(solution)/shard_map/ppermute | solution.py:51
  73.1 3.1 %collective-permute-start.16 = (bf16[256,768]{1,0:T(8,128)(2,1)S(1)}, bf16[256,768]{1,0:T(8,128)(2,1)S(1)}, u32[]{:S(2)}, u32[]{:S(2)}) collective-permute-start(bf16[256,768]{1,0:T(8,128)(2,1)S(1)} %get-tuple-element.56.refs_0_), channel_id=1, source_target_pairs={{0,4},{4,0},{8,12},{12,8},{16,20},{20,16},{24,28},{28,24},{1,5},{5... | collective-permute-start | bytes 1179656 | tf_op jit(solution)/shard_map/ppermute | solution.py:51
  73.1 12.0 %collective-permute-start.20 = (bf16[256,768]{1,0:T(8,128)(2,1)S(1)}, bf16[256,768]{1,0:T(8,128)(2,1)S(1)}, u32[]{:S(2)}, u32[]{:S(2)}) collective-permute-start(bf16[256,768]{1,0:T(8,128)(2,1)S(1)} %get-tuple-element.56.refs_0_), channel_id=1, source_target_pairs={{0,8},{4,12},{8,0},{12,4},{16,24},{20,28},{24,16},{28,20},{1,9},{5... | collective-permute-start | bytes 1179656 | tf_op jit(solution)/shard_map/ppermute | solution.py:51
  74.7 11.2 %collective-permute-start.21 = (bf16[256,768]{1,0:T(8,128)(2,1)S(1)}, bf16[256,768]{1,0:T(8,128)(2,1)S(1)}, u32[]{:S(2)}, u32[]{:S(2)}) collective-permute-start(bf16[256,768]{1,0:T(8,128)(2,1)S(1)} %get-tuple-element.56.refs_0_), channel_id=1, source_target_pairs={{0,16},{4,20},{8,24},{12,28},{16,0},{20,4},{24,8},{28,12},{1,17},{... | collective-permute-start | bytes 1179656 | tf_op jit(solution)/shard_map/ppermute | solution.py:51
  76.2 5.1 %collective-permute-start.17 = (f32[8,256]{1,0:T(8,128)S(1)}, f32[8,256]{1,0:T(8,128)S(1)}, u32[]{:S(2)}, u32[]{:S(2)}) collective-permute-start(f32[8,256]{1,0:T(8,128)S(1)} %hand_on.8), channel_id=1, source_target_pairs={{0,1},{1,0},{2,3},{3,2},{4,5},{5,4},{6,7},{7,6},{8,9},{9,8},{10,11... | collective-permute-start | bytes 24584 | tf_op jit(solution)/shard_map/ppermute | solution.py:51
  76.6 4.7 %collective-permute-start.18 = (f32[8,256]{1,0:T(8,128)S(1)}, f32[8,256]{1,0:T(8,128)S(1)}, u32[]{:S(2)}, u32[]{:S(2)}) collective-permute-start(f32[8,256]{1,0:T(8,128)S(1)} %hand_on.8), channel_id=1, source_target_pairs={{0,2},{1,3},{2,0},{3,1},{4,6},{5,7},{6,4},{7,5},{8,10},{9,11},{10,... | collective-permute-start | bytes 24584 | tf_op jit(solution)/shard_map/ppermute | solution.py:51
  79.7 5.4 %collective-permute-start.19 = (f32[8,256]{1,0:T(8,128)S(1)}, f32[8,256]{1,0:T(8,128)S(1)}, u32[]{:S(2)}, u32[]{:S(2)}) collective-permute-start(f32[8,256]{1,0:T(8,128)S(1)} %hand_on.8), channel_id=1, source_target_pairs={{0,3},{1,2},{2,1},{3,0},{4,7},{5,6},{6,5},{7,4},{8,11},{9,10},{10,... | collective-permute-start | bytes 24584 | tf_op jit(solution)/shard_map/ppermute | solution.py:51
  85.8 3.7 %collective-permute-start.22 = (f32[8,256]{1,0:T(8,128)S(1)}, f32[8,256]{1,0:T(8,128)S(1)}, u32[]{:S(2)}, u32[]{:S(2)}) collective-permute-start(f32[8,256]{1,0:T(8,128)S(1)} %hand_on.9), channel_id=1, source_target_pairs={{0,8},{4,12},{8,0},{12,4},{16,24},{20,28},{24,16},{28,20},{1,9},{5... | collective-permute-start | bytes 24584 | tf_op jit(solution)/shard_map/ppermute | solution.py:51
  86.4 3.7 %collective-permute-start.23 = (f32[8,256]{1,0:T(8,128)S(1)}, f32[8,256]{1,0:T(8,128)S(1)}, u32[]{:S(2)}, u32[]{:S(2)}) collective-permute-start(f32[8,256]{1,0:T(8,128)S(1)} %hand_on.9), channel_id=1, source_target_pairs={{0,16},{4,20},{8,24},{12,28},{16,0},{20,4},{24,8},{28,12},{1,17},{... | collective-permute-start | bytes 24584 | tf_op jit(solution)/shard_map/ppermute | solution.py:51
  87.9 4.5 %collective-permute-start.24 = (f32[8,256]{1,0:T(8,128)S(1)}, f32[8,256]{1,0:T(8,128)S(1)}, u32[]{:S(2)}, u32[]{:S(2)}) collective-permute-start(f32[8,256]{1,0:T(8,128)S(1)} %hand_on.9), channel_id=1, source_target_pairs={{0,24},{4,28},{8,16},{12,20},{16,8},{20,12},{24,0},{28,4},{1,25},{... | collective-permute-start | bytes 24584 | tf_op jit(solution)/shard_map/ppermute | solution.py:51
  92.5 3.1 %collective-permute-start.28 = (bf16[256,768]{1,0:T(8,128)(2,1)S(1)}, bf16[256,768]{1,0:T(8,128)(2,1)S(1)}, u32[]{:S(2)}, u32[]{:S(2)}) collective-permute-start(bf16[256,768]{1,0:T(8,128)(2,1)S(1)} %hand_on.11.refs_2_), channel_id=1, source_target_pairs={{0,4},{4,0},{8,12},{12,8},{16,20},{20,16},{24,28},{28,24},{1,5},{5... | collective-permute-start | bytes 1179656 | tf_op jit(solution)/shard_map/ppermute | solution.py:51
  92.5 3.1 %collective-permute-start.27 = (bf16[256,768]{1,0:T(8,128)(2,1)S(1)}, bf16[256,768]{1,0:T(8,128)(2,1)S(1)}, u32[]{:S(2)}, u32[]{:S(2)}) collective-permute-start(bf16[256,768]{1,0:T(8,128)(2,1)S(1)} %hand_on.10.refs_1_.refs_0_), channel_id=1, source_target_pairs={{0,4},{4,0},{8,12},{12,8},{16,20},{20,16},{24,28},{28,24},{1,5},{5... | collective-permute-start | bytes 1179656 | tf_op jit(solution)/shard_map/ppermute | solution.py:51
  93.0 12.1 %collective-permute-start.26 = (bf16[256,768]{1,0:T(8,128)(2,1)S(1)}, bf16[256,768]{1,0:T(8,128)(2,1)S(1)}, u32[]{:S(2)}, u32[]{:S(2)}) collective-permute-start(bf16[256,768]{1,0:T(8,128)(2,1)S(1)} %hand_on.12.refs_4_.refs_0_), channel_id=1, source_target_pairs={{0,24},{4,28},{8,16},{12,20},{16,8},{20,12},{24,0},{28,4},{1,25},{... | collective-permute-start | bytes 1179656 | tf_op jit(solution)/shard_map/ppermute | solution.py:51
  94.4 1.2 collective-permute-start.25
  105.1 6.7 %collective-permute-start.29 = (bf16[256,768]{1,0:T(8,128)(2,1)S(1)}, bf16[256,768]{1,0:T(8,128)(2,1)S(1)}, u32[]{:S(2)}, u32[]{:S(2)}) collective-permute-start(bf16[256,768]{1,0:T(8,128)(2,1)S(1)} %hand_on.13.refs_0_), channel_id=1, source_target_pairs={{0,4},{4,0},{8,12},{12,8},{16,20},{20,16},{24,28},{28,24},{1,5},{5... | collective-permute-start | bytes 1179656 | tf_op jit(solution)/shard_map/ppermute | solution.py:51

commit v9 on v8

--- a/solution.py
+++ b/solution.py
@@ -314,7 +314,9 @@
     return [x * scale for x in tiles]
 
 
-def chol_inverse_kernel(mine, other, out, work):
+def chol_inverse_kernel(mine, other, weight, out, fetched, work, sem):
+    fetch = pltpu.make_async_copy(weight, fetched, sem)
+    fetch.start()
     n = out.shape[0]
     h = n // 2
     core = lax.bitwise_and(lax.axis_index("row"), jnp.int32(1))
@@ -337,20 +339,21 @@
                 lead, s, (((0,), (0,)), ((), ())), precision=lax.Precision.HIGHEST, preferred_element_type=f32
             )
     out[...] = jnp.where(r_id >= c_id, work[:, n:], 0.0)
-
-
-def chol_inverse(mine, other):
+    fetch.wait()
+
+
+def chol_inverse(mine, other, weight):
     n = mine.shape[1]
     return pl.pallas_call(
         chol_inverse_kernel,
-        out_shape=shape((n, n), f32),
-        in_specs=[VMEM, VMEM],
-        out_specs=VMEM,
-        scratch_shapes=[pltpu.VMEM((n, 2 * n), f32)],
+        out_shape=(shape((n, n), f32), pltpu.VMEM(weight.shape, weight.dtype)),
+        in_specs=[VMEM, VMEM, ANY],
+        out_specs=(VMEM, VMEM),
+        scratch_shapes=[pltpu.VMEM((n, 2 * n), f32), pltpu.SemaphoreType.DMA],
         compiler_params=params(8),
         cost_estimate=cost(*[mine] * 256),
         name="chol_inverse",
-    )(mine, other)
+    )(mine, other, stay(weight))
 
 
 def ortho_kernel(inverse, *refs):
@@ -423,19 +426,17 @@
     )(inverse, own, *received)
 
 
-def result_kernel(pairs, factor, buf0, buf1, ortho_ref, squares, weight, *refs):
+def result_kernel(pairs, momentum_too, weight_too, factor, buf0, buf1, ortho_ref, weight, squares, *refs):
     blocks, rest = refs[: 2 * len(pairs)], refs[2 * len(pairs) :]
-    *_, new_weight, new_momentum, basis, token, mbuf, wbuf, vbuf, nbuf, in_sems, out_sems, basis_sems = rest
+    *outs, token, mbuf, vbuf, nbuf, out_sems, basis_sems = rest
+    new_momentum = outs[-1] if momentum_too else None
+    new_weight, basis = outs[-2 - momentum_too : len(outs) - momentum_too] if weight_too else (None, None)
     r, width = blocks[0].shape
     tile = 256
     tiles = width // tile
     count = len(blocks)
     starts = [i * width for i in block_ids(pairs)]
 
-    def load(b):
-        cols = pl.ds(pl.multiple_of(starts[b], 128), width)
-        return pltpu.make_async_copy(weight.at[:, cols], wbuf.at[b % 2], in_sems.at[b % 2])
-
     def store_basis(b):
         cols = pl.ds(pl.multiple_of(starts[b], 128), width)
         return pltpu.make_async_copy(nbuf.at[b % 2], basis.at[:, cols], basis_sems.at[b % 2])
@@ -445,21 +446,26 @@
 
     def stores(b, t):
         at, there = place(b, t)
-        return (
-            pltpu.make_async_copy(mbuf.at[b % 2, :, at], new_momentum.at[:, there], out_sems.at[0, b % 2, t]),
-            pltpu.make_async_copy(vbuf.at[b % 2, :, at], new_weight.at[:, there], out_sems.at[1, b % 2, t]),
-        )
+        copies = []
+        if momentum_too:
+            copies.append((mbuf, new_momentum))
+        if weight_too:
+            copies.append((vbuf, new_weight))
+        return [
+            pltpu.make_async_copy(src.at[b % 2, :, at], dst.at[:, there], out_sems.at[k, b % 2, t])
+            for k, (src, dst) in enumerate(copies)
+        ]
 
     def finish(b):
-        store_basis(b).wait()
+        if weight_too:
+            store_basis(b).wait()
         for t in range(tiles):
             for store in stores(b, t):
                 store.wait()
 
-    for b in range(2):
-        load(b).start()
-    scale = lax.rsqrt(jnp.sum(squares[...], axis=0, keepdims=True) / FF + epsilon)
-    scale = jnp.transpose(jnp.broadcast_to(scale, (128, r)))[:, :1]
+    if weight_too:
+        scale = lax.rsqrt(jnp.sum(squares[...], axis=0, keepdims=True) / FF + epsilon)
+        scale = jnp.transpose(jnp.broadcast_to(scale, (128, r)))[:, :1]
     token[...] = jnp.zeros_like(token)
     depth = lax.axis_size("col")
     size = buf0.shape[0] // depth
@@ -467,49 +473,56 @@
         k = b % 2
         if b >= 2:
             finish(b - 2)
-        nbuf[k] = (blocks[b][...].astype(f32) * scale).astype(bf16)
-        store_basis(b).start()
-        load(b).wait()
+        if weight_too:
+            nbuf[k] = (blocks[b][...].astype(f32) * scale).astype(bf16)
+            store_basis(b).start()
         for t in range(tiles):
             at, there = place(b, t)
-            correction = dot(ortho_ref[...], blocks[b][:, at])
-            for j in range(2 * depth):
-                rows = slice(j * size, (j + 1) * size)
-                here = slice(j // 2 * size, (j // 2 + 1) * size)
-                old = (buf0, buf1)[j % 2][here, there]
-                mbuf[k, rows, at] = old - (1.0 - momentum_decay) * correction[rows]
-            change = dot(ortho_ref[...], nbuf[k, :, at])
-            vbuf[k, :, at] = (wbuf[k, :, at].astype(f32) - factor * change).astype(bf16)
+            if momentum_too:
+                correction = dot(ortho_ref[...], blocks[b][:, at])
+                for j in range(2 * depth):
+                    rows = slice(j * size, (j + 1) * size)
+                    here = slice(j // 2 * size, (j // 2 + 1) * size)
+                    old = (buf0, buf1)[j % 2][here, there]
+                    mbuf[k, rows, at] = old - (1.0 - momentum_decay) * correction[rows]
+            if weight_too:
+                change = dot(ortho_ref[...], nbuf[k, :, at])
+                vbuf[k, :, at] = (weight[:, there].astype(f32) - factor * change).astype(bf16)
             for store in stores(b, t):
                 store.start()
-        if b + 2 < count:
-            load(b + 2).start()
     for b in range(count - 2, count):
         finish(b)
 
 
-def results(pairs, factor, bufs, ortho_bf, squares, weight, blocks, outs=(), after=()):
+def results(pairs, kinds, factor, bufs, ortho_bf, weight, squares, blocks, outs=(), after=(), last=()):
+    momentum_too, weight_too = kinds
     m, n = weight.shape
     r, width = blocks[0].shape
-    ins = [*map(keep, bufs), ortho_bf, squares, stay(weight), *blocks, *after, *map(stay, outs)]
+    outs = [*outs, *last]
+    ins = [*map(keep, bufs), ortho_bf, keep(weight), squares, *blocks, *after, *map(stay, outs)]
     at = len(ins) - len(outs)
+    skipped = 2 * weight_too + momentum_too - len(outs) if last else 0
+    out_shape = []
+    if weight_too:
+        out_shape += [shape((m, n), bf16), shape((r, n), bf16)]
+    if momentum_too:
+        out_shape += [shape((m, n), f32)]
+    m_rows, w_rows = (m if momentum_too else 8), (m if weight_too else 16)
     *outs, token = pl.pallas_call(
-        functools.partial(result_kernel, pairs, factor),
-        out_shape=[shape((m, n), bf16), shape((m, n), f32), shape((r, n), bf16), shape((8, 128), f32)],
-        in_specs=[VMEM] * 4 + [ANY] + [VMEM] * len(blocks) + [ANY] * (len(after) + len(outs)),
-        out_specs=[ANY] * 3 + [VMEM],
-        input_output_aliases={at + k: k for k in range(len(outs))},
+        functools.partial(result_kernel, pairs, *kinds, factor),
+        out_shape=[*out_shape, shape((8, 128), f32)],
+        in_specs=[VMEM] * (5 + len(blocks)) + [ANY] * (len(after) + len(outs)),
+        out_specs=[ANY] * len(out_shape) + [VMEM],
+        input_output_aliases={at + k: skipped + k for k in range(len(outs))},
         scratch_shapes=[
-            pltpu.VMEM((2, m, width), f32),
-            pltpu.VMEM((2, m, width), bf16),
-            pltpu.VMEM((2, m, width), bf16),
+            pltpu.VMEM((2, m_rows, width), f32),
+            pltpu.VMEM((2, w_rows, width), bf16),
             pltpu.VMEM((2, r, width), bf16),
-            pltpu.SemaphoreType.DMA((2,)),
             pltpu.SemaphoreType.DMA((2, 2, width // 256)),
             pltpu.SemaphoreType.DMA((2,)),
         ],
-        compiler_params=params(15),
-        cost_estimate=cost(*[shape((m, width), f32)] * (2 * len(blocks))),
+        compiler_params=params(12),
+        cost_estimate=cost(*[shape((m, width), f32)] * (len(blocks) * (momentum_too + weight_too))),
         name="results",
     )(*ins)
     return outs, token
@@ -573,7 +586,7 @@
     own, *sent = pair_sum(mine, received, chips, g_mine)
     g_mine = pair_up(exchange(g_mine, "row", chips, 2))
     got = [swap(x, "row", 2 * (d + 1)) for d, x in enumerate(sent)]
-    inverse = chol_inverse(g_mine, swap(g_mine, "row", 1))
+    inverse, weight = chol_inverse(g_mine, swap(g_mine, "row", 1), weight)
 
     share, squares = share_of(inverse, own, got)
     ortho_bf = ortho(inverse, lefts)
@@ -581,8 +594,11 @@
     near = [d for d in range(chips) if d & (d - 1) == 0]
     blocks = {d: swap(share, "row", 2 * d) for d in near[1:]}
     own_pair = swap(share, "row", 1)
-    squares = pair_up(exchange(hand_on(squares, own_pair), "col", depth))
-    squares = hand_on(squares, *blocks.values(), ortho_bf)
+    factor = step_rate * math.sqrt(D / RANK)
+    common = (factor, bufs, ortho_bf, weight)
+    squares = exchange(hand_on(squares, own_pair), "col", depth)
+    (momentum,), token = results((0,), (True, False), *common, squares[0], (share, own_pair))
+    squares = hand_on(pair_up(squares), *blocks.values(), token)
     squares = pair_up(exchange(squares, "row", chips, 2))
     pairs = {}
     for d in near[1:]:
@@ -594,17 +610,19 @@
     far = [d for d in range(chips) if d not in near]
     blocks = {d: swap(share, "row", 2 * d) for d in far}
 
-    factor = step_rate * math.sqrt(D / RANK)
-    common = (factor, bufs, ortho_bf, squares, weight)
-    outs, token = (), share
+    common = (*common, squares)
+    weight_basis = ()
     if near[1:]:
         rest = [x for d in near[1:] for x in pairs[d]]
-        outs, token = results(tuple(near[1:]), *common, rest, (), (share,))
+        (*weight_basis, momentum), token = results(
+            tuple(near[1:]), (True, True), *common, rest, (), (share,), [momentum]
+        )
     blocks = {d: hand_on(block, token) for d, block in blocks.items()}
-    outs, token = results((0,), *common, pairs[0], outs)
+    weight_basis, token = results((0,), (False, True), *common, pairs[0], weight_basis)
+    outs = [*weight_basis, momentum]
     for d, block in blocks.items():
-        outs, token = results((d,), *common, (block, swap(block, "row", 1)), outs)
-    new_weight, new_momentum, new_basis = outs
+        outs, token = results((d,), (True, True), *common, (block, swap(block, "row", 1)), outs)
+    new_weight, new_basis, new_momentum = outs
     return (new_weight, new_momentum, new_basis)
 
 

time: 119 us -> 114 us (0.958)
  waiting for transfers between devices: 28 us -> 23.3 us
  starting transfers between devices: 32.6 us -> 31.3 us
    ppermute x30, waiting for transfers between devices: 28 us -> 23.3 us  [swap(): lax.ppermute(x, axis, [(i, i ^ d) for i in range(lax.axis_size(axis))])]
    ppermute x30, starting transfers between devices: 32.6 us -> 31.3 us  [swap(): lax.ppermute(x, axis, [(i, i ^ d) for i in range(lax.axis_size(axis))])]
    pallas_call x4 -> x5, Pallas kernels: 31.6 us -> 32.4 us  [the longest x4 19.1 us: results(): pl.pallas_call(functools.partial(result_kernel, pairs, *kinds, factor), o...]
  transfers between devices with their start and end apart: 30 -> 30, of which waited for: 13 -> 13; matrix products, arithmetic and copies ran while one was open for 0% -> 0% of each run, Pallas kernels for 34% -> 38%
where the time goes in v9:
time: 114 us
  Pallas kernels  57.7 us (51%)
  starting transfers between devices  31.3 us (27%)
  waiting for transfers between devices  23.3 us (20%)
    ppermute x30, starting transfers between devices, swap(): lax.ppermute(x, axis, [(i, i ^ d) for i in range(lax.axis_size(axis))])  31.3 us
    ppermute x30, waiting for transfers between devices, swap(): lax.ppermute(x, axis, [(i, i ^ d) for i in range(lax.axis_size(axis))])  23.3 us
    pallas_call x4, Pallas kernels, results(): pl.pallas_call(functools.partial(result_kernel, pairs, *kinds, factor), o...  19.1 us
    pallas_call x2, Pallas kernels, project(): pl.pallas_call(functools.partial(project_kernel, part, depth, width), out...  16.5 us
    pallas_call x1, Pallas kernels, chol_inverse(): pl.pallas_call(chol_inverse_kernel, out_shape=(shape((n, n), f32), pltpu....  13.3 us
    pallas_call x1, Pallas kernels, first_product(): pl.pallas_call(functools.partial(first_kernel, depth, width), out_shape=(...  3.36 us
    pallas_call x2, Pallas kernels, last_product(): pl.pallas_call(functools.partial(last_kernel, depth, width, mine), out_sh...  3.31 us
  transfers between devices with their start and end apart: 30, of which 13 were waited for; matrix products, arithmetic and copies ran while one was open for 0% of the time, Pallas kernels for 38%

profile of v9, /device:TPU:0, one launch (start us, length us, event | category | flops | bytes accessed | tf_op | source)
XLA Modules:
  0.0 113.5 jit_solution(3927876082743289469)
XLA Ops:
  0.6 8.7 %project.2 = (f32[512,6144]{1,0:T(8,128)S(1)}, bf16[256,6144]{1,0:T(8,128)(2,1)S(1)}, f32[256,256]{1,0:T(8,128)S(1)}, bf16[256,256]{1,0:T(8,128)(2,1)S(1)}) custom-call(f32[1024,6144]{1,0:T(8,128)} %mom.3, bf16[1024,6144]{1,0:T(8,128)(2,1)} %grad.3, bf16[256,6144]{1,0:T(8,128)(2,1)} %basis.1), custom_call_target="tpu_custom_call" | custom-call | bytes 37748736 | tf_op jit(solution)/shard_map/project/pallas_call | solution.py:104
  9.3 3.1 %collective-permute-start.2 = (bf16[256,256]{1,0:T(8,128)(2,1)S(1)}, bf16[256,256]{1,0:T(8,128)(2,1)S(1)}, u32[]{:S(2)}, u32[]{:S(2)}) collective-permute-start(bf16[256,256]{1,0:T(8,128)(2,1)S(1)} %get-tuple-element.40.rest_0_), channel_id=1, source_target_pairs={{0,1},{1,0},{2,3},{3,2},{4,5},{5,4},{6,7},{7,6},{8,9},{9,8},{10,11... | collective-permute-start | bytes 393224 | tf_op jit(solution)/shard_map/ppermute | solution.py:51
  12.4 7.8 %project.3 = (f32[512,6144]{1,0:T(8,128)S(1)}, f32[256,256]{1,0:T(8,128)S(1)}, bf16[256,256]{1,0:T(8,128)(2,1)S(1)}) custom-call(f32[1024,6144]{1,0:T(8,128)} %mom.3, bf16[1024,6144]{1,0:T(8,128)(2,1)} %grad.3, bf16[256,6144]{1,0:T(8,128)(2,1)S(1)} %get-tuple-element.39.basis, bf16[256,256]{1,0:T(8,128)(2,1)S(1)} %get-tuple-element.40.rest_0_), custom_call_target="tpu_custom_call" | custom-call | bytes 37748736 | tf_op jit(solution)/shard_map/project/pallas_call | solution.py:104
  20.4 3.1 %collective-permute-start.3 = (bf16[256,128]{1,0:T(8,128)(2,1)S(1)}, bf16[256,128]{1,0:T(8,128)(2,1)S(1)}, u32[]{:S(2)}, u32[]{:S(2)}) collective-permute-start(bf16[256,128]{1,0:T(8,128)(2,1)S(1)} %get-tuple-element.48), channel_id=1, source_target_pairs={{0,2},{1,3},{2,0},{3,1},{4,6},{5,7},{6,4},{7,5},{8,10},{9,11},{10,... | collective-permute-start | bytes 196616 | tf_op jit(solution)/shard_map/ppermute | solution.py:51
  23.4 3.2 %collective-permute-done.received = bf16[256,256]{1,0:T(8,128)(2,1)S(1)} collective-permute-done((bf16[256,256]{1,0:T(8,128)(2,1)S(1)}, bf16[256,256]{1,0:T(8,128)(2,1)S(1)}, u32[]{:S(2)}, u32[]{:S(2)}) %collective-permute-start) | collective-permute-done | bytes 131104 | tf_op jit(solution)/shard_map/ppermute | solution.py:51
  26.7 2.3 %collective-permute-start.1 = (bf16[256,128]{1,0:T(8,128)(2,1)S(1)}, bf16[256,128]{1,0:T(8,128)(2,1)S(1)}, u32[]{:S(2)}, u32[]{:S(2)}) collective-permute-start(bf16[256,128]{1,0:T(8,128)(2,1)S(1)} %get-tuple-element.45), channel_id=1, source_target_pairs={{0,2},{1,3},{2,0},{3,1},{4,6},{5,7},{6,4},{7,5},{8,10},{9,11},{10,... | collective-permute-start | bytes 196616 | tf_op jit(solution)/shard_map/ppermute | solution.py:51
  29.0 2.9 %collective-permute-done.1.received = bf16[256,128]{1,0:T(8,128)(2,1)S(1)} collective-permute-done((bf16[256,128]{1,0:T(8,128)(2,1)S(1)}, bf16[256,128]{1,0:T(8,128)(2,1)S(1)}, u32[]{:S(2)}, u32[]{:S(2)}) %collective-permute-start.1) | collective-permute-done | bytes 65568 | tf_op jit(solution)/shard_map/ppermute | solution.py:51
  32.0 2.5 %collective-permute-start.4 = (bf16[256,256]{1,0:T(8,128)(2,1)S(1)}, bf16[256,256]{1,0:T(8,128)(2,1)S(1)}, u32[]{:S(2)}, u32[]{:S(2)}) collective-permute-start(bf16[256,256]{1,0:T(8,128)(2,1)S(1)} %fold_last.3.rest_0_.refs_0_), channel_id=1, source_target_pairs={{0,2},{1,3},{2,0},{3,1},{4,6},{5,7},{6,4},{7,5},{8,10},{9,11},{10,... | collective-permute-start | bytes 393224 | tf_op jit(solution)/shard_map/ppermute | solution.py:51
  34.5 4.4 %collective-permute-done.4.rest_1_.refs_2_ = bf16[256,256]{1,0:T(8,128)(2,1)S(1)} collective-permute-done((bf16[256,256]{1,0:T(8,128)(2,1)S(1)}, bf16[256,256]{1,0:T(8,128)(2,1)S(1)}, u32[]{:S(2)}, u32[]{:S(2)}) %collective-permute-start.4) | collective-permute-done | bytes 131104 | tf_op jit(solution)/shard_map/ppermute | solution.py:51
  38.8 3.4 %first_product.1 = (f32[256,3072]{1,0:T(8,128)S(1)}, f32[256,3072]{1,0:T(8,128)S(1)}, f32[256,256]{1,0:T(8,128)S(1)}) custom-call(f32[512,6144]{1,0:T(8,128)S(1)} %get-tuple-element.38.buf0, f32[512,6144]{1,0:T(8,128)S(1)} %get-tuple-element.41.buf1, bf16[256,256]{1,0:T(8,128)(2,1)S(1)} %fold_last.3.rest_0_.refs_0_, ...), custom_call_target="tpu_custom_call" | custom-call | bytes 31457280 | tf_op jit(solution)/shard_map/first_product/pallas_call | solution.py:211
  42.2 1.6 %collective-permute-done.6.rest_1_.refs_3_ = bf16[256,256]{1,0:T(8,128)(2,1)S(1)} collective-permute-done((bf16[256,256]{1,0:T(8,128)(2,1)S(1)}, bf16[256,256]{1,0:T(8,128)(2,1)S(1)}, u32[]{:S(2)}, u32[]{:S(2)}) %collective-permute-start.6) | collective-permute-done | bytes 131104 | tf_op jit(solution)/shard_map/ppermute | solution.py:51
  43.8 0.3 gram.1
  44.2 1.6 %other_product.1.refs_0_ = bf16[256,3072]{1,0:T(8,128)(2,1)S(1)} custom-call(f32[512,6144]{1,0:T(8,128)S(1)} %get-tuple-element.38.buf0, f32[512,6144]{1,0:T(8,128)S(1)} %get-tuple-element.41.buf1, f32[256,3072]{1,0:T(8,128)S(1)} %get-tuple-element.55.sums, bf16[256,256]{1,0:T(8,128)(2,1)S(1)} %collective-permute-done.5.rest_0_.refs_1_, ...), custom_call_target="tpu_custom_call" | custom-call | bytes 15728640 | tf_op jit(solution)/shard_map/other_product/pallas_call | solution.py:266
  45.8 0.6 collective-permute-start.12
  46.4 2.4 %collective-permute-start.10 = (f32[128,256]{1,0:T(8,128)S(1)}, f32[128,256]{1,0:T(8,128)S(1)}, u32[]{:S(2)}, u32[]{:S(2)}) collective-permute-start(f32[128,256]{1,0:T(8,128)S(1)} %add.33.refs_1_.rest_2_._), channel_id=1, source_target_pairs={{0,24},{4,28},{8,16},{12,20},{16,8},{20,12},{24,0},{28,4},{1,25},{... | collective-permute-start | bytes 393224 | tf_op jit(solution)/shard_map/ppermute | solution.py:51
  48.8 0.5 collective-permute-start.9
  49.3 0.6 collective-permute-start.8
  49.9 1.7 %mine_product.1.mine = f32[256,3072]{1,0:T(8,128)S(1)} custom-call(f32[512,6144]{1,0:T(8,128)S(1)} %get-tuple-element.38.buf0, f32[512,6144]{1,0:T(8,128)S(1)} %get-tuple-element.41.buf1, f32[256,3072]{1,0:T(8,128)S(1)} %get-tuple-element.54.sums, bf16[256,256]{1,0:T(8,128)(2,1)S(1)} %collective-permute-done.5.rest_0_.refs_1_, ...), custom_call_target="tpu_custom_call" | custom-call | bytes 15728640 | tf_op jit(solution)/shard_map/mine_product/pallas_call | solution.py:266
  51.6 0.3 pair_sum.1
  52.0 1.5 %collective-permute-start.13 = (bf16[256,768]{1,0:T(8,128)(2,1)S(1)}, bf16[256,768]{1,0:T(8,128)(2,1)S(1)}, u32[]{:S(2)}, u32[]{:S(2)}) collective-permute-start(bf16[256,768]{1,0:T(8,128)(2,1)S(1)} %get-tuple-element.57), channel_id=1, source_target_pairs={{0,8},{4,12},{8,0},{12,4},{16,24},{20,28},{24,16},{28,20},{1,9},{5... | collective-permute-start | bytes 1179656 | tf_op jit(solution)/shard_map/ppermute | solution.py:51
  53.5 1.5 %collective-permute-start.14 = (bf16[256,768]{1,0:T(8,128)(2,1)S(1)}, bf16[256,768]{1,0:T(8,128)(2,1)S(1)}, u32[]{:S(2)}, u32[]{:S(2)}) collective-permute-start(bf16[256,768]{1,0:T(8,128)(2,1)S(1)} %get-tuple-element.58), channel_id=1, source_target_pairs={{0,16},{4,20},{8,24},{12,28},{16,0},{20,4},{24,8},{28,12},{1,17},{... | collective-permute-start | bytes 1179656 | tf_op jit(solution)/shard_map/ppermute | solution.py:51
  55.0 1.1 collective-permute-start.15
  56.1 0.4 collective-permute-done.8
  56.6 1.3 %collective-permute-done.11.other = f32[128,256]{1,0:T(8,128)S(1)} collective-permute-done((f32[128,256]{1,0:T(8,128)S(1)}, f32[128,256]{1,0:T(8,128)S(1)}, u32[]{:S(2)}, u32[]{:S(2)}) %collective-permute-start.11) | collective-permute-done | bytes 131104 | tf_op jit(solution)/shard_map/ppermute | solution.py:51
  57.9 13.3 %chol_inverse.1 = (f32[256,256]{1,0:T(8,128)S(1)}, bf16[1024,6144]{1,0:T(8,128)(2,1)S(1)}) custom-call(f32[128,256]{1,0:T(8,128)S(1)} %add_add_fusion.mine, f32[128,256]{1,0:T(8,128)S(1)} %collective-permute-done.11.other, bf16[1024,6144]{1,0:T(8,128)(2,1)} %weight.1), custom_call_target="tpu_custom_call" | custom-call | bytes 33554432 | tf_op jit(solution)/shard_map/chol_inverse/pallas_call | solution.py:347
  71.3 1.1 %collective-permute-done.15.refs_2_ = bf16[256,768]{1,0:T(8,128)(2,1)S(1)} collective-permute-done((bf16[256,768]{1,0:T(8,128)(2,1)S(1)}, bf16[256,768]{1,0:T(8,128)(2,1)S(1)}, u32[]{:S(2)}, u32[]{:S(2)}) %collective-permute-start.15) | collective-permute-done | bytes 393248 | tf_op jit(solution)/shard_map/ppermute | solution.py:51
  72.4 0.7 share.1
  73.2 1.6 %collective-permute-start.21 = (bf16[256,768]{1,0:T(8,128)(2,1)S(1)}, bf16[256,768]{1,0:T(8,128)(2,1)S(1)}, u32[]{:S(2)}, u32[]{:S(2)}) collective-permute-start(bf16[256,768]{1,0:T(8,128)(2,1)S(1)} %get-tuple-element.61.refs_0_), channel_id=1, source_target_pairs={{0,16},{4,20},{8,24},{12,28},{16,0},{20,4},{24,8},{28,12},{1,17},{... | collective-permute-start | bytes 1179656 | tf_op jit(solution)/shard_map/ppermute | solution.py:51
  74.7 1.5 %collective-permute-start.20 = (bf16[256,768]{1,0:T(8,128)(2,1)S(1)}, bf16[256,768]{1,0:T(8,128)(2,1)S(1)}, u32[]{:S(2)}, u32[]{:S(2)}) collective-permute-start(bf16[256,768]{1,0:T(8,128)(2,1)S(1)} %get-tuple-element.61.refs_0_), channel_id=1, source_target_pairs={{0,8},{4,12},{8,0},{12,4},{16,24},{20,28},{24,16},{28,20},{1,9},{5... | collective-permute-start | bytes 1179656 | tf_op jit(solution)/shard_map/ppermute | solution.py:51
  76.3 2.9 %collective-permute-start.19 = (f32[8,256]{1,0:T(8,128)S(1)}, f32[8,256]{1,0:T(8,128)S(1)}, u32[]{:S(2)}, u32[]{:S(2)}) collective-permute-start(f32[8,256]{1,0:T(8,128)S(1)} %hand_on.8.squares), channel_id=1, source_target_pairs={{0,3},{1,2},{2,1},{3,0},{4,7},{5,6},{6,5},{7,4},{8,11},{9,10},{10,... | collective-permute-start | bytes 24584 | tf_op jit(solution)/shard_map/ppermute | solution.py:51
  79.2 0.1 collective-permute-start.18
  79.3 1.4 %collective-permute-start.17 = (f32[8,256]{1,0:T(8,128)S(1)}, f32[8,256]{1,0:T(8,128)S(1)}, u32[]{:S(2)}, u32[]{:S(2)}) collective-permute-start(f32[8,256]{1,0:T(8,128)S(1)} %hand_on.8.squares), channel_id=1, source_target_pairs={{0,1},{1,0},{2,3},{3,2},{4,5},{5,4},{6,7},{7,6},{8,9},{9,8},{10,11... | collective-permute-start | bytes 24584 | tf_op jit(solution)/shard_map/ppermute | solution.py:51
  80.7 0.6 ortho.1.ortho_ref
  81.3 3.3 %results.4 = (f32[1024,6144]{1,0:T(8,128)}, f32[8,128]{1,0:T(8,128)S(1)}) custom-call(f32[512,6144]{1,0:T(8,128)S(1)} %get-tuple-element.38.buf0, f32[512,6144]{1,0:T(8,128)S(1)} %copy-done.1, bf16[1024,256]{1,0:T(8,128)(2,1)S(1)} %ortho.1.ortho_ref, bf16[1024,6144]{1,0:T(8,128)(2,1)S(1)} %get-tuple-element.53.weight, f32[8,256]{1,0:T(8,128)S(1)} %hand_on.8.squares, ...), custom_call_target="tpu_custom_call" | custom-call | bytes 6291456 | tf_op jit(solution)/shard_map/results/pallas_call | solution.py:511
  84.7 1.2 %collective-permute-done.20.refs_1_.refs_0_ = bf16[256,768]{1,0:T(8,128)(2,1)S(1)} collective-permute-done((bf16[256,768]{1,0:T(8,128)(2,1)S(1)}, bf16[256,768]{1,0:T(8,128)(2,1)S(1)}, u32[]{:S(2)}, u32[]{:S(2)}) %collective-permute-start.20) | collective-permute-done | bytes 393248 | tf_op jit(solution)/shard_map/ppermute | solution.py:51
  85.9 1.4 %collective-permute-start.24 = (f32[8,256]{1,0:T(8,128)S(1)}, f32[8,256]{1,0:T(8,128)S(1)}, u32[]{:S(2)}, u32[]{:S(2)}) collective-permute-start(f32[8,256]{1,0:T(8,128)S(1)} %hand_on.9), channel_id=1, source_target_pairs={{0,24},{4,28},{8,16},{12,20},{16,8},{20,12},{24,0},{28,4},{1,25},{... | collective-permute-start | bytes 24584 | tf_op jit(solution)/shard_map/ppermute | solution.py:51
  87.4 1.6 %collective-permute-start.23 = (f32[8,256]{1,0:T(8,128)S(1)}, f32[8,256]{1,0:T(8,128)S(1)}, u32[]{:S(2)}, u32[]{:S(2)}) collective-permute-start(f32[8,256]{1,0:T(8,128)S(1)} %hand_on.9), channel_id=1, source_target_pairs={{0,16},{4,20},{8,24},{12,28},{16,0},{20,4},{24,8},{28,12},{1,17},{... | collective-permute-start | bytes 24584 | tf_op jit(solution)/shard_map/ppermute | solution.py:51
  88.9 0.5 collective-permute-start.22
  89.4 1.1 collective-permute-done.24
  90.5 0.5 collective-permute-done.23
  91.0 1.6 %collective-permute-done.22 = f32[8,256]{1,0:T(8,128)S(1)} collective-permute-done((f32[8,256]{1,0:T(8,128)S(1)}, f32[8,256]{1,0:T(8,128)S(1)}, u32[]{:S(2)}, u32[]{:S(2)}) %collective-permute-start.22) | collective-permute-done | bytes 8224 | tf_op jit(solution)/shard_map/ppermute | solution.py:51
  92.6 0.5 collective-permute-start.28
  93.1 0.5 collective-permute-start.26
  93.6 1.3 %collective-permute-done.25 = f32[8,256]{1,0:T(8,128)S(1)} collective-permute-done((f32[8,256]{1,0:T(8,128)S(1)}, f32[8,256]{1,0:T(8,128)S(1)}, u32[]{:S(2)}, u32[]{:S(2)}) %collective-permute-start.25) | collective-permute-done | bytes 8224 | tf_op jit(solution)/shard_map/ppermute | solution.py:51
  94.9 7.5 %results.5 = (bf16[1024,6144]{1,0:T(8,128)(2,1)}, bf16[256,6144]{1,0:T(8,128)(2,1)}, f32[1024,6144]{1,0:T(8,128)}, f32[8,128]{1,0:T(8,128)S(1)}) custom-call(f32[512,6144]{1,0:T(8,128)S(1)} %get-tuple-element.38.buf0, f32[512,6144]{1,0:T(8,128)S(1)} %copy-done.1, bf16[1024,256]{1,0:T(8,128)(2,1)S(1)} %ortho.1.ortho_ref, ...), custom_call_target="tpu_custom_call", output_to_operand_aliasing={{2}: (10, {})} | custom-call | bytes 25165824 | tf_op jit(solution)/shard_map/results/pallas_call | solution.py:511
  102.4 2.7 %collective-permute-done.26.refs_0_ = bf16[256,768]{1,0:T(8,128)(2,1)S(1)} collective-permute-done((bf16[256,768]{1,0:T(8,128)(2,1)S(1)}, bf16[256,768]{1,0:T(8,128)(2,1)S(1)}, u32[]{:S(2)}, u32[]{:S(2)}) %collective-permute-start.26) | collective-permute-done | bytes 393248 | tf_op jit(solution)/shard_map/ppermute | solution.py:51
  105.1 3.2 %results.6 = (bf16[1024,6144]{1,0:T(8,128)(2,1)}, bf16[256,6144]{1,0:T(8,128)(2,1)}, f32[8,128]{1,0:T(8,128)}) custom-call(f32[512,6144]{1,0:T(8,128)S(1)} %get-tuple-element.38.buf0, f32[512,6144]{1,0:T(8,128)S(1)} %copy-done.1, bf16[1024,256]{1,0:T(8,128)(2,1)S(1)} %ortho.1.ortho_ref, ...), custom_call_target="tpu_custom_call", output_to_operand_aliasing={{0}: (7, {}), {1}: (8, {})} | custom-call | bytes 6291456 | tf_op jit(solution)/shard_map/results/pallas_call | solution.py:511
  108.3 5.0 %results.7 = (bf16[1024,6144]{1,0:T(8,128)(2,1)}, bf16[256,6144]{1,0:T(8,128)(2,1)}, f32[1024,6144]{1,0:T(8,128)}, f32[8,128]{1,0:T(8,128)}) custom-call(f32[512,6144]{1,0:T(8,128)S(1)} %get-tuple-element.38.buf0, f32[512,6144]{1,0:T(8,128)S(1)} %copy-done.1, ...), custom_call_target="tpu_custom_call", output_to_operand_aliasing={{0}: (7, {}), {1}: (8, {}), {2}: (9, {})} | custom-call | bytes 12582912 | tf_op jit(solution)/shard_map/results/pallas_call | solution.py:511
  (46 shorter events, 0.5 us)
Async XLA Ops:
  9.3 11.0 %collective-permute-start.2 = (bf16[256,256]{1,0:T(8,128)(2,1)S(1)}, bf16[256,256]{1,0:T(8,128)(2,1)S(1)}, u32[]{:S(2)}, u32[]{:S(2)}) collective-permute-start(bf16[256,256]{1,0:T(8,128)(2,1)S(1)} %get-tuple-element.40.rest_0_), channel_id=1, source_target_pairs={{0,1},{1,0},{2,3},{3,2},{4,5},{5,4},{6,7},{7,6},{8,9},{9,8},{10,11... | collective-permute-start | bytes 393224 | tf_op jit(solution)/shard_map/ppermute | solution.py:51
  20.2 29.6 %copy-start = (f32[512,6144]{1,0:T(8,128)}, f32[512,6144]{1,0:T(8,128)S(1)}, u32[]{:S(2)}) copy-start(f32[512,6144]{1,0:T(8,128)S(1)} %get-tuple-element.41.buf1) | copy-start | bytes 37748740
  20.2 6.4 %collective-permute-start = (bf16[256,256]{1,0:T(8,128)(2,1)S(1)}, bf16[256,256]{1,0:T(8,128)(2,1)S(1)}, u32[]{:S(2)}, u32[]{:S(2)}) collective-permute-start(bf16[256,256]{1,0:T(8,128)(2,1)S(1)} %get-tuple-element.43), channel_id=1, source_target_pairs={{0,1},{1,0},{2,3},{3,2},{4,5},{5,4},{6,7},{7,6},{8,9},{9,8},{10,11... | collective-permute-start | bytes 393224 | tf_op jit(solution)/shard_map/ppermute | solution.py:51
  20.4 8.7 %collective-permute-start.3 = (bf16[256,128]{1,0:T(8,128)(2,1)S(1)}, bf16[256,128]{1,0:T(8,128)(2,1)S(1)}, u32[]{:S(2)}, u32[]{:S(2)}) collective-permute-start(bf16[256,128]{1,0:T(8,128)(2,1)S(1)} %get-tuple-element.48), channel_id=1, source_target_pairs={{0,2},{1,3},{2,0},{3,1},{4,6},{5,7},{6,4},{7,5},{8,10},{9,11},{10,... | collective-permute-start | bytes 196616 | tf_op jit(solution)/shard_map/ppermute | solution.py:51
  26.7 5.2 %collective-permute-start.1 = (bf16[256,128]{1,0:T(8,128)(2,1)S(1)}, bf16[256,128]{1,0:T(8,128)(2,1)S(1)}, u32[]{:S(2)}, u32[]{:S(2)}) collective-permute-start(bf16[256,128]{1,0:T(8,128)(2,1)S(1)} %get-tuple-element.45), channel_id=1, source_target_pairs={{0,2},{1,3},{2,0},{3,1},{4,6},{5,7},{6,4},{7,5},{8,10},{9,11},{10,... | collective-permute-start | bytes 196616 | tf_op jit(solution)/shard_map/ppermute | solution.py:51
  32.0 6.9 %collective-permute-start.4 = (bf16[256,256]{1,0:T(8,128)(2,1)S(1)}, bf16[256,256]{1,0:T(8,128)(2,1)S(1)}, u32[]{:S(2)}, u32[]{:S(2)}) collective-permute-start(bf16[256,256]{1,0:T(8,128)(2,1)S(1)} %fold_last.3.rest_0_.refs_0_), channel_id=1, source_target_pairs={{0,2},{1,3},{2,0},{3,1},{4,6},{5,7},{6,4},{7,5},{8,10},{9,11},{10,... | collective-permute-start | bytes 393224 | tf_op jit(solution)/shard_map/ppermute | solution.py:51
  34.5 7.7 %collective-permute-start.5 = (bf16[256,256]{1,0:T(8,128)(2,1)S(1)}, bf16[256,256]{1,0:T(8,128)(2,1)S(1)}, u32[]{:S(2)}, u32[]{:S(2)}) collective-permute-start(bf16[256,256]{1,0:T(8,128)(2,1)S(1)} %fold_last.3.rest_0_.refs_0_), channel_id=1, source_target_pairs={{0,1},{1,0},{2,3},{3,2},{4,5},{5,4},{6,7},{7,6},{8,9},{9,8},{10,11... | collective-permute-start | bytes 393224 | tf_op jit(solution)/shard_map/ppermute | solution.py:51
  38.8 5.0 %collective-permute-start.6 = (bf16[256,256]{1,0:T(8,128)(2,1)S(1)}, bf16[256,256]{1,0:T(8,128)(2,1)S(1)}, u32[]{:S(2)}, u32[]{:S(2)}) collective-permute-start(bf16[256,256]{1,0:T(8,128)(2,1)S(1)} %collective-permute-done.4.rest_1_.refs_2_), channel_id=1, source_target_pairs={{0,1},{1,0},{2,3},{3,2},{4,5},{5,4},{6,7},{7,6},{8,9},{9,8},{10,11... | collective-permute-start | bytes 393224 | tf_op jit(solution)/shard_map/ppermute | solution.py:51
  44.1 1.7 %collective-permute-start.7 = (f32[128,256]{1,0:T(8,128)S(1)}, f32[128,256]{1,0:T(8,128)S(1)}, u32[]{:S(2)}, u32[]{:S(2)}) collective-permute-start(f32[128,256]{1,0:T(8,128)S(1)} %get-tuple-element.51), channel_id=1, source_target_pairs={{0,4},{4,0},{8,12},{12,8},{16,20},{20,16},{24,28},{28,24},{1,5},{5... | collective-permute-start | bytes 393224 | tf_op jit(solution)/shard_map/ppermute | solution.py:51
  45.8 5.8 %collective-permute-start.12 = (bf16[256,3072]{1,0:T(8,128)(2,1)S(1)}, bf16[256,3072]{1,0:T(8,128)(2,1)S(1)}, u32[]{:S(2)}, u32[]{:S(2)}) collective-permute-start(bf16[256,3072]{1,0:T(8,128)(2,1)S(1)} %hand_on.7.rest_3_), channel_id=1, source_target_pairs={{0,4},{4,0},{8,12},{12,8},{16,20},{20,16},{24,28},{28,24},{1,5},{5... | collective-permute-start | bytes 4718600 | tf_op jit(solution)/shard_map/ppermute | solution.py:51
  46.4 8.6 %collective-permute-start.10 = (f32[128,256]{1,0:T(8,128)S(1)}, f32[128,256]{1,0:T(8,128)S(1)}, u32[]{:S(2)}, u32[]{:S(2)}) collective-permute-start(f32[128,256]{1,0:T(8,128)S(1)} %add.33.refs_1_.rest_2_._), channel_id=1, source_target_pairs={{0,24},{4,28},{8,16},{12,20},{16,8},{20,12},{24,0},{28,4},{1,25},{... | collective-permute-start | bytes 393224 | tf_op jit(solution)/shard_map/ppermute | solution.py:51
  48.8 7.3 %collective-permute-start.9 = (f32[128,256]{1,0:T(8,128)S(1)}, f32[128,256]{1,0:T(8,128)S(1)}, u32[]{:S(2)}, u32[]{:S(2)}) collective-permute-start(f32[128,256]{1,0:T(8,128)S(1)} %add.33.refs_1_.rest_2_._), channel_id=1, source_target_pairs={{0,16},{4,20},{8,24},{12,28},{16,0},{20,4},{24,8},{28,12},{1,17},{... | collective-permute-start | bytes 393224 | tf_op jit(solution)/shard_map/ppermute | solution.py:51
  49.3 7.2 %collective-permute-start.8 = (f32[128,256]{1,0:T(8,128)S(1)}, f32[128,256]{1,0:T(8,128)S(1)}, u32[]{:S(2)}, u32[]{:S(2)}) collective-permute-start(f32[128,256]{1,0:T(8,128)S(1)} %add.33.refs_1_.rest_2_._), channel_id=1, source_target_pairs={{0,8},{4,12},{8,0},{12,4},{16,24},{20,28},{24,16},{28,20},{1,9},{5... | collective-permute-start | bytes 393224 | tf_op jit(solution)/shard_map/ppermute | solution.py:51
  51.6 29.7 %copy-start.1 = (f32[512,6144]{1,0:T(8,128)S(1)}, f32[512,6144]{1,0:T(8,128)}, u32[]{:S(2)}) copy-start(f32[512,6144]{1,0:T(8,128)} %copy-done) | copy-start | bytes 37748740
  52.0 19.3 %collective-permute-start.13 = (bf16[256,768]{1,0:T(8,128)(2,1)S(1)}, bf16[256,768]{1,0:T(8,128)(2,1)S(1)}, u32[]{:S(2)}, u32[]{:S(2)}) collective-permute-start(bf16[256,768]{1,0:T(8,128)(2,1)S(1)} %get-tuple-element.57), channel_id=1, source_target_pairs={{0,8},{4,12},{8,0},{12,4},{16,24},{20,28},{24,16},{28,20},{1,9},{5... | collective-permute-start | bytes 1179656 | tf_op jit(solution)/shard_map/ppermute | solution.py:51
  53.5 17.8 %collective-permute-start.14 = (bf16[256,768]{1,0:T(8,128)(2,1)S(1)}, bf16[256,768]{1,0:T(8,128)(2,1)S(1)}, u32[]{:S(2)}, u32[]{:S(2)}) collective-permute-start(bf16[256,768]{1,0:T(8,128)(2,1)S(1)} %get-tuple-element.58), channel_id=1, source_target_pairs={{0,16},{4,20},{8,24},{12,28},{16,0},{20,4},{24,8},{28,12},{1,17},{... | collective-permute-start | bytes 1179656 | tf_op jit(solution)/shard_map/ppermute | solution.py:51
  55.0 17.4 %collective-permute-start.15 = (bf16[256,768]{1,0:T(8,128)(2,1)S(1)}, bf16[256,768]{1,0:T(8,128)(2,1)S(1)}, u32[]{:S(2)}, u32[]{:S(2)}) collective-permute-start(bf16[256,768]{1,0:T(8,128)(2,1)S(1)} %get-tuple-element.59), channel_id=1, source_target_pairs={{0,24},{4,28},{8,16},{12,20},{16,8},{20,12},{24,0},{28,4},{1,25},{... | collective-permute-start | bytes 1179656 | tf_op jit(solution)/shard_map/ppermute | solution.py:51
  56.5 1.4 %collective-permute-start.11 = (f32[128,256]{1,0:T(8,128)S(1)}, f32[128,256]{1,0:T(8,128)S(1)}, u32[]{:S(2)}, u32[]{:S(2)}) collective-permute-start(f32[128,256]{1,0:T(8,128)S(1)} %add_add_fusion.mine), channel_id=1, source_target_pairs={{0,4},{4,0},{8,12},{12,8},{16,20},{20,16},{24,28},{28,24},{1,5},{5... | collective-permute-start | bytes 393224 | tf_op jit(solution)/shard_map/ppermute | solution.py:51
  73.1 3.1 %collective-permute-start.16 = (bf16[256,768]{1,0:T(8,128)(2,1)S(1)}, bf16[256,768]{1,0:T(8,128)(2,1)S(1)}, u32[]{:S(2)}, u32[]{:S(2)}) collective-permute-start(bf16[256,768]{1,0:T(8,128)(2,1)S(1)} %get-tuple-element.61.refs_0_), channel_id=1, source_target_pairs={{0,4},{4,0},{8,12},{12,8},{16,20},{20,16},{24,28},{28,24},{1,5},{5... | collective-permute-start | bytes 1179656 | tf_op jit(solution)/shard_map/ppermute | solution.py:51
  73.2 11.5 %collective-permute-start.21 = (bf16[256,768]{1,0:T(8,128)(2,1)S(1)}, bf16[256,768]{1,0:T(8,128)(2,1)S(1)}, u32[]{:S(2)}, u32[]{:S(2)}) collective-permute-start(bf16[256,768]{1,0:T(8,128)(2,1)S(1)} %get-tuple-element.61.refs_0_), channel_id=1, source_target_pairs={{0,16},{4,20},{8,24},{12,28},{16,0},{20,4},{24,8},{28,12},{1,17},{... | collective-permute-start | bytes 1179656 | tf_op jit(solution)/shard_map/ppermute | solution.py:51
  74.7 11.2 %collective-permute-start.20 = (bf16[256,768]{1,0:T(8,128)(2,1)S(1)}, bf16[256,768]{1,0:T(8,128)(2,1)S(1)}, u32[]{:S(2)}, u32[]{:S(2)}) collective-permute-start(bf16[256,768]{1,0:T(8,128)(2,1)S(1)} %get-tuple-element.61.refs_0_), channel_id=1, source_target_pairs={{0,8},{4,12},{8,0},{12,4},{16,24},{20,28},{24,16},{28,20},{1,9},{5... | collective-permute-start | bytes 1179656 | tf_op jit(solution)/shard_map/ppermute | solution.py:51
  76.3 8.4 %collective-permute-start.19 = (f32[8,256]{1,0:T(8,128)S(1)}, f32[8,256]{1,0:T(8,128)S(1)}, u32[]{:S(2)}, u32[]{:S(2)}) collective-permute-start(f32[8,256]{1,0:T(8,128)S(1)} %hand_on.8.squares), channel_id=1, source_target_pairs={{0,3},{1,2},{2,1},{3,0},{4,7},{5,6},{6,5},{7,4},{8,11},{9,10},{10,... | collective-permute-start | bytes 24584 | tf_op jit(solution)/shard_map/ppermute | solution.py:51
  79.2 5.5 %collective-permute-start.18 = (f32[8,256]{1,0:T(8,128)S(1)}, f32[8,256]{1,0:T(8,128)S(1)}, u32[]{:S(2)}, u32[]{:S(2)}) collective-permute-start(f32[8,256]{1,0:T(8,128)S(1)} %hand_on.8.squares), channel_id=1, source_target_pairs={{0,2},{1,3},{2,0},{3,1},{4,6},{5,7},{6,4},{7,5},{8,10},{9,11},{10,... | collective-permute-start | bytes 24584 | tf_op jit(solution)/shard_map/ppermute | solution.py:51
  79.3 5.4 %collective-permute-start.17 = (f32[8,256]{1,0:T(8,128)S(1)}, f32[8,256]{1,0:T(8,128)S(1)}, u32[]{:S(2)}, u32[]{:S(2)}) collective-permute-start(f32[8,256]{1,0:T(8,128)S(1)} %hand_on.8.squares), channel_id=1, source_target_pairs={{0,1},{1,0},{2,3},{3,2},{4,5},{5,4},{6,7},{7,6},{8,9},{9,8},{10,11... | collective-permute-start | bytes 24584 | tf_op jit(solution)/shard_map/ppermute | solution.py:51
  85.9 4.6 %collective-permute-start.24 = (f32[8,256]{1,0:T(8,128)S(1)}, f32[8,256]{1,0:T(8,128)S(1)}, u32[]{:S(2)}, u32[]{:S(2)}) collective-permute-start(f32[8,256]{1,0:T(8,128)S(1)} %hand_on.9), channel_id=1, source_target_pairs={{0,24},{4,28},{8,16},{12,20},{16,8},{20,12},{24,0},{28,4},{1,25},{... | collective-permute-start | bytes 24584 | tf_op jit(solution)/shard_map/ppermute | solution.py:51
  87.4 3.7 %collective-permute-start.23 = (f32[8,256]{1,0:T(8,128)S(1)}, f32[8,256]{1,0:T(8,128)S(1)}, u32[]{:S(2)}, u32[]{:S(2)}) collective-permute-start(f32[8,256]{1,0:T(8,128)S(1)} %hand_on.9), channel_id=1, source_target_pairs={{0,16},{4,20},{8,24},{12,28},{16,0},{20,4},{24,8},{28,12},{1,17},{... | collective-permute-start | bytes 24584 | tf_op jit(solution)/shard_map/ppermute | solution.py:51
  88.9 3.7 %collective-permute-start.22 = (f32[8,256]{1,0:T(8,128)S(1)}, f32[8,256]{1,0:T(8,128)S(1)}, u32[]{:S(2)}, u32[]{:S(2)}) collective-permute-start(f32[8,256]{1,0:T(8,128)S(1)} %hand_on.9), channel_id=1, source_target_pairs={{0,8},{4,12},{8,0},{12,4},{16,24},{20,28},{24,16},{28,20},{1,9},{5... | collective-permute-start | bytes 24584 | tf_op jit(solution)/shard_map/ppermute | solution.py:51
  92.6 2.3 %collective-permute-start.27 = (bf16[256,768]{1,0:T(8,128)(2,1)S(1)}, bf16[256,768]{1,0:T(8,128)(2,1)S(1)}, u32[]{:S(2)}, u32[]{:S(2)}) collective-permute-start(bf16[256,768]{1,0:T(8,128)(2,1)S(1)} %hand_on.10.refs_1_.refs_0_), channel_id=1, source_target_pairs={{0,4},{4,0},{8,12},{12,8},{16,20},{20,16},{24,28},{28,24},{1,5},{5... | collective-permute-start | bytes 1179656 | tf_op jit(solution)/shard_map/ppermute | solution.py:51
  92.6 2.3 %collective-permute-start.28 = (bf16[256,768]{1,0:T(8,128)(2,1)S(1)}, bf16[256,768]{1,0:T(8,128)(2,1)S(1)}, u32[]{:S(2)}, u32[]{:S(2)}) collective-permute-start(bf16[256,768]{1,0:T(8,128)(2,1)S(1)} %hand_on.11.refs_2_), channel_id=1, source_target_pairs={{0,4},{4,0},{8,12},{12,8},{16,20},{20,16},{24,28},{28,24},{1,5},{5... | collective-permute-start | bytes 1179656 | tf_op jit(solution)/shard_map/ppermute | solution.py:51
  93.1 12.0 %collective-permute-start.26 = (bf16[256,768]{1,0:T(8,128)(2,1)S(1)}, bf16[256,768]{1,0:T(8,128)(2,1)S(1)}, u32[]{:S(2)}, u32[]{:S(2)}) collective-permute-start(bf16[256,768]{1,0:T(8,128)(2,1)S(1)} %hand_on.12.refs_4_.refs_0_), channel_id=1, source_target_pairs={{0,24},{4,28},{8,16},{12,20},{16,8},{20,12},{24,0},{28,4},{1,25},{... | collective-permute-start | bytes 1179656 | tf_op jit(solution)/shard_map/ppermute | solution.py:51
  93.6 1.3 %collective-permute-start.25 = (f32[8,256]{1,0:T(8,128)S(1)}, f32[8,256]{1,0:T(8,128)S(1)}, u32[]{:S(2)}, u32[]{:S(2)}) collective-permute-start(f32[8,256]{1,0:T(8,128)S(1)} %add_add_fusion.1.refs_1_), channel_id=1, source_target_pairs={{0,4},{4,0},{8,12},{12,8},{16,20},{20,16},{24,28},{28,24},{1,5},{5... | collective-permute-start | bytes 24584 | tf_op jit(solution)/shard_map/ppermute | solution.py:51
  105.1 3.2 %collective-permute-start.29 = (bf16[256,768]{1,0:T(8,128)(2,1)S(1)}, bf16[256,768]{1,0:T(8,128)(2,1)S(1)}, u32[]{:S(2)}, u32[]{:S(2)}) collective-permute-start(bf16[256,768]{1,0:T(8,128)(2,1)S(1)} %hand_on.13.refs_0_), channel_id=1, source_target_pairs={{0,4},{4,0},{8,12},{12,8},{16,20},{20,16},{24,28},{28,24},{1,5},{5... | collective-permute-start | bytes 1179656 | tf_op jit(solution)/shard_map/ppermute | solution.py:51

commit v10 on v9

--- a/solution.py
+++ b/solution.py
@@ -315,8 +315,13 @@
 
 
 def chol_inverse_kernel(mine, other, weight, out, fetched, work, sem):
-    fetch = pltpu.make_async_copy(weight, fetched, sem)
-    fetch.start()
+    piece = weight.shape[0] // sem.shape[0]
+    fetches = [
+        pltpu.make_async_copy(weight.at[pl.ds(k * piece, piece), :], fetched.at[pl.ds(k * piece, piece), :], sem.at[k])
+        for k in range(sem.shape[0])
+    ]
+    for fetch in fetches:
+        fetch.start()
     n = out.shape[0]
     h = n // 2
     core = lax.bitwise_and(lax.axis_index("row"), jnp.int32(1))
@@ -339,7 +344,8 @@
                 lead, s, (((0,), (0,)), ((), ())), precision=lax.Precision.HIGHEST, preferred_element_type=f32
             )
     out[...] = jnp.where(r_id >= c_id, work[:, n:], 0.0)
-    fetch.wait()
+    for fetch in fetches:
+        fetch.wait()
 
 
 def chol_inverse(mine, other, weight):
@@ -349,7 +355,7 @@
         out_shape=(shape((n, n), f32), pltpu.VMEM(weight.shape, weight.dtype)),
         in_specs=[VMEM, VMEM, ANY],
         out_specs=(VMEM, VMEM),
-        scratch_shapes=[pltpu.VMEM((n, 2 * n), f32), pltpu.SemaphoreType.DMA],
+        scratch_shapes=[pltpu.VMEM((n, 2 * n), f32), pltpu.SemaphoreType.DMA((8,))],
         compiler_params=params(8),
         cost_estimate=cost(*[mine] * 256),
         name="chol_inverse",
@@ -451,9 +457,16 @@
             copies.append((mbuf, new_momentum))
         if weight_too:
             copies.append((vbuf, new_weight))
+        pieces = out_sems.shape[3]
+        piece = ortho_ref.shape[0] // pieces
         return [
-            pltpu.make_async_copy(src.at[b % 2, :, at], dst.at[:, there], out_sems.at[k, b % 2, t])
+            pltpu.make_async_copy(
+                src.at[b % 2, pl.ds(i * piece, piece), at],
+                dst.at[pl.ds(i * piece, piece), there],
+                out_sems.at[k, b % 2, t, i],
+            )
             for k, (src, dst) in enumerate(copies)
+            for i in range(pieces)
         ]
 
     def finish(b):
@@ -518,7 +531,7 @@
             pltpu.VMEM((2, m_rows, width), f32),
             pltpu.VMEM((2, w_rows, width), bf16),
             pltpu.VMEM((2, r, width), bf16),
-            pltpu.SemaphoreType.DMA((2, 2, width // 256)),
+            pltpu.SemaphoreType.DMA((2, 2, width // 256, 4)),
             pltpu.SemaphoreType.DMA((2,)),
         ],
         compiler_params=params(12),
@@ -598,26 +611,34 @@
     common = (factor, bufs, ortho_bf, weight)
     squares = exchange(hand_on(squares, own_pair), "col", depth)
     (momentum,), token = results((0,), (True, False), *common, squares[0], (share, own_pair))
-    squares = hand_on(pair_up(squares), *blocks.values(), token)
+    squares = pair_up(squares)
+    squares = squares + swap(squares, "row", 1)
+    squares = hand_on(squares, *blocks.values(), token)
     squares = pair_up(exchange(squares, "row", chips, 2))
     pairs = {}
     for d in near[1:]:
         block = hand_on(blocks[d], squares)
         pairs[d] = (block, swap(block, "row", 1))
-    squares = squares + swap(squares, "row", 1)
-    share = hand_on(share, *[pair[0] for pair in pairs.values()])
     pairs[0] = (share, own_pair)
-    far = [d for d in range(chips) if d not in near]
-    blocks = {d: swap(share, "row", 2 * d) for d in far}
+    h = share.shape[0] // 2
+    blocks = {d: pairs[d][0] for d in near}
+    halves = {}
+    for d in range(chips):
+        if d not in near:
+            least, most = d & -d, 1 << (d.bit_length() - 1)
+            top = swap(blocks[d ^ most][:h], "row", 2 * most)
+            bottom = swap(blocks[d ^ least][h:], "row", 2 * least)
+            halves[d] = top, bottom
+            blocks[d] = jnp.concatenate([top, bottom], axis=0)
 
     common = (*common, squares)
     weight_basis = ()
     if near[1:]:
         rest = [x for d in near[1:] for x in pairs[d]]
         (*weight_basis, momentum), token = results(
-            tuple(near[1:]), (True, True), *common, rest, (), (share,), [momentum]
+            tuple(near[1:]), (True, True), *common, rest, (), (), [momentum]
         )
-    blocks = {d: hand_on(block, token) for d, block in blocks.items()}
+    blocks = {d: jnp.concatenate([hand_on(top, token), bottom], axis=0) for d, (top, bottom) in halves.items()}
     weight_basis, token = results((0,), (False, True), *common, pairs[0], weight_basis)
     outs = [*weight_basis, momentum]
     for d, block in blocks.items():

time: 114 us -> 114 us (level)
  waiting for transfers between devices: 23.3 us -> 20 us
  starting transfers between devices: 31.3 us -> 33.2 us
  Pallas kernels: 57.7 us -> 59 us
    ppermute x30 -> x31, waiting for transfers between devices: 23.3 us -> 20 us  [swap(): lax.ppermute(x, axis, [(i, i ^ d) for i in range(lax.axis_size(axis))])]
    ppermute x30 -> x31, starting transfers between devices: 31.3 us -> 33.2 us  [swap(): lax.ppermute(x, axis, [(i, i ^ d) for i in range(lax.axis_size(axis))])]
  transfers between devices with their start and end apart: 30 -> 31, of which waited for: 13 -> 12; matrix products, arithmetic and copies ran while one was open for 0% -> 0% of each run, Pallas kernels for 38% -> 39%
where the time goes in v10:
time: 114 us; the launch traced here: 113 us
  Pallas kernels  59 us (52%)
  starting transfers between devices  33.2 us (29%)
  waiting for transfers between devices  20 us (18%)
  between operations  1.16 us (1%)
    ppermute x31, starting transfers between devices, swap(): lax.ppermute(x, axis, [(i, i ^ d) for i in range(lax.axis_size(axis))])  33.2 us
    pallas_call x4, Pallas kernels, results(): pl.pallas_call(functools.partial(result_kernel, pairs, *kinds, factor), o...  20.2 us
    ppermute x31, waiting for transfers between devices, swap(): lax.ppermute(x, axis, [(i, i ^ d) for i in range(lax.axis_size(axis))])  20 us
    pallas_call x2, Pallas kernels, project(): pl.pallas_call(functools.partial(project_kernel, part, depth, width), out...  16.5 us
    pallas_call x1, Pallas kernels, chol_inverse(): pl.pallas_call(chol_inverse_kernel, out_shape=(shape((n, n), f32), pltpu....  13.5 us
    pallas_call x1, Pallas kernels, first_product(): pl.pallas_call(functools.partial(first_kernel, depth, width), out_shape=(...  3.36 us
    pallas_call x2, Pallas kernels, last_product(): pl.pallas_call(functools.partial(last_kernel, depth, width, mine), out_sh...  3.31 us
  transfers between devices with their start and end apart: 31, of which 12 were waited for; matrix products, arithmetic and copies ran while one was open for 0% of the time, Pallas kernels for 39%

profile of v10, /device:TPU:0, one launch (start us, length us, event | category | flops | bytes accessed | tf_op | source)
XLA Modules:
  0.0 113.4 jit_solution(7570210728864153553)
XLA Ops:
  0.6 8.7 %project.2 = (f32[512,6144]{1,0:T(8,128)S(1)}, bf16[256,6144]{1,0:T(8,128)(2,1)S(1)}, f32[256,256]{1,0:T(8,128)S(1)}, bf16[256,256]{1,0:T(8,128)(2,1)S(1)}) custom-call(f32[1024,6144]{1,0:T(8,128)} %mom.3, bf16[1024,6144]{1,0:T(8,128)(2,1)} %grad.3, bf16[256,6144]{1,0:T(8,128)(2,1)} %basis.1), custom_call_target="tpu_custom_call" | custom-call | bytes 37748736 | tf_op jit(solution)/shard_map/project/pallas_call | solution.py:104
  9.3 3.1 %collective-permute-start.2 = (bf16[256,256]{1,0:T(8,128)(2,1)S(1)}, bf16[256,256]{1,0:T(8,128)(2,1)S(1)}, u32[]{:S(2)}, u32[]{:S(2)}) collective-permute-start(bf16[256,256]{1,0:T(8,128)(2,1)S(1)} %get-tuple-element.40.rest_0_), channel_id=1, source_target_pairs={{0,1},{1,0},{2,3},{3,2},{4,5},{5,4},{6,7},{7,6},{8,9},{9,8},{10,11... | collective-permute-start | bytes 393224 | tf_op jit(solution)/shard_map/ppermute | solution.py:51
  12.4 7.8 %project.3 = (f32[512,6144]{1,0:T(8,128)S(1)}, f32[256,256]{1,0:T(8,128)S(1)}, bf16[256,256]{1,0:T(8,128)(2,1)S(1)}) custom-call(f32[1024,6144]{1,0:T(8,128)} %mom.3, bf16[1024,6144]{1,0:T(8,128)(2,1)} %grad.3, bf16[256,6144]{1,0:T(8,128)(2,1)S(1)} %get-tuple-element.39.basis, bf16[256,256]{1,0:T(8,128)(2,1)S(1)} %get-tuple-element.40.rest_0_), custom_call_target="tpu_custom_call" | custom-call | bytes 37748736 | tf_op jit(solution)/shard_map/project/pallas_call | solution.py:104
  20.4 3.1 %collective-permute-start.3 = (bf16[256,128]{1,0:T(8,128)(2,1)S(1)}, bf16[256,128]{1,0:T(8,128)(2,1)S(1)}, u32[]{:S(2)}, u32[]{:S(2)}) collective-permute-start(bf16[256,128]{1,0:T(8,128)(2,1)S(1)} %get-tuple-element.48), channel_id=1, source_target_pairs={{0,2},{1,3},{2,0},{3,1},{4,6},{5,7},{6,4},{7,5},{8,10},{9,11},{10,... | collective-permute-start | bytes 196616 | tf_op jit(solution)/shard_map/ppermute | solution.py:51
  23.4 3.2 %collective-permute-done.received = bf16[256,256]{1,0:T(8,128)(2,1)S(1)} collective-permute-done((bf16[256,256]{1,0:T(8,128)(2,1)S(1)}, bf16[256,256]{1,0:T(8,128)(2,1)S(1)}, u32[]{:S(2)}, u32[]{:S(2)}) %collective-permute-start) | collective-permute-done | bytes 131104 | tf_op jit(solution)/shard_map/ppermute | solution.py:51
  26.7 2.3 %collective-permute-start.1 = (bf16[256,128]{1,0:T(8,128)(2,1)S(1)}, bf16[256,128]{1,0:T(8,128)(2,1)S(1)}, u32[]{:S(2)}, u32[]{:S(2)}) collective-permute-start(bf16[256,128]{1,0:T(8,128)(2,1)S(1)} %get-tuple-element.45), channel_id=1, source_target_pairs={{0,2},{1,3},{2,0},{3,1},{4,6},{5,7},{6,4},{7,5},{8,10},{9,11},{10,... | collective-permute-start | bytes 196616 | tf_op jit(solution)/shard_map/ppermute | solution.py:51
  29.0 2.9 %collective-permute-done.1.received = bf16[256,128]{1,0:T(8,128)(2,1)S(1)} collective-permute-done((bf16[256,128]{1,0:T(8,128)(2,1)S(1)}, bf16[256,128]{1,0:T(8,128)(2,1)S(1)}, u32[]{:S(2)}, u32[]{:S(2)}) %collective-permute-start.1) | collective-permute-done | bytes 65568 | tf_op jit(solution)/shard_map/ppermute | solution.py:51
  32.0 2.5 %collective-permute-start.4 = (bf16[256,256]{1,0:T(8,128)(2,1)S(1)}, bf16[256,256]{1,0:T(8,128)(2,1)S(1)}, u32[]{:S(2)}, u32[]{:S(2)}) collective-permute-start(bf16[256,256]{1,0:T(8,128)(2,1)S(1)} %fold_last.3.rest_0_.refs_0_), channel_id=1, source_target_pairs={{0,2},{1,3},{2,0},{3,1},{4,6},{5,7},{6,4},{7,5},{8,10},{9,11},{10,... | collective-permute-start | bytes 393224 | tf_op jit(solution)/shard_map/ppermute | solution.py:51
  34.5 4.4 %collective-permute-done.4.rest_1_.refs_2_ = bf16[256,256]{1,0:T(8,128)(2,1)S(1)} collective-permute-done((bf16[256,256]{1,0:T(8,128)(2,1)S(1)}, bf16[256,256]{1,0:T(8,128)(2,1)S(1)}, u32[]{:S(2)}, u32[]{:S(2)}) %collective-permute-start.4) | collective-permute-done | bytes 131104 | tf_op jit(solution)/shard_map/ppermute | solution.py:51
  38.8 3.4 %first_product.1 = (f32[256,3072]{1,0:T(8,128)S(1)}, f32[256,3072]{1,0:T(8,128)S(1)}, f32[256,256]{1,0:T(8,128)S(1)}) custom-call(f32[512,6144]{1,0:T(8,128)S(1)} %get-tuple-element.38.buf0, f32[512,6144]{1,0:T(8,128)S(1)} %get-tuple-element.41.buf1, bf16[256,256]{1,0:T(8,128)(2,1)S(1)} %fold_last.3.rest_0_.refs_0_, ...), custom_call_target="tpu_custom_call" | custom-call | bytes 31457280 | tf_op jit(solution)/shard_map/first_product/pallas_call | solution.py:211
  42.2 1.6 %collective-permute-done.6.rest_1_.refs_3_ = bf16[256,256]{1,0:T(8,128)(2,1)S(1)} collective-permute-done((bf16[256,256]{1,0:T(8,128)(2,1)S(1)}, bf16[256,256]{1,0:T(8,128)(2,1)S(1)}, u32[]{:S(2)}, u32[]{:S(2)}) %collective-permute-start.6) | collective-permute-done | bytes 131104 | tf_op jit(solution)/shard_map/ppermute | solution.py:51
  43.8 0.3 gram.1
  44.2 1.6 %other_product.1.refs_0_ = bf16[256,3072]{1,0:T(8,128)(2,1)S(1)} custom-call(f32[512,6144]{1,0:T(8,128)S(1)} %get-tuple-element.38.buf0, f32[512,6144]{1,0:T(8,128)S(1)} %get-tuple-element.41.buf1, f32[256,3072]{1,0:T(8,128)S(1)} %get-tuple-element.55.sums, bf16[256,256]{1,0:T(8,128)(2,1)S(1)} %collective-permute-done.5.rest_0_.refs_1_, ...), custom_call_target="tpu_custom_call" | custom-call | bytes 15728640 | tf_op jit(solution)/shard_map/other_product/pallas_call | solution.py:266
  45.8 0.6 collective-permute-start.12
  46.4 2.4 %collective-permute-start.10 = (f32[128,256]{1,0:T(8,128)S(1)}, f32[128,256]{1,0:T(8,128)S(1)}, u32[]{:S(2)}, u32[]{:S(2)}) collective-permute-start(f32[128,256]{1,0:T(8,128)S(1)} %add.33.refs_1_.rest_2_._), channel_id=1, source_target_pairs={{0,24},{4,28},{8,16},{12,20},{16,8},{20,12},{24,0},{28,4},{1,25},{... | collective-permute-start | bytes 393224 | tf_op jit(solution)/shard_map/ppermute | solution.py:51
  48.8 0.5 collective-permute-start.9
  49.3 0.6 collective-permute-start.8
  49.9 1.7 %mine_product.1.mine = f32[256,3072]{1,0:T(8,128)S(1)} custom-call(f32[512,6144]{1,0:T(8,128)S(1)} %get-tuple-element.38.buf0, f32[512,6144]{1,0:T(8,128)S(1)} %get-tuple-element.41.buf1, f32[256,3072]{1,0:T(8,128)S(1)} %get-tuple-element.54.sums, bf16[256,256]{1,0:T(8,128)(2,1)S(1)} %collective-permute-done.5.rest_0_.refs_1_, ...), custom_call_target="tpu_custom_call" | custom-call | bytes 15728640 | tf_op jit(solution)/shard_map/mine_product/pallas_call | solution.py:266
  51.6 0.3 pair_sum.1
  52.0 1.5 %collective-permute-start.13 = (bf16[256,768]{1,0:T(8,128)(2,1)S(1)}, bf16[256,768]{1,0:T(8,128)(2,1)S(1)}, u32[]{:S(2)}, u32[]{:S(2)}) collective-permute-start(bf16[256,768]{1,0:T(8,128)(2,1)S(1)} %get-tuple-element.57), channel_id=1, source_target_pairs={{0,8},{4,12},{8,0},{12,4},{16,24},{20,28},{24,16},{28,20},{1,9},{5... | collective-permute-start | bytes 1179656 | tf_op jit(solution)/shard_map/ppermute | solution.py:51
  53.5 1.5 %collective-permute-start.14 = (bf16[256,768]{1,0:T(8,128)(2,1)S(1)}, bf16[256,768]{1,0:T(8,128)(2,1)S(1)}, u32[]{:S(2)}, u32[]{:S(2)}) collective-permute-start(bf16[256,768]{1,0:T(8,128)(2,1)S(1)} %get-tuple-element.58), channel_id=1, source_target_pairs={{0,16},{4,20},{8,24},{12,28},{16,0},{20,4},{24,8},{28,12},{1,17},{... | collective-permute-start | bytes 1179656 | tf_op jit(solution)/shard_map/ppermute | solution.py:51
  55.0 1.1 collective-permute-start.15
  56.1 0.4 collective-permute-done.8
  56.6 1.3 %collective-permute-done.11.other = f32[128,256]{1,0:T(8,128)S(1)} collective-permute-done((f32[128,256]{1,0:T(8,128)S(1)}, f32[128,256]{1,0:T(8,128)S(1)}, u32[]{:S(2)}, u32[]{:S(2)}) %collective-permute-start.11) | collective-permute-done | bytes 131104 | tf_op jit(solution)/shard_map/ppermute | solution.py:51
  57.9 13.5 %chol_inverse.1 = (f32[256,256]{1,0:T(8,128)S(1)}, bf16[1024,6144]{1,0:T(8,128)(2,1)S(1)}) custom-call(f32[128,256]{1,0:T(8,128)S(1)} %add_add_fusion.mine, f32[128,256]{1,0:T(8,128)S(1)} %collective-permute-done.11.other, bf16[1024,6144]{1,0:T(8,128)(2,1)} %weight.1), custom_call_target="tpu_custom_call" | custom-call | bytes 33554432 | tf_op jit(solution)/shard_map/chol_inverse/pallas_call | solution.py:353
  71.5 0.9 collective-permute-done.15.refs_2_
  72.4 0.7 share.1
  73.2 1.6 %collective-permute-start.22 = (bf16[256,768]{1,0:T(8,128)(2,1)S(1)}, bf16[256,768]{1,0:T(8,128)(2,1)S(1)}, u32[]{:S(2)}, u32[]{:S(2)}) collective-permute-start(bf16[256,768]{1,0:T(8,128)(2,1)S(1)} %get-tuple-element.61.refs_0_), channel_id=1, source_target_pairs={{0,16},{4,20},{8,24},{12,28},{16,0},{20,4},{24,8},{28,12},{1,17},{... | collective-permute-start | bytes 1179656 | tf_op jit(solution)/shard_map/ppermute | solution.py:51
  74.7 1.5 %collective-permute-start.21 = (bf16[256,768]{1,0:T(8,128)(2,1)S(1)}, bf16[256,768]{1,0:T(8,128)(2,1)S(1)}, u32[]{:S(2)}, u32[]{:S(2)}) collective-permute-start(bf16[256,768]{1,0:T(8,128)(2,1)S(1)} %get-tuple-element.61.refs_0_), channel_id=1, source_target_pairs={{0,8},{4,12},{8,0},{12,4},{16,24},{20,28},{24,16},{28,20},{1,9},{5... | collective-permute-start | bytes 1179656 | tf_op jit(solution)/shard_map/ppermute | solution.py:51
  76.2 2.9 %collective-permute-start.19 = (f32[8,256]{1,0:T(8,128)S(1)}, f32[8,256]{1,0:T(8,128)S(1)}, u32[]{:S(2)}, u32[]{:S(2)}) collective-permute-start(f32[8,256]{1,0:T(8,128)S(1)} %hand_on.7.squares), channel_id=1, source_target_pairs={{0,3},{1,2},{2,1},{3,0},{4,7},{5,6},{6,5},{7,4},{8,11},{9,10},{10,... | collective-permute-start | bytes 24584 | tf_op jit(solution)/shard_map/ppermute | solution.py:51
  79.2 0.1 collective-permute-start.18
  79.3 1.4 %collective-permute-start.17 = (f32[8,256]{1,0:T(8,128)S(1)}, f32[8,256]{1,0:T(8,128)S(1)}, u32[]{:S(2)}, u32[]{:S(2)}) collective-permute-start(f32[8,256]{1,0:T(8,128)S(1)} %hand_on.7.squares), channel_id=1, source_target_pairs={{0,1},{1,0},{2,3},{3,2},{4,5},{5,4},{6,7},{7,6},{8,9},{9,8},{10,11... | collective-permute-start | bytes 24584 | tf_op jit(solution)/shard_map/ppermute | solution.py:51
  80.6 1.1 collective-permute-done.19
  81.7 2.0 %collective-permute-done.18 = f32[8,256]{1,0:T(8,128)S(1)} collective-permute-done((f32[8,256]{1,0:T(8,128)S(1)}, f32[8,256]{1,0:T(8,128)S(1)}, u32[]{:S(2)}, u32[]{:S(2)}) %collective-permute-start.18) | collective-permute-done | bytes 8224 | tf_op jit(solution)/shard_map/ppermute | solution.py:51
  83.8 0.6 ortho.1.ortho_ref
  84.4 3.6 %results.4 = (f32[1024,6144]{1,0:T(8,128)}, f32[8,128]{1,0:T(8,128)S(1)}) custom-call(f32[512,6144]{1,0:T(8,128)S(1)} %get-tuple-element.38.buf0, f32[512,6144]{1,0:T(8,128)S(1)} %copy-done.1, bf16[1024,256]{1,0:T(8,128)(2,1)S(1)} %ortho.1.ortho_ref, bf16[1024,6144]{1,0:T(8,128)(2,1)S(1)} %get-tuple-element.53.weight, f32[8,256]{1,0:T(8,128)S(1)} %hand_on.7.squares, ...), custom_call_target="tpu_custom_call" | custom-call | bytes 6291456 | tf_op jit(solution)/shard_map/results/pallas_call | solution.py:524
  88.1 1.1 %collective-permute-start.25 = (f32[8,256]{1,0:T(8,128)S(1)}, f32[8,256]{1,0:T(8,128)S(1)}, u32[]{:S(2)}, u32[]{:S(2)}) collective-permute-start(f32[8,256]{1,0:T(8,128)S(1)} %hand_on.8), channel_id=1, source_target_pairs={{0,24},{4,28},{8,16},{12,20},{16,8},{20,12},{24,0},{28,4},{1,25},{... | collective-permute-start | bytes 24584 | tf_op jit(solution)/shard_map/ppermute | solution.py:51
  89.3 0.9 collective-permute-start.24
  90.2 1.5 %collective-permute-start.23 = (f32[8,256]{1,0:T(8,128)S(1)}, f32[8,256]{1,0:T(8,128)S(1)}, u32[]{:S(2)}, u32[]{:S(2)}) collective-permute-start(f32[8,256]{1,0:T(8,128)S(1)} %hand_on.8), channel_id=1, source_target_pairs={{0,8},{4,12},{8,0},{12,4},{16,24},{20,28},{24,16},{28,20},{1,9},{5... | collective-permute-start | bytes 24584 | tf_op jit(solution)/shard_map/ppermute | solution.py:51
  91.7 1.1 collective-permute-done.25
  92.7 0.2 collective-permute-done.24
  92.9 0.9 collective-permute-done.23
  93.8 0.5 collective-permute-start.28
  94.3 1.2 %collective-permute-start.26 = (bf16[128,768]{1,0:T(8,128)(2,1)S(1)}, bf16[128,768]{1,0:T(8,128)(2,1)S(1)}, u32[]{:S(2)}, u32[]{:S(2)}) collective-permute-start(bf16[128,768]{1,0:T(8,128)(2,1)S(1)} %slice.8), channel_id=1, source_target_pairs={{0,16},{4,20},{8,24},{12,28},{16,0},{20,4},{24,8},{28,12},{1,17},{... | collective-permute-start | bytes 589832 | tf_op jit(solution)/shard_map/ppermute | solution.py:51
  95.6 0.9 collective-permute-start.29
  96.5 7.8 %results.5 = (bf16[1024,6144]{1,0:T(8,128)(2,1)}, bf16[256,6144]{1,0:T(8,128)(2,1)}, f32[1024,6144]{1,0:T(8,128)}, f32[8,128]{1,0:T(8,128)S(1)}) custom-call(f32[512,6144]{1,0:T(8,128)S(1)} %get-tuple-element.38.buf0, f32[512,6144]{1,0:T(8,128)S(1)} %copy-done.1, bf16[1024,256]{1,0:T(8,128)(2,1)S(1)} %ortho.1.ortho_ref, ...), custom_call_target="tpu_custom_call", output_to_operand_aliasing={{2}: (9, {})} | custom-call | bytes 25165824 | tf_op jit(solution)/shard_map/results/pallas_call | solution.py:524
  104.4 3.5 %results.6 = (bf16[1024,6144]{1,0:T(8,128)(2,1)}, bf16[256,6144]{1,0:T(8,128)(2,1)}, f32[8,128]{1,0:T(8,128)}) custom-call(f32[512,6144]{1,0:T(8,128)S(1)} %get-tuple-element.38.buf0, f32[512,6144]{1,0:T(8,128)S(1)} %copy-done.1, bf16[1024,256]{1,0:T(8,128)(2,1)S(1)} %ortho.1.ortho_ref, ...), custom_call_target="tpu_custom_call", output_to_operand_aliasing={{0}: (7, {}), {1}: (8, {})} | custom-call | bytes 6291456 | tf_op jit(solution)/shard_map/results/pallas_call | solution.py:524
  107.9 5.3 %results.7 = (bf16[1024,6144]{1,0:T(8,128)(2,1)}, bf16[256,6144]{1,0:T(8,128)(2,1)}, f32[1024,6144]{1,0:T(8,128)}, f32[8,128]{1,0:T(8,128)}) custom-call(f32[512,6144]{1,0:T(8,128)S(1)} %get-tuple-element.38.buf0, f32[512,6144]{1,0:T(8,128)S(1)} %copy-done.1, ...), custom_call_target="tpu_custom_call", output_to_operand_aliasing={{0}: (7, {}), {1}: (8, {}), {2}: (9, {})} | custom-call | bytes 12582912 | tf_op jit(solution)/shard_map/results/pallas_call | solution.py:524
  (50 shorter events, 0.7 us)
Async XLA Ops:
  9.3 11.0 %collective-permute-start.2 = (bf16[256,256]{1,0:T(8,128)(2,1)S(1)}, bf16[256,256]{1,0:T(8,128)(2,1)S(1)}, u32[]{:S(2)}, u32[]{:S(2)}) collective-permute-start(bf16[256,256]{1,0:T(8,128)(2,1)S(1)} %get-tuple-element.40.rest_0_), channel_id=1, source_target_pairs={{0,1},{1,0},{2,3},{3,2},{4,5},{5,4},{6,7},{7,6},{8,9},{9,8},{10,11... | collective-permute-start | bytes 393224 | tf_op jit(solution)/shard_map/ppermute | solution.py:51
  20.2 29.6 %copy-start = (f32[512,6144]{1,0:T(8,128)}, f32[512,6144]{1,0:T(8,128)S(1)}, u32[]{:S(2)}) copy-start(f32[512,6144]{1,0:T(8,128)S(1)} %get-tuple-element.41.buf1) | copy-start | bytes 37748740
  20.2 6.4 %collective-permute-start = (bf16[256,256]{1,0:T(8,128)(2,1)S(1)}, bf16[256,256]{1,0:T(8,128)(2,1)S(1)}, u32[]{:S(2)}, u32[]{:S(2)}) collective-permute-start(bf16[256,256]{1,0:T(8,128)(2,1)S(1)} %get-tuple-element.43), channel_id=1, source_target_pairs={{0,1},{1,0},{2,3},{3,2},{4,5},{5,4},{6,7},{7,6},{8,9},{9,8},{10,11... | collective-permute-start | bytes 393224 | tf_op jit(solution)/shard_map/ppermute | solution.py:51
  20.4 8.7 %collective-permute-start.3 = (bf16[256,128]{1,0:T(8,128)(2,1)S(1)}, bf16[256,128]{1,0:T(8,128)(2,1)S(1)}, u32[]{:S(2)}, u32[]{:S(2)}) collective-permute-start(bf16[256,128]{1,0:T(8,128)(2,1)S(1)} %get-tuple-element.48), channel_id=1, source_target_pairs={{0,2},{1,3},{2,0},{3,1},{4,6},{5,7},{6,4},{7,5},{8,10},{9,11},{10,... | collective-permute-start | bytes 196616 | tf_op jit(solution)/shard_map/ppermute | solution.py:51
  26.7 5.2 %collective-permute-start.1 = (bf16[256,128]{1,0:T(8,128)(2,1)S(1)}, bf16[256,128]{1,0:T(8,128)(2,1)S(1)}, u32[]{:S(2)}, u32[]{:S(2)}) collective-permute-start(bf16[256,128]{1,0:T(8,128)(2,1)S(1)} %get-tuple-element.45), channel_id=1, source_target_pairs={{0,2},{1,3},{2,0},{3,1},{4,6},{5,7},{6,4},{7,5},{8,10},{9,11},{10,... | collective-permute-start | bytes 196616 | tf_op jit(solution)/shard_map/ppermute | solution.py:51
  32.0 6.9 %collective-permute-start.4 = (bf16[256,256]{1,0:T(8,128)(2,1)S(1)}, bf16[256,256]{1,0:T(8,128)(2,1)S(1)}, u32[]{:S(2)}, u32[]{:S(2)}) collective-permute-start(bf16[256,256]{1,0:T(8,128)(2,1)S(1)} %fold_last.3.rest_0_.refs_0_), channel_id=1, source_target_pairs={{0,2},{1,3},{2,0},{3,1},{4,6},{5,7},{6,4},{7,5},{8,10},{9,11},{10,... | collective-permute-start | bytes 393224 | tf_op jit(solution)/shard_map/ppermute | solution.py:51
  34.5 7.7 %collective-permute-start.5 = (bf16[256,256]{1,0:T(8,128)(2,1)S(1)}, bf16[256,256]{1,0:T(8,128)(2,1)S(1)}, u32[]{:S(2)}, u32[]{:S(2)}) collective-permute-start(bf16[256,256]{1,0:T(8,128)(2,1)S(1)} %fold_last.3.rest_0_.refs_0_), channel_id=1, source_target_pairs={{0,1},{1,0},{2,3},{3,2},{4,5},{5,4},{6,7},{7,6},{8,9},{9,8},{10,11... | collective-permute-start | bytes 393224 | tf_op jit(solution)/shard_map/ppermute | solution.py:51
  38.8 5.0 %collective-permute-start.6 = (bf16[256,256]{1,0:T(8,128)(2,1)S(1)}, bf16[256,256]{1,0:T(8,128)(2,1)S(1)}, u32[]{:S(2)}, u32[]{:S(2)}) collective-permute-start(bf16[256,256]{1,0:T(8,128)(2,1)S(1)} %collective-permute-done.4.rest_1_.refs_2_), channel_id=1, source_target_pairs={{0,1},{1,0},{2,3},{3,2},{4,5},{5,4},{6,7},{7,6},{8,9},{9,8},{10,11... | collective-permute-start | bytes 393224 | tf_op jit(solution)/shard_map/ppermute | solution.py:51
  44.1 1.7 %collective-permute-start.7 = (f32[128,256]{1,0:T(8,128)S(1)}, f32[128,256]{1,0:T(8,128)S(1)}, u32[]{:S(2)}, u32[]{:S(2)}) collective-permute-start(f32[128,256]{1,0:T(8,128)S(1)} %get-tuple-element.51), channel_id=1, source_target_pairs={{0,4},{4,0},{8,12},{12,8},{16,20},{20,16},{24,28},{28,24},{1,5},{5... | collective-permute-start | bytes 393224 | tf_op jit(solution)/shard_map/ppermute | solution.py:51
  45.8 5.8 %collective-permute-start.12 = (bf16[256,3072]{1,0:T(8,128)(2,1)S(1)}, bf16[256,3072]{1,0:T(8,128)(2,1)S(1)}, u32[]{:S(2)}, u32[]{:S(2)}) collective-permute-start(bf16[256,3072]{1,0:T(8,128)(2,1)S(1)} %hand_on.6.rest_3_), channel_id=1, source_target_pairs={{0,4},{4,0},{8,12},{12,8},{16,20},{20,16},{24,28},{28,24},{1,5},{5... | collective-permute-start | bytes 4718600 | tf_op jit(solution)/shard_map/ppermute | solution.py:51
  46.4 8.6 %collective-permute-start.10 = (f32[128,256]{1,0:T(8,128)S(1)}, f32[128,256]{1,0:T(8,128)S(1)}, u32[]{:S(2)}, u32[]{:S(2)}) collective-permute-start(f32[128,256]{1,0:T(8,128)S(1)} %add.33.refs_1_.rest_2_._), channel_id=1, source_target_pairs={{0,24},{4,28},{8,16},{12,20},{16,8},{20,12},{24,0},{28,4},{1,25},{... | collective-permute-start | bytes 393224 | tf_op jit(solution)/shard_map/ppermute | solution.py:51
  48.8 7.3 %collective-permute-start.9 = (f32[128,256]{1,0:T(8,128)S(1)}, f32[128,256]{1,0:T(8,128)S(1)}, u32[]{:S(2)}, u32[]{:S(2)}) collective-permute-start(f32[128,256]{1,0:T(8,128)S(1)} %add.33.refs_1_.rest_2_._), channel_id=1, source_target_pairs={{0,16},{4,20},{8,24},{12,28},{16,0},{20,4},{24,8},{28,12},{1,17},{... | collective-permute-start | bytes 393224 | tf_op jit(solution)/shard_map/ppermute | solution.py:51
  49.3 7.2 %collective-permute-start.8 = (f32[128,256]{1,0:T(8,128)S(1)}, f32[128,256]{1,0:T(8,128)S(1)}, u32[]{:S(2)}, u32[]{:S(2)}) collective-permute-start(f32[128,256]{1,0:T(8,128)S(1)} %add.33.refs_1_.rest_2_._), channel_id=1, source_target_pairs={{0,8},{4,12},{8,0},{12,4},{16,24},{20,28},{24,16},{28,20},{1,9},{5... | collective-permute-start | bytes 393224 | tf_op jit(solution)/shard_map/ppermute | solution.py:51
  51.6 32.8 %copy-start.1 = (f32[512,6144]{1,0:T(8,128)S(1)}, f32[512,6144]{1,0:T(8,128)}, u32[]{:S(2)}) copy-start(f32[512,6144]{1,0:T(8,128)} %copy-done) | copy-start | bytes 37748740
  52.0 19.5 %collective-permute-start.13 = (bf16[256,768]{1,0:T(8,128)(2,1)S(1)}, bf16[256,768]{1,0:T(8,128)(2,1)S(1)}, u32[]{:S(2)}, u32[]{:S(2)}) collective-permute-start(bf16[256,768]{1,0:T(8,128)(2,1)S(1)} %get-tuple-element.57), channel_id=1, source_target_pairs={{0,8},{4,12},{8,0},{12,4},{16,24},{20,28},{24,16},{28,20},{1,9},{5... | collective-permute-start | bytes 1179656 | tf_op jit(solution)/shard_map/ppermute | solution.py:51
  53.5 18.0 %collective-permute-start.14 = (bf16[256,768]{1,0:T(8,128)(2,1)S(1)}, bf16[256,768]{1,0:T(8,128)(2,1)S(1)}, u32[]{:S(2)}, u32[]{:S(2)}) collective-permute-start(bf16[256,768]{1,0:T(8,128)(2,1)S(1)} %get-tuple-element.58), channel_id=1, source_target_pairs={{0,16},{4,20},{8,24},{12,28},{16,0},{20,4},{24,8},{28,12},{1,17},{... | collective-permute-start | bytes 1179656 | tf_op jit(solution)/shard_map/ppermute | solution.py:51
  55.0 17.4 %collective-permute-start.15 = (bf16[256,768]{1,0:T(8,128)(2,1)S(1)}, bf16[256,768]{1,0:T(8,128)(2,1)S(1)}, u32[]{:S(2)}, u32[]{:S(2)}) collective-permute-start(bf16[256,768]{1,0:T(8,128)(2,1)S(1)} %get-tuple-element.59), channel_id=1, source_target_pairs={{0,24},{4,28},{8,16},{12,20},{16,8},{20,12},{24,0},{28,4},{1,25},{... | collective-permute-start | bytes 1179656 | tf_op jit(solution)/shard_map/ppermute | solution.py:51
  56.5 1.4 %collective-permute-start.11 = (f32[128,256]{1,0:T(8,128)S(1)}, f32[128,256]{1,0:T(8,128)S(1)}, u32[]{:S(2)}, u32[]{:S(2)}) collective-permute-start(f32[128,256]{1,0:T(8,128)S(1)} %add_add_fusion.mine), channel_id=1, source_target_pairs={{0,4},{4,0},{8,12},{12,8},{16,20},{20,16},{24,28},{28,24},{1,5},{5... | collective-permute-start | bytes 393224 | tf_op jit(solution)/shard_map/ppermute | solution.py:51
  73.1 3.1 %collective-permute-start.16 = (bf16[256,768]{1,0:T(8,128)(2,1)S(1)}, bf16[256,768]{1,0:T(8,128)(2,1)S(1)}, u32[]{:S(2)}, u32[]{:S(2)}) collective-permute-start(bf16[256,768]{1,0:T(8,128)(2,1)S(1)} %get-tuple-element.61.refs_0_), channel_id=1, source_target_pairs={{0,4},{4,0},{8,12},{12,8},{16,20},{20,16},{24,28},{28,24},{1,5},{5... | collective-permute-start | bytes 1179656 | tf_op jit(solution)/shard_map/ppermute | solution.py:51
  73.2 14.9 %collective-permute-start.22 = (bf16[256,768]{1,0:T(8,128)(2,1)S(1)}, bf16[256,768]{1,0:T(8,128)(2,1)S(1)}, u32[]{:S(2)}, u32[]{:S(2)}) collective-permute-start(bf16[256,768]{1,0:T(8,128)(2,1)S(1)} %get-tuple-element.61.refs_0_), channel_id=1, source_target_pairs={{0,16},{4,20},{8,24},{12,28},{16,0},{20,4},{24,8},{28,12},{1,17},{... | collective-permute-start | bytes 1179656 | tf_op jit(solution)/shard_map/ppermute | solution.py:51
  74.7 13.4 %collective-permute-start.21 = (bf16[256,768]{1,0:T(8,128)(2,1)S(1)}, bf16[256,768]{1,0:T(8,128)(2,1)S(1)}, u32[]{:S(2)}, u32[]{:S(2)}) collective-permute-start(bf16[256,768]{1,0:T(8,128)(2,1)S(1)} %get-tuple-element.61.refs_0_), channel_id=1, source_target_pairs={{0,8},{4,12},{8,0},{12,4},{16,24},{20,28},{24,16},{28,20},{1,9},{5... | collective-permute-start | bytes 1179656 | tf_op jit(solution)/shard_map/ppermute | solution.py:51
  76.2 5.4 %collective-permute-start.19 = (f32[8,256]{1,0:T(8,128)S(1)}, f32[8,256]{1,0:T(8,128)S(1)}, u32[]{:S(2)}, u32[]{:S(2)}) collective-permute-start(f32[8,256]{1,0:T(8,128)S(1)} %hand_on.7.squares), channel_id=1, source_target_pairs={{0,3},{1,2},{2,1},{3,0},{4,7},{5,6},{6,5},{7,4},{8,11},{9,10},{10,... | collective-permute-start | bytes 24584 | tf_op jit(solution)/shard_map/ppermute | solution.py:51
  79.2 4.5 %collective-permute-start.18 = (f32[8,256]{1,0:T(8,128)S(1)}, f32[8,256]{1,0:T(8,128)S(1)}, u32[]{:S(2)}, u32[]{:S(2)}) collective-permute-start(f32[8,256]{1,0:T(8,128)S(1)} %hand_on.7.squares), channel_id=1, source_target_pairs={{0,2},{1,3},{2,0},{3,1},{4,6},{5,7},{6,4},{7,5},{8,10},{9,11},{10,... | collective-permute-start | bytes 24584 | tf_op jit(solution)/shard_map/ppermute | solution.py:51
  79.3 4.4 %collective-permute-start.17 = (f32[8,256]{1,0:T(8,128)S(1)}, f32[8,256]{1,0:T(8,128)S(1)}, u32[]{:S(2)}, u32[]{:S(2)}) collective-permute-start(f32[8,256]{1,0:T(8,128)S(1)} %hand_on.7.squares), channel_id=1, source_target_pairs={{0,1},{1,0},{2,3},{3,2},{4,5},{5,4},{6,7},{7,6},{8,9},{9,8},{10,11... | collective-permute-start | bytes 24584 | tf_op jit(solution)/shard_map/ppermute | solution.py:51
  83.7 4.4 %collective-permute-start.20 = (f32[8,256]{1,0:T(8,128)S(1)}, f32[8,256]{1,0:T(8,128)S(1)}, u32[]{:S(2)}, u32[]{:S(2)}) collective-permute-start(f32[8,256]{1,0:T(8,128)S(1)} %add_add_fusion.2), channel_id=1, source_target_pairs={{0,4},{4,0},{8,12},{12,8},{16,20},{20,16},{24,28},{28,24},{1,5},{5... | collective-permute-start | bytes 24584 | tf_op jit(solution)/shard_map/ppermute | solution.py:51
  88.1 4.6 %collective-permute-start.25 = (f32[8,256]{1,0:T(8,128)S(1)}, f32[8,256]{1,0:T(8,128)S(1)}, u32[]{:S(2)}, u32[]{:S(2)}) collective-permute-start(f32[8,256]{1,0:T(8,128)S(1)} %hand_on.8), channel_id=1, source_target_pairs={{0,24},{4,28},{8,16},{12,20},{16,8},{20,12},{24,0},{28,4},{1,25},{... | collective-permute-start | bytes 24584 | tf_op jit(solution)/shard_map/ppermute | solution.py:51
  89.3 3.7 %collective-permute-start.24 = (f32[8,256]{1,0:T(8,128)S(1)}, f32[8,256]{1,0:T(8,128)S(1)}, u32[]{:S(2)}, u32[]{:S(2)}) collective-permute-start(f32[8,256]{1,0:T(8,128)S(1)} %hand_on.8), channel_id=1, source_target_pairs={{0,16},{4,20},{8,24},{12,28},{16,0},{20,4},{24,8},{28,12},{1,17},{... | collective-permute-start | bytes 24584 | tf_op jit(solution)/shard_map/ppermute | solution.py:51
  90.2 3.7 %collective-permute-start.23 = (f32[8,256]{1,0:T(8,128)S(1)}, f32[8,256]{1,0:T(8,128)S(1)}, u32[]{:S(2)}, u32[]{:S(2)}) collective-permute-start(f32[8,256]{1,0:T(8,128)S(1)} %hand_on.8), channel_id=1, source_target_pairs={{0,8},{4,12},{8,0},{12,4},{16,24},{20,28},{24,16},{28,20},{1,9},{5... | collective-permute-start | bytes 24584 | tf_op jit(solution)/shard_map/ppermute | solution.py:51
  93.8 2.7 %collective-permute-start.27 = (bf16[256,768]{1,0:T(8,128)(2,1)S(1)}, bf16[256,768]{1,0:T(8,128)(2,1)S(1)}, u32[]{:S(2)}, u32[]{:S(2)}) collective-permute-start(bf16[256,768]{1,0:T(8,128)(2,1)S(1)} %hand_on.9.refs_0_), channel_id=1, source_target_pairs={{0,4},{4,0},{8,12},{12,8},{16,20},{20,16},{24,28},{28,24},{1,5},{5... | collective-permute-start | bytes 1179656 | tf_op jit(solution)/shard_map/ppermute | solution.py:51
  93.8 2.7 %collective-permute-start.28 = (bf16[256,768]{1,0:T(8,128)(2,1)S(1)}, bf16[256,768]{1,0:T(8,128)(2,1)S(1)}, u32[]{:S(2)}, u32[]{:S(2)}) collective-permute-start(bf16[256,768]{1,0:T(8,128)(2,1)S(1)} %hand_on.10.refs_2_), channel_id=1, source_target_pairs={{0,4},{4,0},{8,12},{12,8},{16,20},{20,16},{24,28},{28,24},{1,5},{5... | collective-permute-start | bytes 1179656 | tf_op jit(solution)/shard_map/ppermute | solution.py:51
  94.3 10.0 %collective-permute-start.26 = (bf16[128,768]{1,0:T(8,128)(2,1)S(1)}, bf16[128,768]{1,0:T(8,128)(2,1)S(1)}, u32[]{:S(2)}, u32[]{:S(2)}) collective-permute-start(bf16[128,768]{1,0:T(8,128)(2,1)S(1)} %slice.8), channel_id=1, source_target_pairs={{0,16},{4,20},{8,24},{12,28},{16,0},{20,4},{24,8},{28,12},{1,17},{... | collective-permute-start | bytes 589832 | tf_op jit(solution)/shard_map/ppermute | solution.py:51
  95.6 8.8 %collective-permute-start.29 = (bf16[128,768]{1,0:T(8,128)(2,1)S(1)}, bf16[128,768]{1,0:T(8,128)(2,1)S(1)}, u32[]{:S(2)}, u32[]{:S(2)}) collective-permute-start(bf16[128,768]{1,0:T(8,128)(2,1)S(1)} %slice.9), channel_id=1, source_target_pairs={{0,8},{4,12},{8,0},{12,4},{16,24},{20,28},{24,16},{28,20},{1,9},{5... | collective-permute-start | bytes 589832 | tf_op jit(solution)/shard_map/ppermute | solution.py:51
  104.4 3.6 %collective-permute-start.30 = (bf16[256,768]{1,0:T(8,128)(2,1)S(1)}, bf16[256,768]{1,0:T(8,128)(2,1)S(1)}, u32[]{:S(2)}, u32[]{:S(2)}) collective-permute-start(bf16[256,768]{1,0:T(8,128)(2,1)S(1)} %pad_maximum_fusion.refs_0_), channel_id=1, source_target_pairs={{0,4},{4,0},{8,12},{12,8},{16,20},{20,16},{24,28},{28,24},{1,5},{5... | collective-permute-start | bytes 1179656 | tf_op jit(solution)/shard_map/ppermute | solution.py:51

commit v11 on v10

--- a/solution.py
+++ b/solution.py
@@ -448,7 +448,7 @@
         return pltpu.make_async_copy(nbuf.at[b % 2], basis.at[:, cols], basis_sems.at[b % 2])
 
     def place(b, t):
-        return pl.ds(t * tile, tile), pl.ds(pl.multiple_of(starts[b] + t * tile, 128), tile)
+        return pl.ds(pl.multiple_of(t * tile, tile), tile), pl.ds(pl.multiple_of(starts[b] + t * tile, 128), tile)
 
     def stores(b, t):
         at, there = place(b, t)
@@ -457,16 +457,9 @@
             copies.append((mbuf, new_momentum))
         if weight_too:
             copies.append((vbuf, new_weight))
-        pieces = out_sems.shape[3]
-        piece = ortho_ref.shape[0] // pieces
         return [
-            pltpu.make_async_copy(
-                src.at[b % 2, pl.ds(i * piece, piece), at],
-                dst.at[pl.ds(i * piece, piece), there],
-                out_sems.at[k, b % 2, t, i],
-            )
+            pltpu.make_async_copy(src.at[b % 2, :, at], dst.at[:, there], out_sems.at[k, b % 2, t])
             for k, (src, dst) in enumerate(copies)
-            for i in range(pieces)
         ]
 
     def finish(b):
@@ -489,7 +482,8 @@
         if weight_too:
             nbuf[k] = (blocks[b][...].astype(f32) * scale).astype(bf16)
             store_basis(b).start()
-        for t in range(tiles):
+
+        def step(t, carry, b=b, k=k):
             at, there = place(b, t)
             if momentum_too:
                 correction = dot(ortho_ref[...], blocks[b][:, at])
@@ -503,6 +497,9 @@
                 vbuf[k, :, at] = (weight[:, there].astype(f32) - factor * change).astype(bf16)
             for store in stores(b, t):
                 store.start()
+            return carry
+
+        lax.fori_loop(0, tiles, step, 0)
     for b in range(count - 2, count):
         finish(b)
 
@@ -531,7 +528,7 @@
             pltpu.VMEM((2, m_rows, width), f32),
             pltpu.VMEM((2, w_rows, width), bf16),
             pltpu.VMEM((2, r, width), bf16),
-            pltpu.SemaphoreType.DMA((2, 2, width // 256, 4)),
+            pltpu.SemaphoreType.DMA((2, 2, width // 256)),
             pltpu.SemaphoreType.DMA((2,)),
         ],
         compiler_params=params(12),
@@ -611,9 +608,9 @@
     common = (factor, bufs, ortho_bf, weight)
     squares = exchange(hand_on(squares, own_pair), "col", depth)
     (momentum,), token = results((0,), (True, False), *common, squares[0], (share, own_pair))
-    squares = pair_up(squares)
+    squares = pair_up([hand_on(squares[0], token), *squares[1:]])
     squares = squares + swap(squares, "row", 1)
-    squares = hand_on(squares, *blocks.values(), token)
+    squares = hand_on(squares, *blocks.values())
     squares = pair_up(exchange(squares, "row", chips, 2))
     pairs = {}
     for d in near[1:]:

time: 114 us -> 112 us (0.982)
  transfers between devices with their start and end apart: 31 -> 31, of which waited for: 12 -> 13; matrix products, arithmetic and copies ran while one was open for 0% -> 0% of each run, Pallas kernels for 39% -> 39%
where the time goes in v11:
time: 112 us; the launch traced here: 111 us
  Pallas kernels  57.9 us (52%)
  starting transfers between devices  32.5 us (29%)
  waiting for transfers between devices  19.8 us (18%)
  between operations  1.13 us (1%)
    ppermute x31, starting transfers between devices, swap(): lax.ppermute(x, axis, [(i, i ^ d) for i in range(lax.axis_size(axis))])  32.5 us
    ppermute x31, waiting for transfers between devices, swap(): lax.ppermute(x, axis, [(i, i ^ d) for i in range(lax.axis_size(axis))])  19.8 us
    pallas_call x4, Pallas kernels, results(): pl.pallas_call(functools.partial(result_kernel, pairs, *kinds, factor), o...  19.3 us
    pallas_call x2, Pallas kernels, project(): pl.pallas_call(functools.partial(project_kernel, part, depth, width), out...  16.5 us
    pallas_call x1, Pallas kernels, chol_inverse(): pl.pallas_call(chol_inverse_kernel, out_shape=(shape((n, n), f32), pltpu....  13.5 us
    pallas_call x1, Pallas kernels, first_product(): pl.pallas_call(functools.partial(first_kernel, depth, width), out_shape=(...  3.36 us
    pallas_call x2, Pallas kernels, last_product(): pl.pallas_call(functools.partial(last_kernel, depth, width, mine), out_sh...  3.13 us
  transfers between devices with their start and end apart: 31, of which 13 were waited for; matrix products, arithmetic and copies ran while one was open for 0% of the time, Pallas kernels for 39%

profile of v11, /device:TPU:0, one launch (start us, length us, event | category | flops | bytes accessed | tf_op | source)
XLA Modules:
  0.0 111.5 jit_solution(2543136563485585059)
XLA Ops:
  0.6 8.7 %project.2 = (f32[512,6144]{1,0:T(8,128)S(1)}, bf16[256,6144]{1,0:T(8,128)(2,1)S(1)}, f32[256,256]{1,0:T(8,128)S(1)}, bf16[256,256]{1,0:T(8,128)(2,1)S(1)}) custom-call(f32[1024,6144]{1,0:T(8,128)} %mom.3, bf16[1024,6144]{1,0:T(8,128)(2,1)} %grad.3, bf16[256,6144]{1,0:T(8,128)(2,1)} %basis.1), custom_call_target="tpu_custom_call" | custom-call | bytes 37748736 | tf_op jit(solution)/shard_map/project/pallas_call | solution.py:104
  9.3 3.1 %collective-permute-start.2 = (bf16[256,256]{1,0:T(8,128)(2,1)S(1)}, bf16[256,256]{1,0:T(8,128)(2,1)S(1)}, u32[]{:S(2)}, u32[]{:S(2)}) collective-permute-start(bf16[256,256]{1,0:T(8,128)(2,1)S(1)} %get-tuple-element.40.rest_0_), channel_id=1, source_target_pairs={{0,1},{1,0},{2,3},{3,2},{4,5},{5,4},{6,7},{7,6},{8,9},{9,8},{10,11... | collective-permute-start | bytes 393224 | tf_op jit(solution)/shard_map/ppermute | solution.py:51
  12.4 7.8 %project.3 = (f32[512,6144]{1,0:T(8,128)S(1)}, f32[256,256]{1,0:T(8,128)S(1)}, bf16[256,256]{1,0:T(8,128)(2,1)S(1)}) custom-call(f32[1024,6144]{1,0:T(8,128)} %mom.3, bf16[1024,6144]{1,0:T(8,128)(2,1)} %grad.3, bf16[256,6144]{1,0:T(8,128)(2,1)S(1)} %get-tuple-element.39.basis, bf16[256,256]{1,0:T(8,128)(2,1)S(1)} %get-tuple-element.40.rest_0_), custom_call_target="tpu_custom_call" | custom-call | bytes 37748736 | tf_op jit(solution)/shard_map/project/pallas_call | solution.py:104
  20.4 3.1 %collective-permute-start.3 = (bf16[256,128]{1,0:T(8,128)(2,1)S(1)}, bf16[256,128]{1,0:T(8,128)(2,1)S(1)}, u32[]{:S(2)}, u32[]{:S(2)}) collective-permute-start(bf16[256,128]{1,0:T(8,128)(2,1)S(1)} %get-tuple-element.48), channel_id=1, source_target_pairs={{0,2},{1,3},{2,0},{3,1},{4,6},{5,7},{6,4},{7,5},{8,10},{9,11},{10,... | collective-permute-start | bytes 196616 | tf_op jit(solution)/shard_map/ppermute | solution.py:51
  23.4 3.2 %collective-permute-done.received = bf16[256,256]{1,0:T(8,128)(2,1)S(1)} collective-permute-done((bf16[256,256]{1,0:T(8,128)(2,1)S(1)}, bf16[256,256]{1,0:T(8,128)(2,1)S(1)}, u32[]{:S(2)}, u32[]{:S(2)}) %collective-permute-start) | collective-permute-done | bytes 131104 | tf_op jit(solution)/shard_map/ppermute | solution.py:51
  26.7 2.3 %collective-permute-start.1 = (bf16[256,128]{1,0:T(8,128)(2,1)S(1)}, bf16[256,128]{1,0:T(8,128)(2,1)S(1)}, u32[]{:S(2)}, u32[]{:S(2)}) collective-permute-start(bf16[256,128]{1,0:T(8,128)(2,1)S(1)} %get-tuple-element.45), channel_id=1, source_target_pairs={{0,2},{1,3},{2,0},{3,1},{4,6},{5,7},{6,4},{7,5},{8,10},{9,11},{10,... | collective-permute-start | bytes 196616 | tf_op jit(solution)/shard_map/ppermute | solution.py:51
  29.0 2.9 %collective-permute-done.1.received = bf16[256,128]{1,0:T(8,128)(2,1)S(1)} collective-permute-done((bf16[256,128]{1,0:T(8,128)(2,1)S(1)}, bf16[256,128]{1,0:T(8,128)(2,1)S(1)}, u32[]{:S(2)}, u32[]{:S(2)}) %collective-permute-start.1) | collective-permute-done | bytes 65568 | tf_op jit(solution)/shard_map/ppermute | solution.py:51
  32.0 2.5 %collective-permute-start.4 = (bf16[256,256]{1,0:T(8,128)(2,1)S(1)}, bf16[256,256]{1,0:T(8,128)(2,1)S(1)}, u32[]{:S(2)}, u32[]{:S(2)}) collective-permute-start(bf16[256,256]{1,0:T(8,128)(2,1)S(1)} %fold_last.3.rest_0_.refs_0_), channel_id=1, source_target_pairs={{0,2},{1,3},{2,0},{3,1},{4,6},{5,7},{6,4},{7,5},{8,10},{9,11},{10,... | collective-permute-start | bytes 393224 | tf_op jit(solution)/shard_map/ppermute | solution.py:51
  34.5 4.4 %collective-permute-done.4.rest_1_.refs_2_ = bf16[256,256]{1,0:T(8,128)(2,1)S(1)} collective-permute-done((bf16[256,256]{1,0:T(8,128)(2,1)S(1)}, bf16[256,256]{1,0:T(8,128)(2,1)S(1)}, u32[]{:S(2)}, u32[]{:S(2)}) %collective-permute-start.4) | collective-permute-done | bytes 131104 | tf_op jit(solution)/shard_map/ppermute | solution.py:51
  38.8 3.4 %first_product.1 = (f32[256,3072]{1,0:T(8,128)S(1)}, f32[256,3072]{1,0:T(8,128)S(1)}, f32[256,256]{1,0:T(8,128)S(1)}) custom-call(f32[512,6144]{1,0:T(8,128)S(1)} %get-tuple-element.38.buf0, f32[512,6144]{1,0:T(8,128)S(1)} %get-tuple-element.41.buf1, bf16[256,256]{1,0:T(8,128)(2,1)S(1)} %fold_last.3.rest_0_.refs_0_, ...), custom_call_target="tpu_custom_call" | custom-call | bytes 31457280 | tf_op jit(solution)/shard_map/first_product/pallas_call | solution.py:211
  42.2 1.6 %collective-permute-done.6.rest_1_.refs_3_ = bf16[256,256]{1,0:T(8,128)(2,1)S(1)} collective-permute-done((bf16[256,256]{1,0:T(8,128)(2,1)S(1)}, bf16[256,256]{1,0:T(8,128)(2,1)S(1)}, u32[]{:S(2)}, u32[]{:S(2)}) %collective-permute-start.6) | collective-permute-done | bytes 131104 | tf_op jit(solution)/shard_map/ppermute | solution.py:51
  43.8 0.3 gram.1
  44.2 1.6 %other_product.1.refs_0_ = bf16[256,3072]{1,0:T(8,128)(2,1)S(1)} custom-call(f32[512,6144]{1,0:T(8,128)S(1)} %get-tuple-element.38.buf0, f32[512,6144]{1,0:T(8,128)S(1)} %get-tuple-element.41.buf1, f32[256,3072]{1,0:T(8,128)S(1)} %get-tuple-element.55.sums, bf16[256,256]{1,0:T(8,128)(2,1)S(1)} %collective-permute-done.5.rest_0_.refs_1_, ...), custom_call_target="tpu_custom_call" | custom-call | bytes 15728640 | tf_op jit(solution)/shard_map/other_product/pallas_call | solution.py:266
  45.8 0.6 collective-permute-start.12
  46.4 2.4 %collective-permute-start.10 = (f32[128,256]{1,0:T(8,128)S(1)}, f32[128,256]{1,0:T(8,128)S(1)}, u32[]{:S(2)}, u32[]{:S(2)}) collective-permute-start(f32[128,256]{1,0:T(8,128)S(1)} %add.33.refs_1_.rest_2_._), channel_id=1, source_target_pairs={{0,24},{4,28},{8,16},{12,20},{16,8},{20,12},{24,0},{28,4},{1,25},{... | collective-permute-start | bytes 393224 | tf_op jit(solution)/shard_map/ppermute | solution.py:51
  48.8 0.5 collective-permute-start.9
  49.3 0.6 collective-permute-start.8
  49.9 1.6 %mine_product.1.mine = f32[256,3072]{1,0:T(8,128)S(1)} custom-call(f32[512,6144]{1,0:T(8,128)S(1)} %get-tuple-element.38.buf0, f32[512,6144]{1,0:T(8,128)S(1)} %get-tuple-element.41.buf1, f32[256,3072]{1,0:T(8,128)S(1)} %get-tuple-element.54.sums, bf16[256,256]{1,0:T(8,128)(2,1)S(1)} %collective-permute-done.5.rest_0_.refs_1_, ...), custom_call_target="tpu_custom_call" | custom-call | bytes 15728640 | tf_op jit(solution)/shard_map/mine_product/pallas_call | solution.py:266
  51.5 0.3 pair_sum.1
  51.8 1.5 %collective-permute-start.13 = (bf16[256,768]{1,0:T(8,128)(2,1)S(1)}, bf16[256,768]{1,0:T(8,128)(2,1)S(1)}, u32[]{:S(2)}, u32[]{:S(2)}) collective-permute-start(bf16[256,768]{1,0:T(8,128)(2,1)S(1)} %get-tuple-element.57), channel_id=1, source_target_pairs={{0,8},{4,12},{8,0},{12,4},{16,24},{20,28},{24,16},{28,20},{1,9},{5... | collective-permute-start | bytes 1179656 | tf_op jit(solution)/shard_map/ppermute | solution.py:51
  53.3 1.5 %collective-permute-start.14 = (bf16[256,768]{1,0:T(8,128)(2,1)S(1)}, bf16[256,768]{1,0:T(8,128)(2,1)S(1)}, u32[]{:S(2)}, u32[]{:S(2)}) collective-permute-start(bf16[256,768]{1,0:T(8,128)(2,1)S(1)} %get-tuple-element.58), channel_id=1, source_target_pairs={{0,16},{4,20},{8,24},{12,28},{16,0},{20,4},{24,8},{28,12},{1,17},{... | collective-permute-start | bytes 1179656 | tf_op jit(solution)/shard_map/ppermute | solution.py:51
  54.8 1.3 %collective-permute-start.15 = (bf16[256,768]{1,0:T(8,128)(2,1)S(1)}, bf16[256,768]{1,0:T(8,128)(2,1)S(1)}, u32[]{:S(2)}, u32[]{:S(2)}) collective-permute-start(bf16[256,768]{1,0:T(8,128)(2,1)S(1)} %get-tuple-element.59), channel_id=1, source_target_pairs={{0,24},{4,28},{8,16},{12,20},{16,8},{20,12},{24,0},{28,4},{1,25},{... | collective-permute-start | bytes 1179656 | tf_op jit(solution)/shard_map/ppermute | solution.py:51
  56.1 0.4 collective-permute-done.8
  56.6 1.3 %collective-permute-done.11.other = f32[128,256]{1,0:T(8,128)S(1)} collective-permute-done((f32[128,256]{1,0:T(8,128)S(1)}, f32[128,256]{1,0:T(8,128)S(1)}, u32[]{:S(2)}, u32[]{:S(2)}) %collective-permute-start.11) | collective-permute-done | bytes 131104 | tf_op jit(solution)/shard_map/ppermute | solution.py:51
  57.9 13.5 %chol_inverse.1 = (f32[256,256]{1,0:T(8,128)S(1)}, bf16[1024,6144]{1,0:T(8,128)(2,1)S(1)}) custom-call(f32[128,256]{1,0:T(8,128)S(1)} %add_add_fusion.mine, f32[128,256]{1,0:T(8,128)S(1)} %collective-permute-done.11.other, bf16[1024,6144]{1,0:T(8,128)(2,1)} %weight.1), custom_call_target="tpu_custom_call" | custom-call | bytes 33554432 | tf_op jit(solution)/shard_map/chol_inverse/pallas_call | solution.py:353
  71.5 0.9 collective-permute-done.15.refs_2_
  72.4 0.7 share.1
  73.2 1.6 %collective-permute-start.22 = (bf16[256,768]{1,0:T(8,128)(2,1)S(1)}, bf16[256,768]{1,0:T(8,128)(2,1)S(1)}, u32[]{:S(2)}, u32[]{:S(2)}) collective-permute-start(bf16[256,768]{1,0:T(8,128)(2,1)S(1)} %get-tuple-element.61.refs_0_), channel_id=1, source_target_pairs={{0,16},{4,20},{8,24},{12,28},{16,0},{20,4},{24,8},{28,12},{1,17},{... | collective-permute-start | bytes 1179656 | tf_op jit(solution)/shard_map/ppermute | solution.py:51
  74.7 1.5 %collective-permute-start.21 = (bf16[256,768]{1,0:T(8,128)(2,1)S(1)}, bf16[256,768]{1,0:T(8,128)(2,1)S(1)}, u32[]{:S(2)}, u32[]{:S(2)}) collective-permute-start(bf16[256,768]{1,0:T(8,128)(2,1)S(1)} %get-tuple-element.61.refs_0_), channel_id=1, source_target_pairs={{0,8},{4,12},{8,0},{12,4},{16,24},{20,28},{24,16},{28,20},{1,9},{5... | collective-permute-start | bytes 1179656 | tf_op jit(solution)/shard_map/ppermute | solution.py:51
  76.2 2.9 %collective-permute-start.19 = (f32[8,256]{1,0:T(8,128)S(1)}, f32[8,256]{1,0:T(8,128)S(1)}, u32[]{:S(2)}, u32[]{:S(2)}) collective-permute-start(f32[8,256]{1,0:T(8,128)S(1)} %hand_on.8.squares.refs_0_), channel_id=1, source_target_pairs={{0,3},{1,2},{2,1},{3,0},{4,7},{5,6},{6,5},{7,4},{8,11},{9,10},{10,... | collective-permute-start | bytes 24584 | tf_op jit(solution)/shard_map/ppermute | solution.py:51
  79.3 1.4 %collective-permute-start.17 = (f32[8,256]{1,0:T(8,128)S(1)}, f32[8,256]{1,0:T(8,128)S(1)}, u32[]{:S(2)}, u32[]{:S(2)}) collective-permute-start(f32[8,256]{1,0:T(8,128)S(1)} %hand_on.8.squares.refs_0_), channel_id=1, source_target_pairs={{0,1},{1,0},{2,3},{3,2},{4,5},{5,4},{6,7},{7,6},{8,9},{9,8},{10,11... | collective-permute-start | bytes 24584 | tf_op jit(solution)/shard_map/ppermute | solution.py:51
  80.6 0.6 ortho.1.ortho_ref
  81.3 3.1 %results.4 = (f32[1024,6144]{1,0:T(8,128)}, f32[8,128]{1,0:T(8,128)S(1)}) custom-call(f32[512,6144]{1,0:T(8,128)S(1)} %get-tuple-element.38.buf0, f32[512,6144]{1,0:T(8,128)S(1)} %copy-done.1, bf16[1024,256]{1,0:T(8,128)(2,1)S(1)} %ortho.1.ortho_ref, bf16[1024,6144]{1,0:T(8,128)(2,1)S(1)} %get-tuple-element.53.weight, f32[8,256]{1,0:T(8,128)S(1)} %hand_on.8.squares.refs_0_, ...), custom_call_target="tpu_custom_call" | custom-call | bytes 6291456 | tf_op jit(solution)/shard_map/results/pallas_call | solution.py:521
  84.5 1.2 %collective-permute-done.20 = f32[8,256]{1,0:T(8,128)S(1)} collective-permute-done((f32[8,256]{1,0:T(8,128)S(1)}, f32[8,256]{1,0:T(8,128)S(1)}, u32[]{:S(2)}, u32[]{:S(2)}) %collective-permute-start.20) | collective-permute-done | bytes 8224 | tf_op jit(solution)/shard_map/ppermute | solution.py:51
  85.7 0.2 collective-permute-done.21.refs_1_.refs_0_
  85.9 1.4 %collective-permute-start.25 = (f32[8,256]{1,0:T(8,128)S(1)}, f32[8,256]{1,0:T(8,128)S(1)}, u32[]{:S(2)}, u32[]{:S(2)}) collective-permute-start(f32[8,256]{1,0:T(8,128)S(1)} %hand_on.10), channel_id=1, source_target_pairs={{0,24},{4,28},{8,16},{12,20},{16,8},{20,12},{24,0},{28,4},{1,25},{... | collective-permute-start | bytes 24584 | tf_op jit(solution)/shard_map/ppermute | solution.py:51
  87.3 1.6 %collective-permute-start.24 = (f32[8,256]{1,0:T(8,128)S(1)}, f32[8,256]{1,0:T(8,128)S(1)}, u32[]{:S(2)}, u32[]{:S(2)}) collective-permute-start(f32[8,256]{1,0:T(8,128)S(1)} %hand_on.10), channel_id=1, source_target_pairs={{0,16},{4,20},{8,24},{12,28},{16,0},{20,4},{24,8},{28,12},{1,17},{... | collective-permute-start | bytes 24584 | tf_op jit(solution)/shard_map/ppermute | solution.py:51
  88.9 0.5 collective-permute-start.23
  89.4 1.1 collective-permute-done.25
  90.5 0.5 collective-permute-done.24
  91.0 1.6 %collective-permute-done.23 = f32[8,256]{1,0:T(8,128)S(1)} collective-permute-done((f32[8,256]{1,0:T(8,128)S(1)}, f32[8,256]{1,0:T(8,128)S(1)}, u32[]{:S(2)}, u32[]{:S(2)}) %collective-permute-start.23) | collective-permute-done | bytes 8224 | tf_op jit(solution)/shard_map/ppermute | solution.py:51
  92.6 0.5 collective-permute-start.28
  93.1 0.5 collective-permute-start.26
  93.6 0.6 collective-permute-start.29
  94.3 0.6 collective-permute-done.28.refs_3_
  94.8 7.6 %results.5 = (bf16[1024,6144]{1,0:T(8,128)(2,1)}, bf16[256,6144]{1,0:T(8,128)(2,1)}, f32[1024,6144]{1,0:T(8,128)}, f32[8,128]{1,0:T(8,128)S(1)}) custom-call(f32[512,6144]{1,0:T(8,128)S(1)} %get-tuple-element.38.buf0, f32[512,6144]{1,0:T(8,128)S(1)} %copy-done.1, bf16[1024,256]{1,0:T(8,128)(2,1)S(1)} %ortho.1.ortho_ref, ...), custom_call_target="tpu_custom_call", output_to_operand_aliasing={{2}: (9, {})} | custom-call | bytes 25165824 | tf_op jit(solution)/shard_map/results/pallas_call | solution.py:521
  102.7 3.6 %results.6 = (bf16[1024,6144]{1,0:T(8,128)(2,1)}, bf16[256,6144]{1,0:T(8,128)(2,1)}, f32[8,128]{1,0:T(8,128)}) custom-call(f32[512,6144]{1,0:T(8,128)S(1)} %get-tuple-element.38.buf0, f32[512,6144]{1,0:T(8,128)S(1)} %copy-done.1, bf16[1024,256]{1,0:T(8,128)(2,1)S(1)} %ortho.1.ortho_ref, ...), custom_call_target="tpu_custom_call", output_to_operand_aliasing={{0}: (7, {}), {1}: (8, {})} | custom-call | bytes 6291456 | tf_op jit(solution)/shard_map/results/pallas_call | solution.py:521
  106.3 5.1 %results.7 = (bf16[1024,6144]{1,0:T(8,128)(2,1)}, bf16[256,6144]{1,0:T(8,128)(2,1)}, f32[1024,6144]{1,0:T(8,128)}, f32[8,128]{1,0:T(8,128)}) custom-call(f32[512,6144]{1,0:T(8,128)S(1)} %get-tuple-element.38.buf0, f32[512,6144]{1,0:T(8,128)S(1)} %copy-done.1, ...), custom_call_target="tpu_custom_call", output_to_operand_aliasing={{0}: (7, {}), {1}: (8, {}), {2}: (9, {})} | custom-call | bytes 12582912 | tf_op jit(solution)/shard_map/results/pallas_call | solution.py:521
  (51 shorter events, 1.0 us)
Async XLA Ops:
  9.3 11.0 %collective-permute-start.2 = (bf16[256,256]{1,0:T(8,128)(2,1)S(1)}, bf16[256,256]{1,0:T(8,128)(2,1)S(1)}, u32[]{:S(2)}, u32[]{:S(2)}) collective-permute-start(bf16[256,256]{1,0:T(8,128)(2,1)S(1)} %get-tuple-element.40.rest_0_), channel_id=1, source_target_pairs={{0,1},{1,0},{2,3},{3,2},{4,5},{5,4},{6,7},{7,6},{8,9},{9,8},{10,11... | collective-permute-start | bytes 393224 | tf_op jit(solution)/shard_map/ppermute | solution.py:51
  20.2 29.6 %copy-start = (f32[512,6144]{1,0:T(8,128)}, f32[512,6144]{1,0:T(8,128)S(1)}, u32[]{:S(2)}) copy-start(f32[512,6144]{1,0:T(8,128)S(1)} %get-tuple-element.41.buf1) | copy-start | bytes 37748740
  20.2 6.4 %collective-permute-start = (bf16[256,256]{1,0:T(8,128)(2,1)S(1)}, bf16[256,256]{1,0:T(8,128)(2,1)S(1)}, u32[]{:S(2)}, u32[]{:S(2)}) collective-permute-start(bf16[256,256]{1,0:T(8,128)(2,1)S(1)} %get-tuple-element.43), channel_id=1, source_target_pairs={{0,1},{1,0},{2,3},{3,2},{4,5},{5,4},{6,7},{7,6},{8,9},{9,8},{10,11... | collective-permute-start | bytes 393224 | tf_op jit(solution)/shard_map/ppermute | solution.py:51
  20.4 8.7 %collective-permute-start.3 = (bf16[256,128]{1,0:T(8,128)(2,1)S(1)}, bf16[256,128]{1,0:T(8,128)(2,1)S(1)}, u32[]{:S(2)}, u32[]{:S(2)}) collective-permute-start(bf16[256,128]{1,0:T(8,128)(2,1)S(1)} %get-tuple-element.48), channel_id=1, source_target_pairs={{0,2},{1,3},{2,0},{3,1},{4,6},{5,7},{6,4},{7,5},{8,10},{9,11},{10,... | collective-permute-start | bytes 196616 | tf_op jit(solution)/shard_map/ppermute | solution.py:51
  26.7 5.2 %collective-permute-start.1 = (bf16[256,128]{1,0:T(8,128)(2,1)S(1)}, bf16[256,128]{1,0:T(8,128)(2,1)S(1)}, u32[]{:S(2)}, u32[]{:S(2)}) collective-permute-start(bf16[256,128]{1,0:T(8,128)(2,1)S(1)} %get-tuple-element.45), channel_id=1, source_target_pairs={{0,2},{1,3},{2,0},{3,1},{4,6},{5,7},{6,4},{7,5},{8,10},{9,11},{10,... | collective-permute-start | bytes 196616 | tf_op jit(solution)/shard_map/ppermute | solution.py:51
  32.0 6.9 %collective-permute-start.4 = (bf16[256,256]{1,0:T(8,128)(2,1)S(1)}, bf16[256,256]{1,0:T(8,128)(2,1)S(1)}, u32[]{:S(2)}, u32[]{:S(2)}) collective-permute-start(bf16[256,256]{1,0:T(8,128)(2,1)S(1)} %fold_last.3.rest_0_.refs_0_), channel_id=1, source_target_pairs={{0,2},{1,3},{2,0},{3,1},{4,6},{5,7},{6,4},{7,5},{8,10},{9,11},{10,... | collective-permute-start | bytes 393224 | tf_op jit(solution)/shard_map/ppermute | solution.py:51
  34.5 7.7 %collective-permute-start.5 = (bf16[256,256]{1,0:T(8,128)(2,1)S(1)}, bf16[256,256]{1,0:T(8,128)(2,1)S(1)}, u32[]{:S(2)}, u32[]{:S(2)}) collective-permute-start(bf16[256,256]{1,0:T(8,128)(2,1)S(1)} %fold_last.3.rest_0_.refs_0_), channel_id=1, source_target_pairs={{0,1},{1,0},{2,3},{3,2},{4,5},{5,4},{6,7},{7,6},{8,9},{9,8},{10,11... | collective-permute-start | bytes 393224 | tf_op jit(solution)/shard_map/ppermute | solution.py:51
  38.8 5.0 %collective-permute-start.6 = (bf16[256,256]{1,0:T(8,128)(2,1)S(1)}, bf16[256,256]{1,0:T(8,128)(2,1)S(1)}, u32[]{:S(2)}, u32[]{:S(2)}) collective-permute-start(bf16[256,256]{1,0:T(8,128)(2,1)S(1)} %collective-permute-done.4.rest_1_.refs_2_), channel_id=1, source_target_pairs={{0,1},{1,0},{2,3},{3,2},{4,5},{5,4},{6,7},{7,6},{8,9},{9,8},{10,11... | collective-permute-start | bytes 393224 | tf_op jit(solution)/shard_map/ppermute | solution.py:51
  44.1 1.7 %collective-permute-start.7 = (f32[128,256]{1,0:T(8,128)S(1)}, f32[128,256]{1,0:T(8,128)S(1)}, u32[]{:S(2)}, u32[]{:S(2)}) collective-permute-start(f32[128,256]{1,0:T(8,128)S(1)} %get-tuple-element.51), channel_id=1, source_target_pairs={{0,4},{4,0},{8,12},{12,8},{16,20},{20,16},{24,28},{28,24},{1,5},{5... | collective-permute-start | bytes 393224 | tf_op jit(solution)/shard_map/ppermute | solution.py:51
  45.8 5.6 %collective-permute-start.12 = (bf16[256,3072]{1,0:T(8,128)(2,1)S(1)}, bf16[256,3072]{1,0:T(8,128)(2,1)S(1)}, u32[]{:S(2)}, u32[]{:S(2)}) collective-permute-start(bf16[256,3072]{1,0:T(8,128)(2,1)S(1)} %hand_on.7.rest_3_), channel_id=1, source_target_pairs={{0,4},{4,0},{8,12},{12,8},{16,20},{20,16},{24,28},{28,24},{1,5},{5... | collective-permute-start | bytes 4718600 | tf_op jit(solution)/shard_map/ppermute | solution.py:51
  46.4 8.4 %collective-permute-start.10 = (f32[128,256]{1,0:T(8,128)S(1)}, f32[128,256]{1,0:T(8,128)S(1)}, u32[]{:S(2)}, u32[]{:S(2)}) collective-permute-start(f32[128,256]{1,0:T(8,128)S(1)} %add.33.refs_1_.rest_2_._), channel_id=1, source_target_pairs={{0,24},{4,28},{8,16},{12,20},{16,8},{20,12},{24,0},{28,4},{1,25},{... | collective-permute-start | bytes 393224 | tf_op jit(solution)/shard_map/ppermute | solution.py:51
  48.8 7.3 %collective-permute-start.9 = (f32[128,256]{1,0:T(8,128)S(1)}, f32[128,256]{1,0:T(8,128)S(1)}, u32[]{:S(2)}, u32[]{:S(2)}) collective-permute-start(f32[128,256]{1,0:T(8,128)S(1)} %add.33.refs_1_.rest_2_._), channel_id=1, source_target_pairs={{0,16},{4,20},{8,24},{12,28},{16,0},{20,4},{24,8},{28,12},{1,17},{... | collective-permute-start | bytes 393224 | tf_op jit(solution)/shard_map/ppermute | solution.py:51
  49.3 7.2 %collective-permute-start.8 = (f32[128,256]{1,0:T(8,128)S(1)}, f32[128,256]{1,0:T(8,128)S(1)}, u32[]{:S(2)}, u32[]{:S(2)}) collective-permute-start(f32[128,256]{1,0:T(8,128)S(1)} %add.33.refs_1_.rest_2_._), channel_id=1, source_target_pairs={{0,8},{4,12},{8,0},{12,4},{16,24},{20,28},{24,16},{28,20},{1,9},{5... | collective-permute-start | bytes 393224 | tf_op jit(solution)/shard_map/ppermute | solution.py:51
  51.4 29.8 %copy-start.1 = (f32[512,6144]{1,0:T(8,128)S(1)}, f32[512,6144]{1,0:T(8,128)}, u32[]{:S(2)}) copy-start(f32[512,6144]{1,0:T(8,128)} %copy-done) | copy-start | bytes 37748740
  51.8 19.6 %collective-permute-start.13 = (bf16[256,768]{1,0:T(8,128)(2,1)S(1)}, bf16[256,768]{1,0:T(8,128)(2,1)S(1)}, u32[]{:S(2)}, u32[]{:S(2)}) collective-permute-start(bf16[256,768]{1,0:T(8,128)(2,1)S(1)} %get-tuple-element.57), channel_id=1, source_target_pairs={{0,8},{4,12},{8,0},{12,4},{16,24},{20,28},{24,16},{28,20},{1,9},{5... | collective-permute-start | bytes 1179656 | tf_op jit(solution)/shard_map/ppermute | solution.py:51
  53.3 18.1 %collective-permute-start.14 = (bf16[256,768]{1,0:T(8,128)(2,1)S(1)}, bf16[256,768]{1,0:T(8,128)(2,1)S(1)}, u32[]{:S(2)}, u32[]{:S(2)}) collective-permute-start(bf16[256,768]{1,0:T(8,128)(2,1)S(1)} %get-tuple-element.58), channel_id=1, source_target_pairs={{0,16},{4,20},{8,24},{12,28},{16,0},{20,4},{24,8},{28,12},{1,17},{... | collective-permute-start | bytes 1179656 | tf_op jit(solution)/shard_map/ppermute | solution.py:51
  54.8 17.6 %collective-permute-start.15 = (bf16[256,768]{1,0:T(8,128)(2,1)S(1)}, bf16[256,768]{1,0:T(8,128)(2,1)S(1)}, u32[]{:S(2)}, u32[]{:S(2)}) collective-permute-start(bf16[256,768]{1,0:T(8,128)(2,1)S(1)} %get-tuple-element.59), channel_id=1, source_target_pairs={{0,24},{4,28},{8,16},{12,20},{16,8},{20,12},{24,0},{28,4},{1,25},{... | collective-permute-start | bytes 1179656 | tf_op jit(solution)/shard_map/ppermute | solution.py:51
  56.5 1.4 %collective-permute-start.11 = (f32[128,256]{1,0:T(8,128)S(1)}, f32[128,256]{1,0:T(8,128)S(1)}, u32[]{:S(2)}, u32[]{:S(2)}) collective-permute-start(f32[128,256]{1,0:T(8,128)S(1)} %add_add_fusion.mine), channel_id=1, source_target_pairs={{0,4},{4,0},{8,12},{12,8},{16,20},{20,16},{24,28},{28,24},{1,5},{5... | collective-permute-start | bytes 393224 | tf_op jit(solution)/shard_map/ppermute | solution.py:51
  73.1 3.1 %collective-permute-start.16 = (bf16[256,768]{1,0:T(8,128)(2,1)S(1)}, bf16[256,768]{1,0:T(8,128)(2,1)S(1)}, u32[]{:S(2)}, u32[]{:S(2)}) collective-permute-start(bf16[256,768]{1,0:T(8,128)(2,1)S(1)} %get-tuple-element.61.refs_0_), channel_id=1, source_target_pairs={{0,4},{4,0},{8,12},{12,8},{16,20},{20,16},{24,28},{28,24},{1,5},{5... | collective-permute-start | bytes 1179656 | tf_op jit(solution)/shard_map/ppermute | solution.py:51
  73.2 12.5 %collective-permute-start.22 = (bf16[256,768]{1,0:T(8,128)(2,1)S(1)}, bf16[256,768]{1,0:T(8,128)(2,1)S(1)}, u32[]{:S(2)}, u32[]{:S(2)}) collective-permute-start(bf16[256,768]{1,0:T(8,128)(2,1)S(1)} %get-tuple-element.61.refs_0_), channel_id=1, source_target_pairs={{0,16},{4,20},{8,24},{12,28},{16,0},{20,4},{24,8},{28,12},{1,17},{... | collective-permute-start | bytes 1179656 | tf_op jit(solution)/shard_map/ppermute | solution.py:51
  74.7 11.2 %collective-permute-start.21 = (bf16[256,768]{1,0:T(8,128)(2,1)S(1)}, bf16[256,768]{1,0:T(8,128)(2,1)S(1)}, u32[]{:S(2)}, u32[]{:S(2)}) collective-permute-start(bf16[256,768]{1,0:T(8,128)(2,1)S(1)} %get-tuple-element.61.refs_0_), channel_id=1, source_target_pairs={{0,8},{4,12},{8,0},{12,4},{16,24},{20,28},{24,16},{28,20},{1,9},{5... | collective-permute-start | bytes 1179656 | tf_op jit(solution)/shard_map/ppermute | solution.py:51
  76.2 8.2 %collective-permute-start.19 = (f32[8,256]{1,0:T(8,128)S(1)}, f32[8,256]{1,0:T(8,128)S(1)}, u32[]{:S(2)}, u32[]{:S(2)}) collective-permute-start(f32[8,256]{1,0:T(8,128)S(1)} %hand_on.8.squares.refs_0_), channel_id=1, source_target_pairs={{0,3},{1,2},{2,1},{3,0},{4,7},{5,6},{6,5},{7,4},{8,11},{9,10},{10,... | collective-permute-start | bytes 24584 | tf_op jit(solution)/shard_map/ppermute | solution.py:51
  79.2 5.3 %collective-permute-start.18 = (f32[8,256]{1,0:T(8,128)S(1)}, f32[8,256]{1,0:T(8,128)S(1)}, u32[]{:S(2)}, u32[]{:S(2)}) collective-permute-start(f32[8,256]{1,0:T(8,128)S(1)} %hand_on.8.squares.refs_0_), channel_id=1, source_target_pairs={{0,2},{1,3},{2,0},{3,1},{4,6},{5,7},{6,4},{7,5},{8,10},{9,11},{10,... | collective-permute-start | bytes 24584 | tf_op jit(solution)/shard_map/ppermute | solution.py:51
  79.3 5.1 %collective-permute-start.17 = (f32[8,256]{1,0:T(8,128)S(1)}, f32[8,256]{1,0:T(8,128)S(1)}, u32[]{:S(2)}, u32[]{:S(2)}) collective-permute-start(f32[8,256]{1,0:T(8,128)S(1)} %hand_on.8.squares.refs_0_), channel_id=1, source_target_pairs={{0,1},{1,0},{2,3},{3,2},{4,5},{5,4},{6,7},{7,6},{8,9},{9,8},{10,11... | collective-permute-start | bytes 24584 | tf_op jit(solution)/shard_map/ppermute | solution.py:51
  84.5 1.2 %collective-permute-start.20 = (f32[8,256]{1,0:T(8,128)S(1)}, f32[8,256]{1,0:T(8,128)S(1)}, u32[]{:S(2)}, u32[]{:S(2)}) collective-permute-start(f32[8,256]{1,0:T(8,128)S(1)} %add_add_fusion.2), channel_id=1, source_target_pairs={{0,4},{4,0},{8,12},{12,8},{16,20},{20,16},{24,28},{28,24},{1,5},{5... | collective-permute-start | bytes 24584 | tf_op jit(solution)/shard_map/ppermute | solution.py:51
  85.9 4.5 %collective-permute-start.25 = (f32[8,256]{1,0:T(8,128)S(1)}, f32[8,256]{1,0:T(8,128)S(1)}, u32[]{:S(2)}, u32[]{:S(2)}) collective-permute-start(f32[8,256]{1,0:T(8,128)S(1)} %hand_on.10), channel_id=1, source_target_pairs={{0,24},{4,28},{8,16},{12,20},{16,8},{20,12},{24,0},{28,4},{1,25},{... | collective-permute-start | bytes 24584 | tf_op jit(solution)/shard_map/ppermute | solution.py:51
  87.3 3.7 %collective-permute-start.24 = (f32[8,256]{1,0:T(8,128)S(1)}, f32[8,256]{1,0:T(8,128)S(1)}, u32[]{:S(2)}, u32[]{:S(2)}) collective-permute-start(f32[8,256]{1,0:T(8,128)S(1)} %hand_on.10), channel_id=1, source_target_pairs={{0,16},{4,20},{8,24},{12,28},{16,0},{20,4},{24,8},{28,12},{1,17},{... | collective-permute-start | bytes 24584 | tf_op jit(solution)/shard_map/ppermute | solution.py:51
  88.9 3.7 %collective-permute-start.23 = (f32[8,256]{1,0:T(8,128)S(1)}, f32[8,256]{1,0:T(8,128)S(1)}, u32[]{:S(2)}, u32[]{:S(2)}) collective-permute-start(f32[8,256]{1,0:T(8,128)S(1)} %hand_on.10), channel_id=1, source_target_pairs={{0,8},{4,12},{8,0},{12,4},{16,24},{20,28},{24,16},{28,20},{1,9},{5... | collective-permute-start | bytes 24584 | tf_op jit(solution)/shard_map/ppermute | solution.py:51
  92.6 1.7 %collective-permute-start.27 = (bf16[256,768]{1,0:T(8,128)(2,1)S(1)}, bf16[256,768]{1,0:T(8,128)(2,1)S(1)}, u32[]{:S(2)}, u32[]{:S(2)}) collective-permute-start(bf16[256,768]{1,0:T(8,128)(2,1)S(1)} %hand_on.11.refs_0_), channel_id=1, source_target_pairs={{0,4},{4,0},{8,12},{12,8},{16,20},{20,16},{24,28},{28,24},{1,5},{5... | collective-permute-start | bytes 1179656 | tf_op jit(solution)/shard_map/ppermute | solution.py:51
  92.6 2.3 %collective-permute-start.28 = (bf16[256,768]{1,0:T(8,128)(2,1)S(1)}, bf16[256,768]{1,0:T(8,128)(2,1)S(1)}, u32[]{:S(2)}, u32[]{:S(2)}) collective-permute-start(bf16[256,768]{1,0:T(8,128)(2,1)S(1)} %hand_on.12.refs_2_), channel_id=1, source_target_pairs={{0,4},{4,0},{8,12},{12,8},{16,20},{20,16},{24,28},{28,24},{1,5},{5... | collective-permute-start | bytes 1179656 | tf_op jit(solution)/shard_map/ppermute | solution.py:51
  93.1 9.3 %collective-permute-start.26 = (bf16[128,768]{1,0:T(8,128)(2,1)S(1)}, bf16[128,768]{1,0:T(8,128)(2,1)S(1)}, u32[]{:S(2)}, u32[]{:S(2)}) collective-permute-start(bf16[128,768]{1,0:T(8,128)(2,1)S(1)} %slice.8), channel_id=1, source_target_pairs={{0,16},{4,20},{8,24},{12,28},{16,0},{20,4},{24,8},{28,12},{1,17},{... | collective-permute-start | bytes 589832 | tf_op jit(solution)/shard_map/ppermute | solution.py:51
  93.6 8.8 %collective-permute-start.29 = (bf16[128,768]{1,0:T(8,128)(2,1)S(1)}, bf16[128,768]{1,0:T(8,128)(2,1)S(1)}, u32[]{:S(2)}, u32[]{:S(2)}) collective-permute-start(bf16[128,768]{1,0:T(8,128)(2,1)S(1)} %slice.9), channel_id=1, source_target_pairs={{0,8},{4,12},{8,0},{12,4},{16,24},{20,28},{24,16},{28,20},{1,9},{5... | collective-permute-start | bytes 589832 | tf_op jit(solution)/shard_map/ppermute | solution.py:51
  102.5 3.8 %collective-permute-start.30 = (bf16[256,768]{1,0:T(8,128)(2,1)S(1)}, bf16[256,768]{1,0:T(8,128)(2,1)S(1)}, u32[]{:S(2)}, u32[]{:S(2)}) collective-permute-start(bf16[256,768]{1,0:T(8,128)(2,1)S(1)} %pad_maximum_fusion.refs_0_), channel_id=1, source_target_pairs={{0,4},{4,0},{8,12},{12,8},{16,20},{20,16},{24,28},{28,24},{1,5},{5... | collective-permute-start | bytes 1179656 | tf_op jit(solution)/shard_map/ppermute | solution.py:51

commit v12 on v11

--- a/solution.py
+++ b/solution.py
@@ -432,9 +432,11 @@
     )(inverse, own, *received)
 
 
-def result_kernel(pairs, momentum_too, weight_too, factor, buf0, buf1, ortho_ref, weight, squares, *refs):
+def result_kernel(pairs, momenta, weight_too, terms, factor, buf0, buf1, ortho_ref, weight, *refs):
+    squares, refs = refs[:terms], refs[terms:]
     blocks, rest = refs[: 2 * len(pairs)], refs[2 * len(pairs) :]
     *outs, token, mbuf, vbuf, nbuf, out_sems, basis_sems = rest
+    momentum_too = any(momenta)
     new_momentum = outs[-1] if momentum_too else None
     new_weight, basis = outs[-2 - momentum_too : len(outs) - momentum_too] if weight_too else (None, None)
     r, width = blocks[0].shape
@@ -453,7 +455,7 @@
     def stores(b, t):
         at, there = place(b, t)
         copies = []
-        if momentum_too:
+        if momenta[b // 2]:
             copies.append((mbuf, new_momentum))
         if weight_too:
             copies.append((vbuf, new_weight))
@@ -470,7 +472,8 @@
                 store.wait()
 
     if weight_too:
-        scale = lax.rsqrt(jnp.sum(squares[...], axis=0, keepdims=True) / FF + epsilon)
+        total = jnp.sum(pair_up([ref[...] for ref in squares]), axis=0, keepdims=True)
+        scale = lax.rsqrt(total / FF + epsilon)
         scale = jnp.transpose(jnp.broadcast_to(scale, (128, r)))[:, :1]
     token[...] = jnp.zeros_like(token)
     depth = lax.axis_size("col")
@@ -485,7 +488,7 @@
 
         def step(t, carry, b=b, k=k):
             at, there = place(b, t)
-            if momentum_too:
+            if momenta[b // 2]:
                 correction = dot(ortho_ref[...], blocks[b][:, at])
                 for j in range(2 * depth):
                     rows = slice(j * size, (j + 1) * size)
@@ -505,11 +508,12 @@
 
 
 def results(pairs, kinds, factor, bufs, ortho_bf, weight, squares, blocks, outs=(), after=(), last=()):
-    momentum_too, weight_too = kinds
+    momenta, weight_too = kinds
+    momentum_too = any(momenta)
     m, n = weight.shape
     r, width = blocks[0].shape
     outs = [*outs, *last]
-    ins = [*map(keep, bufs), ortho_bf, keep(weight), squares, *blocks, *after, *map(stay, outs)]
+    ins = [*map(keep, bufs), ortho_bf, keep(weight), *squares, *blocks, *after, *map(stay, outs)]
     at = len(ins) - len(outs)
     skipped = 2 * weight_too + momentum_too - len(outs) if last else 0
     out_shape = []
@@ -519,9 +523,9 @@
         out_shape += [shape((m, n), f32)]
     m_rows, w_rows = (m if momentum_too else 8), (m if weight_too else 16)
     *outs, token = pl.pallas_call(
-        functools.partial(result_kernel, pairs, *kinds, factor),
+        functools.partial(result_kernel, pairs, *kinds, len(squares), factor),
         out_shape=[*out_shape, shape((8, 128), f32)],
-        in_specs=[VMEM] * (5 + len(blocks)) + [ANY] * (len(after) + len(outs)),
+        in_specs=[VMEM] * (4 + len(squares) + len(blocks)) + [ANY] * (len(after) + len(outs)),
         out_specs=[ANY] * len(out_shape) + [VMEM],
         input_output_aliases={at + k: skipped + k for k in range(len(outs))},
         scratch_shapes=[
@@ -607,7 +611,7 @@
     factor = step_rate * math.sqrt(D / RANK)
     common = (factor, bufs, ortho_bf, weight)
     squares = exchange(hand_on(squares, own_pair), "col", depth)
-    (momentum,), token = results((0,), (True, False), *common, squares[0], (share, own_pair))
+    (momentum,), token = results((0,), ((True,), False), *common, squares[:1], (share, own_pair))
     squares = pair_up([hand_on(squares[0], token), *squares[1:]])
     squares = squares + swap(squares, "row", 1)
     squares = hand_on(squares, *blocks.values())
@@ -628,18 +632,14 @@
             halves[d] = top, bottom
             blocks[d] = jnp.concatenate([top, bottom], axis=0)
 
-    common = (*common, squares)
-    weight_basis = ()
-    if near[1:]:
-        rest = [x for d in near[1:] for x in pairs[d]]
-        (*weight_basis, momentum), token = results(
-            tuple(near[1:]), (True, True), *common, rest, (), (), [momentum]
-        )
+    common = (*common, [squares])
+    order = (*near[1:], 0)
+    rest = [x for d in order for x in pairs[d]]
+    kinds = (tuple(d > 0 for d in order), True)
+    outs, token = results(order, kinds, *common, rest, (), (), [momentum])
     blocks = {d: jnp.concatenate([hand_on(top, token), bottom], axis=0) for d, (top, bottom) in halves.items()}
-    weight_basis, token = results((0,), (False, True), *common, pairs[0], weight_basis)
-    outs = [*weight_basis, momentum]
     for d, block in blocks.items():
-        outs, token = results((d,), (True, True), *common, (block, swap(block, "row", 1)), outs)
+        outs, token = results((d,), ((True,), True), *common, (block, swap(block, "row", 1)), outs)
     new_weight, new_basis, new_momentum = outs
     return (new_weight, new_momentum, new_basis)
 

time: 112 us -> 111 us (level)
  Pallas kernels: 57.9 us -> 56.1 us
  waiting for transfers between devices: 19.8 us -> 21.4 us
    pallas_call x4 -> x3, Pallas kernels: 19.3 us -> 17.5 us  [results(): pl.pallas_call(functools.partial(result_kernel, pairs, *kinds, len(square...]
    ppermute x31, waiting for transfers between devices: 19.8 us -> 21.4 us  [swap(): lax.ppermute(x, axis, [(i, i ^ d) for i in range(lax.axis_size(axis))])]
  transfers between devices with their start and end apart: 31 -> 31, of which waited for: 13 -> 14; matrix products, arithmetic and copies ran while one was open for 0% -> 0% of each run, Pallas kernels for 39% -> 37%
where the time goes in v12:
time: 111 us
  Pallas kernels  56.1 us (51%)
  starting transfers between devices  32.5 us (29%)
  waiting for transfers between devices  21.4 us (19%)
  between operations  1.12 us (1%)
    ppermute x31, starting transfers between devices, swap(): lax.ppermute(x, axis, [(i, i ^ d) for i in range(lax.axis_size(axis))])  32.5 us
    ppermute x31, waiting for transfers between devices, swap(): lax.ppermute(x, axis, [(i, i ^ d) for i in range(lax.axis_size(axis))])  21.4 us
    pallas_call x3, Pallas kernels, results(): pl.pallas_call(functools.partial(result_kernel, pairs, *kinds, len(square...  17.5 us
    pallas_call x2, Pallas kernels, project(): pl.pallas_call(functools.partial(project_kernel, part, depth, width), out...  16.5 us
    pallas_call x1, Pallas kernels, chol_inverse(): pl.pallas_call(chol_inverse_kernel, out_shape=(shape((n, n), f32), pltpu....  13.5 us
    pallas_call x1, Pallas kernels, first_product(): pl.pallas_call(functools.partial(first_kernel, depth, width), out_shape=(...  3.35 us
    pallas_call x2, Pallas kernels, last_product(): pl.pallas_call(functools.partial(last_kernel, depth, width, mine), out_sh...  3.13 us
  transfers between devices with their start and end apart: 31, of which 14 were waited for; matrix products, arithmetic and copies ran while one was open for 0% of the time, Pallas kernels for 37%

profile of v12, /device:TPU:0, one launch (start us, length us, event | category | flops | bytes accessed | tf_op | source)
XLA Modules:
  0.0 111.3 jit_solution(14067373138101500219)
XLA Ops:
  0.6 8.7 %project.2 = (f32[512,6144]{1,0:T(8,128)S(1)}, bf16[256,6144]{1,0:T(8,128)(2,1)S(1)}, f32[256,256]{1,0:T(8,128)S(1)}, bf16[256,256]{1,0:T(8,128)(2,1)S(1)}) custom-call(f32[1024,6144]{1,0:T(8,128)} %mom.3, bf16[1024,6144]{1,0:T(8,128)(2,1)} %grad.3, bf16[256,6144]{1,0:T(8,128)(2,1)} %basis.1), custom_call_target="tpu_custom_call" | custom-call | bytes 37748736 | tf_op jit(solution)/shard_map/project/pallas_call | solution.py:104
  9.3 3.1 %collective-permute-start.2 = (bf16[256,256]{1,0:T(8,128)(2,1)S(1)}, bf16[256,256]{1,0:T(8,128)(2,1)S(1)}, u32[]{:S(2)}, u32[]{:S(2)}) collective-permute-start(bf16[256,256]{1,0:T(8,128)(2,1)S(1)} %get-tuple-element.38.rest_0_), channel_id=1, source_target_pairs={{0,1},{1,0},{2,3},{3,2},{4,5},{5,4},{6,7},{7,6},{8,9},{9,8},{10,11... | collective-permute-start | bytes 393224 | tf_op jit(solution)/shard_map/ppermute | solution.py:51
  12.4 7.8 %project.3 = (f32[512,6144]{1,0:T(8,128)S(1)}, f32[256,256]{1,0:T(8,128)S(1)}, bf16[256,256]{1,0:T(8,128)(2,1)S(1)}) custom-call(f32[1024,6144]{1,0:T(8,128)} %mom.3, bf16[1024,6144]{1,0:T(8,128)(2,1)} %grad.3, bf16[256,6144]{1,0:T(8,128)(2,1)S(1)} %get-tuple-element.37.basis, bf16[256,256]{1,0:T(8,128)(2,1)S(1)} %get-tuple-element.38.rest_0_), custom_call_target="tpu_custom_call" | custom-call | bytes 37748736 | tf_op jit(solution)/shard_map/project/pallas_call | solution.py:104
  20.4 3.1 %collective-permute-start.3 = (bf16[256,128]{1,0:T(8,128)(2,1)S(1)}, bf16[256,128]{1,0:T(8,128)(2,1)S(1)}, u32[]{:S(2)}, u32[]{:S(2)}) collective-permute-start(bf16[256,128]{1,0:T(8,128)(2,1)S(1)} %get-tuple-element.46), channel_id=1, source_target_pairs={{0,2},{1,3},{2,0},{3,1},{4,6},{5,7},{6,4},{7,5},{8,10},{9,11},{10,... | collective-permute-start | bytes 196616 | tf_op jit(solution)/shard_map/ppermute | solution.py:51
  23.4 3.2 %collective-permute-done.received = bf16[256,256]{1,0:T(8,128)(2,1)S(1)} collective-permute-done((bf16[256,256]{1,0:T(8,128)(2,1)S(1)}, bf16[256,256]{1,0:T(8,128)(2,1)S(1)}, u32[]{:S(2)}, u32[]{:S(2)}) %collective-permute-start) | collective-permute-done | bytes 131104 | tf_op jit(solution)/shard_map/ppermute | solution.py:51
  26.7 2.3 %collective-permute-start.1 = (bf16[256,128]{1,0:T(8,128)(2,1)S(1)}, bf16[256,128]{1,0:T(8,128)(2,1)S(1)}, u32[]{:S(2)}, u32[]{:S(2)}) collective-permute-start(bf16[256,128]{1,0:T(8,128)(2,1)S(1)} %get-tuple-element.43), channel_id=1, source_target_pairs={{0,2},{1,3},{2,0},{3,1},{4,6},{5,7},{6,4},{7,5},{8,10},{9,11},{10,... | collective-permute-start | bytes 196616 | tf_op jit(solution)/shard_map/ppermute | solution.py:51
  29.0 2.9 %collective-permute-done.1.received = bf16[256,128]{1,0:T(8,128)(2,1)S(1)} collective-permute-done((bf16[256,128]{1,0:T(8,128)(2,1)S(1)}, bf16[256,128]{1,0:T(8,128)(2,1)S(1)}, u32[]{:S(2)}, u32[]{:S(2)}) %collective-permute-start.1) | collective-permute-done | bytes 65568 | tf_op jit(solution)/shard_map/ppermute | solution.py:51
  32.0 2.5 %collective-permute-start.4 = (bf16[256,256]{1,0:T(8,128)(2,1)S(1)}, bf16[256,256]{1,0:T(8,128)(2,1)S(1)}, u32[]{:S(2)}, u32[]{:S(2)}) collective-permute-start(bf16[256,256]{1,0:T(8,128)(2,1)S(1)} %fold_last.3.rest_0_.refs_0_), channel_id=1, source_target_pairs={{0,2},{1,3},{2,0},{3,1},{4,6},{5,7},{6,4},{7,5},{8,10},{9,11},{10,... | collective-permute-start | bytes 393224 | tf_op jit(solution)/shard_map/ppermute | solution.py:51
  34.5 4.4 %collective-permute-done.4.rest_1_.refs_2_ = bf16[256,256]{1,0:T(8,128)(2,1)S(1)} collective-permute-done((bf16[256,256]{1,0:T(8,128)(2,1)S(1)}, bf16[256,256]{1,0:T(8,128)(2,1)S(1)}, u32[]{:S(2)}, u32[]{:S(2)}) %collective-permute-start.4) | collective-permute-done | bytes 131104 | tf_op jit(solution)/shard_map/ppermute | solution.py:51
  38.8 3.4 %first_product.1 = (f32[256,3072]{1,0:T(8,128)S(1)}, f32[256,3072]{1,0:T(8,128)S(1)}, f32[256,256]{1,0:T(8,128)S(1)}) custom-call(f32[512,6144]{1,0:T(8,128)S(1)} %get-tuple-element.36.buf0, f32[512,6144]{1,0:T(8,128)S(1)} %get-tuple-element.39.buf1, bf16[256,256]{1,0:T(8,128)(2,1)S(1)} %fold_last.3.rest_0_.refs_0_, ...), custom_call_target="tpu_custom_call" | custom-call | bytes 31457280 | tf_op jit(solution)/shard_map/first_product/pallas_call | solution.py:211
  42.2 1.6 %collective-permute-done.6.rest_1_.refs_3_ = bf16[256,256]{1,0:T(8,128)(2,1)S(1)} collective-permute-done((bf16[256,256]{1,0:T(8,128)(2,1)S(1)}, bf16[256,256]{1,0:T(8,128)(2,1)S(1)}, u32[]{:S(2)}, u32[]{:S(2)}) %collective-permute-start.6) | collective-permute-done | bytes 131104 | tf_op jit(solution)/shard_map/ppermute | solution.py:51
  43.8 0.3 gram.1
  44.2 1.6 %other_product.1.refs_0_ = bf16[256,3072]{1,0:T(8,128)(2,1)S(1)} custom-call(f32[512,6144]{1,0:T(8,128)S(1)} %get-tuple-element.36.buf0, f32[512,6144]{1,0:T(8,128)S(1)} %get-tuple-element.39.buf1, f32[256,3072]{1,0:T(8,128)S(1)} %get-tuple-element.53.sums, bf16[256,256]{1,0:T(8,128)(2,1)S(1)} %collective-permute-done.5.rest_0_.refs_1_, ...), custom_call_target="tpu_custom_call" | custom-call | bytes 15728640 | tf_op jit(solution)/shard_map/other_product/pallas_call | solution.py:266
  45.8 0.6 collective-permute-start.12
  46.4 2.4 %collective-permute-start.10 = (f32[128,256]{1,0:T(8,128)S(1)}, f32[128,256]{1,0:T(8,128)S(1)}, u32[]{:S(2)}, u32[]{:S(2)}) collective-permute-start(f32[128,256]{1,0:T(8,128)S(1)} %add.33.refs_1_.rest_2_._), channel_id=1, source_target_pairs={{0,24},{4,28},{8,16},{12,20},{16,8},{20,12},{24,0},{28,4},{1,25},{... | collective-permute-start | bytes 393224 | tf_op jit(solution)/shard_map/ppermute | solution.py:51
  48.8 0.5 collective-permute-start.9
  49.3 0.6 collective-permute-start.8
  49.9 1.6 %mine_product.1.mine = f32[256,3072]{1,0:T(8,128)S(1)} custom-call(f32[512,6144]{1,0:T(8,128)S(1)} %get-tuple-element.36.buf0, f32[512,6144]{1,0:T(8,128)S(1)} %get-tuple-element.39.buf1, f32[256,3072]{1,0:T(8,128)S(1)} %get-tuple-element.52.sums, bf16[256,256]{1,0:T(8,128)(2,1)S(1)} %collective-permute-done.5.rest_0_.refs_1_, ...), custom_call_target="tpu_custom_call" | custom-call | bytes 15728640 | tf_op jit(solution)/shard_map/mine_product/pallas_call | solution.py:266
  51.5 0.3 pair_sum.1
  51.8 1.5 %collective-permute-start.13 = (bf16[256,768]{1,0:T(8,128)(2,1)S(1)}, bf16[256,768]{1,0:T(8,128)(2,1)S(1)}, u32[]{:S(2)}, u32[]{:S(2)}) collective-permute-start(bf16[256,768]{1,0:T(8,128)(2,1)S(1)} %get-tuple-element.55), channel_id=1, source_target_pairs={{0,8},{4,12},{8,0},{12,4},{16,24},{20,28},{24,16},{28,20},{1,9},{5... | collective-permute-start | bytes 1179656 | tf_op jit(solution)/shard_map/ppermute | solution.py:51
  53.3 1.5 %collective-permute-start.14 = (bf16[256,768]{1,0:T(8,128)(2,1)S(1)}, bf16[256,768]{1,0:T(8,128)(2,1)S(1)}, u32[]{:S(2)}, u32[]{:S(2)}) collective-permute-start(bf16[256,768]{1,0:T(8,128)(2,1)S(1)} %get-tuple-element.56), channel_id=1, source_target_pairs={{0,16},{4,20},{8,24},{12,28},{16,0},{20,4},{24,8},{28,12},{1,17},{... | collective-permute-start | bytes 1179656 | tf_op jit(solution)/shard_map/ppermute | solution.py:51
  54.8 1.2 %collective-permute-start.15 = (bf16[256,768]{1,0:T(8,128)(2,1)S(1)}, bf16[256,768]{1,0:T(8,128)(2,1)S(1)}, u32[]{:S(2)}, u32[]{:S(2)}) collective-permute-start(bf16[256,768]{1,0:T(8,128)(2,1)S(1)} %get-tuple-element.57), channel_id=1, source_target_pairs={{0,24},{4,28},{8,16},{12,20},{16,8},{20,12},{24,0},{28,4},{1,25},{... | collective-permute-start | bytes 1179656 | tf_op jit(solution)/shard_map/ppermute | solution.py:51
  56.1 0.4 collective-permute-done.8
  56.6 1.3 %collective-permute-done.11.other = f32[128,256]{1,0:T(8,128)S(1)} collective-permute-done((f32[128,256]{1,0:T(8,128)S(1)}, f32[128,256]{1,0:T(8,128)S(1)}, u32[]{:S(2)}, u32[]{:S(2)}) %collective-permute-start.11) | collective-permute-done | bytes 131104 | tf_op jit(solution)/shard_map/ppermute | solution.py:51
  57.9 13.5 %chol_inverse.1 = (f32[256,256]{1,0:T(8,128)S(1)}, bf16[1024,6144]{1,0:T(8,128)(2,1)S(1)}) custom-call(f32[128,256]{1,0:T(8,128)S(1)} %add_add_fusion.mine, f32[128,256]{1,0:T(8,128)S(1)} %collective-permute-done.11.other, bf16[1024,6144]{1,0:T(8,128)(2,1)} %weight.1), custom_call_target="tpu_custom_call" | custom-call | bytes 33554432 | tf_op jit(solution)/shard_map/chol_inverse/pallas_call | solution.py:353
  71.5 0.9 collective-permute-done.15.refs_2_
  72.4 0.7 share.1
  73.2 1.6 %collective-permute-start.22 = (bf16[256,768]{1,0:T(8,128)(2,1)S(1)}, bf16[256,768]{1,0:T(8,128)(2,1)S(1)}, u32[]{:S(2)}, u32[]{:S(2)}) collective-permute-start(bf16[256,768]{1,0:T(8,128)(2,1)S(1)} %get-tuple-element.59.refs_1_.refs_5_), channel_id=1, source_target_pairs={{0,16},{4,20},{8,24},{12,28},{16,0},{20,4},{24,8},{28,12},{1,17},{... | collective-permute-start | bytes 1179656 | tf_op jit(solution)/shard_map/ppermute | solution.py:51
  74.7 1.5 %collective-permute-start.21 = (bf16[256,768]{1,0:T(8,128)(2,1)S(1)}, bf16[256,768]{1,0:T(8,128)(2,1)S(1)}, u32[]{:S(2)}, u32[]{:S(2)}) collective-permute-start(bf16[256,768]{1,0:T(8,128)(2,1)S(1)} %get-tuple-element.59.refs_1_.refs_5_), channel_id=1, source_target_pairs={{0,8},{4,12},{8,0},{12,4},{16,24},{20,28},{24,16},{28,20},{1,9},{5... | collective-permute-start | bytes 1179656 | tf_op jit(solution)/shard_map/ppermute | solution.py:51
  76.3 2.9 %collective-permute-start.19 = (f32[8,256]{1,0:T(8,128)S(1)}, f32[8,256]{1,0:T(8,128)S(1)}, u32[]{:S(2)}, u32[]{:S(2)}) collective-permute-start(f32[8,256]{1,0:T(8,128)S(1)} %hand_on.8.refs_0_), channel_id=1, source_target_pairs={{0,3},{1,2},{2,1},{3,0},{4,7},{5,6},{6,5},{7,4},{8,11},{9,10},{10,... | collective-permute-start | bytes 24584 | tf_op jit(solution)/shard_map/ppermute | solution.py:51
  79.3 1.4 %collective-permute-start.17 = (f32[8,256]{1,0:T(8,128)S(1)}, f32[8,256]{1,0:T(8,128)S(1)}, u32[]{:S(2)}, u32[]{:S(2)}) collective-permute-start(f32[8,256]{1,0:T(8,128)S(1)} %hand_on.8.refs_0_), channel_id=1, source_target_pairs={{0,1},{1,0},{2,3},{3,2},{4,5},{5,4},{6,7},{7,6},{8,9},{9,8},{10,11... | collective-permute-start | bytes 24584 | tf_op jit(solution)/shard_map/ppermute | solution.py:51
  80.7 0.6 ortho.1.ortho_ref
  81.3 3.1 %results.3 = (f32[1024,6144]{1,0:T(8,128)}, f32[8,128]{1,0:T(8,128)S(1)}) custom-call(f32[512,6144]{1,0:T(8,128)S(1)} %get-tuple-element.36.buf0, f32[512,6144]{1,0:T(8,128)S(1)} %copy-done.1, bf16[1024,256]{1,0:T(8,128)(2,1)S(1)} %ortho.1.ortho_ref, bf16[1024,6144]{1,0:T(8,128)(2,1)S(1)} %get-tuple-element.51.weight, f32[8,256]{1,0:T(8,128)S(1)} %hand_on.8.refs_0_, ...), custom_call_target="tpu_custom_call" | custom-call | bytes 6291456 | tf_op jit(solution)/shard_map/results/pallas_call | solution.py:525
  84.6 1.2 %collective-permute-done.20 = f32[8,256]{1,0:T(8,128)S(1)} collective-permute-done((f32[8,256]{1,0:T(8,128)S(1)}, f32[8,256]{1,0:T(8,128)S(1)}, u32[]{:S(2)}, u32[]{:S(2)}) %collective-permute-start.20) | collective-permute-done | bytes 8224 | tf_op jit(solution)/shard_map/ppermute | solution.py:51
  85.7 0.2 collective-permute-done.21.refs_1_.refs_0_
  85.9 1.4 %collective-permute-start.25 = (f32[8,256]{1,0:T(8,128)S(1)}, f32[8,256]{1,0:T(8,128)S(1)}, u32[]{:S(2)}, u32[]{:S(2)}) collective-permute-start(f32[8,256]{1,0:T(8,128)S(1)} %hand_on.10), channel_id=1, source_target_pairs={{0,24},{4,28},{8,16},{12,20},{16,8},{20,12},{24,0},{28,4},{1,25},{... | collective-permute-start | bytes 24584 | tf_op jit(solution)/shard_map/ppermute | solution.py:51
  87.4 1.5 %collective-permute-start.24 = (f32[8,256]{1,0:T(8,128)S(1)}, f32[8,256]{1,0:T(8,128)S(1)}, u32[]{:S(2)}, u32[]{:S(2)}) collective-permute-start(f32[8,256]{1,0:T(8,128)S(1)} %hand_on.10), channel_id=1, source_target_pairs={{0,16},{4,20},{8,24},{12,28},{16,0},{20,4},{24,8},{28,12},{1,17},{... | collective-permute-start | bytes 24584 | tf_op jit(solution)/shard_map/ppermute | solution.py:51
  88.9 0.5 collective-permute-start.23
  89.4 1.1 collective-permute-done.25
  90.5 0.5 collective-permute-done.24
  91.0 1.5 %collective-permute-done.23 = f32[8,256]{1,0:T(8,128)S(1)} collective-permute-done((f32[8,256]{1,0:T(8,128)S(1)}, f32[8,256]{1,0:T(8,128)S(1)}, u32[]{:S(2)}, u32[]{:S(2)}) %collective-permute-start.23) | collective-permute-done | bytes 8224 | tf_op jit(solution)/shard_map/ppermute | solution.py:51
  92.6 0.5 collective-permute-start.28
  93.1 0.5 collective-permute-start.26
  93.7 0.6 collective-permute-start.29
  94.3 0.6 collective-permute-done.28.refs_4_
  94.9 9.3 %results.4 = (bf16[1024,6144]{1,0:T(8,128)(2,1)}, bf16[256,6144]{1,0:T(8,128)(2,1)}, f32[1024,6144]{1,0:T(8,128)}, f32[8,128]{1,0:T(8,128)S(1)}) custom-call(f32[512,6144]{1,0:T(8,128)S(1)} %get-tuple-element.36.buf0, f32[512,6144]{1,0:T(8,128)S(1)} %copy-done.1, bf16[1024,256]{1,0:T(8,128)(2,1)S(1)} %ortho.1.ortho_ref, ...), custom_call_target="tpu_custom_call", output_to_operand_aliasing={{2}: (11, {})} | custom-call | bytes 37748736 | tf_op jit(solution)/shard_map/results/pallas_call | solution.py:525
  104.4 1.6 %collective-permute-done.30.refs_2_ = bf16[256,768]{1,0:T(8,128)(2,1)S(1)} collective-permute-done((bf16[256,768]{1,0:T(8,128)(2,1)S(1)}, bf16[256,768]{1,0:T(8,128)(2,1)S(1)}, u32[]{:S(2)}, u32[]{:S(2)}) %collective-permute-start.30) | collective-permute-done | bytes 393248 | tf_op jit(solution)/shard_map/ppermute | solution.py:51
  106.0 5.1 %results.5 = (bf16[1024,6144]{1,0:T(8,128)(2,1)}, bf16[256,6144]{1,0:T(8,128)(2,1)}, f32[1024,6144]{1,0:T(8,128)}, f32[8,128]{1,0:T(8,128)}) custom-call(f32[512,6144]{1,0:T(8,128)S(1)} %get-tuple-element.36.buf0, f32[512,6144]{1,0:T(8,128)S(1)} %copy-done.1, ...), custom_call_target="tpu_custom_call", output_to_operand_aliasing={{0}: (7, {}), {1}: (8, {}), {2}: (9, {})} | custom-call | bytes 12582912 | tf_op jit(solution)/shard_map/results/pallas_call | solution.py:525
  (50 shorter events, 1.0 us)
Async XLA Ops:
  9.3 11.0 %collective-permute-start.2 = (bf16[256,256]{1,0:T(8,128)(2,1)S(1)}, bf16[256,256]{1,0:T(8,128)(2,1)S(1)}, u32[]{:S(2)}, u32[]{:S(2)}) collective-permute-start(bf16[256,256]{1,0:T(8,128)(2,1)S(1)} %get-tuple-element.38.rest_0_), channel_id=1, source_target_pairs={{0,1},{1,0},{2,3},{3,2},{4,5},{5,4},{6,7},{7,6},{8,9},{9,8},{10,11... | collective-permute-start | bytes 393224 | tf_op jit(solution)/shard_map/ppermute | solution.py:51
  20.2 29.6 %copy-start = (f32[512,6144]{1,0:T(8,128)}, f32[512,6144]{1,0:T(8,128)S(1)}, u32[]{:S(2)}) copy-start(f32[512,6144]{1,0:T(8,128)S(1)} %get-tuple-element.39.buf1) | copy-start | bytes 37748740
  20.2 6.4 %collective-permute-start = (bf16[256,256]{1,0:T(8,128)(2,1)S(1)}, bf16[256,256]{1,0:T(8,128)(2,1)S(1)}, u32[]{:S(2)}, u32[]{:S(2)}) collective-permute-start(bf16[256,256]{1,0:T(8,128)(2,1)S(1)} %get-tuple-element.41), channel_id=1, source_target_pairs={{0,1},{1,0},{2,3},{3,2},{4,5},{5,4},{6,7},{7,6},{8,9},{9,8},{10,11... | collective-permute-start | bytes 393224 | tf_op jit(solution)/shard_map/ppermute | solution.py:51
  20.4 8.7 %collective-permute-start.3 = (bf16[256,128]{1,0:T(8,128)(2,1)S(1)}, bf16[256,128]{1,0:T(8,128)(2,1)S(1)}, u32[]{:S(2)}, u32[]{:S(2)}) collective-permute-start(bf16[256,128]{1,0:T(8,128)(2,1)S(1)} %get-tuple-element.46), channel_id=1, source_target_pairs={{0,2},{1,3},{2,0},{3,1},{4,6},{5,7},{6,4},{7,5},{8,10},{9,11},{10,... | collective-permute-start | bytes 196616 | tf_op jit(solution)/shard_map/ppermute | solution.py:51
  26.7 5.2 %collective-permute-start.1 = (bf16[256,128]{1,0:T(8,128)(2,1)S(1)}, bf16[256,128]{1,0:T(8,128)(2,1)S(1)}, u32[]{:S(2)}, u32[]{:S(2)}) collective-permute-start(bf16[256,128]{1,0:T(8,128)(2,1)S(1)} %get-tuple-element.43), channel_id=1, source_target_pairs={{0,2},{1,3},{2,0},{3,1},{4,6},{5,7},{6,4},{7,5},{8,10},{9,11},{10,... | collective-permute-start | bytes 196616 | tf_op jit(solution)/shard_map/ppermute | solution.py:51
  32.0 6.9 %collective-permute-start.4 = (bf16[256,256]{1,0:T(8,128)(2,1)S(1)}, bf16[256,256]{1,0:T(8,128)(2,1)S(1)}, u32[]{:S(2)}, u32[]{:S(2)}) collective-permute-start(bf16[256,256]{1,0:T(8,128)(2,1)S(1)} %fold_last.3.rest_0_.refs_0_), channel_id=1, source_target_pairs={{0,2},{1,3},{2,0},{3,1},{4,6},{5,7},{6,4},{7,5},{8,10},{9,11},{10,... | collective-permute-start | bytes 393224 | tf_op jit(solution)/shard_map/ppermute | solution.py:51
  34.5 7.7 %collective-permute-start.5 = (bf16[256,256]{1,0:T(8,128)(2,1)S(1)}, bf16[256,256]{1,0:T(8,128)(2,1)S(1)}, u32[]{:S(2)}, u32[]{:S(2)}) collective-permute-start(bf16[256,256]{1,0:T(8,128)(2,1)S(1)} %fold_last.3.rest_0_.refs_0_), channel_id=1, source_target_pairs={{0,1},{1,0},{2,3},{3,2},{4,5},{5,4},{6,7},{7,6},{8,9},{9,8},{10,11... | collective-permute-start | bytes 393224 | tf_op jit(solution)/shard_map/ppermute | solution.py:51
  38.8 5.0 %collective-permute-start.6 = (bf16[256,256]{1,0:T(8,128)(2,1)S(1)}, bf16[256,256]{1,0:T(8,128)(2,1)S(1)}, u32[]{:S(2)}, u32[]{:S(2)}) collective-permute-start(bf16[256,256]{1,0:T(8,128)(2,1)S(1)} %collective-permute-done.4.rest_1_.refs_2_), channel_id=1, source_target_pairs={{0,1},{1,0},{2,3},{3,2},{4,5},{5,4},{6,7},{7,6},{8,9},{9,8},{10,11... | collective-permute-start | bytes 393224 | tf_op jit(solution)/shard_map/ppermute | solution.py:51
  44.1 1.7 %collective-permute-start.7 = (f32[128,256]{1,0:T(8,128)S(1)}, f32[128,256]{1,0:T(8,128)S(1)}, u32[]{:S(2)}, u32[]{:S(2)}) collective-permute-start(f32[128,256]{1,0:T(8,128)S(1)} %get-tuple-element.49), channel_id=1, source_target_pairs={{0,4},{4,0},{8,12},{12,8},{16,20},{20,16},{24,28},{28,24},{1,5},{5... | collective-permute-start | bytes 393224 | tf_op jit(solution)/shard_map/ppermute | solution.py:51
  45.8 5.6 %collective-permute-start.12 = (bf16[256,3072]{1,0:T(8,128)(2,1)S(1)}, bf16[256,3072]{1,0:T(8,128)(2,1)S(1)}, u32[]{:S(2)}, u32[]{:S(2)}) collective-permute-start(bf16[256,3072]{1,0:T(8,128)(2,1)S(1)} %hand_on.7.rest_3_), channel_id=1, source_target_pairs={{0,4},{4,0},{8,12},{12,8},{16,20},{20,16},{24,28},{28,24},{1,5},{5... | collective-permute-start | bytes 4718600 | tf_op jit(solution)/shard_map/ppermute | solution.py:51
  46.4 8.5 %collective-permute-start.10 = (f32[128,256]{1,0:T(8,128)S(1)}, f32[128,256]{1,0:T(8,128)S(1)}, u32[]{:S(2)}, u32[]{:S(2)}) collective-permute-start(f32[128,256]{1,0:T(8,128)S(1)} %add.33.refs_1_.rest_2_._), channel_id=1, source_target_pairs={{0,24},{4,28},{8,16},{12,20},{16,8},{20,12},{24,0},{28,4},{1,25},{... | collective-permute-start | bytes 393224 | tf_op jit(solution)/shard_map/ppermute | solution.py:51
  48.8 7.3 %collective-permute-start.9 = (f32[128,256]{1,0:T(8,128)S(1)}, f32[128,256]{1,0:T(8,128)S(1)}, u32[]{:S(2)}, u32[]{:S(2)}) collective-permute-start(f32[128,256]{1,0:T(8,128)S(1)} %add.33.refs_1_.rest_2_._), channel_id=1, source_target_pairs={{0,16},{4,20},{8,24},{12,28},{16,0},{20,4},{24,8},{28,12},{1,17},{... | collective-permute-start | bytes 393224 | tf_op jit(solution)/shard_map/ppermute | solution.py:51
  49.3 7.2 %collective-permute-start.8 = (f32[128,256]{1,0:T(8,128)S(1)}, f32[128,256]{1,0:T(8,128)S(1)}, u32[]{:S(2)}, u32[]{:S(2)}) collective-permute-start(f32[128,256]{1,0:T(8,128)S(1)} %add.33.refs_1_.rest_2_._), channel_id=1, source_target_pairs={{0,8},{4,12},{8,0},{12,4},{16,24},{20,28},{24,16},{28,20},{1,9},{5... | collective-permute-start | bytes 393224 | tf_op jit(solution)/shard_map/ppermute | solution.py:51
  51.4 29.9 %copy-start.1 = (f32[512,6144]{1,0:T(8,128)S(1)}, f32[512,6144]{1,0:T(8,128)}, u32[]{:S(2)}) copy-start(f32[512,6144]{1,0:T(8,128)} %copy-done) | copy-start | bytes 37748740
  51.8 19.6 %collective-permute-start.13 = (bf16[256,768]{1,0:T(8,128)(2,1)S(1)}, bf16[256,768]{1,0:T(8,128)(2,1)S(1)}, u32[]{:S(2)}, u32[]{:S(2)}) collective-permute-start(bf16[256,768]{1,0:T(8,128)(2,1)S(1)} %get-tuple-element.55), channel_id=1, source_target_pairs={{0,8},{4,12},{8,0},{12,4},{16,24},{20,28},{24,16},{28,20},{1,9},{5... | collective-permute-start | bytes 1179656 | tf_op jit(solution)/shard_map/ppermute | solution.py:51
  53.3 18.1 %collective-permute-start.14 = (bf16[256,768]{1,0:T(8,128)(2,1)S(1)}, bf16[256,768]{1,0:T(8,128)(2,1)S(1)}, u32[]{:S(2)}, u32[]{:S(2)}) collective-permute-start(bf16[256,768]{1,0:T(8,128)(2,1)S(1)} %get-tuple-element.56), channel_id=1, source_target_pairs={{0,16},{4,20},{8,24},{12,28},{16,0},{20,4},{24,8},{28,12},{1,17},{... | collective-permute-start | bytes 1179656 | tf_op jit(solution)/shard_map/ppermute | solution.py:51
  54.8 17.6 %collective-permute-start.15 = (bf16[256,768]{1,0:T(8,128)(2,1)S(1)}, bf16[256,768]{1,0:T(8,128)(2,1)S(1)}, u32[]{:S(2)}, u32[]{:S(2)}) collective-permute-start(bf16[256,768]{1,0:T(8,128)(2,1)S(1)} %get-tuple-element.57), channel_id=1, source_target_pairs={{0,24},{4,28},{8,16},{12,20},{16,8},{20,12},{24,0},{28,4},{1,25},{... | collective-permute-start | bytes 1179656 | tf_op jit(solution)/shard_map/ppermute | solution.py:51
  56.5 1.4 %collective-permute-start.11 = (f32[128,256]{1,0:T(8,128)S(1)}, f32[128,256]{1,0:T(8,128)S(1)}, u32[]{:S(2)}, u32[]{:S(2)}) collective-permute-start(f32[128,256]{1,0:T(8,128)S(1)} %add_add_fusion.mine), channel_id=1, source_target_pairs={{0,4},{4,0},{8,12},{12,8},{16,20},{20,16},{24,28},{28,24},{1,5},{5... | collective-permute-start | bytes 393224 | tf_op jit(solution)/shard_map/ppermute | solution.py:51
  73.1 3.1 %collective-permute-start.16 = (bf16[256,768]{1,0:T(8,128)(2,1)S(1)}, bf16[256,768]{1,0:T(8,128)(2,1)S(1)}, u32[]{:S(2)}, u32[]{:S(2)}) collective-permute-start(bf16[256,768]{1,0:T(8,128)(2,1)S(1)} %get-tuple-element.59.refs_1_.refs_5_), channel_id=1, source_target_pairs={{0,4},{4,0},{8,12},{12,8},{16,20},{20,16},{24,28},{28,24},{1,5},{5... | collective-permute-start | bytes 1179656 | tf_op jit(solution)/shard_map/ppermute | solution.py:51
  73.2 12.5 %collective-permute-start.22 = (bf16[256,768]{1,0:T(8,128)(2,1)S(1)}, bf16[256,768]{1,0:T(8,128)(2,1)S(1)}, u32[]{:S(2)}, u32[]{:S(2)}) collective-permute-start(bf16[256,768]{1,0:T(8,128)(2,1)S(1)} %get-tuple-element.59.refs_1_.refs_5_), channel_id=1, source_target_pairs={{0,16},{4,20},{8,24},{12,28},{16,0},{20,4},{24,8},{28,12},{1,17},{... | collective-permute-start | bytes 1179656 | tf_op jit(solution)/shard_map/ppermute | solution.py:51
  74.7 11.2 %collective-permute-start.21 = (bf16[256,768]{1,0:T(8,128)(2,1)S(1)}, bf16[256,768]{1,0:T(8,128)(2,1)S(1)}, u32[]{:S(2)}, u32[]{:S(2)}) collective-permute-start(bf16[256,768]{1,0:T(8,128)(2,1)S(1)} %get-tuple-element.59.refs_1_.refs_5_), channel_id=1, source_target_pairs={{0,8},{4,12},{8,0},{12,4},{16,24},{20,28},{24,16},{28,20},{1,9},{5... | collective-permute-start | bytes 1179656 | tf_op jit(solution)/shard_map/ppermute | solution.py:51
  76.3 8.2 %collective-permute-start.19 = (f32[8,256]{1,0:T(8,128)S(1)}, f32[8,256]{1,0:T(8,128)S(1)}, u32[]{:S(2)}, u32[]{:S(2)}) collective-permute-start(f32[8,256]{1,0:T(8,128)S(1)} %hand_on.8.refs_0_), channel_id=1, source_target_pairs={{0,3},{1,2},{2,1},{3,0},{4,7},{5,6},{6,5},{7,4},{8,11},{9,10},{10,... | collective-permute-start | bytes 24584 | tf_op jit(solution)/shard_map/ppermute | solution.py:51
  79.2 5.3 %collective-permute-start.18 = (f32[8,256]{1,0:T(8,128)S(1)}, f32[8,256]{1,0:T(8,128)S(1)}, u32[]{:S(2)}, u32[]{:S(2)}) collective-permute-start(f32[8,256]{1,0:T(8,128)S(1)} %hand_on.8.refs_0_), channel_id=1, source_target_pairs={{0,2},{1,3},{2,0},{3,1},{4,6},{5,7},{6,4},{7,5},{8,10},{9,11},{10,... | collective-permute-start | bytes 24584 | tf_op jit(solution)/shard_map/ppermute | solution.py:51
  79.3 5.1 %collective-permute-start.17 = (f32[8,256]{1,0:T(8,128)S(1)}, f32[8,256]{1,0:T(8,128)S(1)}, u32[]{:S(2)}, u32[]{:S(2)}) collective-permute-start(f32[8,256]{1,0:T(8,128)S(1)} %hand_on.8.refs_0_), channel_id=1, source_target_pairs={{0,1},{1,0},{2,3},{3,2},{4,5},{5,4},{6,7},{7,6},{8,9},{9,8},{10,11... | collective-permute-start | bytes 24584 | tf_op jit(solution)/shard_map/ppermute | solution.py:51
  84.5 1.2 %collective-permute-start.20 = (f32[8,256]{1,0:T(8,128)S(1)}, f32[8,256]{1,0:T(8,128)S(1)}, u32[]{:S(2)}, u32[]{:S(2)}) collective-permute-start(f32[8,256]{1,0:T(8,128)S(1)} %add_add_fusion.2), channel_id=1, source_target_pairs={{0,4},{4,0},{8,12},{12,8},{16,20},{20,16},{24,28},{28,24},{1,5},{5... | collective-permute-start | bytes 24584 | tf_op jit(solution)/shard_map/ppermute | solution.py:51
  85.9 4.5 %collective-permute-start.25 = (f32[8,256]{1,0:T(8,128)S(1)}, f32[8,256]{1,0:T(8,128)S(1)}, u32[]{:S(2)}, u32[]{:S(2)}) collective-permute-start(f32[8,256]{1,0:T(8,128)S(1)} %hand_on.10), channel_id=1, source_target_pairs={{0,24},{4,28},{8,16},{12,20},{16,8},{20,12},{24,0},{28,4},{1,25},{... | collective-permute-start | bytes 24584 | tf_op jit(solution)/shard_map/ppermute | solution.py:51
  87.4 3.7 %collective-permute-start.24 = (f32[8,256]{1,0:T(8,128)S(1)}, f32[8,256]{1,0:T(8,128)S(1)}, u32[]{:S(2)}, u32[]{:S(2)}) collective-permute-start(f32[8,256]{1,0:T(8,128)S(1)} %hand_on.10), channel_id=1, source_target_pairs={{0,16},{4,20},{8,24},{12,28},{16,0},{20,4},{24,8},{28,12},{1,17},{... | collective-permute-start | bytes 24584 | tf_op jit(solution)/shard_map/ppermute | solution.py:51
  88.9 3.7 %collective-permute-start.23 = (f32[8,256]{1,0:T(8,128)S(1)}, f32[8,256]{1,0:T(8,128)S(1)}, u32[]{:S(2)}, u32[]{:S(2)}) collective-permute-start(f32[8,256]{1,0:T(8,128)S(1)} %hand_on.10), channel_id=1, source_target_pairs={{0,8},{4,12},{8,0},{12,4},{16,24},{20,28},{24,16},{28,20},{1,9},{5... | collective-permute-start | bytes 24584 | tf_op jit(solution)/shard_map/ppermute | solution.py:51
  92.6 1.7 %collective-permute-start.27 = (bf16[256,768]{1,0:T(8,128)(2,1)S(1)}, bf16[256,768]{1,0:T(8,128)(2,1)S(1)}, u32[]{:S(2)}, u32[]{:S(2)}) collective-permute-start(bf16[256,768]{1,0:T(8,128)(2,1)S(1)} %hand_on.11.refs_1_), channel_id=1, source_target_pairs={{0,4},{4,0},{8,12},{12,8},{16,20},{20,16},{24,28},{28,24},{1,5},{5... | collective-permute-start | bytes 1179656 | tf_op jit(solution)/shard_map/ppermute | solution.py:51
  92.6 2.3 %collective-permute-start.28 = (bf16[256,768]{1,0:T(8,128)(2,1)S(1)}, bf16[256,768]{1,0:T(8,128)(2,1)S(1)}, u32[]{:S(2)}, u32[]{:S(2)}) collective-permute-start(bf16[256,768]{1,0:T(8,128)(2,1)S(1)} %hand_on.12.refs_3_), channel_id=1, source_target_pairs={{0,4},{4,0},{8,12},{12,8},{16,20},{20,16},{24,28},{28,24},{1,5},{5... | collective-permute-start | bytes 1179656 | tf_op jit(solution)/shard_map/ppermute | solution.py:51
  93.1 11.1 %collective-permute-start.26 = (bf16[128,768]{1,0:T(8,128)(2,1)S(1)}, bf16[128,768]{1,0:T(8,128)(2,1)S(1)}, u32[]{:S(2)}, u32[]{:S(2)}) collective-permute-start(bf16[128,768]{1,0:T(8,128)(2,1)S(1)} %slice.8), channel_id=1, source_target_pairs={{0,16},{4,20},{8,24},{12,28},{16,0},{20,4},{24,8},{28,12},{1,17},{... | collective-permute-start | bytes 589832 | tf_op jit(solution)/shard_map/ppermute | solution.py:51
  93.7 10.5 %collective-permute-start.29 = (bf16[128,768]{1,0:T(8,128)(2,1)S(1)}, bf16[128,768]{1,0:T(8,128)(2,1)S(1)}, u32[]{:S(2)}, u32[]{:S(2)}) collective-permute-start(bf16[128,768]{1,0:T(8,128)(2,1)S(1)} %slice.9), channel_id=1, source_target_pairs={{0,8},{4,12},{8,0},{12,4},{16,24},{20,28},{24,16},{28,20},{1,9},{5... | collective-permute-start | bytes 589832 | tf_op jit(solution)/shard_map/ppermute | solution.py:51
  104.2 1.8 %collective-permute-start.30 = (bf16[256,768]{1,0:T(8,128)(2,1)S(1)}, bf16[256,768]{1,0:T(8,128)(2,1)S(1)}, u32[]{:S(2)}, u32[]{:S(2)}) collective-permute-start(bf16[256,768]{1,0:T(8,128)(2,1)S(1)} %pad_maximum_fusion.refs_1_), channel_id=1, source_target_pairs={{0,4},{4,0},{8,12},{12,8},{16,20},{20,16},{24,28},{28,24},{1,5},{5... | collective-permute-start | bytes 1179656 | tf_op jit(solution)/shard_map/ppermute | solution.py:51

commit v13 on v12

--- a/solution.py
+++ b/solution.py
@@ -615,11 +615,12 @@
     squares = pair_up([hand_on(squares[0], token), *squares[1:]])
     squares = squares + swap(squares, "row", 1)
     squares = hand_on(squares, *blocks.values())
-    squares = pair_up(exchange(squares, "row", chips, 2))
     pairs = {}
     for d in near[1:]:
         block = hand_on(blocks[d], squares)
         pairs[d] = (block, swap(block, "row", 1))
+    squares = pair_up(exchange(squares, "row", chips, 2))
+    pairs = {d: (hand_on(block, squares), partner) for d, (block, partner) in pairs.items()}
     pairs[0] = (share, own_pair)
     h = share.shape[0] // 2
     blocks = {d: pairs[d][0] for d in near}

time: 111 us -> 111 us (level)
  transfers between devices with their start and end apart: 31 -> 31, of which waited for: 14 -> 13; matrix products, arithmetic and copies ran while one was open for 0% -> 0% of each run, Pallas kernels for 37% -> 37%
where the time goes in v13:
time: 111 us
  Pallas kernels  56.1 us (51%)
  starting transfers between devices  32.4 us (29%)
  waiting for transfers between devices  21 us (19%)
  between operations  1.13 us (1%)
    ppermute x31, starting transfers between devices, swap(): lax.ppermute(x, axis, [(i, i ^ d) for i in range(lax.axis_size(axis))])  32.4 us
    ppermute x31, waiting for transfers between devices, swap(): lax.ppermute(x, axis, [(i, i ^ d) for i in range(lax.axis_size(axis))])  21 us
    pallas_call x3, Pallas kernels, results(): pl.pallas_call(functools.partial(result_kernel, pairs, *kinds, len(square...  17.5 us
    pallas_call x2, Pallas kernels, project(): pl.pallas_call(functools.partial(project_kernel, part, depth, width), out...  16.5 us
    pallas_call x1, Pallas kernels, chol_inverse(): pl.pallas_call(chol_inverse_kernel, out_shape=(shape((n, n), f32), pltpu....  13.5 us
    pallas_call x1, Pallas kernels, first_product(): pl.pallas_call(functools.partial(first_kernel, depth, width), out_shape=(...  3.35 us
    pallas_call x2, Pallas kernels, last_product(): pl.pallas_call(functools.partial(last_kernel, depth, width, mine), out_sh...  3.13 us
  transfers between devices with their start and end apart: 31, of which 13 were waited for; matrix products, arithmetic and copies ran while one was open for 0% of the time, Pallas kernels for 37%

profile of v13, /device:TPU:0, one launch (start us, length us, event | category | flops | bytes accessed | tf_op | source)
XLA Modules:
  0.0 110.7 jit_solution(9176284375303265008)
XLA Ops:
  0.6 8.7 %project.2 = (f32[512,6144]{1,0:T(8,128)S(1)}, bf16[256,6144]{1,0:T(8,128)(2,1)S(1)}, f32[256,256]{1,0:T(8,128)S(1)}, bf16[256,256]{1,0:T(8,128)(2,1)S(1)}) custom-call(f32[1024,6144]{1,0:T(8,128)} %mom.3, bf16[1024,6144]{1,0:T(8,128)(2,1)} %grad.3, bf16[256,6144]{1,0:T(8,128)(2,1)} %basis.1), custom_call_target="tpu_custom_call" | custom-call | bytes 37748736 | tf_op jit(solution)/shard_map/project/pallas_call | solution.py:104
  9.3 3.1 %collective-permute-start.2 = (bf16[256,256]{1,0:T(8,128)(2,1)S(1)}, bf16[256,256]{1,0:T(8,128)(2,1)S(1)}, u32[]{:S(2)}, u32[]{:S(2)}) collective-permute-start(bf16[256,256]{1,0:T(8,128)(2,1)S(1)} %get-tuple-element.38.rest_0_), channel_id=1, source_target_pairs={{0,1},{1,0},{2,3},{3,2},{4,5},{5,4},{6,7},{7,6},{8,9},{9,8},{10,11... | collective-permute-start | bytes 393224 | tf_op jit(solution)/shard_map/ppermute | solution.py:51
  12.4 7.8 %project.3 = (f32[512,6144]{1,0:T(8,128)S(1)}, f32[256,256]{1,0:T(8,128)S(1)}, bf16[256,256]{1,0:T(8,128)(2,1)S(1)}) custom-call(f32[1024,6144]{1,0:T(8,128)} %mom.3, bf16[1024,6144]{1,0:T(8,128)(2,1)} %grad.3, bf16[256,6144]{1,0:T(8,128)(2,1)S(1)} %get-tuple-element.37.basis, bf16[256,256]{1,0:T(8,128)(2,1)S(1)} %get-tuple-element.38.rest_0_), custom_call_target="tpu_custom_call" | custom-call | bytes 37748736 | tf_op jit(solution)/shard_map/project/pallas_call | solution.py:104
  20.4 3.1 %collective-permute-start.3 = (bf16[256,128]{1,0:T(8,128)(2,1)S(1)}, bf16[256,128]{1,0:T(8,128)(2,1)S(1)}, u32[]{:S(2)}, u32[]{:S(2)}) collective-permute-start(bf16[256,128]{1,0:T(8,128)(2,1)S(1)} %get-tuple-element.46), channel_id=1, source_target_pairs={{0,2},{1,3},{2,0},{3,1},{4,6},{5,7},{6,4},{7,5},{8,10},{9,11},{10,... | collective-permute-start | bytes 196616 | tf_op jit(solution)/shard_map/ppermute | solution.py:51
  23.4 3.2 %collective-permute-done.received = bf16[256,256]{1,0:T(8,128)(2,1)S(1)} collective-permute-done((bf16[256,256]{1,0:T(8,128)(2,1)S(1)}, bf16[256,256]{1,0:T(8,128)(2,1)S(1)}, u32[]{:S(2)}, u32[]{:S(2)}) %collective-permute-start) | collective-permute-done | bytes 131104 | tf_op jit(solution)/shard_map/ppermute | solution.py:51
  26.7 2.3 %collective-permute-start.1 = (bf16[256,128]{1,0:T(8,128)(2,1)S(1)}, bf16[256,128]{1,0:T(8,128)(2,1)S(1)}, u32[]{:S(2)}, u32[]{:S(2)}) collective-permute-start(bf16[256,128]{1,0:T(8,128)(2,1)S(1)} %get-tuple-element.43), channel_id=1, source_target_pairs={{0,2},{1,3},{2,0},{3,1},{4,6},{5,7},{6,4},{7,5},{8,10},{9,11},{10,... | collective-permute-start | bytes 196616 | tf_op jit(solution)/shard_map/ppermute | solution.py:51
  29.0 2.9 %collective-permute-done.1.received = bf16[256,128]{1,0:T(8,128)(2,1)S(1)} collective-permute-done((bf16[256,128]{1,0:T(8,128)(2,1)S(1)}, bf16[256,128]{1,0:T(8,128)(2,1)S(1)}, u32[]{:S(2)}, u32[]{:S(2)}) %collective-permute-start.1) | collective-permute-done | bytes 65568 | tf_op jit(solution)/shard_map/ppermute | solution.py:51
  32.0 2.5 %collective-permute-start.4 = (bf16[256,256]{1,0:T(8,128)(2,1)S(1)}, bf16[256,256]{1,0:T(8,128)(2,1)S(1)}, u32[]{:S(2)}, u32[]{:S(2)}) collective-permute-start(bf16[256,256]{1,0:T(8,128)(2,1)S(1)} %fold_last.3.rest_0_.refs_0_), channel_id=1, source_target_pairs={{0,2},{1,3},{2,0},{3,1},{4,6},{5,7},{6,4},{7,5},{8,10},{9,11},{10,... | collective-permute-start | bytes 393224 | tf_op jit(solution)/shard_map/ppermute | solution.py:51
  34.5 4.4 %collective-permute-done.4.rest_1_.refs_2_ = bf16[256,256]{1,0:T(8,128)(2,1)S(1)} collective-permute-done((bf16[256,256]{1,0:T(8,128)(2,1)S(1)}, bf16[256,256]{1,0:T(8,128)(2,1)S(1)}, u32[]{:S(2)}, u32[]{:S(2)}) %collective-permute-start.4) | collective-permute-done | bytes 131104 | tf_op jit(solution)/shard_map/ppermute | solution.py:51
  38.8 3.4 %first_product.1 = (f32[256,3072]{1,0:T(8,128)S(1)}, f32[256,3072]{1,0:T(8,128)S(1)}, f32[256,256]{1,0:T(8,128)S(1)}) custom-call(f32[512,6144]{1,0:T(8,128)S(1)} %get-tuple-element.36.buf0, f32[512,6144]{1,0:T(8,128)S(1)} %get-tuple-element.39.buf1, bf16[256,256]{1,0:T(8,128)(2,1)S(1)} %fold_last.3.rest_0_.refs_0_, ...), custom_call_target="tpu_custom_call" | custom-call | bytes 31457280 | tf_op jit(solution)/shard_map/first_product/pallas_call | solution.py:211
  42.2 1.6 %collective-permute-done.6.rest_1_.refs_3_ = bf16[256,256]{1,0:T(8,128)(2,1)S(1)} collective-permute-done((bf16[256,256]{1,0:T(8,128)(2,1)S(1)}, bf16[256,256]{1,0:T(8,128)(2,1)S(1)}, u32[]{:S(2)}, u32[]{:S(2)}) %collective-permute-start.6) | collective-permute-done | bytes 131104 | tf_op jit(solution)/shard_map/ppermute | solution.py:51
  43.8 0.3 gram.1
  44.2 1.6 %other_product.1.refs_0_ = bf16[256,3072]{1,0:T(8,128)(2,1)S(1)} custom-call(f32[512,6144]{1,0:T(8,128)S(1)} %get-tuple-element.36.buf0, f32[512,6144]{1,0:T(8,128)S(1)} %get-tuple-element.39.buf1, f32[256,3072]{1,0:T(8,128)S(1)} %get-tuple-element.53.sums, bf16[256,256]{1,0:T(8,128)(2,1)S(1)} %collective-permute-done.5.rest_0_.refs_1_, ...), custom_call_target="tpu_custom_call" | custom-call | bytes 15728640 | tf_op jit(solution)/shard_map/other_product/pallas_call | solution.py:266
  45.8 0.6 collective-permute-start.12
  46.4 2.4 %collective-permute-start.10 = (f32[128,256]{1,0:T(8,128)S(1)}, f32[128,256]{1,0:T(8,128)S(1)}, u32[]{:S(2)}, u32[]{:S(2)}) collective-permute-start(f32[128,256]{1,0:T(8,128)S(1)} %add.33.refs_1_.rest_2_._), channel_id=1, source_target_pairs={{0,24},{4,28},{8,16},{12,20},{16,8},{20,12},{24,0},{28,4},{1,25},{... | collective-permute-start | bytes 393224 | tf_op jit(solution)/shard_map/ppermute | solution.py:51
  48.8 0.5 collective-permute-start.9
  49.3 0.6 collective-permute-start.8
  49.9 1.6 %mine_product.1.mine = f32[256,3072]{1,0:T(8,128)S(1)} custom-call(f32[512,6144]{1,0:T(8,128)S(1)} %get-tuple-element.36.buf0, f32[512,6144]{1,0:T(8,128)S(1)} %get-tuple-element.39.buf1, f32[256,3072]{1,0:T(8,128)S(1)} %get-tuple-element.52.sums, bf16[256,256]{1,0:T(8,128)(2,1)S(1)} %collective-permute-done.5.rest_0_.refs_1_, ...), custom_call_target="tpu_custom_call" | custom-call | bytes 15728640 | tf_op jit(solution)/shard_map/mine_product/pallas_call | solution.py:266
  51.5 0.3 pair_sum.1
  51.8 1.5 %collective-permute-start.13 = (bf16[256,768]{1,0:T(8,128)(2,1)S(1)}, bf16[256,768]{1,0:T(8,128)(2,1)S(1)}, u32[]{:S(2)}, u32[]{:S(2)}) collective-permute-start(bf16[256,768]{1,0:T(8,128)(2,1)S(1)} %get-tuple-element.55), channel_id=1, source_target_pairs={{0,8},{4,12},{8,0},{12,4},{16,24},{20,28},{24,16},{28,20},{1,9},{5... | collective-permute-start | bytes 1179656 | tf_op jit(solution)/shard_map/ppermute | solution.py:51
  53.3 1.5 %collective-permute-start.14 = (bf16[256,768]{1,0:T(8,128)(2,1)S(1)}, bf16[256,768]{1,0:T(8,128)(2,1)S(1)}, u32[]{:S(2)}, u32[]{:S(2)}) collective-permute-start(bf16[256,768]{1,0:T(8,128)(2,1)S(1)} %get-tuple-element.56), channel_id=1, source_target_pairs={{0,16},{4,20},{8,24},{12,28},{16,0},{20,4},{24,8},{28,12},{1,17},{... | collective-permute-start | bytes 1179656 | tf_op jit(solution)/shard_map/ppermute | solution.py:51
  54.8 1.2 %collective-permute-start.15 = (bf16[256,768]{1,0:T(8,128)(2,1)S(1)}, bf16[256,768]{1,0:T(8,128)(2,1)S(1)}, u32[]{:S(2)}, u32[]{:S(2)}) collective-permute-start(bf16[256,768]{1,0:T(8,128)(2,1)S(1)} %get-tuple-element.57), channel_id=1, source_target_pairs={{0,24},{4,28},{8,16},{12,20},{16,8},{20,12},{24,0},{28,4},{1,25},{... | collective-permute-start | bytes 1179656 | tf_op jit(solution)/shard_map/ppermute | solution.py:51
  56.1 0.4 collective-permute-done.8
  56.6 1.3 %collective-permute-done.11.other = f32[128,256]{1,0:T(8,128)S(1)} collective-permute-done((f32[128,256]{1,0:T(8,128)S(1)}, f32[128,256]{1,0:T(8,128)S(1)}, u32[]{:S(2)}, u32[]{:S(2)}) %collective-permute-start.11) | collective-permute-done | bytes 131104 | tf_op jit(solution)/shard_map/ppermute | solution.py:51
  57.9 13.5 %chol_inverse.1 = (f32[256,256]{1,0:T(8,128)S(1)}, bf16[1024,6144]{1,0:T(8,128)(2,1)S(1)}) custom-call(f32[128,256]{1,0:T(8,128)S(1)} %add_add_fusion.mine, f32[128,256]{1,0:T(8,128)S(1)} %collective-permute-done.11.other, bf16[1024,6144]{1,0:T(8,128)(2,1)} %weight.1), custom_call_target="tpu_custom_call" | custom-call | bytes 33554432 | tf_op jit(solution)/shard_map/chol_inverse/pallas_call | solution.py:353
  71.5 0.9 collective-permute-done.15.refs_2_
  72.4 0.7 share.1
  73.2 1.6 %collective-permute-start.22 = (bf16[256,768]{1,0:T(8,128)(2,1)S(1)}, bf16[256,768]{1,0:T(8,128)(2,1)S(1)}, u32[]{:S(2)}, u32[]{:S(2)}) collective-permute-start(bf16[256,768]{1,0:T(8,128)(2,1)S(1)} %get-tuple-element.59.refs_1_.refs_5_), channel_id=1, source_target_pairs={{0,16},{4,20},{8,24},{12,28},{16,0},{20,4},{24,8},{28,12},{1,17},{... | collective-permute-start | bytes 1179656 | tf_op jit(solution)/shard_map/ppermute | solution.py:51
  74.7 1.5 %collective-permute-start.21 = (bf16[256,768]{1,0:T(8,128)(2,1)S(1)}, bf16[256,768]{1,0:T(8,128)(2,1)S(1)}, u32[]{:S(2)}, u32[]{:S(2)}) collective-permute-start(bf16[256,768]{1,0:T(8,128)(2,1)S(1)} %get-tuple-element.59.refs_1_.refs_5_), channel_id=1, source_target_pairs={{0,8},{4,12},{8,0},{12,4},{16,24},{20,28},{24,16},{28,20},{1,9},{5... | collective-permute-start | bytes 1179656 | tf_op jit(solution)/shard_map/ppermute | solution.py:51
  76.3 2.9 %collective-permute-start.19 = (f32[8,256]{1,0:T(8,128)S(1)}, f32[8,256]{1,0:T(8,128)S(1)}, u32[]{:S(2)}, u32[]{:S(2)}) collective-permute-start(f32[8,256]{1,0:T(8,128)S(1)} %hand_on.10.refs_0_), channel_id=1, source_target_pairs={{0,3},{1,2},{2,1},{3,0},{4,7},{5,6},{6,5},{7,4},{8,11},{9,10},{10,... | collective-permute-start | bytes 24584 | tf_op jit(solution)/shard_map/ppermute | solution.py:51
  79.2 0.1 collective-permute-start.18
  79.3 1.4 %collective-permute-start.17 = (f32[8,256]{1,0:T(8,128)S(1)}, f32[8,256]{1,0:T(8,128)S(1)}, u32[]{:S(2)}, u32[]{:S(2)}) collective-permute-start(f32[8,256]{1,0:T(8,128)S(1)} %hand_on.10.refs_0_), channel_id=1, source_target_pairs={{0,1},{1,0},{2,3},{3,2},{4,5},{5,4},{6,7},{7,6},{8,9},{9,8},{10,11... | collective-permute-start | bytes 24584 | tf_op jit(solution)/shard_map/ppermute | solution.py:51
  80.7 0.6 ortho.1.ortho_ref
  81.3 3.1 %results.3 = (f32[1024,6144]{1,0:T(8,128)}, f32[8,128]{1,0:T(8,128)S(1)}) custom-call(f32[512,6144]{1,0:T(8,128)S(1)} %get-tuple-element.36.buf0, f32[512,6144]{1,0:T(8,128)S(1)} %copy-done.1, bf16[1024,256]{1,0:T(8,128)(2,1)S(1)} %ortho.1.ortho_ref, bf16[1024,6144]{1,0:T(8,128)(2,1)S(1)} %get-tuple-element.51.weight, f32[8,256]{1,0:T(8,128)S(1)} %hand_on.10.refs_0_, ...), custom_call_target="tpu_custom_call" | custom-call | bytes 6291456 | tf_op jit(solution)/shard_map/results/pallas_call | solution.py:525
  84.6 1.2 %collective-permute-done.20 = f32[8,256]{1,0:T(8,128)S(1)} collective-permute-done((f32[8,256]{1,0:T(8,128)S(1)}, f32[8,256]{1,0:T(8,128)S(1)}, u32[]{:S(2)}, u32[]{:S(2)}) %collective-permute-start.20) | collective-permute-done | bytes 8224 | tf_op jit(solution)/shard_map/ppermute | solution.py:51
  85.7 0.2 collective-permute-done.21.refs_1_.refs_0_
  86.0 0.5 collective-permute-start.28
  86.4 1.4 %collective-permute-start.25 = (f32[8,256]{1,0:T(8,128)S(1)}, f32[8,256]{1,0:T(8,128)S(1)}, u32[]{:S(2)}, u32[]{:S(2)}) collective-permute-start(f32[8,256]{1,0:T(8,128)S(1)} %hand_on.12.refs_1_), channel_id=1, source_target_pairs={{0,24},{4,28},{8,16},{12,20},{16,8},{20,12},{24,0},{28,4},{1,25},{... | collective-permute-start | bytes 24584 | tf_op jit(solution)/shard_map/ppermute | solution.py:51
  87.9 1.5 %collective-permute-start.24 = (f32[8,256]{1,0:T(8,128)S(1)}, f32[8,256]{1,0:T(8,128)S(1)}, u32[]{:S(2)}, u32[]{:S(2)}) collective-permute-start(f32[8,256]{1,0:T(8,128)S(1)} %hand_on.12.refs_1_), channel_id=1, source_target_pairs={{0,16},{4,20},{8,24},{12,28},{16,0},{20,4},{24,8},{28,12},{1,17},{... | collective-permute-start | bytes 24584 | tf_op jit(solution)/shard_map/ppermute | solution.py:51
  89.4 0.5 collective-permute-start.23
  89.9 1.1 collective-permute-done.25
  91.0 0.5 collective-permute-done.24
  91.5 1.5 %collective-permute-done.23 = f32[8,256]{1,0:T(8,128)S(1)} collective-permute-done((f32[8,256]{1,0:T(8,128)S(1)}, f32[8,256]{1,0:T(8,128)S(1)}, u32[]{:S(2)}, u32[]{:S(2)}) %collective-permute-start.23) | collective-permute-done | bytes 8224 | tf_op jit(solution)/shard_map/ppermute | solution.py:51
  93.1 0.5 collective-permute-start.26
  93.7 0.6 collective-permute-start.29
  94.3 9.3 %results.4 = (bf16[1024,6144]{1,0:T(8,128)(2,1)}, bf16[256,6144]{1,0:T(8,128)(2,1)}, f32[1024,6144]{1,0:T(8,128)}, f32[8,128]{1,0:T(8,128)S(1)}) custom-call(f32[512,6144]{1,0:T(8,128)S(1)} %get-tuple-element.36.buf0, f32[512,6144]{1,0:T(8,128)S(1)} %copy-done.1, bf16[1024,256]{1,0:T(8,128)(2,1)S(1)} %ortho.1.ortho_ref, ...), custom_call_target="tpu_custom_call", output_to_operand_aliasing={{2}: (11, {})} | custom-call | bytes 37748736 | tf_op jit(solution)/shard_map/results/pallas_call | solution.py:525
  103.8 1.7 %collective-permute-done.30.refs_2_ = bf16[256,768]{1,0:T(8,128)(2,1)S(1)} collective-permute-done((bf16[256,768]{1,0:T(8,128)(2,1)S(1)}, bf16[256,768]{1,0:T(8,128)(2,1)S(1)}, u32[]{:S(2)}, u32[]{:S(2)}) %collective-permute-start.30) | collective-permute-done | bytes 393248 | tf_op jit(solution)/shard_map/ppermute | solution.py:51
  105.5 5.1 %results.5 = (bf16[1024,6144]{1,0:T(8,128)(2,1)}, bf16[256,6144]{1,0:T(8,128)(2,1)}, f32[1024,6144]{1,0:T(8,128)}, f32[8,128]{1,0:T(8,128)}) custom-call(f32[512,6144]{1,0:T(8,128)S(1)} %get-tuple-element.36.buf0, f32[512,6144]{1,0:T(8,128)S(1)} %copy-done.1, ...), custom_call_target="tpu_custom_call", output_to_operand_aliasing={{0}: (7, {}), {1}: (8, {}), {2}: (9, {})} | custom-call | bytes 12582912 | tf_op jit(solution)/shard_map/results/pallas_call | solution.py:525
  (52 shorter events, 0.8 us)
Async XLA Ops:
  9.3 11.0 %collective-permute-start.2 = (bf16[256,256]{1,0:T(8,128)(2,1)S(1)}, bf16[256,256]{1,0:T(8,128)(2,1)S(1)}, u32[]{:S(2)}, u32[]{:S(2)}) collective-permute-start(bf16[256,256]{1,0:T(8,128)(2,1)S(1)} %get-tuple-element.38.rest_0_), channel_id=1, source_target_pairs={{0,1},{1,0},{2,3},{3,2},{4,5},{5,4},{6,7},{7,6},{8,9},{9,8},{10,11... | collective-permute-start | bytes 393224 | tf_op jit(solution)/shard_map/ppermute | solution.py:51
  20.2 29.6 %copy-start = (f32[512,6144]{1,0:T(8,128)}, f32[512,6144]{1,0:T(8,128)S(1)}, u32[]{:S(2)}) copy-start(f32[512,6144]{1,0:T(8,128)S(1)} %get-tuple-element.39.buf1) | copy-start | bytes 37748740
  20.2 6.4 %collective-permute-start = (bf16[256,256]{1,0:T(8,128)(2,1)S(1)}, bf16[256,256]{1,0:T(8,128)(2,1)S(1)}, u32[]{:S(2)}, u32[]{:S(2)}) collective-permute-start(bf16[256,256]{1,0:T(8,128)(2,1)S(1)} %get-tuple-element.41), channel_id=1, source_target_pairs={{0,1},{1,0},{2,3},{3,2},{4,5},{5,4},{6,7},{7,6},{8,9},{9,8},{10,11... | collective-permute-start | bytes 393224 | tf_op jit(solution)/shard_map/ppermute | solution.py:51
  20.4 8.7 %collective-permute-start.3 = (bf16[256,128]{1,0:T(8,128)(2,1)S(1)}, bf16[256,128]{1,0:T(8,128)(2,1)S(1)}, u32[]{:S(2)}, u32[]{:S(2)}) collective-permute-start(bf16[256,128]{1,0:T(8,128)(2,1)S(1)} %get-tuple-element.46), channel_id=1, source_target_pairs={{0,2},{1,3},{2,0},{3,1},{4,6},{5,7},{6,4},{7,5},{8,10},{9,11},{10,... | collective-permute-start | bytes 196616 | tf_op jit(solution)/shard_map/ppermute | solution.py:51
  26.7 5.2 %collective-permute-start.1 = (bf16[256,128]{1,0:T(8,128)(2,1)S(1)}, bf16[256,128]{1,0:T(8,128)(2,1)S(1)}, u32[]{:S(2)}, u32[]{:S(2)}) collective-permute-start(bf16[256,128]{1,0:T(8,128)(2,1)S(1)} %get-tuple-element.43), channel_id=1, source_target_pairs={{0,2},{1,3},{2,0},{3,1},{4,6},{5,7},{6,4},{7,5},{8,10},{9,11},{10,... | collective-permute-start | bytes 196616 | tf_op jit(solution)/shard_map/ppermute | solution.py:51
  32.0 6.9 %collective-permute-start.4 = (bf16[256,256]{1,0:T(8,128)(2,1)S(1)}, bf16[256,256]{1,0:T(8,128)(2,1)S(1)}, u32[]{:S(2)}, u32[]{:S(2)}) collective-permute-start(bf16[256,256]{1,0:T(8,128)(2,1)S(1)} %fold_last.3.rest_0_.refs_0_), channel_id=1, source_target_pairs={{0,2},{1,3},{2,0},{3,1},{4,6},{5,7},{6,4},{7,5},{8,10},{9,11},{10,... | collective-permute-start | bytes 393224 | tf_op jit(solution)/shard_map/ppermute | solution.py:51
  34.5 7.7 %collective-permute-start.5 = (bf16[256,256]{1,0:T(8,128)(2,1)S(1)}, bf16[256,256]{1,0:T(8,128)(2,1)S(1)}, u32[]{:S(2)}, u32[]{:S(2)}) collective-permute-start(bf16[256,256]{1,0:T(8,128)(2,1)S(1)} %fold_last.3.rest_0_.refs_0_), channel_id=1, source_target_pairs={{0,1},{1,0},{2,3},{3,2},{4,5},{5,4},{6,7},{7,6},{8,9},{9,8},{10,11... | collective-permute-start | bytes 393224 | tf_op jit(solution)/shard_map/ppermute | solution.py:51
  38.8 5.0 %collective-permute-start.6 = (bf16[256,256]{1,0:T(8,128)(2,1)S(1)}, bf16[256,256]{1,0:T(8,128)(2,1)S(1)}, u32[]{:S(2)}, u32[]{:S(2)}) collective-permute-start(bf16[256,256]{1,0:T(8,128)(2,1)S(1)} %collective-permute-done.4.rest_1_.refs_2_), channel_id=1, source_target_pairs={{0,1},{1,0},{2,3},{3,2},{4,5},{5,4},{6,7},{7,6},{8,9},{9,8},{10,11... | collective-permute-start | bytes 393224 | tf_op jit(solution)/shard_map/ppermute | solution.py:51
  44.1 1.7 %collective-permute-start.7 = (f32[128,256]{1,0:T(8,128)S(1)}, f32[128,256]{1,0:T(8,128)S(1)}, u32[]{:S(2)}, u32[]{:S(2)}) collective-permute-start(f32[128,256]{1,0:T(8,128)S(1)} %get-tuple-element.49), channel_id=1, source_target_pairs={{0,4},{4,0},{8,12},{12,8},{16,20},{20,16},{24,28},{28,24},{1,5},{5... | collective-permute-start | bytes 393224 | tf_op jit(solution)/shard_map/ppermute | solution.py:51
  45.8 5.6 %collective-permute-start.12 = (bf16[256,3072]{1,0:T(8,128)(2,1)S(1)}, bf16[256,3072]{1,0:T(8,128)(2,1)S(1)}, u32[]{:S(2)}, u32[]{:S(2)}) collective-permute-start(bf16[256,3072]{1,0:T(8,128)(2,1)S(1)} %hand_on.9.rest_3_), channel_id=1, source_target_pairs={{0,4},{4,0},{8,12},{12,8},{16,20},{20,16},{24,28},{28,24},{1,5},{5... | collective-permute-start | bytes 4718600 | tf_op jit(solution)/shard_map/ppermute | solution.py:51
  46.4 8.5 %collective-permute-start.10 = (f32[128,256]{1,0:T(8,128)S(1)}, f32[128,256]{1,0:T(8,128)S(1)}, u32[]{:S(2)}, u32[]{:S(2)}) collective-permute-start(f32[128,256]{1,0:T(8,128)S(1)} %add.33.refs_1_.rest_2_._), channel_id=1, source_target_pairs={{0,24},{4,28},{8,16},{12,20},{16,8},{20,12},{24,0},{28,4},{1,25},{... | collective-permute-start | bytes 393224 | tf_op jit(solution)/shard_map/ppermute | solution.py:51
  48.8 7.3 %collective-permute-start.9 = (f32[128,256]{1,0:T(8,128)S(1)}, f32[128,256]{1,0:T(8,128)S(1)}, u32[]{:S(2)}, u32[]{:S(2)}) collective-permute-start(f32[128,256]{1,0:T(8,128)S(1)} %add.33.refs_1_.rest_2_._), channel_id=1, source_target_pairs={{0,16},{4,20},{8,24},{12,28},{16,0},{20,4},{24,8},{28,12},{1,17},{... | collective-permute-start | bytes 393224 | tf_op jit(solution)/shard_map/ppermute | solution.py:51
  49.3 7.2 %collective-permute-start.8 = (f32[128,256]{1,0:T(8,128)S(1)}, f32[128,256]{1,0:T(8,128)S(1)}, u32[]{:S(2)}, u32[]{:S(2)}) collective-permute-start(f32[128,256]{1,0:T(8,128)S(1)} %add.33.refs_1_.rest_2_._), channel_id=1, source_target_pairs={{0,8},{4,12},{8,0},{12,4},{16,24},{20,28},{24,16},{28,20},{1,9},{5... | collective-permute-start | bytes 393224 | tf_op jit(solution)/shard_map/ppermute | solution.py:51
  51.4 29.9 %copy-start.1 = (f32[512,6144]{1,0:T(8,128)S(1)}, f32[512,6144]{1,0:T(8,128)}, u32[]{:S(2)}) copy-start(f32[512,6144]{1,0:T(8,128)} %copy-done) | copy-start | bytes 37748740
  51.8 19.6 %collective-permute-start.13 = (bf16[256,768]{1,0:T(8,128)(2,1)S(1)}, bf16[256,768]{1,0:T(8,128)(2,1)S(1)}, u32[]{:S(2)}, u32[]{:S(2)}) collective-permute-start(bf16[256,768]{1,0:T(8,128)(2,1)S(1)} %get-tuple-element.55), channel_id=1, source_target_pairs={{0,8},{4,12},{8,0},{12,4},{16,24},{20,28},{24,16},{28,20},{1,9},{5... | collective-permute-start | bytes 1179656 | tf_op jit(solution)/shard_map/ppermute | solution.py:51
  53.3 18.1 %collective-permute-start.14 = (bf16[256,768]{1,0:T(8,128)(2,1)S(1)}, bf16[256,768]{1,0:T(8,128)(2,1)S(1)}, u32[]{:S(2)}, u32[]{:S(2)}) collective-permute-start(bf16[256,768]{1,0:T(8,128)(2,1)S(1)} %get-tuple-element.56), channel_id=1, source_target_pairs={{0,16},{4,20},{8,24},{12,28},{16,0},{20,4},{24,8},{28,12},{1,17},{... | collective-permute-start | bytes 1179656 | tf_op jit(solution)/shard_map/ppermute | solution.py:51
  54.8 17.6 %collective-permute-start.15 = (bf16[256,768]{1,0:T(8,128)(2,1)S(1)}, bf16[256,768]{1,0:T(8,128)(2,1)S(1)}, u32[]{:S(2)}, u32[]{:S(2)}) collective-permute-start(bf16[256,768]{1,0:T(8,128)(2,1)S(1)} %get-tuple-element.57), channel_id=1, source_target_pairs={{0,24},{4,28},{8,16},{12,20},{16,8},{20,12},{24,0},{28,4},{1,25},{... | collective-permute-start | bytes 1179656 | tf_op jit(solution)/shard_map/ppermute | solution.py:51
  56.5 1.4 %collective-permute-start.11 = (f32[128,256]{1,0:T(8,128)S(1)}, f32[128,256]{1,0:T(8,128)S(1)}, u32[]{:S(2)}, u32[]{:S(2)}) collective-permute-start(f32[128,256]{1,0:T(8,128)S(1)} %add_add_fusion.mine), channel_id=1, source_target_pairs={{0,4},{4,0},{8,12},{12,8},{16,20},{20,16},{24,28},{28,24},{1,5},{5... | collective-permute-start | bytes 393224 | tf_op jit(solution)/shard_map/ppermute | solution.py:51
  73.1 3.1 %collective-permute-start.16 = (bf16[256,768]{1,0:T(8,128)(2,1)S(1)}, bf16[256,768]{1,0:T(8,128)(2,1)S(1)}, u32[]{:S(2)}, u32[]{:S(2)}) collective-permute-start(bf16[256,768]{1,0:T(8,128)(2,1)S(1)} %get-tuple-element.59.refs_1_.refs_5_), channel_id=1, source_target_pairs={{0,4},{4,0},{8,12},{12,8},{16,20},{20,16},{24,28},{28,24},{1,5},{5... | collective-permute-start | bytes 1179656 | tf_op jit(solution)/shard_map/ppermute | solution.py:51
  73.2 12.5 %collective-permute-start.22 = (bf16[256,768]{1,0:T(8,128)(2,1)S(1)}, bf16[256,768]{1,0:T(8,128)(2,1)S(1)}, u32[]{:S(2)}, u32[]{:S(2)}) collective-permute-start(bf16[256,768]{1,0:T(8,128)(2,1)S(1)} %get-tuple-element.59.refs_1_.refs_5_), channel_id=1, source_target_pairs={{0,16},{4,20},{8,24},{12,28},{16,0},{20,4},{24,8},{28,12},{1,17},{... | collective-permute-start | bytes 1179656 | tf_op jit(solution)/shard_map/ppermute | solution.py:51
  74.7 11.2 %collective-permute-start.21 = (bf16[256,768]{1,0:T(8,128)(2,1)S(1)}, bf16[256,768]{1,0:T(8,128)(2,1)S(1)}, u32[]{:S(2)}, u32[]{:S(2)}) collective-permute-start(bf16[256,768]{1,0:T(8,128)(2,1)S(1)} %get-tuple-element.59.refs_1_.refs_5_), channel_id=1, source_target_pairs={{0,8},{4,12},{8,0},{12,4},{16,24},{20,28},{24,16},{28,20},{1,9},{5... | collective-permute-start | bytes 1179656 | tf_op jit(solution)/shard_map/ppermute | solution.py:51
  76.3 8.2 %collective-permute-start.19 = (f32[8,256]{1,0:T(8,128)S(1)}, f32[8,256]{1,0:T(8,128)S(1)}, u32[]{:S(2)}, u32[]{:S(2)}) collective-permute-start(f32[8,256]{1,0:T(8,128)S(1)} %hand_on.10.refs_0_), channel_id=1, source_target_pairs={{0,3},{1,2},{2,1},{3,0},{4,7},{5,6},{6,5},{7,4},{8,11},{9,10},{10,... | collective-permute-start | bytes 24584 | tf_op jit(solution)/shard_map/ppermute | solution.py:51
  79.2 5.3 %collective-permute-start.18 = (f32[8,256]{1,0:T(8,128)S(1)}, f32[8,256]{1,0:T(8,128)S(1)}, u32[]{:S(2)}, u32[]{:S(2)}) collective-permute-start(f32[8,256]{1,0:T(8,128)S(1)} %hand_on.10.refs_0_), channel_id=1, source_target_pairs={{0,2},{1,3},{2,0},{3,1},{4,6},{5,7},{6,4},{7,5},{8,10},{9,11},{10,... | collective-permute-start | bytes 24584 | tf_op jit(solution)/shard_map/ppermute | solution.py:51
  79.3 5.1 %collective-permute-start.17 = (f32[8,256]{1,0:T(8,128)S(1)}, f32[8,256]{1,0:T(8,128)S(1)}, u32[]{:S(2)}, u32[]{:S(2)}) collective-permute-start(f32[8,256]{1,0:T(8,128)S(1)} %hand_on.10.refs_0_), channel_id=1, source_target_pairs={{0,1},{1,0},{2,3},{3,2},{4,5},{5,4},{6,7},{7,6},{8,9},{9,8},{10,11... | collective-permute-start | bytes 24584 | tf_op jit(solution)/shard_map/ppermute | solution.py:51
  84.5 1.2 %collective-permute-start.20 = (f32[8,256]{1,0:T(8,128)S(1)}, f32[8,256]{1,0:T(8,128)S(1)}, u32[]{:S(2)}, u32[]{:S(2)}) collective-permute-start(f32[8,256]{1,0:T(8,128)S(1)} %add_add_fusion.2), channel_id=1, source_target_pairs={{0,4},{4,0},{8,12},{12,8},{16,20},{20,16},{24,28},{28,24},{1,5},{5... | collective-permute-start | bytes 24584 | tf_op jit(solution)/shard_map/ppermute | solution.py:51
  85.9 7.2 %collective-permute-start.27 = (bf16[256,768]{1,0:T(8,128)(2,1)S(1)}, bf16[256,768]{1,0:T(8,128)(2,1)S(1)}, u32[]{:S(2)}, u32[]{:S(2)}) collective-permute-start(bf16[256,768]{1,0:T(8,128)(2,1)S(1)} %hand_on.13.refs_0_), channel_id=1, source_target_pairs={{0,4},{4,0},{8,12},{12,8},{16,20},{20,16},{24,28},{28,24},{1,5},{5... | collective-permute-start | bytes 1179656 | tf_op jit(solution)/shard_map/ppermute | solution.py:51
  86.0 7.7 %collective-permute-start.28 = (bf16[256,768]{1,0:T(8,128)(2,1)S(1)}, bf16[256,768]{1,0:T(8,128)(2,1)S(1)}, u32[]{:S(2)}, u32[]{:S(2)}) collective-permute-start(bf16[256,768]{1,0:T(8,128)(2,1)S(1)} %hand_on.15.refs_0_), channel_id=1, source_target_pairs={{0,4},{4,0},{8,12},{12,8},{16,20},{20,16},{24,28},{28,24},{1,5},{5... | collective-permute-start | bytes 1179656 | tf_op jit(solution)/shard_map/ppermute | solution.py:51
  86.4 4.5 %collective-permute-start.25 = (f32[8,256]{1,0:T(8,128)S(1)}, f32[8,256]{1,0:T(8,128)S(1)}, u32[]{:S(2)}, u32[]{:S(2)}) collective-permute-start(f32[8,256]{1,0:T(8,128)S(1)} %hand_on.12.refs_1_), channel_id=1, source_target_pairs={{0,24},{4,28},{8,16},{12,20},{16,8},{20,12},{24,0},{28,4},{1,25},{... | collective-permute-start | bytes 24584 | tf_op jit(solution)/shard_map/ppermute | solution.py:51
  87.9 3.7 %collective-permute-start.24 = (f32[8,256]{1,0:T(8,128)S(1)}, f32[8,256]{1,0:T(8,128)S(1)}, u32[]{:S(2)}, u32[]{:S(2)}) collective-permute-start(f32[8,256]{1,0:T(8,128)S(1)} %hand_on.12.refs_1_), channel_id=1, source_target_pairs={{0,16},{4,20},{8,24},{12,28},{16,0},{20,4},{24,8},{28,12},{1,17},{... | collective-permute-start | bytes 24584 | tf_op jit(solution)/shard_map/ppermute | solution.py:51
  89.4 3.7 %collective-permute-start.23 = (f32[8,256]{1,0:T(8,128)S(1)}, f32[8,256]{1,0:T(8,128)S(1)}, u32[]{:S(2)}, u32[]{:S(2)}) collective-permute-start(f32[8,256]{1,0:T(8,128)S(1)} %hand_on.12.refs_1_), channel_id=1, source_target_pairs={{0,8},{4,12},{8,0},{12,4},{16,24},{20,28},{24,16},{28,20},{1,9},{5... | collective-permute-start | bytes 24584 | tf_op jit(solution)/shard_map/ppermute | solution.py:51
  93.1 10.5 %collective-permute-start.26 = (bf16[128,768]{1,0:T(8,128)(2,1)S(1)}, bf16[128,768]{1,0:T(8,128)(2,1)S(1)}, u32[]{:S(2)}, u32[]{:S(2)}) collective-permute-start(bf16[128,768]{1,0:T(8,128)(2,1)S(1)} %slice.8), channel_id=1, source_target_pairs={{0,16},{4,20},{8,24},{12,28},{16,0},{20,4},{24,8},{28,12},{1,17},{... | collective-permute-start | bytes 589832 | tf_op jit(solution)/shard_map/ppermute | solution.py:51
  93.7 10.0 %collective-permute-start.29 = (bf16[128,768]{1,0:T(8,128)(2,1)S(1)}, bf16[128,768]{1,0:T(8,128)(2,1)S(1)}, u32[]{:S(2)}, u32[]{:S(2)}) collective-permute-start(bf16[128,768]{1,0:T(8,128)(2,1)S(1)} %slice.9), channel_id=1, source_target_pairs={{0,8},{4,12},{8,0},{12,4},{16,24},{20,28},{24,16},{28,20},{1,9},{5... | collective-permute-start | bytes 589832 | tf_op jit(solution)/shard_map/ppermute | solution.py:51
  103.7 1.8 %collective-permute-start.30 = (bf16[256,768]{1,0:T(8,128)(2,1)S(1)}, bf16[256,768]{1,0:T(8,128)(2,1)S(1)}, u32[]{:S(2)}, u32[]{:S(2)}) collective-permute-start(bf16[256,768]{1,0:T(8,128)(2,1)S(1)} %pad_maximum_fusion.refs_1_), channel_id=1, source_target_pairs={{0,4},{4,0},{8,12},{12,8},{16,20},{20,16},{24,28},{28,24},{1,5},{5... | collective-permute-start | bytes 1179656 | tf_op jit(solution)/shard_map/ppermute | solution.py:51
